TPU v7x, 512 devices: a whole 4x4x16 slice. The times are simulated.
512 devices in a mesh: hier: 256 (over x_lo, z, y, core), rep: 2 (over x_hi).
Axes of the slice: x: 4 (x_hi: 2, x_lo: 2; x = x_hi * 2 + x_lo), y: 4, z: 16, core: 2. Of those that a mesh axis runs over, the one named last changes fastest.
Arguments:
- rho_real: float32 [512, 256, 256], P('hier', 'rep'), may hold values from -6 to 6
- rho_imag: float32 [512, 256, 256], P('hier', 'rep'), may hold values from -6 to 6
- ham: bfloat16 [2, 256, 256], replicated, as said below
- couple: bfloat16 [12, 256, 256], replicated, as said below
- rates: float32 [12], replicated, may hold values from 0.1 to 2
- coeff_real: float32 [12], replicated, may hold values from 0.2 to 1.5
- coeff_imag: float32 [12], replicated, may hold values from -1 to 1
- occupation: int32 [512, 12], P('hier'), may hold values from 0 to 2, as said below
- upper: int32 [512, 12], P('hier'), may hold values from -1 to 511, as said below
- lower: int32 [512, 12], P('hier'), may hold values from -1 to 511, as said below
Outputs:
- new_real: float32 [512, 256, 256], P('hier', 'rep')
- new_imag: float32 [512, 256, 256], P('hier', 'rep')
Inputs may be any that keep to these rules, and one draw needn't show every extreme that they name: `occupation`: each row is the multi-index of one matrix. The window holds all tuples base + b, where b is 0 or 1 in each of 9 modes and 0 elsewhere, and base is 1 in one of those modes and 0 elsewhere; bit j of a matrix's index is b in the j-th of those modes, the same assignment for all rows. upper[a, k] is the matrix whose tuple is occupation[a] plus one in mode k, or -1 where that tuple lies outside the window; such a matrix's index differs from a in exactly one bit, and for each bit every matrix finds the matrix across that bit in exactly one of upper or lower. lower[a, k] is the matrix whose tuple is occupation[a] minus one in mode k, or -1 where that tuple lies outside the window; such a matrix's index differs from a in exactly one bit. ham[0] is symmetric and ham[1] antisymmetric. Each couple[k] is symmetric.
All inputs are finite; a program needn't handle non-finite values.
Results may differ from a plain program's by a relative error of at most 0.0055.
Values may be sent and summed in bfloat16 or wider, within the bound.
No kernel may reach another device: no remote copies, remote signals or barrier semaphores. Data moves between devices by JAX's collectives and lax.ppermute only.
A program may use at most 64 MiB of HBM per device.

v0:
```python
import jax
import jax.numpy as jnp
from jax import lax
from jax.sharding import PartitionSpec as P

step_size = 0.1


def swapped(value, axis, distance):
    mask = 2**distance
    pairs = [(source, source ^ mask) for source in range(lax.axis_size(axis))]
    return lax.ppermute(value, axis, pairs)


def coupling_parts(couple_rows, couple_sel, gathered, own_rows, coeff_a, coeff_b):
    left_prod = jnp.einsum(
        "mrl,pmlc->pmrc", couple_rows, gathered, preferred_element_type=jnp.float32
    )
    right_prod = jnp.einsum(
        "pmrl,mlc->pmrc", own_rows, couple_sel, preferred_element_type=jnp.float32
    )
    differ = left_prod - right_prod
    summed = left_prod + right_prod
    weight_a = coeff_a[:, None, None]
    weight_b = coeff_b[:, None, None]
    upward = jnp.stack([differ[1], -differ[0]])
    cross_real = weight_a * differ[0] - weight_b * summed[1]
    cross_imag = weight_a * differ[1] + weight_b * summed[0]
    downward = jnp.stack([cross_imag, -cross_real])
    return (upward, downward)


def local(rho_real, rho_imag, ham, couple, rates, coeff_real, coeff_imag, occupation, upper, lower):
    row_count = rho_real.shape[1]
    per_device = rho_real.shape[0]
    row_start = lax.axis_index("rep") * row_count
    ham_rows = lax.dynamic_slice_in_dim(ham, row_start, row_count, 1)
    own_index = per_device * lax.axis_index("hier") + jnp.arange(per_device, dtype=jnp.int32)
    occ_float = occupation.astype(jnp.float32)
    decay_rate = jnp.dot(occ_float, rates)
    hier_bits = lax.axis_size("hier").bit_length() - 1
    tables = []
    for bit_pos in range(hier_bits + 1):
        partner = jnp.bitwise_xor(own_index, jnp.int32(1 << bit_pos))
        is_above = upper == partner[:, None]
        is_below = lower == partner[:, None]
        mode_sel = jnp.logical_or(is_above, is_below).astype(jnp.float32)
        couple_sel = jnp.einsum(
            "mk,kij->mij", mode_sel.astype(jnp.bfloat16), couple, preferred_element_type=jnp.float32
        ).astype(jnp.bfloat16)
        couple_rows = lax.dynamic_slice_in_dim(couple_sel, row_start, row_count, 1)
        coeff_a = jnp.dot(mode_sel, coeff_real)
        coeff_b = jnp.dot(mode_sel, coeff_imag)
        sender_up = jnp.any(is_below, axis=1)
        receiver_up = jnp.any(is_above, axis=1)
        factor = jnp.sum(is_above.astype(jnp.float32), axis=1) + jnp.sum(
            is_below.astype(jnp.float32) * occ_float, axis=1
        )
        tables.append((couple_rows, couple_sel, coeff_a, coeff_b, sender_up, receiver_up, factor))

    def derivative(states):
        rounded = states.astype(jnp.bfloat16)
        gathered = lax.all_gather(rounded, "rep", axis=2, tiled=True)
        ham_left = jnp.einsum(
            "hrl,pmlc->hpmrc", ham_rows, gathered, preferred_element_type=jnp.float32
        )
        ham_right = jnp.einsum("pmrl,hlc->hpmrc", rounded, ham, preferred_element_type=jnp.float32)
        comm_real = ham_left[0, 0] - ham_left[1, 1] - (ham_right[0, 0] - ham_right[1, 1])
        comm_imag = ham_left[0, 1] + ham_left[1, 0] - (ham_right[1, 0] + ham_right[0, 1])
        running = jnp.stack([comm_imag, -comm_real]) - decay_rate[None, :, None, None] * states
        for bit_pos in range(hier_bits + 1):
            couple_rows, couple_sel, coeff_a, coeff_b, sender_up, receiver_up, factor = tables[
                bit_pos
            ]
            if bit_pos == 0:
                partner_whole = gathered[:, ::-1]
            else:
                partner_whole = swapped(gathered, "hier", bit_pos - 1)
            partner_rows = lax.dynamic_slice_in_dim(partner_whole, row_start, row_count, 2)
            upward, downward = coupling_parts(
                couple_rows, couple_sel, partner_whole, partner_rows, coeff_a, coeff_b
            )
            incoming = jnp.where(receiver_up[None, :, None, None], upward, downward).astype(
                jnp.bfloat16
            )
            running = running + factor[None, :, None, None] * incoming.astype(jnp.float32)
        return running

    states = jnp.stack([rho_real, rho_imag])
    first_slope = derivative(states)
    middle = states + step_size * first_slope
    second = derivative(middle)
    result = states + 0.5 * step_size * (first_slope + second)
    return (result[0], result[1])


def solution(mesh):
    placed = (
        P("hier", "rep", None),
        P("hier", "rep", None),
        P(),
        P(),
        P(),
        P(),
        P(),
        P("hier", None),
        P("hier", None),
        P("hier", None),
    )
    return jax.shard_map(
        local,
        mesh=mesh,
        in_specs=placed,
        out_specs=(P("hier", "rep", None), P("hier", "rep", None)),
        check_vma=False,
    )
```

profile of v0, /device:TPU:1, one launch (start us, length us, event | category | flops | bytes accessed | tf_op | source)
XLA Modules:
  0.0 326.1 jit_solution(1401595734811137297)
XLA Ops:
  3.0 8.1 %all_gather.6 = bf16[2,2,256,256]{2,3,1,0:T(8,128)(2,1)S(1)} all-gather(bf16[2,2,128,256]{2,3,1,0:T(8,128)(2,1)S(1)} %fusion.191), channel_id=1, replica_groups=mesh['hier'=256,'rep'=2] {'rep'}, dimensions={2}, use_global_device_ids=true | all-gather | bytes 786432 | tf_op jit(solution)/shard_map/all_gather | solution.py:63
  11.0 9.3 %collective-permute-start = (bf16[2,2,256,256]{2,3,1,0:T(8,128)(2,1)S(1)}, bf16[2,2,256,256]{2,3,1,0:T(8,128)(2,1)}, u32[]{:S(2)}, u32[]{:S(2)}) collective-permute-start(bf16[2,2,256,256]{2,3,1,0:T(8,128)(2,1)S(1)} %all_gather.6), channel_id=1, source_target_pairs={{0,2},{2,0},{4,6},{6,4},{8,10},{10,8},{12,14},{14,12},{16,18},{18,... | collective-permute-start | bytes 1572872 | tf_op jit(solution)/shard_map/ppermute | solution.py:12
  20.4 1.9 collective-permute-start.1
  22.3 2.1 collective-permute-start.2
  24.4 3.5 %collective-permute-start.3 = (bf16[2,2,256,256]{2,3,1,0:T(8,128)(2,1)S(1)}, bf16[2,2,256,256]{2,3,1,0:T(8,128)(2,1)}, u32[]{:S(2)}, u32[]{:S(2)}) collective-permute-start(bf16[2,2,256,256]{2,3,1,0:T(8,128)(2,1)S(1)} %all_gather.6), channel_id=1, source_target_pairs={{0,16},{2,18},{4,20},{6,22},{8,24},{10,26},{12,28},{14,30},{16,0},... | collective-permute-start | bytes 1572872 | tf_op jit(solution)/shard_map/ppermute | solution.py:12
  28.0 4.9 %collective-permute-start.4 = (bf16[2,2,256,256]{2,3,1,0:T(8,128)(2,1)S(1)}, bf16[2,2,256,256]{2,3,1,0:T(8,128)(2,1)}, u32[]{:S(2)}, u32[]{:S(2)}) collective-permute-start(bf16[2,2,256,256]{2,3,1,0:T(8,128)(2,1)S(1)} %all_gather.6), channel_id=1, source_target_pairs={{0,32},{2,34},{4,36},{6,38},{8,40},{10,42},{12,44},{14,46},{16,48}... | collective-permute-start | bytes 1572872 | tf_op jit(solution)/shard_map/ppermute | solution.py:12
  54.9 1.7 fusion.18
  56.6 1.8 copy.21
  61.3 1.7 fusion.36
  63.0 1.8 copy.63
  64.8 1.6 constant_dynamic-slice_fusion.2
  67.7 1.7 fusion.39
  69.5 1.8 copy.70
  71.3 1.6 constant_dynamic-slice_fusion.1
  74.3 1.7 fusion.42
  76.0 2.0 copy.77
  91.1 8.8 %collective-permute-start.5 = (bf16[2,2,256,256]{2,3,1,0:T(8,128)(2,1)S(1)}, bf16[2,2,256,256]{2,3,1,0:T(8,128)(2,1)S(1)}, u32[]{:S(2)}, u32[]{:S(2)}) collective-permute-start(bf16[2,2,256,256]{2,3,1,0:T(8,128)(2,1)S(1)} %all_gather.6), channel_id=1, source_target_pairs={{0,64},{2,66},{4,68},{6,70},{8,72},{10,74},{12,76},{14,78},{16,80}... | collective-permute-start | bytes 1572872 | tf_op jit(solution)/shard_map/ppermute | solution.py:12
  102.7 7.9 %collective-permute-start.6 = (bf16[2,2,256,256]{2,3,1,0:T(8,128)(2,1)S(1)}, bf16[2,2,256,256]{2,3,1,0:T(8,128)(2,1)S(1)}, u32[]{:S(2)}, u32[]{:S(2)}) collective-permute-start(bf16[2,2,256,256]{2,3,1,0:T(8,128)(2,1)S(1)} %all_gather.6), channel_id=1, source_target_pairs={{0,128},{2,130},{4,132},{6,134},{8,136},{10,138},{12,140},{14,142}... | collective-permute-start | bytes 1572872 | tf_op jit(solution)/shard_map/ppermute | solution.py:12
  113.5 3.1 collective-permute-start.7
  125.1 65.3 %collective-permute-done.5 = bf16[2,2,256,256]{2,3,1,0:T(8,128)(2,1)S(1)} collective-permute-done((bf16[2,2,256,256]{2,3,1,0:T(8,128)(2,1)S(1)}, bf16[2,2,256,256]{2,3,1,0:T(8,128)(2,1)S(1)}, u32[]{:S(2)}, u32[]{:S(2)}) %collective-permute-start.5) | collective-permute-done | bytes 524320 | tf_op jit(solution)/shard_map/ppermute | solution.py:12
  193.8 2.2 fusion.86
  196.0 9.5 %all_gather.7 = bf16[2,2,256,256]{2,3,1,0:T(8,128)(2,1)S(1)} all-gather(bf16[2,2,128,256]{2,3,1,0:T(8,128)(2,1)S(1)} %get-tuple-element.13), channel_id=1, replica_groups=mesh['hier'=256,'rep'=2] {'rep'}, dimensions={2}, use_global_device_ids=true | all-gather | bytes 786432 | tf_op jit(solution)/shard_map/all_gather | solution.py:63
  205.5 3.4 %collective-permute-start.8 = (bf16[2,2,256,256]{2,3,1,0:T(8,128)(2,1)S(1)}, bf16[2,2,256,256]{2,3,1,0:T(8,128)(2,1)S(1)}, u32[]{:S(2)}, u32[]{:S(2)}) collective-permute-start(bf16[2,2,256,256]{2,3,1,0:T(8,128)(2,1)S(1)} %all_gather.7), channel_id=1, source_target_pairs={{0,2},{2,0},{4,6},{6,4},{8,10},{10,8},{12,14},{14,12},{16,18},{18,... | collective-permute-start | bytes 1572872 | tf_op jit(solution)/shard_map/ppermute | solution.py:12
  209.0 1.9 collective-permute-start.9
  210.9 3.3 %collective-permute-start.10 = (bf16[2,2,256,256]{2,3,1,0:T(8,128)(2,1)S(1)}, bf16[2,2,256,256]{2,3,1,0:T(8,128)(2,1)S(1)}, u32[]{:S(2)}, u32[]{:S(2)}) collective-permute-start(bf16[2,2,256,256]{2,3,1,0:T(8,128)(2,1)S(1)} %all_gather.7), channel_id=1, source_target_pairs={{0,8},{2,10},{4,12},{6,14},{8,0},{10,2},{12,4},{14,6},{16,24},{18,... | collective-permute-start | bytes 1572872 | tf_op jit(solution)/shard_map/ppermute | solution.py:12
  214.2 1.9 collective-permute-start.11
  216.1 1.9 collective-permute-start.12
  221.6 6.5 %collective-permute-start.13 = (bf16[2,2,256,256]{2,3,1,0:T(8,128)(2,1)S(1)}, bf16[2,2,256,256]{2,3,1,0:T(8,128)(2,1)S(1)}, u32[]{:S(2)}, u32[]{:S(2)}) collective-permute-start(bf16[2,2,256,256]{2,3,1,0:T(8,128)(2,1)S(1)} %all_gather.7), channel_id=1, source_target_pairs={{0,64},{2,66},{4,68},{6,70},{8,72},{10,74},{12,76},{14,78},{16,80}... | collective-permute-start | bytes 1572872 | tf_op jit(solution)/shard_map/ppermute | solution.py:12
  228.9 10.3 %collective-permute-start.14 = (bf16[2,2,256,256]{2,3,1,0:T(8,128)(2,1)S(1)}, bf16[2,2,256,256]{2,3,1,0:T(8,128)(2,1)S(1)}, u32[]{:S(2)}, u32[]{:S(2)}) collective-permute-start(bf16[2,2,256,256]{2,3,1,0:T(8,128)(2,1)S(1)} %all_gather.7), channel_id=1, source_target_pairs={{0,128},{2,130},{4,132},{6,134},{8,136},{10,138},{12,140},{14,142}... | collective-permute-start | bytes 1572872 | tf_op jit(solution)/shard_map/ppermute | solution.py:12
  240.1 3.3 %collective-permute-start.15 = (bf16[2,2,256,256]{2,3,1,0:T(8,128)(2,1)S(1)}, bf16[2,2,256,256]{2,3,1,0:T(8,128)(2,1)S(1)}, u32[]{:S(2)}, u32[]{:S(2)}) collective-permute-start(bf16[2,2,256,256]{2,3,1,0:T(8,128)(2,1)S(1)} %all_gather.7), channel_id=1, source_target_pairs={{0,256},{2,258},{4,260},{6,262},{8,264},{10,266},{12,268},{14,270}... | collective-permute-start | bytes 1572872 | tf_op jit(solution)/shard_map/ppermute | solution.py:12
  245.4 47.6 %collective-permute-done.12 = bf16[2,2,256,256]{2,3,1,0:T(8,128)(2,1)S(1)} collective-permute-done((bf16[2,2,256,256]{2,3,1,0:T(8,128)(2,1)S(1)}, bf16[2,2,256,256]{2,3,1,0:T(8,128)(2,1)S(1)}, u32[]{:S(2)}, u32[]{:S(2)}) %collective-permute-start.12) | collective-permute-done | bytes 524320 | tf_op jit(solution)/shard_map/ppermute | solution.py:12
  293.8 25.3 %collective-permute-done.13 = bf16[2,2,256,256]{2,3,1,0:T(8,128)(2,1)S(1)} collective-permute-done((bf16[2,2,256,256]{2,3,1,0:T(8,128)(2,1)S(1)}, bf16[2,2,256,256]{2,3,1,0:T(8,128)(2,1)S(1)}, u32[]{:S(2)}, u32[]{:S(2)}) %collective-permute-start.13) | collective-permute-done | bytes 524320 | tf_op jit(solution)/shard_map/ppermute | solution.py:12
  (412 shorter events, 73.3 us)
Async XLA Ops:
  11.0 80.1 %collective-permute-start = (bf16[2,2,256,256]{2,3,1,0:T(8,128)(2,1)S(1)}, bf16[2,2,256,256]{2,3,1,0:T(8,128)(2,1)}, u32[]{:S(2)}, u32[]{:S(2)}) collective-permute-start(bf16[2,2,256,256]{2,3,1,0:T(8,128)(2,1)S(1)} %all_gather.6), channel_id=1, source_target_pairs={{0,2},{2,0},{4,6},{6,4},{8,10},{10,8},{12,14},{14,12},{16,18},{18,... | collective-permute-start | bytes 1572872 | tf_op jit(solution)/shard_map/ppermute | solution.py:12
  20.4 82.4 %collective-permute-start.1 = (bf16[2,2,256,256]{2,3,1,0:T(8,128)(2,1)S(1)}, bf16[2,2,256,256]{2,3,1,0:T(8,128)(2,1)}, u32[]{:S(2)}, u32[]{:S(2)}) collective-permute-start(bf16[2,2,256,256]{2,3,1,0:T(8,128)(2,1)S(1)} %all_gather.6), channel_id=1, source_target_pairs={{0,4},{2,6},{4,0},{6,2},{8,12},{10,14},{12,8},{14,10},{16,20},{18,... | collective-permute-start | bytes 1572872 | tf_op jit(solution)/shard_map/ppermute | solution.py:12
  22.3 91.2 %collective-permute-start.2 = (bf16[2,2,256,256]{2,3,1,0:T(8,128)(2,1)S(1)}, bf16[2,2,256,256]{2,3,1,0:T(8,128)(2,1)}, u32[]{:S(2)}, u32[]{:S(2)}) collective-permute-start(bf16[2,2,256,256]{2,3,1,0:T(8,128)(2,1)S(1)} %all_gather.6), channel_id=1, source_target_pairs={{0,8},{2,10},{4,12},{6,14},{8,0},{10,2},{12,4},{14,6},{16,24},{18,... | collective-permute-start | bytes 1572872 | tf_op jit(solution)/shard_map/ppermute | solution.py:12
  24.4 95.1 %collective-permute-start.3 = (bf16[2,2,256,256]{2,3,1,0:T(8,128)(2,1)S(1)}, bf16[2,2,256,256]{2,3,1,0:T(8,128)(2,1)}, u32[]{:S(2)}, u32[]{:S(2)}) collective-permute-start(bf16[2,2,256,256]{2,3,1,0:T(8,128)(2,1)S(1)} %all_gather.6), channel_id=1, source_target_pairs={{0,16},{2,18},{4,20},{6,22},{8,24},{10,26},{12,28},{14,30},{16,0},... | collective-permute-start | bytes 1572872 | tf_op jit(solution)/shard_map/ppermute | solution.py:12
  28.0 94.3 %collective-permute-start.4 = (bf16[2,2,256,256]{2,3,1,0:T(8,128)(2,1)S(1)}, bf16[2,2,256,256]{2,3,1,0:T(8,128)(2,1)}, u32[]{:S(2)}, u32[]{:S(2)}) collective-permute-start(bf16[2,2,256,256]{2,3,1,0:T(8,128)(2,1)S(1)} %all_gather.6), channel_id=1, source_target_pairs={{0,32},{2,34},{4,36},{6,38},{8,40},{10,42},{12,44},{14,46},{16,48}... | collective-permute-start | bytes 1572872 | tf_op jit(solution)/shard_map/ppermute | solution.py:12
  79.8 113.6 %copy-start.52 = (f32[2]{0:T(128)}, f32[2]{0:T(128)S(1)}, u32[]{:S(2)}) copy-start(f32[2]{0:T(128)S(1)} %convolution_bitcast_fusion.40) | copy-start | bytes 28
  80.6 112.8 %copy-start.54 = (f32[2]{0:T(128)}, f32[2]{0:T(128)S(1)}, u32[]{:S(2)}) copy-start(f32[2]{0:T(128)S(1)} %convolution_bitcast_fusion.41) | copy-start | bytes 28
  89.2 104.4 %copy-start.48 = (f32[2]{0:T(128)}, f32[2]{0:T(128)S(1)}, u32[]{:S(2)}) copy-start(f32[2]{0:T(128)S(1)} %convolution_bitcast_fusion.58) | copy-start | bytes 28
  89.4 104.2 %copy-start.50 = (f32[2]{0:T(128)}, f32[2]{0:T(128)S(1)}, u32[]{:S(2)}) copy-start(f32[2]{0:T(128)S(1)} %add.365) | copy-start | bytes 28
  89.5 104.2 %copy-start.56 = (f32[2]{0:T(128)}, f32[2]{0:T(128)S(1)}, u32[]{:S(2)}) copy-start(f32[2]{0:T(128)S(1)} %add.369) | copy-start | bytes 28
  89.5 104.1 %copy-start.58 = (f32[2]{0:T(128)}, f32[2]{0:T(128)S(1)}, u32[]{:S(2)}) copy-start(f32[2]{0:T(128)S(1)} %add.373) | copy-start | bytes 28
  89.5 104.1 %copy-start.60 = (f32[2]{0:T(128)}, f32[2]{0:T(128)S(1)}, u32[]{:S(2)}) copy-start(f32[2]{0:T(128)S(1)} %add.377) | copy-start | bytes 28
  89.6 104.1 %copy-start.62 = (f32[2]{0:T(128)}, f32[2]{0:T(128)S(1)}, u32[]{:S(2)}) copy-start(f32[2]{0:T(128)S(1)} %add.381) | copy-start | bytes 28
  89.6 104.1 %copy-start.64 = (f32[2]{0:T(128)}, f32[2]{0:T(128)S(1)}, u32[]{:S(2)}) copy-start(f32[2]{0:T(128)S(1)} %add.385) | copy-start | bytes 28
  89.6 104.0 %copy-start.66 = (f32[2]{0:T(128)}, f32[2]{0:T(128)S(1)}, u32[]{:S(2)}) copy-start(f32[2]{0:T(128)S(1)} %add.389) | copy-start | bytes 28
  89.7 104.0 %copy-start.68 = (f32[2]{0:T(128)}, f32[2]{0:T(128)S(1)}, u32[]{:S(2)}) copy-start(f32[2]{0:T(128)S(1)} %add.393) | copy-start | bytes 28
  89.7 104.0 %copy-start.74 = (f32[2]{0:T(128)}, f32[2]{0:T(128)S(1)}, u32[]{:S(2)}) copy-start(f32[2]{0:T(128)S(1)} %add.397) | copy-start | bytes 28
  91.1 99.3 %collective-permute-start.5 = (bf16[2,2,256,256]{2,3,1,0:T(8,128)(2,1)S(1)}, bf16[2,2,256,256]{2,3,1,0:T(8,128)(2,1)S(1)}, u32[]{:S(2)}, u32[]{:S(2)}) collective-permute-start(bf16[2,2,256,256]{2,3,1,0:T(8,128)(2,1)S(1)} %all_gather.6), channel_id=1, source_target_pairs={{0,64},{2,66},{4,68},{6,70},{8,72},{10,74},{12,76},{14,78},{16,80}... | collective-permute-start | bytes 1572872 | tf_op jit(solution)/shard_map/ppermute | solution.py:12
  102.7 88.4 %collective-permute-start.6 = (bf16[2,2,256,256]{2,3,1,0:T(8,128)(2,1)S(1)}, bf16[2,2,256,256]{2,3,1,0:T(8,128)(2,1)S(1)}, u32[]{:S(2)}, u32[]{:S(2)}) collective-permute-start(bf16[2,2,256,256]{2,3,1,0:T(8,128)(2,1)S(1)} %all_gather.6), channel_id=1, source_target_pairs={{0,128},{2,130},{4,132},{6,134},{8,136},{10,138},{12,140},{14,142}... | collective-permute-start | bytes 1572872 | tf_op jit(solution)/shard_map/ppermute | solution.py:12
  113.5 78.9 %collective-permute-start.7 = (bf16[2,2,256,256]{2,3,1,0:T(8,128)(2,1)S(1)}, bf16[2,2,256,256]{2,3,1,0:T(8,128)(2,1)S(1)}, u32[]{:S(2)}, u32[]{:S(2)}) collective-permute-start(bf16[2,2,256,256]{2,3,1,0:T(8,128)(2,1)S(1)} %all_gather.6), channel_id=1, source_target_pairs={{0,256},{2,258},{4,260},{6,262},{8,264},{10,266},{12,268},{14,270}... | collective-permute-start | bytes 1572872 | tf_op jit(solution)/shard_map/ppermute | solution.py:12
  123.5 66.9 %copy-start.7 = (bf16[2,256,256]{1,2,0:T(8,128)(2,1)S(1)}, bf16[2,256,256]{1,2,0:T(8,128)(2,1)}, u32[]{:S(2)}) copy-start(bf16[2,256,256]{1,2,0:T(8,128)(2,1)} %copy.63) | copy-start | bytes 786436
  124.9 65.8 %copy-start.24 = (bf16[2,128,256]{2,0,1:T(2,128)(2,1)S(1)}, bf16[2,128,256]{2,0,1:T(2,128)(2,1)}, u32[]{:S(2)}) copy-start(bf16[2,128,256]{2,0,1:T(2,128)(2,1)} %constant_dynamic-slice_fusion.2) | copy-start | bytes 393220
  125.1 65.9 %copy-start.76 = (f32[2]{0:T(128)S(1)}, f32[2]{0:T(128)}, u32[]{:S(2)}) copy-start(f32[2]{0:T(128)} %convolution_bitcast_fusion.44) | copy-start | bytes 28
  125.1 65.9 %copy-start.78 = (f32[2]{0:T(128)S(1)}, f32[2]{0:T(128)}, u32[]{:S(2)}) copy-start(f32[2]{0:T(128)} %convolution_bitcast_fusion.45) | copy-start | bytes 28
  205.5 16.1 %collective-permute-start.8 = (bf16[2,2,256,256]{2,3,1,0:T(8,128)(2,1)S(1)}, bf16[2,2,256,256]{2,3,1,0:T(8,128)(2,1)S(1)}, u32[]{:S(2)}, u32[]{:S(2)}) collective-permute-start(bf16[2,2,256,256]{2,3,1,0:T(8,128)(2,1)S(1)} %all_gather.7), channel_id=1, source_target_pairs={{0,2},{2,0},{4,6},{6,4},{8,10},{10,8},{12,14},{14,12},{16,18},{18,... | collective-permute-start | bytes 1572872 | tf_op jit(solution)/shard_map/ppermute | solution.py:12
  209.0 19.9 %collective-permute-start.9 = (bf16[2,2,256,256]{2,3,1,0:T(8,128)(2,1)S(1)}, bf16[2,2,256,256]{2,3,1,0:T(8,128)(2,1)S(1)}, u32[]{:S(2)}, u32[]{:S(2)}) collective-permute-start(bf16[2,2,256,256]{2,3,1,0:T(8,128)(2,1)S(1)} %all_gather.7), channel_id=1, source_target_pairs={{0,4},{2,6},{4,0},{6,2},{8,12},{10,14},{12,8},{14,10},{16,20},{18,... | collective-permute-start | bytes 1572872 | tf_op jit(solution)/shard_map/ppermute | solution.py:12
  210.9 29.2 %collective-permute-start.10 = (bf16[2,2,256,256]{2,3,1,0:T(8,128)(2,1)S(1)}, bf16[2,2,256,256]{2,3,1,0:T(8,128)(2,1)S(1)}, u32[]{:S(2)}, u32[]{:S(2)}) collective-permute-start(bf16[2,2,256,256]{2,3,1,0:T(8,128)(2,1)S(1)} %all_gather.7), channel_id=1, source_target_pairs={{0,8},{2,10},{4,12},{6,14},{8,0},{10,2},{12,4},{14,6},{16,24},{18,... | collective-permute-start | bytes 1572872 | tf_op jit(solution)/shard_map/ppermute | solution.py:12
  214.2 30.0 %collective-permute-start.11 = (bf16[2,2,256,256]{2,3,1,0:T(8,128)(2,1)S(1)}, bf16[2,2,256,256]{2,3,1,0:T(8,128)(2,1)S(1)}, u32[]{:S(2)}, u32[]{:S(2)}) collective-permute-start(bf16[2,2,256,256]{2,3,1,0:T(8,128)(2,1)S(1)} %all_gather.7), channel_id=1, source_target_pairs={{0,16},{2,18},{4,20},{6,22},{8,24},{10,26},{12,28},{14,30},{16,0},... | collective-permute-start | bytes 1572872 | tf_op jit(solution)/shard_map/ppermute | solution.py:12
  216.1 76.9 %collective-permute-start.12 = (bf16[2,2,256,256]{2,3,1,0:T(8,128)(2,1)S(1)}, bf16[2,2,256,256]{2,3,1,0:T(8,128)(2,1)S(1)}, u32[]{:S(2)}, u32[]{:S(2)}) collective-permute-start(bf16[2,2,256,256]{2,3,1,0:T(8,128)(2,1)S(1)} %all_gather.7), channel_id=1, source_target_pairs={{0,32},{2,34},{4,36},{6,38},{8,40},{10,42},{12,44},{14,46},{16,48}... | collective-permute-start | bytes 1572872 | tf_op jit(solution)/shard_map/ppermute | solution.py:12
  221.6 97.4 %collective-permute-start.13 = (bf16[2,2,256,256]{2,3,1,0:T(8,128)(2,1)S(1)}, bf16[2,2,256,256]{2,3,1,0:T(8,128)(2,1)S(1)}, u32[]{:S(2)}, u32[]{:S(2)}) collective-permute-start(bf16[2,2,256,256]{2,3,1,0:T(8,128)(2,1)S(1)} %all_gather.7), channel_id=1, source_target_pairs={{0,64},{2,66},{4,68},{6,70},{8,72},{10,74},{12,76},{14,78},{16,80}... | collective-permute-start | bytes 1572872 | tf_op jit(solution)/shard_map/ppermute | solution.py:12
  228.9 90.9 %collective-permute-start.14 = (bf16[2,2,256,256]{2,3,1,0:T(8,128)(2,1)S(1)}, bf16[2,2,256,256]{2,3,1,0:T(8,128)(2,1)S(1)}, u32[]{:S(2)}, u32[]{:S(2)}) collective-permute-start(bf16[2,2,256,256]{2,3,1,0:T(8,128)(2,1)S(1)} %all_gather.7), channel_id=1, source_target_pairs={{0,128},{2,130},{4,132},{6,134},{8,136},{10,138},{12,140},{14,142}... | collective-permute-start | bytes 1572872 | tf_op jit(solution)/shard_map/ppermute | solution.py:12
  240.1 81.0 %collective-permute-start.15 = (bf16[2,2,256,256]{2,3,1,0:T(8,128)(2,1)S(1)}, bf16[2,2,256,256]{2,3,1,0:T(8,128)(2,1)S(1)}, u32[]{:S(2)}, u32[]{:S(2)}) collective-permute-start(bf16[2,2,256,256]{2,3,1,0:T(8,128)(2,1)S(1)} %all_gather.7), channel_id=1, source_target_pairs={{0,256},{2,258},{4,260},{6,262},{8,264},{10,266},{12,268},{14,270}... | collective-permute-start | bytes 1572872 | tf_op jit(solution)/shard_map/ppermute | solution.py:12
  (114 other events, 906.6 us)
where the time goes:
time: 329 us; the launch traced here: 326 us
  waiting for transfers between devices  138 us (42%)
  starting transfers between devices  74.3 us (23%)
  matrix products  46.9 us (14%)
  local copies, waits for them, and re-layouts  30.7 us (9%)
  blocking collectives  17.6 us (5%)
  other arithmetic  15.3 us (5%)
    ppermute x16, waiting for transfers between devices, swapped(): return lax.ppermute(value, axis, pairs)  138 us
    ppermute x16, starting transfers between devices, swapped(): return lax.ppermute(value, axis, pairs)  74.3 us
    all_gather x2, blocking collectives, derivative(): gathered = lax.all_gather(rounded, 'rep', axis=2, tiled=True)  17.6 us
    dot_general x9, matrix products, local(): jnp.einsum('mk,kij->mij', mode_sel.astype(jnp.bfloat16), couple, preferre...  11.9 us
    convert_element_type x9, local copies, waits for them, and re-layouts, local(): couple_sel = jnp.einsum('mk,kij->mij', mode_sel.astype(jnp.bfloat16), cou...  11.9 us
    dot_general x18, matrix products, coupling_parts(): jnp.einsum('mrl,pmlc->pmrc', couple_rows, gathered, preferred_element_typ...  10.8 us
    dynamic_slice x9, local copies, waits for them, and re-layouts, local(): couple_rows = lax.dynamic_slice_in_dim(couple_sel, row_start, row_count, 1)  9.66 us
    unnamed x264, local copies, waits for them, and re-layouts  9.1 us
  transfers between devices with their start and end apart: 16, of which 3 were waited for; matrix products, arithmetic and copies ran while one was open for 24% of the time, Pallas kernels for 0%

commit v1 on v0

v1 whole, which is shorter than its diff:
```python
import jax
import jax.numpy as jnp
from jax import lax
from jax.experimental import pallas as pl
from jax.experimental.pallas import tpu as pltpu
from jax.sharding import PartitionSpec as P

step_size = 0.1
half_step = 0.5 * step_size
float32 = jnp.float32
bfloat16 = jnp.bfloat16


def swapped(value, axis, distance):
    pairs = [(source, source ^ distance) for source in range(lax.axis_size(axis))]
    return lax.ppermute(value, axis, pairs)


def forwarded(value, axis, stride):
    ring = 4 * stride
    pairs = []
    for source in range(lax.axis_size(axis)):
        base, place = source - source % ring, source % ring
        shift = stride if source & stride else -stride
        pairs.append((source, base + (place + shift) % ring))
    return lax.ppermute(value, axis, pairs)


def dot(left, right):
    return jnp.dot(left, right, preferred_element_type=float32)


def add_term(total, matrix, real, imag, weight_a, weight_b):
    left_real = dot(matrix, real)
    right_real = dot(real, matrix)
    left_imag = dot(matrix, imag)
    right_imag = dot(imag, matrix)
    total[0] += weight_b * (left_real + right_real) + weight_a * (left_imag - right_imag)
    total[1] += weight_b * (left_imag + right_imag) - weight_a * (left_real - right_real)


def add_commutator(total, ham_ref, real, imag):
    ham_real, ham_imag = ham_ref[0], ham_ref[1]
    total[0] += dot(ham_real, imag) + dot(ham_imag, real) - dot(real, ham_imag) - dot(imag, ham_real)
    total[1] += dot(ham_imag, imag) - dot(ham_real, real) + dot(real, ham_real) - dot(imag, ham_imag)


def rows_of(first):
    return pl.ds(pl.multiple_of(first * 128, 128), 128)


def early_kernel(bits, with_prior, index_ref, coef_ref, ham_ref, couple_ref, own_ref, *refs):
    if with_prior:
        prior_ref, *refs = refs
    partner_refs, total = refs[:-1], refs[-1]
    if with_prior:
        total[...] = coef_ref[2, 1] * prior_ref[...]
    else:
        total[...] = jnp.zeros_like(total)
    add_commutator(total, ham_ref, own_ref[0], own_ref[1])
    for bit, ref in zip(bits, partner_refs, strict=True):
        matrix = couple_ref[index_ref[1 + bit]]
        add_term(total, matrix, ref[0], ref[1], coef_ref[0, bit], coef_ref[1, bit])


def gather_rows(whole, index_ref, near_ref, far_ref):
    near = index_ref[0]
    whole[:, rows_of(near), :] = near_ref[...]
    whole[:, rows_of(1 - near), :] = far_ref[...]


def late_total(bits, index_ref, coef_ref, couple_ref, total_ref, pairs, whole, total):
    total[...] = total_ref[...]
    for bit, (near_ref, far_ref) in zip(bits, pairs, strict=True):
        gather_rows(whole, index_ref, near_ref, far_ref)
        matrix = couple_ref[index_ref[1 + bit]]
        add_term(total, matrix, whole[0], whole[1], coef_ref[0, bit], coef_ref[1, bit])


def middle_kernel(bits, index_ref, coef_ref, couple_ref, own_ref, total_ref, *refs):
    count = 2 * len(bits)
    pairs = list(zip(refs[0:count:2], refs[1:count:2]))
    slope_ref, middle_ref, near_ref, far_ref, whole = refs[count:]
    late_total(bits, index_ref, coef_ref, couple_ref, total_ref, pairs, whole, slope_ref)
    near = index_ref[0]
    middle = coef_ref[2, 0] * own_ref[...].astype(float32) + step_size * slope_ref[...]
    middle_ref[...] = middle.astype(bfloat16)
    near_ref[...] = middle_ref[:, rows_of(near), :]
    far_ref[...] = middle_ref[:, rows_of(1 - near), :]


def last_kernel(bits, index_ref, coef_ref, couple_ref, total_ref, *refs):
    count = 2 * len(bits)
    pairs = list(zip(refs[0:count:2], refs[1:count:2]))
    near_ref, far_ref, whole, total = refs[count:]
    late_total(bits, index_ref, coef_ref, couple_ref, total_ref, pairs, whole, total)
    near = index_ref[0]
    near_ref[...] = half_step * total[:, rows_of(near), :]
    far_ref[...] = (half_step * total[:, rows_of(1 - near), :]).astype(bfloat16)


in_vmem = pl.BlockSpec(memory_space=pltpu.VMEM)
in_smem = pl.BlockSpec(memory_space=pltpu.SMEM)


def call(body, terms, outs, scratch, *operands):
    specs = [in_smem, in_smem] + [in_vmem] * (len(operands) - 2)
    moved = sum(x.size * x.dtype.itemsize for x in operands) + sum(x.size * x.dtype.itemsize for x in outs)
    return pl.pallas_call(
        body,
        out_shape=outs,
        in_specs=specs,
        out_specs=[in_vmem] * len(outs),
        scratch_shapes=scratch,
        cost_estimate=pl.CostEstimate(flops=terms * 8 * 256**3, bytes_accessed=moved, transcendentals=0),
        compiler_params=pltpu.CompilerParams(vmem_limit_bytes=24 * 2**20),
    )(*operands)


def shaped(kind, *dims):
    return jax.ShapeDtypeStruct(dims, kind)


def local(rho_real, rho_imag, ham, couple, rates, coeff_real, coeff_imag, occupation, upper, lower):
    rep = lax.axis_index("rep")
    hier = lax.axis_index("hier")
    rows, levels = rho_real.shape[1:]
    bit_count = lax.axis_size("hier").bit_length()
    x_dist = lax.axis_size("hier") // 2

    own_index = 2 * hier + rep
    occ_float = occupation.astype(float32)
    decay = jnp.sum(occ_float * rates[None, :], axis=1)
    pick = lambda table: jnp.where(rep == 0, table[0], table[1])
    own_occ, own_up, own_low, own_decay = pick(occ_float), pick(upper), pick(lower), pick(decay)
    partner = jnp.bitwise_xor(own_index, jnp.left_shift(1, jnp.arange(bit_count, dtype=jnp.int32)))
    is_above = own_up[None, :] == partner[:, None]
    is_below = own_low[None, :] == partner[:, None]
    mode_range = jnp.arange(couple.shape[0], dtype=jnp.int32)
    modes = jnp.sum(jnp.where(is_above | is_below, mode_range[None, :], 0), axis=1)
    weight_a = jnp.sum(jnp.where(is_above, 1.0, jnp.where(is_below, (own_occ * coeff_real)[None, :], 0.0)), axis=1)
    weight_b = jnp.sum(jnp.where(is_below, (own_occ * coeff_imag)[None, :], 0.0), axis=1)
    keep = 1.0 - step_size * own_decay
    index = jnp.concatenate([rep[None], modes]).astype(jnp.int32)
    keeps = jnp.where(jnp.arange(bit_count) < 2, keep, 0.0)
    coef = jnp.stack([weight_a, weight_b, keeps]).astype(float32)

    whole = shaped(bfloat16, 2, levels, levels)
    slope = shaped(float32, 2, levels, levels)
    half = shaped(bfloat16, 2, rows, levels)
    half_float = shaped(float32, 2, rows, levels)

    def exchange(near, far, full):
        z4_near = swapped(near, "hier", 32)
        z4_far = swapped(far, "hier", 32)
        z2 = swapped(full, "hier", 16)
        z1 = swapped(full, "hier", 8)
        z8_near = forwarded(z4_near, "hier", 32)
        y2 = swapped(full, "hier", 4)
        y1 = swapped(full, "hier", 2)
        z8_far = forwarded(z4_far, "hier", 32)
        x1 = swapped(full, "hier", x_dist)
        x2 = swapped(full, "rep", 1)
        core = swapped(full, "hier", 1)
        return (x2, core, y1, y2, z1, z2, x1), (z4_near, z4_far, z8_near, z8_far)

    early_bits = (0, 1, 2, 3, 4, 5, 8)
    late_bits = (6, 7)

    rounded = jnp.stack([rho_real, rho_imag]).astype(bfloat16)
    near = jnp.where(rep == 0, rounded[:, 0], rounded[:, 1])
    away = jnp.where(rep == 0, rounded[:, 1], rounded[:, 0])
    far = swapped(away, "rep", 1)
    full = jnp.where(rep == 0, jnp.concatenate([near, far], axis=1), jnp.concatenate([far, near], axis=1))

    early, late = exchange(near, far, full)
    total = call(
        lambda *refs: early_kernel(early_bits, False, *refs), 2 + len(early_bits), [slope], [],
        index, coef, ham, couple, full, *early,
    )[0]
    first, middle, near, far = call(
        lambda *refs: middle_kernel(late_bits, *refs), len(late_bits), [slope, whole, half, half],
        [pltpu.VMEM((2, levels, levels), bfloat16)],
        index, coef, couple, full, total, *late,
    )

    early, late = exchange(near, far, middle)
    total = call(
        lambda *refs: early_kernel(early_bits, True, *refs), 2 + len(early_bits), [slope], [],
        index, coef, ham, couple, middle, first, *early,
    )[0]
    near, away = call(
        lambda *refs: last_kernel(late_bits, *refs), len(late_bits), [half_float, half],
        [pltpu.VMEM((2, levels, levels), bfloat16), pltpu.VMEM((2, levels, levels), float32)],
        index, coef, couple, total, *late,
    )
    far = swapped(away, "rep", 1).astype(float32)
    stay = 1.0 - step_size * decay + (0.5 * step_size * step_size) * decay * decay
    is_own = (jnp.arange(2) == rep)[:, None, None]
    outs = []
    for part, state in enumerate((rho_real, rho_imag)):
        change = jnp.where(is_own, near[part][None], far[part][None])
        outs.append(stay[:, None, None] * state + change)
    return tuple(outs)


def solution(mesh):
    placed = (
        P("hier", "rep", None),
        P("hier", "rep", None),
        P(),
        P(),
        P(),
        P(),
        P(),
        P("hier", None),
        P("hier", None),
        P("hier", None),
    )
    return jax.shard_map(
        local,
        mesh=mesh,
        in_specs=placed,
        out_specs=(P("hier", "rep", None), P("hier", "rep", None)),
        check_vma=False,
    )
```

time: 329 us -> 169 us (0.51)
  waiting for transfers between devices: 138 us -> 57.2 us
  matrix products: 46.9 us -> 0 us
  local copies, waits for them, and re-layouts: 30.7 us -> 0.65 us
  starting transfers between devices: 74.3 us -> 93.6 us
  blocking collectives: 17.6 us -> 0 us
  other arithmetic: 15.3 us -> 4.99 us
  Pallas kernels: 0 us -> 7.21 us
    ppermute x16 -> x20, waiting for transfers between devices: 138 us -> 29.7 us  [swapped(): return lax.ppermute(value, axis, pairs)]
    dot_general x68 -> x0, matrix products: 46.9 us -> none  [the longest x9 11.9 us: local(): jnp.einsum('mk,kij->mij', mode_sel.astype(jnp.bfloat16), couple, preferre...]
    ppermute x0 -> x4, waiting for transfers between devices: none -> 27.5 us  [forwarded(): return lax.ppermute(value, axis, pairs)]
    ppermute x0 -> x4, starting transfers between devices: none -> 21.8 us  [forwarded(): return lax.ppermute(value, axis, pairs)]
    all_gather x2 -> x0, blocking collectives: 17.6 us -> none  [derivative(): gathered = lax.all_gather(rounded, 'rep', axis=2, tiled=True)]
    convert_element_type x9 -> x0, local copies, waits for them, and re-layouts: 11.9 us -> none  [local(): couple_sel = jnp.einsum('mk,kij->mij', mode_sel.astype(jnp.bfloat16), cou...]
    dynamic_slice x9 -> x0, local copies, waits for them, and re-layouts: 9.66 us -> none  [local(): couple_rows = lax.dynamic_slice_in_dim(couple_sel, row_start, row_count, 1)]
    unnamed x264 -> x12, local copies, waits for them, and re-layouts: 9.1 us -> 0.03 us
  transfers between devices with their start and end apart: 16 -> 24, of which waited for: 3 -> 7; matrix products, arithmetic and copies ran while one was open for 24% -> 2% of each run, Pallas kernels for 0% -> 3%
where the time goes in v1:
time: 169 us; the launch traced here: 166 us
  starting transfers between devices  93.6 us (55%)
  waiting for transfers between devices  57.2 us (34%)
  Pallas kernels  7.21 us (4%)
  other arithmetic  4.99 us (3%)
  between operations  2.41 us (1%)
    ppermute x20, starting transfers between devices, swapped(): return lax.ppermute(value, axis, pairs)  71.8 us
    ppermute x20, waiting for transfers between devices, swapped(): return lax.ppermute(value, axis, pairs)  29.7 us
    ppermute x4, waiting for transfers between devices, forwarded(): return lax.ppermute(value, axis, pairs)  27.5 us
    ppermute x4, starting transfers between devices, forwarded(): return lax.ppermute(value, axis, pairs)  21.8 us
    pallas_call x4, Pallas kernels, call(): pl.pallas_call(body, out_shape=outs, in_specs=specs, out_specs=[in_vmem]...  7.21 us
  transfers between devices with their start and end apart: 24, of which 7 were waited for; matrix products, arithmetic and copies ran while one was open for 2% of the time, Pallas kernels for 3%

profile of v1, /device:TPU:1, one launch (start us, length us, event | category | flops | bytes accessed | tf_op | source)
XLA Modules:
  0.0 166.1 jit_solution(16392366405681158300)
XLA Ops:
  1.9 5.5 %collective-permute-start = (bf16[2,128,256]{2,1,0:T(8,128)(2,1)S(1)}, bf16[2,128,256]{2,1,0:T(8,128)(2,1)S(1)}, u32[]{:S(2)}, u32[]{:S(2)}) collective-permute-start(bf16[2,128,256]{2,1,0:T(8,128)(2,1)S(1)} %get-tuple-element.21), channel_id=1, source_target_pairs={{0,1},{1,0},{2,3},{3,2},{4,5},{5,4},{6,7},{7,6},{8,9},{9,8},{10,11... | collective-permute-start | bytes 393224 | tf_op jit(solution)/shard_map/ppermute | solution.py:16
  7.4 8.8 %collective-permute-start.8 = (bf16[2,128,256]{2,1,0:T(8,128)(2,1)S(1)}, bf16[2,128,256]{2,1,0:T(8,128)(2,1)S(1)}, u32[]{:S(2)}, u32[]{:S(2)}) collective-permute-start(bf16[2,128,256]{2,1,0:T(8,128)(2,1)S(1)} %get-tuple-element.20), channel_id=1, source_target_pairs={{0,64},{2,66},{4,68},{6,70},{8,72},{10,74},{12,76},{14,78},{16,80}... | collective-permute-start | bytes 393224 | tf_op jit(solution)/shard_map/ppermute | solution.py:16
  18.7 2.1 %collective-permute-start.1 = (bf16[2,256,256]{2,1,0:T(8,128)(2,1)S(1)}, bf16[2,256,256]{2,1,0:T(8,128)(2,1)S(1)}, u32[]{:S(2)}, u32[]{:S(2)}) collective-permute-start(bf16[2,256,256]{2,1,0:T(8,128)(2,1)S(1)} %maximum_select_fusion.refs_4_.refs_3_), channel_id=1, source_target_pairs={{0,1},{1,0},{2,3},{3,2},{4,5},{5,4},{6,7},{7,6},{8,9},{9,8},{10,11... | collective-permute-start | bytes 786440 | tf_op jit(solution)/shard_map/ppermute | solution.py:16
  20.8 3.4 %collective-permute-start.2 = (bf16[2,256,256]{2,1,0:T(8,128)(2,1)S(1)}, bf16[2,256,256]{2,1,0:T(8,128)(2,1)S(1)}, u32[]{:S(2)}, u32[]{:S(2)}) collective-permute-start(bf16[2,256,256]{2,1,0:T(8,128)(2,1)S(1)} %maximum_select_fusion.refs_4_.refs_3_), channel_id=1, source_target_pairs={{0,2},{2,0},{4,6},{6,4},{8,10},{10,8},{12,14},{14,12},{16,18},{18,... | collective-permute-start | bytes 786440 | tf_op jit(solution)/shard_map/ppermute | solution.py:16
  24.4 5.7 %collective-permute-start.9 = (bf16[2,128,256]{2,1,0:T(8,128)(2,1)S(1)}, bf16[2,128,256]{2,1,0:T(8,128)(2,1)S(1)}, u32[]{:S(2)}, u32[]{:S(2)}) collective-permute-start(bf16[2,128,256]{2,1,0:T(8,128)(2,1)S(1)} %collective-permute-done), channel_id=1, source_target_pairs={{0,64},{2,66},{4,68},{6,70},{8,72},{10,74},{12,76},{14,78},{16,80}... | collective-permute-start | bytes 393224 | tf_op jit(solution)/shard_map/ppermute | solution.py:16
  32.0 1.9 %collective-permute-start.3 = (bf16[2,256,256]{2,1,0:T(8,128)(2,1)S(1)}, bf16[2,256,256]{2,1,0:T(8,128)(2,1)S(1)}, u32[]{:S(2)}, u32[]{:S(2)}) collective-permute-start(bf16[2,256,256]{2,1,0:T(8,128)(2,1)S(1)} %maximum_select_fusion.refs_4_.refs_3_), channel_id=1, source_target_pairs={{0,4},{2,6},{4,0},{6,2},{8,12},{10,14},{12,8},{14,10},{16,20},{18,... | collective-permute-start | bytes 786440 | tf_op jit(solution)/shard_map/ppermute | solution.py:16
  33.9 3.7 %collective-permute-start.4 = (bf16[2,256,256]{2,1,0:T(8,128)(2,1)S(1)}, bf16[2,256,256]{2,1,0:T(8,128)(2,1)S(1)}, u32[]{:S(2)}, u32[]{:S(2)}) collective-permute-start(bf16[2,256,256]{2,1,0:T(8,128)(2,1)S(1)} %maximum_select_fusion.refs_4_.refs_3_), channel_id=1, source_target_pairs={{0,8},{2,10},{4,12},{6,14},{8,0},{10,2},{12,4},{14,6},{16,24},{18,... | collective-permute-start | bytes 786440 | tf_op jit(solution)/shard_map/ppermute | solution.py:16
  37.6 6.1 %collective-permute-done.9.refs_6_ = bf16[2,128,256]{2,1,0:T(8,128)(2,1)S(1)} collective-permute-done((bf16[2,128,256]{2,1,0:T(8,128)(2,1)S(1)}, bf16[2,128,256]{2,1,0:T(8,128)(2,1)S(1)}, u32[]{:S(2)}, u32[]{:S(2)}) %collective-permute-start.9) | collective-permute-done | bytes 131104 | tf_op jit(solution)/shard_map/ppermute | solution.py:16
  45.6 1.9 %collective-permute-start.6 = (bf16[2,256,256]{2,1,0:T(8,128)(2,1)S(1)}, bf16[2,256,256]{2,1,0:T(8,128)(2,1)S(1)}, u32[]{:S(2)}, u32[]{:S(2)}) collective-permute-start(bf16[2,256,256]{2,1,0:T(8,128)(2,1)S(1)} %maximum_select_fusion.refs_4_.refs_3_), channel_id=1, source_target_pairs={{0,32},{2,34},{4,36},{6,38},{8,40},{10,42},{12,44},{14,46},{16,48}... | collective-permute-start | bytes 786440 | tf_op jit(solution)/shard_map/ppermute | solution.py:16
  47.6 3.1 %collective-permute-start.7 = (bf16[2,256,256]{2,1,0:T(8,128)(2,1)S(1)}, bf16[2,256,256]{2,1,0:T(8,128)(2,1)S(1)}, u32[]{:S(2)}, u32[]{:S(2)}) collective-permute-start(bf16[2,256,256]{2,1,0:T(8,128)(2,1)S(1)} %maximum_select_fusion.refs_4_.refs_3_), channel_id=1, source_target_pairs={{0,256},{2,258},{4,260},{6,262},{8,264},{10,266},{12,268},{14,270}... | collective-permute-start | bytes 786440 | tf_op jit(solution)/shard_map/ppermute | solution.py:16
  50.9 10.7 %collective-permute-start.10 = (bf16[2,128,256]{2,1,0:T(8,128)(2,1)S(1)}, bf16[2,128,256]{2,1,0:T(8,128)(2,1)S(1)}, u32[]{:S(2)}, u32[]{:S(2)}) collective-permute-start(bf16[2,128,256]{2,1,0:T(8,128)(2,1)S(1)} %collective-permute-done.8.refs_5_), channel_id=1, source_target_pairs={{0,192},{2,194},{4,196},{6,198},{8,200},{10,202},{12,204},{14,206}... | collective-permute-start | bytes 393224 | tf_op jit(solution)/shard_map/ppermute | solution.py:26
  61.7 1.9 %collective-permute-start.11 = (bf16[2,128,256]{2,1,0:T(8,128)(2,1)S(1)}, bf16[2,128,256]{2,1,0:T(8,128)(2,1)S(1)}, u32[]{:S(2)}, u32[]{:S(2)}) collective-permute-start(bf16[2,128,256]{2,1,0:T(8,128)(2,1)S(1)} %collective-permute-done.9.refs_6_), channel_id=1, source_target_pairs={{0,192},{2,194},{4,196},{6,198},{8,200},{10,202},{12,204},{14,206}... | collective-permute-start | bytes 393224 | tf_op jit(solution)/shard_map/ppermute | solution.py:26
  63.7 2.4 %shard_map.113.refs_4_ = f32[2,256,256]{2,1,0:T(8,128)S(1)} custom-call(s32[10]{0:T(128)S(1)} %pad_add_fusion.refs_0_, f32[3,9]{1,0:T(4,128)S(1)} %pad_maximum_fusion.1.refs_1_, bf16[2,256,256]{2,1,0:T(8,128)(2,1)S(1)} %copy-done.1, bf16[12,256,256]{2,1,0:T(8,128)(2,1)S(1)} %copy-done, bf16[2,256,256]{2,1,0:T(8,128)(2,1)S(1)} %maximum_select_fusion.refs_4_.refs_3_, ...), custom_call_target="tpu_custom_call" | custom-call | flops 1207959552 | bytes 4456596 | tf_op jit(solution)/shard_map/pallas_call | solution.py:109
  66.1 15.0 %collective-permute-done.10.refs_7_ = bf16[2,128,256]{2,1,0:T(8,128)(2,1)S(1)} collective-permute-done((bf16[2,128,256]{2,1,0:T(8,128)(2,1)S(1)}, bf16[2,128,256]{2,1,0:T(8,128)(2,1)S(1)}, u32[]{:S(2)}, u32[]{:S(2)}) %collective-permute-start.10) | collective-permute-done | bytes 131104 | tf_op jit(solution)/shard_map/ppermute | solution.py:26
  81.2 2.8 %collective-permute-done.11.refs_8_ = bf16[2,128,256]{2,1,0:T(8,128)(2,1)S(1)} collective-permute-done((bf16[2,128,256]{2,1,0:T(8,128)(2,1)S(1)}, bf16[2,128,256]{2,1,0:T(8,128)(2,1)S(1)}, u32[]{:S(2)}, u32[]{:S(2)}) %collective-permute-start.11) | collective-permute-done | bytes 131104 | tf_op jit(solution)/shard_map/ppermute | solution.py:26
  85.2 4.5 %collective-permute-start.12 = (bf16[2,256,256]{2,1,0:T(8,128)(2,1)S(1)}, bf16[2,256,256]{2,1,0:T(8,128)(2,1)S(1)}, u32[]{:S(2)}, u32[]{:S(2)}) collective-permute-start(bf16[2,256,256]{2,1,0:T(8,128)(2,1)S(1)} %get-tuple-element.8.refs_4_), channel_id=1, source_target_pairs={{0,1},{1,0},{2,3},{3,2},{4,5},{5,4},{6,7},{7,6},{8,9},{9,8},{10,11... | collective-permute-start | bytes 786440 | tf_op jit(solution)/shard_map/ppermute | solution.py:16
  89.6 2.7 %collective-permute-start.13 = (bf16[2,256,256]{2,1,0:T(8,128)(2,1)S(1)}, bf16[2,256,256]{2,1,0:T(8,128)(2,1)S(1)}, u32[]{:S(2)}, u32[]{:S(2)}) collective-permute-start(bf16[2,256,256]{2,1,0:T(8,128)(2,1)S(1)} %get-tuple-element.8.refs_4_), channel_id=1, source_target_pairs={{0,2},{2,0},{4,6},{6,4},{8,10},{10,8},{12,14},{14,12},{16,18},{18,... | collective-permute-start | bytes 786440 | tf_op jit(solution)/shard_map/ppermute | solution.py:16
  92.3 1.9 %collective-permute-start.19 = (bf16[2,128,256]{2,1,0:T(8,128)(2,1)S(1)}, bf16[2,128,256]{2,1,0:T(8,128)(2,1)S(1)}, u32[]{:S(2)}, u32[]{:S(2)}) collective-permute-start(bf16[2,128,256]{2,1,0:T(8,128)(2,1)S(1)} %get-tuple-element.10), channel_id=1, source_target_pairs={{0,64},{2,66},{4,68},{6,70},{8,72},{10,74},{12,76},{14,78},{16,80}... | collective-permute-start | bytes 393224 | tf_op jit(solution)/shard_map/ppermute | solution.py:16
  94.2 7.3 %collective-permute-start.20 = (bf16[2,128,256]{2,1,0:T(8,128)(2,1)S(1)}, bf16[2,128,256]{2,1,0:T(8,128)(2,1)S(1)}, u32[]{:S(2)}, u32[]{:S(2)}) collective-permute-start(bf16[2,128,256]{2,1,0:T(8,128)(2,1)S(1)} %get-tuple-element.11), channel_id=1, source_target_pairs={{0,64},{2,66},{4,68},{6,70},{8,72},{10,74},{12,76},{14,78},{16,80}... | collective-permute-start | bytes 393224 | tf_op jit(solution)/shard_map/ppermute | solution.py:16
  101.5 3.2 %collective-permute-start.14 = (bf16[2,256,256]{2,1,0:T(8,128)(2,1)S(1)}, bf16[2,256,256]{2,1,0:T(8,128)(2,1)S(1)}, u32[]{:S(2)}, u32[]{:S(2)}) collective-permute-start(bf16[2,256,256]{2,1,0:T(8,128)(2,1)S(1)} %get-tuple-element.8.refs_4_), channel_id=1, source_target_pairs={{0,4},{2,6},{4,0},{6,2},{8,12},{10,14},{12,8},{14,10},{16,20},{18,... | collective-permute-start | bytes 786440 | tf_op jit(solution)/shard_map/ppermute | solution.py:16
  104.7 12.7 %collective-permute-done.19.refs_4_ = bf16[2,128,256]{2,1,0:T(8,128)(2,1)S(1)} collective-permute-done((bf16[2,128,256]{2,1,0:T(8,128)(2,1)S(1)}, bf16[2,128,256]{2,1,0:T(8,128)(2,1)S(1)}, u32[]{:S(2)}, u32[]{:S(2)}) %collective-permute-start.19) | collective-permute-done | bytes 131104 | tf_op jit(solution)/shard_map/ppermute | solution.py:16
  117.4 4.8 %collective-permute-start.15 = (bf16[2,256,256]{2,1,0:T(8,128)(2,1)S(1)}, bf16[2,256,256]{2,1,0:T(8,128)(2,1)S(1)}, u32[]{:S(2)}, u32[]{:S(2)}) collective-permute-start(bf16[2,256,256]{2,1,0:T(8,128)(2,1)S(1)} %get-tuple-element.8.refs_4_), channel_id=1, source_target_pairs={{0,8},{2,10},{4,12},{6,14},{8,0},{10,2},{12,4},{14,6},{16,24},{18,... | collective-permute-start | bytes 786440 | tf_op jit(solution)/shard_map/ppermute | solution.py:16
  122.2 1.9 %collective-permute-start.16 = (bf16[2,256,256]{2,1,0:T(8,128)(2,1)S(1)}, bf16[2,256,256]{2,1,0:T(8,128)(2,1)S(1)}, u32[]{:S(2)}, u32[]{:S(2)}) collective-permute-start(bf16[2,256,256]{2,1,0:T(8,128)(2,1)S(1)} %get-tuple-element.8.refs_4_), channel_id=1, source_target_pairs={{0,16},{2,18},{4,20},{6,22},{8,24},{10,26},{12,28},{14,30},{16,0},... | collective-permute-start | bytes 786440 | tf_op jit(solution)/shard_map/ppermute | solution.py:16
  124.2 1.9 %collective-permute-start.17 = (bf16[2,256,256]{2,1,0:T(8,128)(2,1)S(1)}, bf16[2,256,256]{2,1,0:T(8,128)(2,1)S(1)}, u32[]{:S(2)}, u32[]{:S(2)}) collective-permute-start(bf16[2,256,256]{2,1,0:T(8,128)(2,1)S(1)} %get-tuple-element.8.refs_4_), channel_id=1, source_target_pairs={{0,32},{2,34},{4,36},{6,38},{8,40},{10,42},{12,44},{14,46},{16,48}... | collective-permute-start | bytes 786440 | tf_op jit(solution)/shard_map/ppermute | solution.py:16
  126.1 1.9 %collective-permute-start.18 = (bf16[2,256,256]{2,1,0:T(8,128)(2,1)S(1)}, bf16[2,256,256]{2,1,0:T(8,128)(2,1)S(1)}, u32[]{:S(2)}, u32[]{:S(2)}) collective-permute-start(bf16[2,256,256]{2,1,0:T(8,128)(2,1)S(1)} %get-tuple-element.8.refs_4_), channel_id=1, source_target_pairs={{0,256},{2,258},{4,260},{6,262},{8,264},{10,266},{12,268},{14,270}... | collective-permute-start | bytes 786440 | tf_op jit(solution)/shard_map/ppermute | solution.py:16
  128.1 5.7 %collective-permute-start.21 = (bf16[2,128,256]{2,1,0:T(8,128)(2,1)S(1)}, bf16[2,128,256]{2,1,0:T(8,128)(2,1)S(1)}, u32[]{:S(2)}, u32[]{:S(2)}) collective-permute-start(bf16[2,128,256]{2,1,0:T(8,128)(2,1)S(1)} %collective-permute-done.19.refs_4_), channel_id=1, source_target_pairs={{0,192},{2,194},{4,196},{6,198},{8,200},{10,202},{12,204},{14,206}... | collective-permute-start | bytes 393224 | tf_op jit(solution)/shard_map/ppermute | solution.py:26
  133.8 3.5 %collective-permute-start.22 = (bf16[2,128,256]{2,1,0:T(8,128)(2,1)S(1)}, bf16[2,128,256]{2,1,0:T(8,128)(2,1)S(1)}, u32[]{:S(2)}, u32[]{:S(2)}) collective-permute-start(bf16[2,128,256]{2,1,0:T(8,128)(2,1)S(1)} %collective-permute-done.20.refs_5_), channel_id=1, source_target_pairs={{0,192},{2,194},{4,196},{6,198},{8,200},{10,202},{12,204},{14,206}... | collective-permute-start | bytes 393224 | tf_op jit(solution)/shard_map/ppermute | solution.py:26
  137.3 6.7 %collective-permute-done.17.refs_11_ = bf16[2,256,256]{2,1,0:T(8,128)(2,1)S(1)} collective-permute-done((bf16[2,256,256]{2,1,0:T(8,128)(2,1)S(1)}, bf16[2,256,256]{2,1,0:T(8,128)(2,1)S(1)}, u32[]{:S(2)}, u32[]{:S(2)}) %collective-permute-start.17) | collective-permute-done | bytes 262176 | tf_op jit(solution)/shard_map/ppermute | solution.py:16
  144.0 2.5 %shard_map.115.refs_3_ = f32[2,256,256]{2,1,0:T(8,128)S(1)} custom-call(s32[10]{0:T(128)S(1)} %pad_add_fusion.refs_0_, f32[3,9]{1,0:T(4,128)S(1)} %pad_maximum_fusion.1.refs_1_, bf16[2,256,256]{2,1,0:T(8,128)(2,1)S(1)} %copy-done.1, bf16[12,256,256]{2,1,0:T(8,128)(2,1)S(1)} %copy-done, bf16[2,256,256]{2,1,0:T(8,128)(2,1)S(1)} %get-tuple-element.8.refs_4_, ...), custom_call_target="tpu_custom_call" | custom-call | flops 1207959552 | bytes 4980884 | tf_op jit(solution)/shard_map/pallas_call | solution.py:109
  146.5 9.7 %collective-permute-done.22.refs_7_ = bf16[2,128,256]{2,1,0:T(8,128)(2,1)S(1)} collective-permute-done((bf16[2,128,256]{2,1,0:T(8,128)(2,1)S(1)}, bf16[2,128,256]{2,1,0:T(8,128)(2,1)S(1)}, u32[]{:S(2)}, u32[]{:S(2)}) %collective-permute-start.22) | collective-permute-done | bytes 131104 | tf_op jit(solution)/shard_map/ppermute | solution.py:26
  157.3 3.6 %collective-permute-start.23 = (bf16[2,128,256]{2,1,0:T(8,128)(2,1)S(1)}, bf16[2,128,256]{2,1,0:T(8,128)(2,1)S(1)}, u32[]{:S(2)}, u32[]{:S(2)}) collective-permute-start(bf16[2,128,256]{2,1,0:T(8,128)(2,1)S(1)} %get-tuple-element.13), channel_id=1, source_target_pairs={{0,1},{1,0},{2,3},{3,2},{4,5},{5,4},{6,7},{7,6},{8,9},{9,8},{10,11... | collective-permute-start | bytes 393224 | tf_op jit(solution)/shard_map/ppermute | solution.py:16
  160.9 4.2 %collective-permute-done.23 = bf16[2,128,256]{2,1,0:T(8,128)(2,1)S(1)} collective-permute-done((bf16[2,128,256]{2,1,0:T(8,128)(2,1)S(1)}, bf16[2,128,256]{2,1,0:T(8,128)(2,1)S(1)}, u32[]{:S(2)}, u32[]{:S(2)}) %collective-permute-start.23) | collective-permute-done | bytes 131104 | tf_op jit(solution)/shard_map/ppermute | solution.py:16
  (52 shorter events, 9.9 us)
Async XLA Ops:
  0.6 23.6 %copy-start.4 = (s32[2,12]{1,0:T(2,128)S(1)}, s32[2,12]{1,0:T(2,128)}, u32[]{:S(2)}) copy-start(s32[2,12]{1,0:T(2,128)} %param.17) | copy-start | bytes 292
  0.6 23.6 %copy-start.5 = (f32[12]{0:T(128)S(1)}, f32[12]{0:T(128)}, u32[]{:S(2)}) copy-start(f32[12]{0:T(128)} %param.14) | copy-start | bytes 148
  0.7 63.0 %copy-start.1 = (bf16[2,256,256]{2,1,0:T(8,128)(2,1)S(1)}, bf16[2,256,256]{2,1,0:T(8,128)(2,1)}, u32[]{:S(2)}) copy-start(bf16[2,256,256]{2,1,0:T(8,128)(2,1)} %refs_2_.6) | copy-start | bytes 786436
  0.7 63.0 %copy-start = (bf16[12,256,256]{2,1,0:T(8,128)(2,1)S(1)}, bf16[12,256,256]{2,1,0:T(8,128)(2,1)}, u32[]{:S(2)}) copy-start(bf16[12,256,256]{2,1,0:T(8,128)(2,1)} %refs_2_.7) | copy-start | bytes 4718596
  1.9 16.6 %collective-permute-start = (bf16[2,128,256]{2,1,0:T(8,128)(2,1)S(1)}, bf16[2,128,256]{2,1,0:T(8,128)(2,1)S(1)}, u32[]{:S(2)}, u32[]{:S(2)}) collective-permute-start(bf16[2,128,256]{2,1,0:T(8,128)(2,1)S(1)} %get-tuple-element.21), channel_id=1, source_target_pairs={{0,1},{1,0},{2,3},{3,2},{4,5},{5,4},{6,7},{7,6},{8,9},{9,8},{10,11... | collective-permute-start | bytes 393224 | tf_op jit(solution)/shard_map/ppermute | solution.py:16
  7.4 26.5 %collective-permute-start.8 = (bf16[2,128,256]{2,1,0:T(8,128)(2,1)S(1)}, bf16[2,128,256]{2,1,0:T(8,128)(2,1)S(1)}, u32[]{:S(2)}, u32[]{:S(2)}) collective-permute-start(bf16[2,128,256]{2,1,0:T(8,128)(2,1)S(1)} %get-tuple-element.20), channel_id=1, source_target_pairs={{0,64},{2,66},{4,68},{6,70},{8,72},{10,74},{12,76},{14,78},{16,80}... | collective-permute-start | bytes 393224 | tf_op jit(solution)/shard_map/ppermute | solution.py:16
  18.7 27.0 %collective-permute-start.1 = (bf16[2,256,256]{2,1,0:T(8,128)(2,1)S(1)}, bf16[2,256,256]{2,1,0:T(8,128)(2,1)S(1)}, u32[]{:S(2)}, u32[]{:S(2)}) collective-permute-start(bf16[2,256,256]{2,1,0:T(8,128)(2,1)S(1)} %maximum_select_fusion.refs_4_.refs_3_), channel_id=1, source_target_pairs={{0,1},{1,0},{2,3},{3,2},{4,5},{5,4},{6,7},{7,6},{8,9},{9,8},{10,11... | collective-permute-start | bytes 786440 | tf_op jit(solution)/shard_map/ppermute | solution.py:16
  20.8 26.8 %collective-permute-start.2 = (bf16[2,256,256]{2,1,0:T(8,128)(2,1)S(1)}, bf16[2,256,256]{2,1,0:T(8,128)(2,1)S(1)}, u32[]{:S(2)}, u32[]{:S(2)}) collective-permute-start(bf16[2,256,256]{2,1,0:T(8,128)(2,1)S(1)} %maximum_select_fusion.refs_4_.refs_3_), channel_id=1, source_target_pairs={{0,2},{2,0},{4,6},{6,4},{8,10},{10,8},{12,14},{14,12},{16,18},{18,... | collective-permute-start | bytes 786440 | tf_op jit(solution)/shard_map/ppermute | solution.py:16
  24.4 19.3 %collective-permute-start.9 = (bf16[2,128,256]{2,1,0:T(8,128)(2,1)S(1)}, bf16[2,128,256]{2,1,0:T(8,128)(2,1)S(1)}, u32[]{:S(2)}, u32[]{:S(2)}) collective-permute-start(bf16[2,128,256]{2,1,0:T(8,128)(2,1)S(1)} %collective-permute-done), channel_id=1, source_target_pairs={{0,64},{2,66},{4,68},{6,70},{8,72},{10,74},{12,76},{14,78},{16,80}... | collective-permute-start | bytes 393224 | tf_op jit(solution)/shard_map/ppermute | solution.py:16
  32.0 18.9 %collective-permute-start.3 = (bf16[2,256,256]{2,1,0:T(8,128)(2,1)S(1)}, bf16[2,256,256]{2,1,0:T(8,128)(2,1)S(1)}, u32[]{:S(2)}, u32[]{:S(2)}) collective-permute-start(bf16[2,256,256]{2,1,0:T(8,128)(2,1)S(1)} %maximum_select_fusion.refs_4_.refs_3_), channel_id=1, source_target_pairs={{0,4},{2,6},{4,0},{6,2},{8,12},{10,14},{12,8},{14,10},{16,20},{18,... | collective-permute-start | bytes 786440 | tf_op jit(solution)/shard_map/ppermute | solution.py:16
  33.9 27.7 %collective-permute-start.4 = (bf16[2,256,256]{2,1,0:T(8,128)(2,1)S(1)}, bf16[2,256,256]{2,1,0:T(8,128)(2,1)S(1)}, u32[]{:S(2)}, u32[]{:S(2)}) collective-permute-start(bf16[2,256,256]{2,1,0:T(8,128)(2,1)S(1)} %maximum_select_fusion.refs_4_.refs_3_), channel_id=1, source_target_pairs={{0,8},{2,10},{4,12},{6,14},{8,0},{10,2},{12,4},{14,6},{16,24},{18,... | collective-permute-start | bytes 786440 | tf_op jit(solution)/shard_map/ppermute | solution.py:16
  43.7 20.0 %collective-permute-start.5 = (bf16[2,256,256]{2,1,0:T(8,128)(2,1)S(1)}, bf16[2,256,256]{2,1,0:T(8,128)(2,1)S(1)}, u32[]{:S(2)}, u32[]{:S(2)}) collective-permute-start(bf16[2,256,256]{2,1,0:T(8,128)(2,1)S(1)} %maximum_select_fusion.refs_4_.refs_3_), channel_id=1, source_target_pairs={{0,16},{2,18},{4,20},{6,22},{8,24},{10,26},{12,28},{14,30},{16,0},... | collective-permute-start | bytes 786440 | tf_op jit(solution)/shard_map/ppermute | solution.py:16
  45.6 18.0 %collective-permute-start.6 = (bf16[2,256,256]{2,1,0:T(8,128)(2,1)S(1)}, bf16[2,256,256]{2,1,0:T(8,128)(2,1)S(1)}, u32[]{:S(2)}, u32[]{:S(2)}) collective-permute-start(bf16[2,256,256]{2,1,0:T(8,128)(2,1)S(1)} %maximum_select_fusion.refs_4_.refs_3_), channel_id=1, source_target_pairs={{0,32},{2,34},{4,36},{6,38},{8,40},{10,42},{12,44},{14,46},{16,48}... | collective-permute-start | bytes 786440 | tf_op jit(solution)/shard_map/ppermute | solution.py:16
  47.6 16.1 %collective-permute-start.7 = (bf16[2,256,256]{2,1,0:T(8,128)(2,1)S(1)}, bf16[2,256,256]{2,1,0:T(8,128)(2,1)S(1)}, u32[]{:S(2)}, u32[]{:S(2)}) collective-permute-start(bf16[2,256,256]{2,1,0:T(8,128)(2,1)S(1)} %maximum_select_fusion.refs_4_.refs_3_), channel_id=1, source_target_pairs={{0,256},{2,258},{4,260},{6,262},{8,264},{10,266},{12,268},{14,270}... | collective-permute-start | bytes 786440 | tf_op jit(solution)/shard_map/ppermute | solution.py:16
  50.9 30.2 %collective-permute-start.10 = (bf16[2,128,256]{2,1,0:T(8,128)(2,1)S(1)}, bf16[2,128,256]{2,1,0:T(8,128)(2,1)S(1)}, u32[]{:S(2)}, u32[]{:S(2)}) collective-permute-start(bf16[2,128,256]{2,1,0:T(8,128)(2,1)S(1)} %collective-permute-done.8.refs_5_), channel_id=1, source_target_pairs={{0,192},{2,194},{4,196},{6,198},{8,200},{10,202},{12,204},{14,206}... | collective-permute-start | bytes 393224 | tf_op jit(solution)/shard_map/ppermute | solution.py:26
  61.7 22.3 %collective-permute-start.11 = (bf16[2,128,256]{2,1,0:T(8,128)(2,1)S(1)}, bf16[2,128,256]{2,1,0:T(8,128)(2,1)S(1)}, u32[]{:S(2)}, u32[]{:S(2)}) collective-permute-start(bf16[2,128,256]{2,1,0:T(8,128)(2,1)S(1)} %collective-permute-done.9.refs_6_), channel_id=1, source_target_pairs={{0,192},{2,194},{4,196},{6,198},{8,200},{10,202},{12,204},{14,206}... | collective-permute-start | bytes 393224 | tf_op jit(solution)/shard_map/ppermute | solution.py:26
  85.2 39.0 %collective-permute-start.12 = (bf16[2,256,256]{2,1,0:T(8,128)(2,1)S(1)}, bf16[2,256,256]{2,1,0:T(8,128)(2,1)S(1)}, u32[]{:S(2)}, u32[]{:S(2)}) collective-permute-start(bf16[2,256,256]{2,1,0:T(8,128)(2,1)S(1)} %get-tuple-element.8.refs_4_), channel_id=1, source_target_pairs={{0,1},{1,0},{2,3},{3,2},{4,5},{5,4},{6,7},{7,6},{8,9},{9,8},{10,11... | collective-permute-start | bytes 786440 | tf_op jit(solution)/shard_map/ppermute | solution.py:16
  89.6 36.5 %collective-permute-start.13 = (bf16[2,256,256]{2,1,0:T(8,128)(2,1)S(1)}, bf16[2,256,256]{2,1,0:T(8,128)(2,1)S(1)}, u32[]{:S(2)}, u32[]{:S(2)}) collective-permute-start(bf16[2,256,256]{2,1,0:T(8,128)(2,1)S(1)} %get-tuple-element.8.refs_4_), channel_id=1, source_target_pairs={{0,2},{2,0},{4,6},{6,4},{8,10},{10,8},{12,14},{14,12},{16,18},{18,... | collective-permute-start | bytes 786440 | tf_op jit(solution)/shard_map/ppermute | solution.py:16
  92.3 25.1 %collective-permute-start.19 = (bf16[2,128,256]{2,1,0:T(8,128)(2,1)S(1)}, bf16[2,128,256]{2,1,0:T(8,128)(2,1)S(1)}, u32[]{:S(2)}, u32[]{:S(2)}) collective-permute-start(bf16[2,128,256]{2,1,0:T(8,128)(2,1)S(1)} %get-tuple-element.10), channel_id=1, source_target_pairs={{0,64},{2,66},{4,68},{6,70},{8,72},{10,74},{12,76},{14,78},{16,80}... | collective-permute-start | bytes 393224 | tf_op jit(solution)/shard_map/ppermute | solution.py:16
  94.2 28.0 %collective-permute-start.20 = (bf16[2,128,256]{2,1,0:T(8,128)(2,1)S(1)}, bf16[2,128,256]{2,1,0:T(8,128)(2,1)S(1)}, u32[]{:S(2)}, u32[]{:S(2)}) collective-permute-start(bf16[2,128,256]{2,1,0:T(8,128)(2,1)S(1)} %get-tuple-element.11), channel_id=1, source_target_pairs={{0,64},{2,66},{4,68},{6,70},{8,72},{10,74},{12,76},{14,78},{16,80}... | collective-permute-start | bytes 393224 | tf_op jit(solution)/shard_map/ppermute | solution.py:16
  101.5 26.5 %collective-permute-start.14 = (bf16[2,256,256]{2,1,0:T(8,128)(2,1)S(1)}, bf16[2,256,256]{2,1,0:T(8,128)(2,1)S(1)}, u32[]{:S(2)}, u32[]{:S(2)}) collective-permute-start(bf16[2,256,256]{2,1,0:T(8,128)(2,1)S(1)} %get-tuple-element.8.refs_4_), channel_id=1, source_target_pairs={{0,4},{2,6},{4,0},{6,2},{8,12},{10,14},{12,8},{14,10},{16,20},{18,... | collective-permute-start | bytes 786440 | tf_op jit(solution)/shard_map/ppermute | solution.py:16
  117.4 16.3 %collective-permute-start.15 = (bf16[2,256,256]{2,1,0:T(8,128)(2,1)S(1)}, bf16[2,256,256]{2,1,0:T(8,128)(2,1)S(1)}, u32[]{:S(2)}, u32[]{:S(2)}) collective-permute-start(bf16[2,256,256]{2,1,0:T(8,128)(2,1)S(1)} %get-tuple-element.8.refs_4_), channel_id=1, source_target_pairs={{0,8},{2,10},{4,12},{6,14},{8,0},{10,2},{12,4},{14,6},{16,24},{18,... | collective-permute-start | bytes 786440 | tf_op jit(solution)/shard_map/ppermute | solution.py:16
  122.2 15.1 %collective-permute-start.16 = (bf16[2,256,256]{2,1,0:T(8,128)(2,1)S(1)}, bf16[2,256,256]{2,1,0:T(8,128)(2,1)S(1)}, u32[]{:S(2)}, u32[]{:S(2)}) collective-permute-start(bf16[2,256,256]{2,1,0:T(8,128)(2,1)S(1)} %get-tuple-element.8.refs_4_), channel_id=1, source_target_pairs={{0,16},{2,18},{4,20},{6,22},{8,24},{10,26},{12,28},{14,30},{16,0},... | collective-permute-start | bytes 786440 | tf_op jit(solution)/shard_map/ppermute | solution.py:16
  124.2 19.8 %collective-permute-start.17 = (bf16[2,256,256]{2,1,0:T(8,128)(2,1)S(1)}, bf16[2,256,256]{2,1,0:T(8,128)(2,1)S(1)}, u32[]{:S(2)}, u32[]{:S(2)}) collective-permute-start(bf16[2,256,256]{2,1,0:T(8,128)(2,1)S(1)} %get-tuple-element.8.refs_4_), channel_id=1, source_target_pairs={{0,32},{2,34},{4,36},{6,38},{8,40},{10,42},{12,44},{14,46},{16,48}... | collective-permute-start | bytes 786440 | tf_op jit(solution)/shard_map/ppermute | solution.py:16
  126.1 17.9 %collective-permute-start.18 = (bf16[2,256,256]{2,1,0:T(8,128)(2,1)S(1)}, bf16[2,256,256]{2,1,0:T(8,128)(2,1)S(1)}, u32[]{:S(2)}, u32[]{:S(2)}) collective-permute-start(bf16[2,256,256]{2,1,0:T(8,128)(2,1)S(1)} %get-tuple-element.8.refs_4_), channel_id=1, source_target_pairs={{0,256},{2,258},{4,260},{6,262},{8,264},{10,266},{12,268},{14,270}... | collective-permute-start | bytes 786440 | tf_op jit(solution)/shard_map/ppermute | solution.py:16
  128.1 18.4 %collective-permute-start.21 = (bf16[2,128,256]{2,1,0:T(8,128)(2,1)S(1)}, bf16[2,128,256]{2,1,0:T(8,128)(2,1)S(1)}, u32[]{:S(2)}, u32[]{:S(2)}) collective-permute-start(bf16[2,128,256]{2,1,0:T(8,128)(2,1)S(1)} %collective-permute-done.19.refs_4_), channel_id=1, source_target_pairs={{0,192},{2,194},{4,196},{6,198},{8,200},{10,202},{12,204},{14,206}... | collective-permute-start | bytes 393224 | tf_op jit(solution)/shard_map/ppermute | solution.py:26
  133.8 22.4 %collective-permute-start.22 = (bf16[2,128,256]{2,1,0:T(8,128)(2,1)S(1)}, bf16[2,128,256]{2,1,0:T(8,128)(2,1)S(1)}, u32[]{:S(2)}, u32[]{:S(2)}) collective-permute-start(bf16[2,128,256]{2,1,0:T(8,128)(2,1)S(1)} %collective-permute-done.20.refs_5_), channel_id=1, source_target_pairs={{0,192},{2,194},{4,196},{6,198},{8,200},{10,202},{12,204},{14,206}... | collective-permute-start | bytes 393224 | tf_op jit(solution)/shard_map/ppermute | solution.py:26
  146.4 18.7 %copy-start.2 = (f32[2,128,256]{2,1,0:T(8,128)S(1)}, f32[2,128,256]{2,1,0:T(8,128)}, u32[]{:S(2)}) copy-start(f32[2,128,256]{2,1,0:T(8,128)} %param.11) | copy-start | bytes 786436
  146.5 18.7 %copy-start.3 = (f32[2,128,256]{2,1,0:T(8,128)S(1)}, f32[2,128,256]{2,1,0:T(8,128)}, u32[]{:S(2)}) copy-start(f32[2,128,256]{2,1,0:T(8,128)} %param.10) | copy-start | bytes 786436
  157.3 7.8 %collective-permute-start.23 = (bf16[2,128,256]{2,1,0:T(8,128)(2,1)S(1)}, bf16[2,128,256]{2,1,0:T(8,128)(2,1)S(1)}, u32[]{:S(2)}, u32[]{:S(2)}) collective-permute-start(bf16[2,128,256]{2,1,0:T(8,128)(2,1)S(1)} %get-tuple-element.13), channel_id=1, source_target_pairs={{0,1},{1,0},{2,3},{3,2},{4,5},{5,4},{6,7},{7,6},{8,9},{9,8},{10,11... | collective-permute-start | bytes 393224 | tf_op jit(solution)/shard_map/ppermute | solution.py:16

commit v2 on v1

v2 whole, which is shorter than its diff:
```python
import functools

import jax
import jax.numpy as jnp
from jax import lax
from jax.experimental import pallas as pl
from jax.experimental.pallas import tpu as pltpu
from jax.sharding import Mesh, PartitionSpec as P

step_size = 0.1
half_step = 0.5 * step_size
float32 = jnp.float32
bfloat16 = jnp.bfloat16

hier = ("x_lo", "z", "y", "core")
hier_sizes = (2, 16, 4, 2)


def swapped(value, axis, distance):
    pairs = [(source, source ^ distance) for source in range(lax.axis_size(axis))]
    return lax.ppermute(value, axis, pairs)


def across(value, near_core, far_core):
    ring, cores = lax.axis_size("z"), lax.axis_size("core")
    pairs = []
    for source in range(ring):
        for core, target in enumerate((near_core, far_core)):
            if target is not None:
                pairs.append((source * cores + core, target(source) % ring * cores + core))
    return lax.ppermute(value, ("z", "core"), pairs)


def inward(source):
    return source ^ 4


def outward(source):
    return source - 4 if not source & 4 else source + 4


def after(value, *earlier):
    return lax.optimization_barrier((value, *earlier))[0]


def dot(left, right):
    return jnp.dot(left, right, preferred_element_type=float32)


def add_term(total, matrix, real, imag, weight_a, weight_b):
    left_real = dot(matrix, real)
    right_real = dot(real, matrix)
    left_imag = dot(matrix, imag)
    right_imag = dot(imag, matrix)
    total[0] += weight_b * (left_real + right_real) + weight_a * (left_imag - right_imag)
    total[1] += weight_b * (left_imag + right_imag) - weight_a * (left_real - right_real)


def add_commutator(total, ham_ref, real, imag):
    ham_real, ham_imag = ham_ref[0], ham_ref[1]
    total[0] += dot(ham_real, imag) + dot(ham_imag, real) - dot(real, ham_imag) - dot(imag, ham_real)
    total[1] += dot(ham_imag, imag) - dot(ham_real, real) + dot(real, ham_real) - dot(imag, ham_imag)


def rows_of(first, count):
    return pl.ds(pl.multiple_of(first * count, count), count)


def add_bits(total, parts, index_ref, coef_ref, couple_ref, refs, whole):
    for bit, places in parts:
        source = refs[places[0]]
        if len(places) == 2:
            other = refs[places[1]]
            is_first = index_ref[19] == 0
            whole[...] = jnp.where(is_first, source[...], other[...])
            source = whole
        elif len(source.shape) == 4:
            source = source.at[index_ref[10 + bit]]
        matrix = couple_ref[index_ref[1 + bit]]
        add_term(total, matrix, source[0], source[1], coef_ref[0, bit], coef_ref[1, bit])


def early_kernel(parts, index_ref, coef_ref, couple_ref, ham_ref, own_ref, *refs, with_prior):
    if with_prior:
        prior_ref, *refs = refs
    *partner_refs, total, whole = refs
    if with_prior:
        total[...] = coef_ref[2, 0] * prior_ref[...]
    else:
        total[...] = jnp.zeros_like(total)
    add_commutator(total, ham_ref, own_ref[0], own_ref[1])
    add_bits(total, parts, index_ref, coef_ref, couple_ref, partner_refs, whole)


def middle_kernel(parts, index_ref, coef_ref, couple_ref, own_ref, total_ref, *refs):
    *partner_refs, slope_ref, middle_ref, whole = refs
    slope_ref[...] = total_ref[...]
    add_bits(slope_ref, parts, index_ref, coef_ref, couple_ref, partner_refs, whole)
    middle = coef_ref[2, 0] * own_ref[...].astype(float32) + step_size * slope_ref[...]
    middle_ref[...] = middle.astype(bfloat16)


def last_kernel(parts, index_ref, coef_ref, couple_ref, total_ref, *refs):
    *partner_refs, near_ref, far_ref, whole, total = refs
    total[...] = total_ref[...]
    add_bits(total, parts, index_ref, coef_ref, couple_ref, partner_refs, whole)
    near = index_ref[0]
    rows = near_ref.shape[1]
    near_ref[...] = half_step * total[:, rows_of(near, rows), :]
    far_ref[...] = (half_step * total[:, rows_of(1 - near, rows), :]).astype(bfloat16)


in_vmem = pl.BlockSpec(memory_space=pltpu.VMEM)
in_smem = pl.BlockSpec(memory_space=pltpu.SMEM)


def shaped(kind, *dims):
    return jax.ShapeDtypeStruct(dims, kind)


def local(rho_real, rho_imag, ham, couple, rates, coeff_real, coeff_imag, occupation, upper, lower):
    rep = lax.axis_index("rep")
    rows, levels = rho_real.shape[1:]
    bit_count = lax.axis_size(hier).bit_length()

    own_index = 2 * lax.axis_index(hier) + rep
    occ_float = occupation.astype(float32)
    decay = jnp.sum(occ_float * rates[None, :], axis=1)
    pick = lambda table: jnp.where(rep == 0, table[0], table[1])
    own_occ, own_up, own_low, own_decay = pick(occ_float), pick(upper), pick(lower), pick(decay)
    partner = jnp.bitwise_xor(own_index, jnp.left_shift(1, jnp.arange(bit_count, dtype=jnp.int32)))
    is_above = own_up[None, :] == partner[:, None]
    is_below = own_low[None, :] == partner[:, None]
    mode_range = jnp.arange(couple.shape[0], dtype=jnp.int32)
    modes = jnp.sum(jnp.where(is_above | is_below, mode_range[None, :], 0), axis=1)
    weight_a = jnp.sum(jnp.where(is_above, 1.0, jnp.where(is_below, (own_occ * coeff_real)[None, :], 0.0)), axis=1)
    weight_b = jnp.sum(jnp.where(is_below, (own_occ * coeff_imag)[None, :], 0.0), axis=1)
    keep = 1.0 - step_size * own_decay
    x_place = 2 * rep + lax.axis_index("x_lo")
    y_place = lax.axis_index("y")
    places = jnp.array([2, 0, 1, 2, 0, 0, 0, 0, 1], jnp.int32)
    places = jnp.bitwise_xor(jnp.where(jnp.array([i in (0, 8) for i in range(9)]), x_place, y_place), places)
    index = jnp.concatenate([rep[None], modes, places, lax.axis_index("core")[None]]).astype(jnp.int32)
    keeps = jnp.where(jnp.arange(bit_count) < 2, keep, 0.0)
    coef = jnp.stack([weight_a, weight_b, keeps]).astype(float32)

    whole = shaped(bfloat16, 2, levels, levels)
    slope = shaped(float32, 2, levels, levels)
    half = shaped(bfloat16, 2, rows, levels)
    half_float = shaped(float32, 2, rows, levels)

    def exchange(full):
        first = across(full, inward, outward)
        z2 = swapped(full, "z", 2)
        z1 = swapped(full, "z", 1)
        own = across(full, None, inward)
        second = across(first, outward, inward)
        along_y = lax.all_gather(full, "y", axis=0)
        core = swapped(full, "core", 1)
        x2 = swapped(after(full, z1), "rep", 1)
        x1 = swapped(after(full, z1), "x_lo", 1)
        early = {6: [first, own], 4: [z1], 5: [z2], 1: [core], 8: [x1], 0: [x2], 2: [along_y], 3: [along_y]}
        return early, {7: [second]}

    def call(body, parts, outs, scratch, *operands):
        held = []
        places = []
        for bit, arrays in parts.items():
            for array in arrays:
                if not any(array is other for other in held):
                    held.append(array)
            places.append((bit, tuple(next(i for i, x in enumerate(held) if x is array) for array in arrays)))
        arrays = (index, coef, couple, *operands, *held)
        counts = tuple(places)
        moved = sum(x.size * x.dtype.itemsize for x in (*arrays, *outs))
        return pl.pallas_call(
            lambda *refs: body(counts, *refs),
            out_shape=outs,
            in_specs=[in_smem, in_smem] + [in_vmem] * (len(arrays) - 2),
            out_specs=[in_vmem] * len(outs),
            scratch_shapes=[pltpu.VMEM((2, levels, levels), bfloat16), *scratch],
            cost_estimate=pl.CostEstimate(flops=len(parts) * 8 * levels**3, bytes_accessed=moved, transcendentals=0),
            compiler_params=pltpu.CompilerParams(vmem_limit_bytes=24 * 2**20),
        )(*arrays)

    rounded = jnp.stack([rho_real, rho_imag]).astype(bfloat16)
    near = jnp.where(rep == 0, rounded[:, 0], rounded[:, 1])
    away = jnp.where(rep == 0, rounded[:, 1], rounded[:, 0])
    far = swapped(away, "rep", 1)
    full = jnp.where(rep == 0, jnp.concatenate([near, far], axis=1), jnp.concatenate([far, near], axis=1))

    early, late = exchange(full)
    (total,) = call(functools.partial(early_kernel, with_prior=False), early, [slope], [], ham, full)
    first, middle = call(middle_kernel, late, [slope, whole], [], full, total)

    early, late = exchange(middle)
    (total,) = call(functools.partial(early_kernel, with_prior=True), early, [slope], [], ham, middle, first)
    near, away = call(last_kernel, late, [half_float, half], [pltpu.VMEM((2, levels, levels), float32)], total)
    far = swapped(away, "rep", 1).astype(float32)
    stay = 1.0 - step_size * decay + (0.5 * step_size * step_size) * decay * decay
    is_own = (jnp.arange(2) == rep)[:, None, None]
    outs = []
    for part, state in enumerate((rho_real, rho_imag)):
        change = jnp.where(is_own, near[part][None], far[part][None])
        outs.append(stay[:, None, None] * state + change)
    return tuple(outs)


def solution(mesh):
    axes = Mesh(mesh.devices.reshape(*hier_sizes, mesh.shape["rep"]), (*hier, "rep"))
    placed = (
        P(hier, "rep", None),
        P(hier, "rep", None),
        P(),
        P(),
        P(),
        P(),
        P(),
        P(hier, None),
        P(hier, None),
        P(hier, None),
    )
    return jax.shard_map(
        local,
        mesh=axes,
        in_specs=placed,
        out_specs=(P(hier, "rep", None), P(hier, "rep", None)),
        check_vma=False,
    )
```

time: 169 us -> 160 us (0.947)
  the two profiles are of different devices: /device:TPU:1 before, /device:TPU:65 now
where the time goes in v2:
time: 160 us; the launch traced here: 159 us
  starting transfers between devices  85.4 us (53%)
  waiting for transfers between devices  31.8 us (20%)
  between operations  15.8 us (10%)
  local copies, waits for them, and re-layouts  13.1 us (8%)
  Pallas kernels  8.72 us (5%)
  other arithmetic  4.4 us (3%)
    ppermute x6, starting transfers between devices, across(): return lax.ppermute(value, ('z', 'core'), pairs)  45.4 us
    ppermute x12, starting transfers between devices, swapped(): return lax.ppermute(value, axis, pairs)  39.9 us
    ppermute x6, waiting for transfers between devices, across(): return lax.ppermute(value, ('z', 'core'), pairs)  15.9 us
    ppermute x12, waiting for transfers between devices, swapped(): return lax.ppermute(value, axis, pairs)  15.8 us
    unnamed x52, local copies, waits for them, and re-layouts  12.5 us
    pallas_call x4, Pallas kernels, call(): pl.pallas_call(lambda *refs: body(counts, *refs), out_shape=outs, in_spec...  8.72 us
  transfers between devices with their start and end apart: 20, of which 6 were waited for; matrix products, arithmetic and copies ran while one was open for 1% of the time, Pallas kernels for 4%

profile of v2, /device:TPU:65, one launch (start us, length us, event | category | flops | bytes accessed | tf_op | source)
XLA Modules:
  0.0 159.2 jit_solution(9066408253255924438)
XLA Ops:
  7.3 1.2 convert_bitcast_fusion
  8.6 4.7 %collective-permute-start = (bf16[2,128,256]{2,1,0:T(8,128)(2,1)S(1)}, bf16[2,128,256]{2,1,0:T(8,128)(2,1)S(1)}, u32[]{:S(2)}, u32[]{:S(2)}) collective-permute-start(bf16[2,128,256]{2,1,0:T(8,128)(2,1)S(1)} %get-tuple-element.21), channel_id=1, source_target_pairs={{0,1},{1,0},{2,3},{3,2},{4,5},{5,4},{6,7},{7,6},{8,9},{9,8},{10,11... | collective-permute-start | bytes 393224 | tf_op jit(solution)/shard_map/ppermute | solution.py:21
  13.9 2.4 %collective-permute-done = bf16[2,128,256]{2,1,0:T(8,128)(2,1)S(1)} collective-permute-done((bf16[2,128,256]{2,1,0:T(8,128)(2,1)S(1)}, bf16[2,128,256]{2,1,0:T(8,128)(2,1)S(1)}, u32[]{:S(2)}, u32[]{:S(2)}) %collective-permute-start) | collective-permute-done | bytes 131104 | tf_op jit(solution)/shard_map/ppermute | solution.py:21
  17.6 3.5 %collective-permute-start.5 = (bf16[2,256,256]{2,1,0:T(8,128)(2,1)S(1)}, bf16[2,256,256]{2,1,0:T(8,128)(2,1)S(1)}, u32[]{:S(2)}, u32[]{:S(2)}) collective-permute-start(bf16[2,256,256]{2,1,0:T(8,128)(2,1)S(1)} %maximum_select_fusion.refs_4_.refs_3_), channel_id=1, source_target_pairs={{0,2},{2,0},{1,3},{3,1},{4,6},{6,4},{5,7},{7,5},{8,10},{10,8},{9,1... | collective-permute-start | bytes 786440 | tf_op jit(solution)/shard_map/ppermute | solution.py:21
  21.1 3.5 %collective-permute-start.3 = (bf16[2,256,256]{2,1,0:T(8,128)(2,1)S(1)}, bf16[2,256,256]{2,1,0:T(8,128)(2,1)S(1)}, u32[]{:S(2)}, u32[]{:S(2)}) collective-permute-start(bf16[2,256,256]{2,1,0:T(8,128)(2,1)S(1)} %maximum_select_fusion.refs_4_.refs_3_), channel_id=1, source_target_pairs={{0,16},{16,0},{32,48},{48,32},{64,80},{80,64},{96,112},{112,96},{1... | collective-permute-start | bytes 786440 | tf_op jit(solution)/shard_map/ppermute | solution.py:21
  24.7 9.8 %collective-permute-start.1 = (bf16[2,256,256]{2,1,0:T(8,128)(2,1)S(1)}, bf16[2,256,256]{2,1,0:T(8,128)(2,1)S(1)}, u32[]{:S(2)}, u32[]{:S(2)}) collective-permute-start(bf16[2,256,256]{2,1,0:T(8,128)(2,1)S(1)} %maximum_select_fusion.refs_4_.refs_3_), channel_id=1, source_target_pairs={{0,64},{2,194},{16,80},{18,210},{32,96},{34,226},{48,112},{50,242}... | collective-permute-start | bytes 786440 | tf_op jit(solution)/shard_map/ppermute | solution.py:31
  36.5 3.1 %collective-permute-start.4 = (bf16[2,256,256]{2,1,0:T(8,128)(2,1)S(1)}, bf16[2,256,256]{2,1,0:T(8,128)(2,1)S(1)}, u32[]{:S(2)}, u32[]{:S(2)}) collective-permute-start(bf16[2,256,256]{2,1,0:T(8,128)(2,1)S(1)} %maximum_select_fusion.refs_4_.refs_3_), channel_id=1, source_target_pairs={{0,32},{16,48},{32,0},{48,16},{64,96},{80,112},{96,64},{112,80},{1... | collective-permute-start | bytes 786440 | tf_op jit(solution)/shard_map/ppermute | solution.py:21
  39.6 5.2 %collective-permute-start.2 = (bf16[2,256,256]{2,1,0:T(8,128)(2,1)S(1)}, bf16[2,256,256]{2,1,0:T(8,128)(2,1)S(1)}, u32[]{:S(2)}, u32[]{:S(2)}) collective-permute-start(bf16[2,256,256]{2,1,0:T(8,128)(2,1)S(1)} %maximum_select_fusion.refs_4_.refs_3_), channel_id=1, source_target_pairs={{2,66},{18,82},{34,98},{50,114},{66,2},{82,18},{98,34},{114,50},{1... | collective-permute-start | bytes 786440 | tf_op jit(solution)/shard_map/ppermute | solution.py:31
  44.8 4.7 %collective-permute-start.7 = (bf16[2,256,256]{2,1,0:T(8,128)(2,1)S(1)}, bf16[2,256,256]{2,1,0:T(8,128)(2,1)S(1)}, u32[]{:S(2)}, u32[]{:S(2)}) collective-permute-start(bf16[2,256,256]{2,1,0:T(8,128)(2,1)S(1)} %maximum_select_fusion.refs_4_.refs_3_), channel_id=1, source_target_pairs={{0,1},{1,0},{2,3},{3,2},{4,5},{5,4},{6,7},{7,6},{8,9},{9,8},{10,11... | collective-permute-start | bytes 786440 | tf_op jit(solution)/shard_map/ppermute | solution.py:21
  49.5 2.2 %collective-permute-start.6 = (bf16[2,256,256]{2,1,0:T(8,128)(2,1)S(1)}, bf16[2,256,256]{2,1,0:T(8,128)(2,1)S(1)}, u32[]{:S(2)}, u32[]{:S(2)}) collective-permute-start(bf16[2,256,256]{2,1,0:T(8,128)(2,1)S(1)} %maximum_select_fusion.refs_4_.refs_3_), channel_id=1, source_target_pairs={{0,256},{256,0},{1,257},{257,1},{2,258},{258,2},{3,259},{259,3},{4... | collective-permute-start | bytes 786440 | tf_op jit(solution)/shard_map/ppermute | solution.py:21
  51.7 5.8 %collective-permute-done.1.refs_5_ = bf16[2,256,256]{2,1,0:T(8,128)(2,1)S(1)} collective-permute-done((bf16[2,256,256]{2,1,0:T(8,128)(2,1)S(1)}, bf16[2,256,256]{2,1,0:T(8,128)(2,1)S(1)}, u32[]{:S(2)}, u32[]{:S(2)}) %collective-permute-start.1) | collective-permute-done | bytes 262176 | tf_op jit(solution)/shard_map/ppermute | solution.py:31
  57.5 1.9 %collective-permute-start.8 = (bf16[2,256,256]{2,1,0:T(8,128)(2,1)S(1)}, bf16[2,256,256]{2,1,0:T(8,128)(2,1)S(1)}, u32[]{:S(2)}, u32[]{:S(2)}) collective-permute-start(bf16[2,256,256]{2,1,0:T(8,128)(2,1)S(1)} %collective-permute-done.1.refs_5_), channel_id=1, source_target_pairs={{0,192},{2,66},{16,208},{18,82},{32,224},{34,98},{48,240},{50,114}... | collective-permute-start | bytes 786440 | tf_op jit(solution)/shard_map/ppermute | solution.py:31
  59.5 8.1 %collective-permute-done.4.refs_8_ = bf16[2,256,256]{2,1,0:T(8,128)(2,1)S(1)} collective-permute-done((bf16[2,256,256]{2,1,0:T(8,128)(2,1)S(1)}, bf16[2,256,256]{2,1,0:T(8,128)(2,1)S(1)}, u32[]{:S(2)}, u32[]{:S(2)}) %collective-permute-start.4) | collective-permute-done | bytes 262176 | tf_op jit(solution)/shard_map/ppermute | solution.py:21
  67.7 2.0 %collective-permute-done.2.refs_6_ = bf16[2,256,256]{2,1,0:T(8,128)(2,1)S(1)} collective-permute-done((bf16[2,256,256]{2,1,0:T(8,128)(2,1)S(1)}, bf16[2,256,256]{2,1,0:T(8,128)(2,1)S(1)}, u32[]{:S(2)}, u32[]{:S(2)}) %collective-permute-start.2) | collective-permute-done | bytes 262176 | tf_op jit(solution)/shard_map/ppermute | solution.py:31
  71.8 1.2 copy-done.1
  75.9 2.6 %shard_map.131.refs_4_ = f32[2,256,256]{2,1,0:T(8,128)S(1)} custom-call(s32[20]{0:T(128)S(1)} %pad_add_fusion.refs_0_, f32[3,9]{1,0:T(4,128)S(1)} %pad_maximum_fusion.1.refs_1_, bf16[12,256,256]{2,1,0:T(8,128)(2,1)S(1)} %copy-done, bf16[2,256,256]{2,1,0:T(8,128)(2,1)S(1)} %copy-done.3, bf16[2,256,256]{2,1,0:T(8,128)(2,1)S(1)} %maximum_select_fusion.refs_4_.refs_3_, ...), custom_call_target="tpu_custom_call" | custom-call | flops 1073741824 | bytes 5505212 | tf_op jit(solution)/shard_map/pallas_call | solution.py:176
  78.5 1.7 %shard_map.132 = (f32[2,256,256]{2,1,0:T(8,128)S(1)}, bf16[2,256,256]{2,1,0:T(8,128)(2,1)}) custom-call(s32[20]{0:T(128)S(1)} %pad_add_fusion.refs_0_, f32[3,9]{1,0:T(4,128)S(1)} %pad_maximum_fusion.1.refs_1_, bf16[12,256,256]{2,1,0:T(8,128)(2,1)S(1)} %copy-done, bf16[2,256,256]{2,1,0:T(8,128)(2,1)S(1)} %maximum_select_fusion.refs_4_.refs_3_, ...), custom_call_target="tpu_custom_call" | custom-call | flops 134217728 | bytes 3408060 | tf_op jit(solution)/shard_map/pallas_call | solution.py:176
  80.2 1.9 %collective-permute-start.11 = (bf16[2,256,256]{2,1,0:T(8,128)(2,1)}, bf16[2,256,256]{2,1,0:T(8,128)(2,1)S(1)}, u32[]{:S(2)}, u32[]{:S(2)}) collective-permute-start(bf16[2,256,256]{2,1,0:T(8,128)(2,1)} %get-tuple-element.11.refs_4_), channel_id=1, source_target_pairs={{0,16},{16,0},{32,48},{48,32},{64,80},{80,64},{96,112},{112,96},{1... | collective-permute-start | bytes 786440 | tf_op jit(solution)/shard_map/ppermute | solution.py:21
  82.1 1.9 %collective-permute-start.13 = (bf16[2,256,256]{2,1,0:T(8,128)(2,1)}, bf16[2,256,256]{2,1,0:T(8,128)(2,1)S(1)}, u32[]{:S(2)}, u32[]{:S(2)}) collective-permute-start(bf16[2,256,256]{2,1,0:T(8,128)(2,1)} %get-tuple-element.11.refs_4_), channel_id=1, source_target_pairs={{0,2},{2,0},{1,3},{3,1},{4,6},{6,4},{5,7},{7,5},{8,10},{10,8},{9,1... | collective-permute-start | bytes 786440 | tf_op jit(solution)/shard_map/ppermute | solution.py:21
  84.1 5.8 %collective-permute-start.9 = (bf16[2,256,256]{2,1,0:T(8,128)(2,1)}, bf16[2,256,256]{2,1,0:T(8,128)(2,1)S(1)}, u32[]{:S(2)}, u32[]{:S(2)}) collective-permute-start(bf16[2,256,256]{2,1,0:T(8,128)(2,1)} %get-tuple-element.11.refs_4_), channel_id=1, source_target_pairs={{0,64},{2,194},{16,80},{18,210},{32,96},{34,226},{48,112},{50,242}... | collective-permute-start | bytes 786440 | tf_op jit(solution)/shard_map/ppermute | solution.py:31
  89.9 6.8 %collective-permute-start.12 = (bf16[2,256,256]{2,1,0:T(8,128)(2,1)}, bf16[2,256,256]{2,1,0:T(8,128)(2,1)S(1)}, u32[]{:S(2)}, u32[]{:S(2)}) collective-permute-start(bf16[2,256,256]{2,1,0:T(8,128)(2,1)} %get-tuple-element.11.refs_4_), channel_id=1, source_target_pairs={{0,32},{16,48},{32,0},{48,16},{64,96},{80,112},{96,64},{112,80},{1... | collective-permute-start | bytes 786440 | tf_op jit(solution)/shard_map/ppermute | solution.py:21
  96.7 3.6 %collective-permute-start.10 = (bf16[2,256,256]{2,1,0:T(8,128)(2,1)}, bf16[2,256,256]{2,1,0:T(8,128)(2,1)S(1)}, u32[]{:S(2)}, u32[]{:S(2)}) collective-permute-start(bf16[2,256,256]{2,1,0:T(8,128)(2,1)} %get-tuple-element.11.refs_4_), channel_id=1, source_target_pairs={{2,66},{18,82},{34,98},{50,114},{66,2},{82,18},{98,34},{114,50},{1... | collective-permute-start | bytes 786440 | tf_op jit(solution)/shard_map/ppermute | solution.py:31
  100.3 3.5 %collective-permute-start.15 = (bf16[2,256,256]{2,1,0:T(8,128)(2,1)}, bf16[2,256,256]{2,1,0:T(8,128)(2,1)S(1)}, u32[]{:S(2)}, u32[]{:S(2)}) collective-permute-start(bf16[2,256,256]{2,1,0:T(8,128)(2,1)} %get-tuple-element.11.refs_4_), channel_id=1, source_target_pairs={{0,1},{1,0},{2,3},{3,2},{4,5},{5,4},{6,7},{7,6},{8,9},{9,8},{10,11... | collective-permute-start | bytes 786440 | tf_op jit(solution)/shard_map/ppermute | solution.py:21
  103.8 2.2 %collective-permute-start.14 = (bf16[2,256,256]{2,1,0:T(8,128)(2,1)}, bf16[2,256,256]{2,1,0:T(8,128)(2,1)S(1)}, u32[]{:S(2)}, u32[]{:S(2)}) collective-permute-start(bf16[2,256,256]{2,1,0:T(8,128)(2,1)} %get-tuple-element.11.refs_4_), channel_id=1, source_target_pairs={{0,256},{256,0},{1,257},{257,1},{2,258},{258,2},{3,259},{259,3},{4... | collective-permute-start | bytes 786440 | tf_op jit(solution)/shard_map/ppermute | solution.py:21
  106.1 8.2 %collective-permute-done.9.refs_6_ = bf16[2,256,256]{2,1,0:T(8,128)(2,1)S(1)} collective-permute-done((bf16[2,256,256]{2,1,0:T(8,128)(2,1)}, bf16[2,256,256]{2,1,0:T(8,128)(2,1)S(1)}, u32[]{:S(2)}, u32[]{:S(2)}) %collective-permute-start.9) | collective-permute-done | bytes 262176 | tf_op jit(solution)/shard_map/ppermute | solution.py:31
  114.2 19.1 %collective-permute-start.16 = (bf16[2,256,256]{2,1,0:T(8,128)(2,1)S(1)}, bf16[2,256,256]{2,1,0:T(8,128)(2,1)}, u32[]{:S(2)}, u32[]{:S(2)}) collective-permute-start(bf16[2,256,256]{2,1,0:T(8,128)(2,1)S(1)} %collective-permute-done.9.refs_6_), channel_id=1, source_target_pairs={{0,192},{2,66},{16,208},{18,82},{32,224},{34,98},{48,240},{50,114}... | collective-permute-start | bytes 786440 | tf_op jit(solution)/shard_map/ppermute | solution.py:31
  135.6 1.2 copy-done.2
  139.7 3.0 %shard_map.133.refs_3_ = f32[2,256,256]{2,1,0:T(8,128)S(1)} custom-call(s32[20]{0:T(128)S(1)} %pad_add_fusion.refs_0_, f32[3,9]{1,0:T(4,128)S(1)} %pad_maximum_fusion.1.refs_1_, bf16[12,256,256]{2,1,0:T(8,128)(2,1)S(1)} %copy-done, bf16[2,256,256]{2,1,0:T(8,128)(2,1)S(1)} %copy-done.3, bf16[2,256,256]{2,1,0:T(8,128)(2,1)} %get-tuple-element.11.refs_4_, ...), custom_call_target="tpu_custom_call" | custom-call | flops 1073741824 | bytes 6029500 | tf_op jit(solution)/shard_map/pallas_call | solution.py:176
  142.7 1.4 shard_map.134
  144.1 1.9 %collective-permute-start.17 = (bf16[2,128,256]{2,1,0:T(8,128)(2,1)S(1)}, bf16[2,128,256]{2,1,0:T(8,128)(2,1)S(1)}, u32[]{:S(2)}, u32[]{:S(2)}) collective-permute-start(bf16[2,128,256]{2,1,0:T(8,128)(2,1)S(1)} %get-tuple-element.13), channel_id=1, source_target_pairs={{0,1},{1,0},{2,3},{3,2},{4,5},{5,4},{6,7},{7,6},{8,9},{9,8},{10,11... | collective-permute-start | bytes 393224 | tf_op jit(solution)/shard_map/ppermute | solution.py:21
  146.1 5.3 %collective-permute-done.17 = bf16[2,128,256]{2,1,0:T(8,128)(2,1)S(1)} collective-permute-done((bf16[2,128,256]{2,1,0:T(8,128)(2,1)S(1)}, bf16[2,128,256]{2,1,0:T(8,128)(2,1)S(1)}, u32[]{:S(2)}, u32[]{:S(2)}) %collective-permute-start.17) | collective-permute-done | bytes 131104 | tf_op jit(solution)/shard_map/ppermute | solution.py:21
  151.4 0.9 select_add_fusion
  (88 shorter events, 13.1 us)
Async XLA Ops:
  7.2 10.3 %copy-start.23 = (pred[9]{0:T(512)(128)(4,1)S(1)}, pred[9]{0:T(512)(128)(4,1)}, u32[]{:S(2)}) copy-start(pred[9]{0:T(512)(128)(4,1)} %constant.46.clone) | copy-start | bytes 31
  7.2 10.2 %copy-start.24 = (s32[9]{0:T(128)S(1)}, s32[9]{0:T(128)}, u32[]{:S(2)}) copy-start(s32[9]{0:T(128)} %constant.45.clone) | copy-start | bytes 112
  7.2 17.4 %copy-start.18 = (s32[2,12]{1,0:T(2,128)S(1)}, s32[2,12]{1,0:T(2,128)}, u32[]{:S(2)}) copy-start(s32[2,12]{1,0:T(2,128)} %param.19) | copy-start | bytes 292
  7.2 10.0 %copy-start.20 = (s32[2,12]{1,0:T(2,128)S(1)}, s32[2,12]{1,0:T(2,128)}, u32[]{:S(2)}) copy-start(s32[2,12]{1,0:T(2,128)} %param.21) | copy-start | bytes 292
  7.2 10.0 %copy-start.19 = (s32[2,12]{1,0:T(2,128)S(1)}, s32[2,12]{1,0:T(2,128)}, u32[]{:S(2)}) copy-start(s32[2,12]{1,0:T(2,128)} %param.20) | copy-start | bytes 292
  7.2 10.2 %copy-start.21 = (f32[12]{0:T(128)S(1)}, f32[12]{0:T(128)}, u32[]{:S(2)}) copy-start(f32[12]{0:T(128)} %param.18) | copy-start | bytes 148
  7.2 10.2 %copy-start.22 = (f32[12]{0:T(128)S(1)}, f32[12]{0:T(128)}, u32[]{:S(2)}) copy-start(f32[12]{0:T(128)} %param.17) | copy-start | bytes 148
  7.2 17.4 %copy-start.25 = (f32[12]{0:T(128)S(1)}, f32[12]{0:T(128)}, u32[]{:S(2)}) copy-start(f32[12]{0:T(128)} %param.16) | copy-start | bytes 148
  7.3 64.5 %copy-start = (bf16[12,256,256]{2,1,0:T(8,128)(2,1)S(1)}, bf16[12,256,256]{2,1,0:T(8,128)(2,1)}, u32[]{:S(2)}) copy-start(bf16[12,256,256]{2,1,0:T(8,128)(2,1)} %refs_2_.7) | copy-start | bytes 4718596
  7.3 64.5 %copy-start.3 = (bf16[2,256,256]{2,1,0:T(8,128)(2,1)S(1)}, bf16[2,256,256]{2,1,0:T(8,128)(2,1)}, u32[]{:S(2)}) copy-start(bf16[2,256,256]{2,1,0:T(8,128)(2,1)} %refs_3_.3) | copy-start | bytes 786436
  7.3 64.5 %all-gather.4.cloned.1.call-start = ((), (), s32[]{:S(2)}) async-start(), calls=%async_computation | async-start | bytes 1310720 | tf_op jit(solution)/shard_map/all_gather | solution.py:158
  8.6 7.8 %collective-permute-start = (bf16[2,128,256]{2,1,0:T(8,128)(2,1)S(1)}, bf16[2,128,256]{2,1,0:T(8,128)(2,1)S(1)}, u32[]{:S(2)}, u32[]{:S(2)}) collective-permute-start(bf16[2,128,256]{2,1,0:T(8,128)(2,1)S(1)} %get-tuple-element.21), channel_id=1, source_target_pairs={{0,1},{1,0},{2,3},{3,2},{4,5},{5,4},{6,7},{7,6},{8,9},{9,8},{10,11... | collective-permute-start | bytes 393224 | tf_op jit(solution)/shard_map/ppermute | solution.py:21
  17.2 118.4 %all-gather.6.cloned.1.call-start = ((), (), s32[]{:S(2)}) async-start(), calls=%async_computation.1 | async-start | bytes 1310720 | tf_op jit(solution)/shard_map/all_gather | solution.py:158
  17.6 31.9 %collective-permute-start.5 = (bf16[2,256,256]{2,1,0:T(8,128)(2,1)S(1)}, bf16[2,256,256]{2,1,0:T(8,128)(2,1)S(1)}, u32[]{:S(2)}, u32[]{:S(2)}) collective-permute-start(bf16[2,256,256]{2,1,0:T(8,128)(2,1)S(1)} %maximum_select_fusion.refs_4_.refs_3_), channel_id=1, source_target_pairs={{0,2},{2,0},{1,3},{3,1},{4,6},{6,4},{5,7},{7,5},{8,10},{10,8},{9,1... | collective-permute-start | bytes 786440 | tf_op jit(solution)/shard_map/ppermute | solution.py:21
  21.1 23.8 %collective-permute-start.3 = (bf16[2,256,256]{2,1,0:T(8,128)(2,1)S(1)}, bf16[2,256,256]{2,1,0:T(8,128)(2,1)S(1)}, u32[]{:S(2)}, u32[]{:S(2)}) collective-permute-start(bf16[2,256,256]{2,1,0:T(8,128)(2,1)S(1)} %maximum_select_fusion.refs_4_.refs_3_), channel_id=1, source_target_pairs={{0,16},{16,0},{32,48},{48,32},{64,80},{80,64},{96,112},{112,96},{1... | collective-permute-start | bytes 786440 | tf_op jit(solution)/shard_map/ppermute | solution.py:21
  24.7 32.8 %collective-permute-start.1 = (bf16[2,256,256]{2,1,0:T(8,128)(2,1)S(1)}, bf16[2,256,256]{2,1,0:T(8,128)(2,1)S(1)}, u32[]{:S(2)}, u32[]{:S(2)}) collective-permute-start(bf16[2,256,256]{2,1,0:T(8,128)(2,1)S(1)} %maximum_select_fusion.refs_4_.refs_3_), channel_id=1, source_target_pairs={{0,64},{2,194},{16,80},{18,210},{32,96},{34,226},{48,112},{50,242}... | collective-permute-start | bytes 786440 | tf_op jit(solution)/shard_map/ppermute | solution.py:31
  36.5 31.1 %collective-permute-start.4 = (bf16[2,256,256]{2,1,0:T(8,128)(2,1)S(1)}, bf16[2,256,256]{2,1,0:T(8,128)(2,1)S(1)}, u32[]{:S(2)}, u32[]{:S(2)}) collective-permute-start(bf16[2,256,256]{2,1,0:T(8,128)(2,1)S(1)} %maximum_select_fusion.refs_4_.refs_3_), channel_id=1, source_target_pairs={{0,32},{16,48},{32,0},{48,16},{64,96},{80,112},{96,64},{112,80},{1... | collective-permute-start | bytes 786440 | tf_op jit(solution)/shard_map/ppermute | solution.py:21
  39.6 30.0 %collective-permute-start.2 = (bf16[2,256,256]{2,1,0:T(8,128)(2,1)S(1)}, bf16[2,256,256]{2,1,0:T(8,128)(2,1)S(1)}, u32[]{:S(2)}, u32[]{:S(2)}) collective-permute-start(bf16[2,256,256]{2,1,0:T(8,128)(2,1)S(1)} %maximum_select_fusion.refs_4_.refs_3_), channel_id=1, source_target_pairs={{2,66},{18,82},{34,98},{50,114},{66,2},{82,18},{98,34},{114,50},{1... | collective-permute-start | bytes 786440 | tf_op jit(solution)/shard_map/ppermute | solution.py:31
  44.8 25.5 %collective-permute-start.7 = (bf16[2,256,256]{2,1,0:T(8,128)(2,1)S(1)}, bf16[2,256,256]{2,1,0:T(8,128)(2,1)S(1)}, u32[]{:S(2)}, u32[]{:S(2)}) collective-permute-start(bf16[2,256,256]{2,1,0:T(8,128)(2,1)S(1)} %maximum_select_fusion.refs_4_.refs_3_), channel_id=1, source_target_pairs={{0,1},{1,0},{2,3},{3,2},{4,5},{5,4},{6,7},{7,6},{8,9},{9,8},{10,11... | collective-permute-start | bytes 786440 | tf_op jit(solution)/shard_map/ppermute | solution.py:21
  49.5 21.6 %collective-permute-start.6 = (bf16[2,256,256]{2,1,0:T(8,128)(2,1)S(1)}, bf16[2,256,256]{2,1,0:T(8,128)(2,1)S(1)}, u32[]{:S(2)}, u32[]{:S(2)}) collective-permute-start(bf16[2,256,256]{2,1,0:T(8,128)(2,1)S(1)} %maximum_select_fusion.refs_4_.refs_3_), channel_id=1, source_target_pairs={{0,256},{256,0},{1,257},{257,1},{2,258},{258,2},{3,259},{259,3},{4... | collective-permute-start | bytes 786440 | tf_op jit(solution)/shard_map/ppermute | solution.py:21
  57.5 21.0 %collective-permute-start.8 = (bf16[2,256,256]{2,1,0:T(8,128)(2,1)S(1)}, bf16[2,256,256]{2,1,0:T(8,128)(2,1)S(1)}, u32[]{:S(2)}, u32[]{:S(2)}) collective-permute-start(bf16[2,256,256]{2,1,0:T(8,128)(2,1)S(1)} %collective-permute-done.1.refs_5_), channel_id=1, source_target_pairs={{0,192},{2,66},{16,208},{18,82},{32,224},{34,98},{48,240},{50,114}... | collective-permute-start | bytes 786440 | tf_op jit(solution)/shard_map/ppermute | solution.py:31
  80.2 20.1 %collective-permute-start.11 = (bf16[2,256,256]{2,1,0:T(8,128)(2,1)}, bf16[2,256,256]{2,1,0:T(8,128)(2,1)S(1)}, u32[]{:S(2)}, u32[]{:S(2)}) collective-permute-start(bf16[2,256,256]{2,1,0:T(8,128)(2,1)} %get-tuple-element.11.refs_4_), channel_id=1, source_target_pairs={{0,16},{16,0},{32,48},{48,32},{64,80},{80,64},{96,112},{112,96},{1... | collective-permute-start | bytes 786440 | tf_op jit(solution)/shard_map/ppermute | solution.py:21
  82.1 21.7 %collective-permute-start.13 = (bf16[2,256,256]{2,1,0:T(8,128)(2,1)}, bf16[2,256,256]{2,1,0:T(8,128)(2,1)S(1)}, u32[]{:S(2)}, u32[]{:S(2)}) collective-permute-start(bf16[2,256,256]{2,1,0:T(8,128)(2,1)} %get-tuple-element.11.refs_4_), channel_id=1, source_target_pairs={{0,2},{2,0},{1,3},{3,1},{4,6},{6,4},{5,7},{7,5},{8,10},{10,8},{9,1... | collective-permute-start | bytes 786440 | tf_op jit(solution)/shard_map/ppermute | solution.py:21
  84.1 30.2 %collective-permute-start.9 = (bf16[2,256,256]{2,1,0:T(8,128)(2,1)}, bf16[2,256,256]{2,1,0:T(8,128)(2,1)S(1)}, u32[]{:S(2)}, u32[]{:S(2)}) collective-permute-start(bf16[2,256,256]{2,1,0:T(8,128)(2,1)} %get-tuple-element.11.refs_4_), channel_id=1, source_target_pairs={{0,64},{2,194},{16,80},{18,210},{32,96},{34,226},{48,112},{50,242}... | collective-permute-start | bytes 786440 | tf_op jit(solution)/shard_map/ppermute | solution.py:31
  89.9 43.5 %collective-permute-start.12 = (bf16[2,256,256]{2,1,0:T(8,128)(2,1)}, bf16[2,256,256]{2,1,0:T(8,128)(2,1)S(1)}, u32[]{:S(2)}, u32[]{:S(2)}) collective-permute-start(bf16[2,256,256]{2,1,0:T(8,128)(2,1)} %get-tuple-element.11.refs_4_), channel_id=1, source_target_pairs={{0,32},{16,48},{32,0},{48,16},{64,96},{80,112},{96,64},{112,80},{1... | collective-permute-start | bytes 786440 | tf_op jit(solution)/shard_map/ppermute | solution.py:21
  96.7 36.7 %collective-permute-start.10 = (bf16[2,256,256]{2,1,0:T(8,128)(2,1)}, bf16[2,256,256]{2,1,0:T(8,128)(2,1)S(1)}, u32[]{:S(2)}, u32[]{:S(2)}) collective-permute-start(bf16[2,256,256]{2,1,0:T(8,128)(2,1)} %get-tuple-element.11.refs_4_), channel_id=1, source_target_pairs={{2,66},{18,82},{34,98},{50,114},{66,2},{82,18},{98,34},{114,50},{1... | collective-permute-start | bytes 786440 | tf_op jit(solution)/shard_map/ppermute | solution.py:31
  100.3 33.8 %collective-permute-start.15 = (bf16[2,256,256]{2,1,0:T(8,128)(2,1)}, bf16[2,256,256]{2,1,0:T(8,128)(2,1)S(1)}, u32[]{:S(2)}, u32[]{:S(2)}) collective-permute-start(bf16[2,256,256]{2,1,0:T(8,128)(2,1)} %get-tuple-element.11.refs_4_), channel_id=1, source_target_pairs={{0,1},{1,0},{2,3},{3,2},{4,5},{5,4},{6,7},{7,6},{8,9},{9,8},{10,11... | collective-permute-start | bytes 786440 | tf_op jit(solution)/shard_map/ppermute | solution.py:21
  103.8 31.0 %collective-permute-start.14 = (bf16[2,256,256]{2,1,0:T(8,128)(2,1)}, bf16[2,256,256]{2,1,0:T(8,128)(2,1)S(1)}, u32[]{:S(2)}, u32[]{:S(2)}) collective-permute-start(bf16[2,256,256]{2,1,0:T(8,128)(2,1)} %get-tuple-element.11.refs_4_), channel_id=1, source_target_pairs={{0,256},{256,0},{1,257},{257,1},{2,258},{258,2},{3,259},{259,3},{4... | collective-permute-start | bytes 786440 | tf_op jit(solution)/shard_map/ppermute | solution.py:21
  114.2 28.5 %collective-permute-start.16 = (bf16[2,256,256]{2,1,0:T(8,128)(2,1)S(1)}, bf16[2,256,256]{2,1,0:T(8,128)(2,1)}, u32[]{:S(2)}, u32[]{:S(2)}) collective-permute-start(bf16[2,256,256]{2,1,0:T(8,128)(2,1)S(1)} %collective-permute-done.9.refs_6_), channel_id=1, source_target_pairs={{0,192},{2,66},{16,208},{18,82},{32,224},{34,98},{48,240},{50,114}... | collective-permute-start | bytes 786440 | tf_op jit(solution)/shard_map/ppermute | solution.py:31
  142.7 8.7 %copy-start.16 = (f32[2,128,256]{2,1,0:T(8,128)S(1)}, f32[2,128,256]{2,1,0:T(8,128)}, u32[]{:S(2)}) copy-start(f32[2,128,256]{2,1,0:T(8,128)} %param.13) | copy-start | bytes 786436
  142.7 8.7 %copy-start.17 = (f32[2,128,256]{2,1,0:T(8,128)S(1)}, f32[2,128,256]{2,1,0:T(8,128)}, u32[]{:S(2)}) copy-start(f32[2,128,256]{2,1,0:T(8,128)} %param.12) | copy-start | bytes 786436
  144.1 7.2 %collective-permute-start.17 = (bf16[2,128,256]{2,1,0:T(8,128)(2,1)S(1)}, bf16[2,128,256]{2,1,0:T(8,128)(2,1)S(1)}, u32[]{:S(2)}, u32[]{:S(2)}) collective-permute-start(bf16[2,128,256]{2,1,0:T(8,128)(2,1)S(1)} %get-tuple-element.13), channel_id=1, source_target_pairs={{0,1},{1,0},{2,3},{3,2},{4,5},{5,4},{6,7},{7,6},{8,9},{9,8},{10,11... | collective-permute-start | bytes 393224 | tf_op jit(solution)/shard_map/ppermute | solution.py:21
  (14 other events, 12.4 us)
Sparse Core Ops, SparseCore 0:
  17.3 35.3 all-gather.3
  80.3 31.2 all-gather.5

commit v3 on v2

--- a/solution.py
+++ b/solution.py
@@ -35,6 +35,10 @@
     return source ^ 4
 
 
+def opposite(source):
+    return source ^ 8
+
+
 def outward(source):
     return source - 4 if not source & 4 else source + 4
 
@@ -70,12 +74,8 @@
     for bit, places in parts:
         source = refs[places[0]]
         if len(places) == 2:
-            other = refs[places[1]]
-            is_first = index_ref[19] == 0
-            whole[...] = jnp.where(is_first, source[...], other[...])
+            whole[...] = jnp.where(index_ref[10] == 0, source[...], refs[places[1]][...])
             source = whole
-        elif len(source.shape) == 4:
-            source = source.at[index_ref[10 + bit]]
         matrix = couple_ref[index_ref[1 + bit]]
         add_term(total, matrix, source[0], source[1], coef_ref[0, bit], coef_ref[1, bit])
 
@@ -136,31 +136,28 @@
     weight_a = jnp.sum(jnp.where(is_above, 1.0, jnp.where(is_below, (own_occ * coeff_real)[None, :], 0.0)), axis=1)
     weight_b = jnp.sum(jnp.where(is_below, (own_occ * coeff_imag)[None, :], 0.0), axis=1)
     keep = 1.0 - step_size * own_decay
-    x_place = 2 * rep + lax.axis_index("x_lo")
-    y_place = lax.axis_index("y")
-    places = jnp.array([2, 0, 1, 2, 0, 0, 0, 0, 1], jnp.int32)
-    places = jnp.bitwise_xor(jnp.where(jnp.array([i in (0, 8) for i in range(9)]), x_place, y_place), places)
-    index = jnp.concatenate([rep[None], modes, places, lax.axis_index("core")[None]]).astype(jnp.int32)
+    index = jnp.concatenate([rep[None], modes, lax.axis_index("core")[None]]).astype(jnp.int32)
     keeps = jnp.where(jnp.arange(bit_count) < 2, keep, 0.0)
     coef = jnp.stack([weight_a, weight_b, keeps]).astype(float32)
 
+    on_first = lax.axis_index("core") == 0
     whole = shaped(bfloat16, 2, levels, levels)
     slope = shaped(float32, 2, levels, levels)
     half = shaped(bfloat16, 2, rows, levels)
     half_float = shaped(float32, 2, rows, levels)
 
     def exchange(full):
-        first = across(full, inward, outward)
+        z1 = swapped(full, "z", 1)
+        core = swapped(full, "core", 1)
+        first = across(full, inward, opposite)
         z2 = swapped(full, "z", 2)
-        z1 = swapped(full, "z", 1)
-        own = across(full, None, inward)
-        second = across(first, outward, inward)
-        along_y = lax.all_gather(full, "y", axis=0)
-        core = swapped(full, "core", 1)
+        x1 = swapped(full, "x_lo", 1)
         x2 = swapped(after(full, z1), "rep", 1)
-        x1 = swapped(after(full, z1), "x_lo", 1)
-        early = {6: [first, own], 4: [z1], 5: [z2], 1: [core], 8: [x1], 0: [x2], 2: [along_y], 3: [along_y]}
-        return early, {7: [second]}
+        y1 = swapped(after(full, core), "y", 1)
+        y2 = swapped(after(full, x1), "y", 2)
+        second = across(jnp.where(on_first, first, full), outward, inward)
+        early = {4: [z1], 1: [core], 5: [z2], 8: [x1], 0: [x2], 2: [y1], 3: [y2]}
+        return early, {6: [first, second], 7: [second, first]}
 
     def call(body, parts, outs, scratch, *operands):
         held = []
@@ -180,7 +177,7 @@
             out_specs=[in_vmem] * len(outs),
             scratch_shapes=[pltpu.VMEM((2, levels, levels), bfloat16), *scratch],
             cost_estimate=pl.CostEstimate(flops=len(parts) * 8 * levels**3, bytes_accessed=moved, transcendentals=0),
-            compiler_params=pltpu.CompilerParams(vmem_limit_bytes=24 * 2**20),
+            compiler_params=pltpu.CompilerParams(vmem_limit_bytes=12 * 2**20),
         )(*arrays)
 
     rounded = jnp.stack([rho_real, rho_imag]).astype(bfloat16)

time: 160 us -> 144 us (0.900)
  the two profiles are of different devices: /device:TPU:65 before, /device:TPU:33 now
where the time goes in v3:
time: 144 us; the launch traced here: 143 us
  starting transfers between devices  88.4 us (61%)
  waiting for transfers between devices  38.9 us (27%)
  Pallas kernels  7.21 us (5%)
  other arithmetic  5.77 us (4%)
  between operations  2.31 us (2%)
    ppermute x16, starting transfers between devices, swapped(): return lax.ppermute(value, axis, pairs)  58.1 us
    ppermute x4, starting transfers between devices, across(): return lax.ppermute(value, ('z', 'core'), pairs)  30.3 us
    ppermute x4, waiting for transfers between devices, across(): return lax.ppermute(value, ('z', 'core'), pairs)  23.6 us
    ppermute x16, waiting for transfers between devices, swapped(): return lax.ppermute(value, axis, pairs)  15.3 us
    pallas_call x4, Pallas kernels, call(): pl.pallas_call(lambda *refs: body(counts, *refs), out_shape=outs, in_spec...  7.21 us
  transfers between devices with their start and end apart: 20, of which 5 were waited for; matrix products, arithmetic and copies ran while one was open for 3% of the time, Pallas kernels for 3%

profile of v3, /device:TPU:33, one launch (start us, length us, event | category | flops | bytes accessed | tf_op | source)
XLA Modules:
  0.0 143.3 jit_solution(9961743188888087322)
XLA Ops:
  0.7 1.2 convert_bitcast_fusion
  1.9 4.7 %collective-permute-start = (bf16[2,128,256]{2,1,0:T(8,128)(2,1)S(1)}, bf16[2,128,256]{2,1,0:T(8,128)(2,1)S(1)}, u32[]{:S(2)}, u32[]{:S(2)}) collective-permute-start(bf16[2,128,256]{2,1,0:T(8,128)(2,1)S(1)} %get-tuple-element.29), channel_id=1, source_target_pairs={{0,1},{1,0},{2,3},{3,2},{4,5},{5,4},{6,7},{7,6},{8,9},{9,8},{10,11... | collective-permute-start | bytes 393224 | tf_op jit(solution)/shard_map/ppermute | solution.py:21
  7.2 0.8 multiply_reduce_fusion
  11.5 1.9 %collective-permute-start.1 = (bf16[2,256,256]{2,1,0:T(8,128)(2,1)S(1)}, bf16[2,256,256]{2,1,0:T(8,128)(2,1)S(1)}, u32[]{:S(2)}, u32[]{:S(2)}) collective-permute-start(bf16[2,256,256]{2,1,0:T(8,128)(2,1)S(1)} %maximum_select_fusion.refs_4_.refs_3_), channel_id=1, source_target_pairs={{0,16},{16,0},{32,48},{48,32},{64,80},{80,64},{96,112},{112,96},{1... | collective-permute-start | bytes 786440 | tf_op jit(solution)/shard_map/ppermute | solution.py:21
  13.4 6.9 %collective-permute-start.2 = (bf16[2,256,256]{2,1,0:T(8,128)(2,1)S(1)}, bf16[2,256,256]{2,1,0:T(8,128)(2,1)S(1)}, u32[]{:S(2)}, u32[]{:S(2)}) collective-permute-start(bf16[2,256,256]{2,1,0:T(8,128)(2,1)S(1)} %maximum_select_fusion.refs_4_.refs_3_), channel_id=1, source_target_pairs={{0,2},{2,0},{1,3},{3,1},{4,6},{6,4},{5,7},{7,5},{8,10},{10,8},{9,1... | collective-permute-start | bytes 786440 | tf_op jit(solution)/shard_map/ppermute | solution.py:21
  20.3 1.9 %collective-permute-start.4 = (bf16[2,256,256]{2,1,0:T(8,128)(2,1)S(1)}, bf16[2,256,256]{2,1,0:T(8,128)(2,1)S(1)}, u32[]{:S(2)}, u32[]{:S(2)}) collective-permute-start(bf16[2,256,256]{2,1,0:T(8,128)(2,1)S(1)} %maximum_select_fusion.refs_4_.refs_3_), channel_id=1, source_target_pairs={{0,256},{256,0},{1,257},{257,1},{2,258},{258,2},{3,259},{259,3},{4... | collective-permute-start | bytes 786440 | tf_op jit(solution)/shard_map/ppermute | solution.py:21
  22.3 11.8 %collective-permute-start.8 = (bf16[2,256,256]{2,1,0:T(8,128)(2,1)S(1)}, bf16[2,256,256]{2,1,0:T(8,128)(2,1)S(1)}, u32[]{:S(2)}, u32[]{:S(2)}) collective-permute-start(bf16[2,256,256]{2,1,0:T(8,128)(2,1)S(1)} %maximum_select_fusion.refs_4_.refs_3_), channel_id=1, source_target_pairs={{0,64},{2,130},{16,80},{18,146},{32,96},{34,162},{48,112},{50,178}... | collective-permute-start | bytes 786440 | tf_op jit(solution)/shard_map/ppermute | solution.py:31
  34.5 3.1 %collective-permute-start.3 = (bf16[2,256,256]{2,1,0:T(8,128)(2,1)S(1)}, bf16[2,256,256]{2,1,0:T(8,128)(2,1)S(1)}, u32[]{:S(2)}, u32[]{:S(2)}) collective-permute-start(bf16[2,256,256]{2,1,0:T(8,128)(2,1)S(1)} %maximum_select_fusion.refs_4_.refs_3_), channel_id=1, source_target_pairs={{0,32},{16,48},{32,0},{48,16},{64,96},{80,112},{96,64},{112,80},{1... | collective-permute-start | bytes 786440 | tf_op jit(solution)/shard_map/ppermute | solution.py:21
  37.6 4.1 %collective-permute-start.5 = (bf16[2,256,256]{2,1,0:T(8,128)(2,1)S(1)}, bf16[2,256,256]{2,1,0:T(8,128)(2,1)S(1)}, u32[]{:S(2)}, u32[]{:S(2)}) collective-permute-start(bf16[2,256,256]{2,1,0:T(8,128)(2,1)S(1)} %maximum_select_fusion.refs_4_.refs_3_), channel_id=1, source_target_pairs={{0,1},{1,0},{2,3},{3,2},{4,5},{5,4},{6,7},{7,6},{8,9},{9,8},{10,11... | collective-permute-start | bytes 786440 | tf_op jit(solution)/shard_map/ppermute | solution.py:21
  41.7 3.2 %collective-permute-start.6 = (bf16[2,256,256]{2,1,0:T(8,128)(2,1)S(1)}, bf16[2,256,256]{2,1,0:T(8,128)(2,1)S(1)}, u32[]{:S(2)}, u32[]{:S(2)}) collective-permute-start(bf16[2,256,256]{2,1,0:T(8,128)(2,1)S(1)} %maximum_select_fusion.refs_4_.refs_3_), channel_id=1, source_target_pairs={{0,4},{4,0},{8,12},{12,8},{1,5},{5,1},{9,13},{13,9},{2,6},{6,2},{1... | collective-permute-start | bytes 786440 | tf_op jit(solution)/shard_map/ppermute | solution.py:21
  44.9 4.5 %collective-permute-start.7 = (bf16[2,256,256]{2,1,0:T(8,128)(2,1)S(1)}, bf16[2,256,256]{2,1,0:T(8,128)(2,1)S(1)}, u32[]{:S(2)}, u32[]{:S(2)}) collective-permute-start(bf16[2,256,256]{2,1,0:T(8,128)(2,1)S(1)} %maximum_select_fusion.refs_4_.refs_3_), channel_id=1, source_target_pairs={{0,8},{4,12},{8,0},{12,4},{1,9},{5,13},{9,1},{13,5},{2,10},{6,14},... | collective-permute-start | bytes 786440 | tf_op jit(solution)/shard_map/ppermute | solution.py:21
  49.5 4.0 %collective-permute-start.9 = (bf16[2,256,256]{2,1,0:T(8,128)(2,1)S(1)}, bf16[2,256,256]{2,1,0:T(8,128)(2,1)S(1)}, u32[]{:S(2)}, u32[]{:S(2)}) collective-permute-start(bf16[2,256,256]{2,1,0:T(8,128)(2,1)S(1)} %broadcast_select_fusion.1), channel_id=1, source_target_pairs={{0,192},{2,66},{16,208},{18,82},{32,224},{34,98},{48,240},{50,114}... | collective-permute-start | bytes 786440 | tf_op jit(solution)/shard_map/ppermute | solution.py:31
  53.6 3.7 %collective-permute-done.3.refs_7_ = bf16[2,256,256]{2,1,0:T(8,128)(2,1)S(1)} collective-permute-done((bf16[2,256,256]{2,1,0:T(8,128)(2,1)S(1)}, bf16[2,256,256]{2,1,0:T(8,128)(2,1)S(1)}, u32[]{:S(2)}, u32[]{:S(2)}) %collective-permute-start.3) | collective-permute-done | bytes 262176 | tf_op jit(solution)/shard_map/ppermute | solution.py:21
  57.4 2.4 %shard_map.113.refs_4_ = f32[2,256,256]{2,1,0:T(8,128)S(1)} custom-call(s32[11]{0:T(128)S(1)} %pad_add_fusion.refs_0_, f32[3,9]{1,0:T(4,128)S(1)} %pad_maximum_fusion.1.refs_1_, bf16[12,256,256]{2,1,0:T(8,128)(2,1)S(1)} %copy-done, bf16[2,256,256]{2,1,0:T(8,128)(2,1)S(1)} %copy-done.1, bf16[2,256,256]{2,1,0:T(8,128)(2,1)S(1)} %maximum_select_fusion.refs_4_.refs_3_, ...), custom_call_target="tpu_custom_call" | custom-call | flops 939524096 | bytes 4456600 | tf_op jit(solution)/shard_map/pallas_call | solution.py:173
  59.8 11.5 %collective-permute-done.9.refs_6_ = bf16[2,256,256]{2,1,0:T(8,128)(2,1)S(1)} collective-permute-done((bf16[2,256,256]{2,1,0:T(8,128)(2,1)S(1)}, bf16[2,256,256]{2,1,0:T(8,128)(2,1)S(1)}, u32[]{:S(2)}, u32[]{:S(2)}) %collective-permute-start.9) | collective-permute-done | bytes 262176 | tf_op jit(solution)/shard_map/ppermute | solution.py:31
  71.3 1.2 shard_map.114
  72.5 1.9 %collective-permute-start.10 = (bf16[2,256,256]{2,1,0:T(8,128)(2,1)S(1)}, bf16[2,256,256]{2,1,0:T(8,128)(2,1)S(1)}, u32[]{:S(2)}, u32[]{:S(2)}) collective-permute-start(bf16[2,256,256]{2,1,0:T(8,128)(2,1)S(1)} %get-tuple-element.19.refs_4_), channel_id=1, source_target_pairs={{0,16},{16,0},{32,48},{48,32},{64,80},{80,64},{96,112},{112,96},{1... | collective-permute-start | bytes 786440 | tf_op jit(solution)/shard_map/ppermute | solution.py:21
  74.4 3.2 %collective-permute-start.11 = (bf16[2,256,256]{2,1,0:T(8,128)(2,1)S(1)}, bf16[2,256,256]{2,1,0:T(8,128)(2,1)S(1)}, u32[]{:S(2)}, u32[]{:S(2)}) collective-permute-start(bf16[2,256,256]{2,1,0:T(8,128)(2,1)S(1)} %get-tuple-element.19.refs_4_), channel_id=1, source_target_pairs={{0,2},{2,0},{1,3},{3,1},{4,6},{6,4},{5,7},{7,5},{8,10},{10,8},{9,1... | collective-permute-start | bytes 786440 | tf_op jit(solution)/shard_map/ppermute | solution.py:21
  77.6 2.6 %collective-permute-start.13 = (bf16[2,256,256]{2,1,0:T(8,128)(2,1)S(1)}, bf16[2,256,256]{2,1,0:T(8,128)(2,1)S(1)}, u32[]{:S(2)}, u32[]{:S(2)}) collective-permute-start(bf16[2,256,256]{2,1,0:T(8,128)(2,1)S(1)} %get-tuple-element.19.refs_4_), channel_id=1, source_target_pairs={{0,256},{256,0},{1,257},{257,1},{2,258},{258,2},{3,259},{259,3},{4... | collective-permute-start | bytes 786440 | tf_op jit(solution)/shard_map/ppermute | solution.py:21
  80.2 10.5 %collective-permute-start.17 = (bf16[2,256,256]{2,1,0:T(8,128)(2,1)S(1)}, bf16[2,256,256]{2,1,0:T(8,128)(2,1)S(1)}, u32[]{:S(2)}, u32[]{:S(2)}) collective-permute-start(bf16[2,256,256]{2,1,0:T(8,128)(2,1)S(1)} %get-tuple-element.19.refs_4_), channel_id=1, source_target_pairs={{0,64},{2,130},{16,80},{18,146},{32,96},{34,162},{48,112},{50,178}... | collective-permute-start | bytes 786440 | tf_op jit(solution)/shard_map/ppermute | solution.py:31
  90.8 5.4 %collective-permute-start.12 = (bf16[2,256,256]{2,1,0:T(8,128)(2,1)S(1)}, bf16[2,256,256]{2,1,0:T(8,128)(2,1)S(1)}, u32[]{:S(2)}, u32[]{:S(2)}) collective-permute-start(bf16[2,256,256]{2,1,0:T(8,128)(2,1)S(1)} %get-tuple-element.19.refs_4_), channel_id=1, source_target_pairs={{0,32},{16,48},{32,0},{48,16},{64,96},{80,112},{96,64},{112,80},{1... | collective-permute-start | bytes 786440 | tf_op jit(solution)/shard_map/ppermute | solution.py:21
  96.2 3.5 %collective-permute-start.14 = (bf16[2,256,256]{2,1,0:T(8,128)(2,1)S(1)}, bf16[2,256,256]{2,1,0:T(8,128)(2,1)S(1)}, u32[]{:S(2)}, u32[]{:S(2)}) collective-permute-start(bf16[2,256,256]{2,1,0:T(8,128)(2,1)S(1)} %get-tuple-element.19.refs_4_), channel_id=1, source_target_pairs={{0,1},{1,0},{2,3},{3,2},{4,5},{5,4},{6,7},{7,6},{8,9},{9,8},{10,11... | collective-permute-start | bytes 786440 | tf_op jit(solution)/shard_map/ppermute | solution.py:21
  99.7 3.2 %collective-permute-start.15 = (bf16[2,256,256]{2,1,0:T(8,128)(2,1)S(1)}, bf16[2,256,256]{2,1,0:T(8,128)(2,1)S(1)}, u32[]{:S(2)}, u32[]{:S(2)}) collective-permute-start(bf16[2,256,256]{2,1,0:T(8,128)(2,1)S(1)} %get-tuple-element.19.refs_4_), channel_id=1, source_target_pairs={{0,4},{4,0},{8,12},{12,8},{1,5},{5,1},{9,13},{13,9},{2,6},{6,2},{1... | collective-permute-start | bytes 786440 | tf_op jit(solution)/shard_map/ppermute | solution.py:21
  102.9 4.5 %collective-permute-start.16 = (bf16[2,256,256]{2,1,0:T(8,128)(2,1)S(1)}, bf16[2,256,256]{2,1,0:T(8,128)(2,1)S(1)}, u32[]{:S(2)}, u32[]{:S(2)}) collective-permute-start(bf16[2,256,256]{2,1,0:T(8,128)(2,1)S(1)} %get-tuple-element.19.refs_4_), channel_id=1, source_target_pairs={{0,8},{4,12},{8,0},{12,4},{1,9},{5,13},{9,1},{13,5},{2,10},{6,14},... | collective-permute-start | bytes 786440 | tf_op jit(solution)/shard_map/ppermute | solution.py:21
  107.5 4.0 %collective-permute-start.18 = (bf16[2,256,256]{2,1,0:T(8,128)(2,1)S(1)}, bf16[2,256,256]{2,1,0:T(8,128)(2,1)S(1)}, u32[]{:S(2)}, u32[]{:S(2)}) collective-permute-start(bf16[2,256,256]{2,1,0:T(8,128)(2,1)S(1)} %broadcast_select_fusion), channel_id=1, source_target_pairs={{0,192},{2,66},{16,208},{18,82},{32,224},{34,98},{48,240},{50,114}... | collective-permute-start | bytes 786440 | tf_op jit(solution)/shard_map/ppermute | solution.py:31
  111.5 6.4 %collective-permute-done.12.refs_8_ = bf16[2,256,256]{2,1,0:T(8,128)(2,1)S(1)} collective-permute-done((bf16[2,256,256]{2,1,0:T(8,128)(2,1)S(1)}, bf16[2,256,256]{2,1,0:T(8,128)(2,1)S(1)}, u32[]{:S(2)}, u32[]{:S(2)}) %collective-permute-start.12) | collective-permute-done | bytes 262176 | tf_op jit(solution)/shard_map/ppermute | solution.py:21
  117.9 2.5 %shard_map.115.refs_3_ = f32[2,256,256]{2,1,0:T(8,128)S(1)} custom-call(s32[11]{0:T(128)S(1)} %pad_add_fusion.refs_0_, f32[3,9]{1,0:T(4,128)S(1)} %pad_maximum_fusion.1.refs_1_, bf16[12,256,256]{2,1,0:T(8,128)(2,1)S(1)} %copy-done, bf16[2,256,256]{2,1,0:T(8,128)(2,1)S(1)} %copy-done.1, bf16[2,256,256]{2,1,0:T(8,128)(2,1)S(1)} %get-tuple-element.19.refs_4_, ...), custom_call_target="tpu_custom_call" | custom-call | flops 939524096 | bytes 4980888 | tf_op jit(solution)/shard_map/pallas_call | solution.py:173
  120.4 12.1 %collective-permute-done.18.refs_5_ = bf16[2,256,256]{2,1,0:T(8,128)(2,1)S(1)} collective-permute-done((bf16[2,256,256]{2,1,0:T(8,128)(2,1)S(1)}, bf16[2,256,256]{2,1,0:T(8,128)(2,1)S(1)}, u32[]{:S(2)}, u32[]{:S(2)}) %collective-permute-start.18) | collective-permute-done | bytes 262176 | tf_op jit(solution)/shard_map/ppermute | solution.py:31
  132.5 1.1 shard_map.116
  133.7 3.4 %collective-permute-start.19 = (bf16[2,128,256]{2,1,0:T(8,128)(2,1)S(1)}, bf16[2,128,256]{2,1,0:T(8,128)(2,1)S(1)}, u32[]{:S(2)}, u32[]{:S(2)}) collective-permute-start(bf16[2,128,256]{2,1,0:T(8,128)(2,1)S(1)} %get-tuple-element.21), channel_id=1, source_target_pairs={{0,1},{1,0},{2,3},{3,2},{4,5},{5,4},{6,7},{7,6},{8,9},{9,8},{10,11... | collective-permute-start | bytes 393224 | tf_op jit(solution)/shard_map/ppermute | solution.py:21
  137.2 5.1 %collective-permute-done.19 = bf16[2,128,256]{2,1,0:T(8,128)(2,1)S(1)} collective-permute-done((bf16[2,128,256]{2,1,0:T(8,128)(2,1)S(1)}, bf16[2,128,256]{2,1,0:T(8,128)(2,1)S(1)}, u32[]{:S(2)}, u32[]{:S(2)}) %collective-permute-start.19) | collective-permute-done | bytes 131104 | tf_op jit(solution)/shard_map/ppermute | solution.py:21
  142.4 1.0 select_add_fusion
  (42 shorter events, 3.6 us)
Async XLA Ops:
  0.6 56.8 %copy-start = (bf16[12,256,256]{2,1,0:T(8,128)(2,1)S(1)}, bf16[12,256,256]{2,1,0:T(8,128)(2,1)}, u32[]{:S(2)}) copy-start(bf16[12,256,256]{2,1,0:T(8,128)(2,1)} %refs_2_.7) | copy-start | bytes 4718596
  0.6 56.8 %copy-start.1 = (bf16[2,256,256]{2,1,0:T(8,128)(2,1)S(1)}, bf16[2,256,256]{2,1,0:T(8,128)(2,1)}, u32[]{:S(2)}) copy-start(bf16[2,256,256]{2,1,0:T(8,128)(2,1)} %refs_3_.3) | copy-start | bytes 786436
  1.9 9.5 %collective-permute-start = (bf16[2,128,256]{2,1,0:T(8,128)(2,1)S(1)}, bf16[2,128,256]{2,1,0:T(8,128)(2,1)S(1)}, u32[]{:S(2)}, u32[]{:S(2)}) collective-permute-start(bf16[2,128,256]{2,1,0:T(8,128)(2,1)S(1)} %get-tuple-element.29), channel_id=1, source_target_pairs={{0,1},{1,0},{2,3},{3,2},{4,5},{5,4},{6,7},{7,6},{8,9},{9,8},{10,11... | collective-permute-start | bytes 393224 | tf_op jit(solution)/shard_map/ppermute | solution.py:21
  11.5 26.1 %collective-permute-start.1 = (bf16[2,256,256]{2,1,0:T(8,128)(2,1)S(1)}, bf16[2,256,256]{2,1,0:T(8,128)(2,1)S(1)}, u32[]{:S(2)}, u32[]{:S(2)}) collective-permute-start(bf16[2,256,256]{2,1,0:T(8,128)(2,1)S(1)} %maximum_select_fusion.refs_4_.refs_3_), channel_id=1, source_target_pairs={{0,16},{16,0},{32,48},{48,32},{64,80},{80,64},{96,112},{112,96},{1... | collective-permute-start | bytes 786440 | tf_op jit(solution)/shard_map/ppermute | solution.py:21
  13.4 28.3 %collective-permute-start.2 = (bf16[2,256,256]{2,1,0:T(8,128)(2,1)S(1)}, bf16[2,256,256]{2,1,0:T(8,128)(2,1)S(1)}, u32[]{:S(2)}, u32[]{:S(2)}) collective-permute-start(bf16[2,256,256]{2,1,0:T(8,128)(2,1)S(1)} %maximum_select_fusion.refs_4_.refs_3_), channel_id=1, source_target_pairs={{0,2},{2,0},{1,3},{3,1},{4,6},{6,4},{5,7},{7,5},{8,10},{10,8},{9,1... | collective-permute-start | bytes 786440 | tf_op jit(solution)/shard_map/ppermute | solution.py:21
  20.3 24.6 %collective-permute-start.4 = (bf16[2,256,256]{2,1,0:T(8,128)(2,1)S(1)}, bf16[2,256,256]{2,1,0:T(8,128)(2,1)S(1)}, u32[]{:S(2)}, u32[]{:S(2)}) collective-permute-start(bf16[2,256,256]{2,1,0:T(8,128)(2,1)S(1)} %maximum_select_fusion.refs_4_.refs_3_), channel_id=1, source_target_pairs={{0,256},{256,0},{1,257},{257,1},{2,258},{258,2},{3,259},{259,3},{4... | collective-permute-start | bytes 786440 | tf_op jit(solution)/shard_map/ppermute | solution.py:21
  22.3 27.2 %collective-permute-start.8 = (bf16[2,256,256]{2,1,0:T(8,128)(2,1)S(1)}, bf16[2,256,256]{2,1,0:T(8,128)(2,1)S(1)}, u32[]{:S(2)}, u32[]{:S(2)}) collective-permute-start(bf16[2,256,256]{2,1,0:T(8,128)(2,1)S(1)} %maximum_select_fusion.refs_4_.refs_3_), channel_id=1, source_target_pairs={{0,64},{2,130},{16,80},{18,146},{32,96},{34,162},{48,112},{50,178}... | collective-permute-start | bytes 786440 | tf_op jit(solution)/shard_map/ppermute | solution.py:31
  34.5 22.9 %collective-permute-start.3 = (bf16[2,256,256]{2,1,0:T(8,128)(2,1)S(1)}, bf16[2,256,256]{2,1,0:T(8,128)(2,1)S(1)}, u32[]{:S(2)}, u32[]{:S(2)}) collective-permute-start(bf16[2,256,256]{2,1,0:T(8,128)(2,1)S(1)} %maximum_select_fusion.refs_4_.refs_3_), channel_id=1, source_target_pairs={{0,32},{16,48},{32,0},{48,16},{64,96},{80,112},{96,64},{112,80},{1... | collective-permute-start | bytes 786440 | tf_op jit(solution)/shard_map/ppermute | solution.py:21
  37.6 19.8 %collective-permute-start.5 = (bf16[2,256,256]{2,1,0:T(8,128)(2,1)S(1)}, bf16[2,256,256]{2,1,0:T(8,128)(2,1)S(1)}, u32[]{:S(2)}, u32[]{:S(2)}) collective-permute-start(bf16[2,256,256]{2,1,0:T(8,128)(2,1)S(1)} %maximum_select_fusion.refs_4_.refs_3_), channel_id=1, source_target_pairs={{0,1},{1,0},{2,3},{3,2},{4,5},{5,4},{6,7},{7,6},{8,9},{9,8},{10,11... | collective-permute-start | bytes 786440 | tf_op jit(solution)/shard_map/ppermute | solution.py:21
  41.7 15.7 %collective-permute-start.6 = (bf16[2,256,256]{2,1,0:T(8,128)(2,1)S(1)}, bf16[2,256,256]{2,1,0:T(8,128)(2,1)S(1)}, u32[]{:S(2)}, u32[]{:S(2)}) collective-permute-start(bf16[2,256,256]{2,1,0:T(8,128)(2,1)S(1)} %maximum_select_fusion.refs_4_.refs_3_), channel_id=1, source_target_pairs={{0,4},{4,0},{8,12},{12,8},{1,5},{5,1},{9,13},{13,9},{2,6},{6,2},{1... | collective-permute-start | bytes 786440 | tf_op jit(solution)/shard_map/ppermute | solution.py:21
  44.9 12.4 %collective-permute-start.7 = (bf16[2,256,256]{2,1,0:T(8,128)(2,1)S(1)}, bf16[2,256,256]{2,1,0:T(8,128)(2,1)S(1)}, u32[]{:S(2)}, u32[]{:S(2)}) collective-permute-start(bf16[2,256,256]{2,1,0:T(8,128)(2,1)S(1)} %maximum_select_fusion.refs_4_.refs_3_), channel_id=1, source_target_pairs={{0,8},{4,12},{8,0},{12,4},{1,9},{5,13},{9,1},{13,5},{2,10},{6,14},... | collective-permute-start | bytes 786440 | tf_op jit(solution)/shard_map/ppermute | solution.py:21
  49.5 21.8 %collective-permute-start.9 = (bf16[2,256,256]{2,1,0:T(8,128)(2,1)S(1)}, bf16[2,256,256]{2,1,0:T(8,128)(2,1)S(1)}, u32[]{:S(2)}, u32[]{:S(2)}) collective-permute-start(bf16[2,256,256]{2,1,0:T(8,128)(2,1)S(1)} %broadcast_select_fusion.1), channel_id=1, source_target_pairs={{0,192},{2,66},{16,208},{18,82},{32,224},{34,98},{48,240},{50,114}... | collective-permute-start | bytes 786440 | tf_op jit(solution)/shard_map/ppermute | solution.py:31
  72.5 23.7 %collective-permute-start.10 = (bf16[2,256,256]{2,1,0:T(8,128)(2,1)S(1)}, bf16[2,256,256]{2,1,0:T(8,128)(2,1)S(1)}, u32[]{:S(2)}, u32[]{:S(2)}) collective-permute-start(bf16[2,256,256]{2,1,0:T(8,128)(2,1)S(1)} %get-tuple-element.19.refs_4_), channel_id=1, source_target_pairs={{0,16},{16,0},{32,48},{48,32},{64,80},{80,64},{96,112},{112,96},{1... | collective-permute-start | bytes 786440 | tf_op jit(solution)/shard_map/ppermute | solution.py:21
  74.4 25.3 %collective-permute-start.11 = (bf16[2,256,256]{2,1,0:T(8,128)(2,1)S(1)}, bf16[2,256,256]{2,1,0:T(8,128)(2,1)S(1)}, u32[]{:S(2)}, u32[]{:S(2)}) collective-permute-start(bf16[2,256,256]{2,1,0:T(8,128)(2,1)S(1)} %get-tuple-element.19.refs_4_), channel_id=1, source_target_pairs={{0,2},{2,0},{1,3},{3,1},{4,6},{6,4},{5,7},{7,5},{8,10},{10,8},{9,1... | collective-permute-start | bytes 786440 | tf_op jit(solution)/shard_map/ppermute | solution.py:21
  77.6 25.4 %collective-permute-start.13 = (bf16[2,256,256]{2,1,0:T(8,128)(2,1)S(1)}, bf16[2,256,256]{2,1,0:T(8,128)(2,1)S(1)}, u32[]{:S(2)}, u32[]{:S(2)}) collective-permute-start(bf16[2,256,256]{2,1,0:T(8,128)(2,1)S(1)} %get-tuple-element.19.refs_4_), channel_id=1, source_target_pairs={{0,256},{256,0},{1,257},{257,1},{2,258},{258,2},{3,259},{259,3},{4... | collective-permute-start | bytes 786440 | tf_op jit(solution)/shard_map/ppermute | solution.py:21
  80.2 27.3 %collective-permute-start.17 = (bf16[2,256,256]{2,1,0:T(8,128)(2,1)S(1)}, bf16[2,256,256]{2,1,0:T(8,128)(2,1)S(1)}, u32[]{:S(2)}, u32[]{:S(2)}) collective-permute-start(bf16[2,256,256]{2,1,0:T(8,128)(2,1)S(1)} %get-tuple-element.19.refs_4_), channel_id=1, source_target_pairs={{0,64},{2,130},{16,80},{18,146},{32,96},{34,162},{48,112},{50,178}... | collective-permute-start | bytes 786440 | tf_op jit(solution)/shard_map/ppermute | solution.py:31
  90.8 27.1 %collective-permute-start.12 = (bf16[2,256,256]{2,1,0:T(8,128)(2,1)S(1)}, bf16[2,256,256]{2,1,0:T(8,128)(2,1)S(1)}, u32[]{:S(2)}, u32[]{:S(2)}) collective-permute-start(bf16[2,256,256]{2,1,0:T(8,128)(2,1)S(1)} %get-tuple-element.19.refs_4_), channel_id=1, source_target_pairs={{0,32},{16,48},{32,0},{48,16},{64,96},{80,112},{96,64},{112,80},{1... | collective-permute-start | bytes 786440 | tf_op jit(solution)/shard_map/ppermute | solution.py:21
  96.2 21.7 %collective-permute-start.14 = (bf16[2,256,256]{2,1,0:T(8,128)(2,1)S(1)}, bf16[2,256,256]{2,1,0:T(8,128)(2,1)S(1)}, u32[]{:S(2)}, u32[]{:S(2)}) collective-permute-start(bf16[2,256,256]{2,1,0:T(8,128)(2,1)S(1)} %get-tuple-element.19.refs_4_), channel_id=1, source_target_pairs={{0,1},{1,0},{2,3},{3,2},{4,5},{5,4},{6,7},{7,6},{8,9},{9,8},{10,11... | collective-permute-start | bytes 786440 | tf_op jit(solution)/shard_map/ppermute | solution.py:21
  99.7 18.2 %collective-permute-start.15 = (bf16[2,256,256]{2,1,0:T(8,128)(2,1)S(1)}, bf16[2,256,256]{2,1,0:T(8,128)(2,1)S(1)}, u32[]{:S(2)}, u32[]{:S(2)}) collective-permute-start(bf16[2,256,256]{2,1,0:T(8,128)(2,1)S(1)} %get-tuple-element.19.refs_4_), channel_id=1, source_target_pairs={{0,4},{4,0},{8,12},{12,8},{1,5},{5,1},{9,13},{13,9},{2,6},{6,2},{1... | collective-permute-start | bytes 786440 | tf_op jit(solution)/shard_map/ppermute | solution.py:21
  102.9 15.0 %collective-permute-start.16 = (bf16[2,256,256]{2,1,0:T(8,128)(2,1)S(1)}, bf16[2,256,256]{2,1,0:T(8,128)(2,1)S(1)}, u32[]{:S(2)}, u32[]{:S(2)}) collective-permute-start(bf16[2,256,256]{2,1,0:T(8,128)(2,1)S(1)} %get-tuple-element.19.refs_4_), channel_id=1, source_target_pairs={{0,8},{4,12},{8,0},{12,4},{1,9},{5,13},{9,1},{13,5},{2,10},{6,14},... | collective-permute-start | bytes 786440 | tf_op jit(solution)/shard_map/ppermute | solution.py:21
  107.5 25.0 %collective-permute-start.18 = (bf16[2,256,256]{2,1,0:T(8,128)(2,1)S(1)}, bf16[2,256,256]{2,1,0:T(8,128)(2,1)S(1)}, u32[]{:S(2)}, u32[]{:S(2)}) collective-permute-start(bf16[2,256,256]{2,1,0:T(8,128)(2,1)S(1)} %broadcast_select_fusion), channel_id=1, source_target_pairs={{0,192},{2,66},{16,208},{18,82},{32,224},{34,98},{48,240},{50,114}... | collective-permute-start | bytes 786440 | tf_op jit(solution)/shard_map/ppermute | solution.py:31
  120.4 22.0 %copy-start.2 = (f32[2,128,256]{2,1,0:T(8,128)S(1)}, f32[2,128,256]{2,1,0:T(8,128)}, u32[]{:S(2)}) copy-start(f32[2,128,256]{2,1,0:T(8,128)} %param.11) | copy-start | bytes 786436
  120.4 22.0 %copy-start.3 = (f32[2,128,256]{2,1,0:T(8,128)S(1)}, f32[2,128,256]{2,1,0:T(8,128)}, u32[]{:S(2)}) copy-start(f32[2,128,256]{2,1,0:T(8,128)} %param.10) | copy-start | bytes 786436
  133.7 8.6 %collective-permute-start.19 = (bf16[2,128,256]{2,1,0:T(8,128)(2,1)S(1)}, bf16[2,128,256]{2,1,0:T(8,128)(2,1)S(1)}, u32[]{:S(2)}, u32[]{:S(2)}) collective-permute-start(bf16[2,128,256]{2,1,0:T(8,128)(2,1)S(1)} %get-tuple-element.21), channel_id=1, source_target_pairs={{0,1},{1,0},{2,3},{3,2},{4,5},{5,4},{6,7},{7,6},{8,9},{9,8},{10,11... | collective-permute-start | bytes 393224 | tf_op jit(solution)/shard_map/ppermute | solution.py:21

commit v4 on v3

--- a/solution.py
+++ b/solution.py
@@ -90,6 +90,12 @@
         total[...] = jnp.zeros_like(total)
     add_commutator(total, ham_ref, own_ref[0], own_ref[1])
     add_bits(total, parts, index_ref, coef_ref, couple_ref, partner_refs, whole)
+
+
+def add_kernel(parts, index_ref, coef_ref, couple_ref, total_ref, *refs):
+    *partner_refs, out_ref, whole = refs
+    out_ref[...] = total_ref[...]
+    add_bits(out_ref, parts, index_ref, coef_ref, couple_ref, partner_refs, whole)
 
 
 def middle_kernel(parts, index_ref, coef_ref, couple_ref, own_ref, total_ref, *refs):
@@ -147,17 +153,16 @@
     half_float = shaped(float32, 2, rows, levels)
 
     def exchange(full):
+        z2 = swapped(full, "z", 2)
+        first = across(full, inward, opposite)
         z1 = swapped(full, "z", 1)
         core = swapped(full, "core", 1)
-        first = across(full, inward, opposite)
-        z2 = swapped(full, "z", 2)
         x1 = swapped(full, "x_lo", 1)
-        x2 = swapped(after(full, z1), "rep", 1)
-        y1 = swapped(after(full, core), "y", 1)
-        y2 = swapped(after(full, x1), "y", 2)
+        x2 = swapped(after(full, z2), "rep", 1)
+        y1 = swapped(after(full, first, z1), "y", 1)
+        y2 = swapped(after(full, first, core), "y", 2)
         second = across(jnp.where(on_first, first, full), outward, inward)
-        early = {4: [z1], 1: [core], 5: [z2], 8: [x1], 0: [x2], 2: [y1], 3: [y2]}
-        return early, {6: [first, second], 7: [second, first]}
+        return {5: [z2], 4: [z1], 1: [core], 8: [x1], 0: [x2]}, {6: [first, second], 7: [second, first]}, {2: [y1], 3: [y2]}
 
     def call(body, parts, outs, scratch, *operands):
         held = []
@@ -186,12 +191,14 @@
     far = swapped(away, "rep", 1)
     full = jnp.where(rep == 0, jnp.concatenate([near, far], axis=1), jnp.concatenate([far, near], axis=1))
 
-    early, late = exchange(full)
+    early, inner, late = exchange(full)
     (total,) = call(functools.partial(early_kernel, with_prior=False), early, [slope], [], ham, full)
+    (total,) = call(add_kernel, inner, [slope], [], total)
     first, middle = call(middle_kernel, late, [slope, whole], [], full, total)
 
-    early, late = exchange(middle)
+    early, inner, late = exchange(middle)
     (total,) = call(functools.partial(early_kernel, with_prior=True), early, [slope], [], ham, middle, first)
+    (total,) = call(add_kernel, inner, [slope], [], total)
     near, away = call(last_kernel, late, [half_float, half], [pltpu.VMEM((2, levels, levels), float32)], total)
     far = swapped(away, "rep", 1).astype(float32)
     stay = 1.0 - step_size * decay + (0.5 * step_size * step_size) * decay * decay

time: 144 us -> 148 us (1.028)
  the two profiles are of different devices: /device:TPU:33 before, /device:TPU:388 now
where the time goes in v4:
time: 148 us; the launch traced here: 147 us
  waiting for transfers between devices  76.7 us (52%)
  starting transfers between devices  52.9 us (36%)
  Pallas kernels  8.53 us (6%)
  other arithmetic  5.74 us (4%)
  between operations  2.35 us (2%)
    ppermute x16, waiting for transfers between devices, swapped(): return lax.ppermute(value, axis, pairs)  76.7 us
    ppermute x16, starting transfers between devices, swapped(): return lax.ppermute(value, axis, pairs)  41.7 us
    ppermute x4, starting transfers between devices, across(): return lax.ppermute(value, ('z', 'core'), pairs)  11.2 us
    pallas_call x6, Pallas kernels, call(): pl.pallas_call(lambda *refs: body(counts, *refs), out_shape=outs, in_spec...  8.53 us
  transfers between devices with their start and end apart: 20, of which 9 were waited for; matrix products, arithmetic and copies ran while one was open for 3% of the time, Pallas kernels for 4%

profile of v4, /device:TPU:388, one launch (start us, length us, event | category | flops | bytes accessed | tf_op | source)
XLA Modules:
  0.0 146.9 jit_solution(11268575310239744391)
XLA Ops:
  0.7 1.2 convert_bitcast_fusion
  1.9 2.4 %collective-permute-start = (bf16[2,128,256]{2,1,0:T(8,128)(2,1)S(1)}, bf16[2,128,256]{2,1,0:T(8,128)(2,1)S(1)}, u32[]{:S(2)}, u32[]{:S(2)}) collective-permute-start(bf16[2,128,256]{2,1,0:T(8,128)(2,1)S(1)} %get-tuple-element.29), channel_id=1, source_target_pairs={{0,1},{1,0},{2,3},{3,2},{4,5},{5,4},{6,7},{7,6},{8,9},{9,8},{10,11... | collective-permute-start | bytes 393224 | tf_op jit(solution)/shard_map/ppermute | solution.py:21
  7.5 3.1 %collective-permute-done = bf16[2,128,256]{2,1,0:T(8,128)(2,1)S(1)} collective-permute-done((bf16[2,128,256]{2,1,0:T(8,128)(2,1)S(1)}, bf16[2,128,256]{2,1,0:T(8,128)(2,1)S(1)}, u32[]{:S(2)}, u32[]{:S(2)}) %collective-permute-start) | collective-permute-done | bytes 131104 | tf_op jit(solution)/shard_map/ppermute | solution.py:21
  10.6 3.4 %collective-permute-start.1 = (bf16[2,256,256]{2,1,0:T(8,128)(2,1)S(1)}, bf16[2,256,256]{2,1,0:T(8,128)(2,1)S(1)}, u32[]{:S(2)}, u32[]{:S(2)}) collective-permute-start(bf16[2,256,256]{2,1,0:T(8,128)(2,1)S(1)} %maximum_select_fusion.refs_4_.refs_3_), channel_id=1, source_target_pairs={{0,32},{16,48},{32,0},{48,16},{64,96},{80,112},{96,64},{112,80},{1... | collective-permute-start | bytes 786440 | tf_op jit(solution)/shard_map/ppermute | solution.py:21
  14.0 5.5 %collective-permute-start.6 = (bf16[2,256,256]{2,1,0:T(8,128)(2,1)S(1)}, bf16[2,256,256]{2,1,0:T(8,128)(2,1)S(1)}, u32[]{:S(2)}, u32[]{:S(2)}) collective-permute-start(bf16[2,256,256]{2,1,0:T(8,128)(2,1)S(1)} %maximum_select_fusion.refs_4_.refs_3_), channel_id=1, source_target_pairs={{0,64},{2,130},{16,80},{18,146},{32,96},{34,162},{48,112},{50,178}... | collective-permute-start | bytes 786440 | tf_op jit(solution)/shard_map/ppermute | solution.py:31
  21.6 2.9 %collective-permute-start.2 = (bf16[2,256,256]{2,1,0:T(8,128)(2,1)S(1)}, bf16[2,256,256]{2,1,0:T(8,128)(2,1)S(1)}, u32[]{:S(2)}, u32[]{:S(2)}) collective-permute-start(bf16[2,256,256]{2,1,0:T(8,128)(2,1)S(1)} %maximum_select_fusion.refs_4_.refs_3_), channel_id=1, source_target_pairs={{0,16},{16,0},{32,48},{48,32},{64,80},{80,64},{96,112},{112,96},{1... | collective-permute-start | bytes 786440 | tf_op jit(solution)/shard_map/ppermute | solution.py:21
  24.5 1.9 %collective-permute-start.3 = (bf16[2,256,256]{2,1,0:T(8,128)(2,1)S(1)}, bf16[2,256,256]{2,1,0:T(8,128)(2,1)S(1)}, u32[]{:S(2)}, u32[]{:S(2)}) collective-permute-start(bf16[2,256,256]{2,1,0:T(8,128)(2,1)S(1)} %maximum_select_fusion.refs_4_.refs_3_), channel_id=1, source_target_pairs={{0,2},{2,0},{1,3},{3,1},{4,6},{6,4},{5,7},{7,5},{8,10},{10,8},{9,1... | collective-permute-start | bytes 786440 | tf_op jit(solution)/shard_map/ppermute | solution.py:21
  26.5 3.1 %collective-permute-start.4 = (bf16[2,256,256]{2,1,0:T(8,128)(2,1)S(1)}, bf16[2,256,256]{2,1,0:T(8,128)(2,1)S(1)}, u32[]{:S(2)}, u32[]{:S(2)}) collective-permute-start(bf16[2,256,256]{2,1,0:T(8,128)(2,1)S(1)} %maximum_select_fusion.refs_4_.refs_3_), channel_id=1, source_target_pairs={{0,256},{256,0},{1,257},{257,1},{2,258},{258,2},{3,259},{259,3},{4... | collective-permute-start | bytes 786440 | tf_op jit(solution)/shard_map/ppermute | solution.py:21
  29.6 8.3 %collective-permute-done.1.refs_5_ = bf16[2,256,256]{2,1,0:T(8,128)(2,1)S(1)} collective-permute-done((bf16[2,256,256]{2,1,0:T(8,128)(2,1)S(1)}, bf16[2,256,256]{2,1,0:T(8,128)(2,1)S(1)}, u32[]{:S(2)}, u32[]{:S(2)}) %collective-permute-start.1) | collective-permute-done | bytes 262176 | tf_op jit(solution)/shard_map/ppermute | solution.py:21
  37.9 1.9 %collective-permute-start.5 = (bf16[2,256,256]{2,1,0:T(8,128)(2,1)S(1)}, bf16[2,256,256]{2,1,0:T(8,128)(2,1)S(1)}, u32[]{:S(2)}, u32[]{:S(2)}) collective-permute-start(bf16[2,256,256]{2,1,0:T(8,128)(2,1)S(1)} %maximum_select_fusion.refs_4_.refs_3_), channel_id=1, source_target_pairs={{0,1},{1,0},{2,3},{3,2},{4,5},{5,4},{6,7},{7,6},{8,9},{9,8},{10,11... | collective-permute-start | bytes 786440 | tf_op jit(solution)/shard_map/ppermute | solution.py:21
  39.8 1.9 %collective-permute-start.7 = (bf16[2,256,256]{2,1,0:T(8,128)(2,1)S(1)}, bf16[2,256,256]{2,1,0:T(8,128)(2,1)S(1)}, u32[]{:S(2)}, u32[]{:S(2)}) collective-permute-start(bf16[2,256,256]{2,1,0:T(8,128)(2,1)S(1)} %broadcast_select_fusion.1), channel_id=1, source_target_pairs={{0,192},{2,66},{16,208},{18,82},{32,224},{34,98},{48,240},{50,114}... | collective-permute-start | bytes 786440 | tf_op jit(solution)/shard_map/ppermute | solution.py:31
  41.8 18.4 %collective-permute-done.2.refs_6_ = bf16[2,256,256]{2,1,0:T(8,128)(2,1)S(1)} collective-permute-done((bf16[2,256,256]{2,1,0:T(8,128)(2,1)S(1)}, bf16[2,256,256]{2,1,0:T(8,128)(2,1)S(1)}, u32[]{:S(2)}, u32[]{:S(2)}) %collective-permute-start.2) | collective-permute-done | bytes 262176 | tf_op jit(solution)/shard_map/ppermute | solution.py:21
  60.2 3.5 %collective-permute-start.8 = (bf16[2,256,256]{2,1,0:T(8,128)(2,1)S(1)}, bf16[2,256,256]{2,1,0:T(8,128)(2,1)S(1)}, u32[]{:S(2)}, u32[]{:S(2)}) collective-permute-start(bf16[2,256,256]{2,1,0:T(8,128)(2,1)S(1)} %maximum_select_fusion.refs_4_.refs_3_), channel_id=1, source_target_pairs={{0,4},{4,0},{8,12},{12,8},{1,5},{5,1},{9,13},{13,9},{2,6},{6,2},{1... | collective-permute-start | bytes 786440 | tf_op jit(solution)/shard_map/ppermute | solution.py:21
  63.6 4.8 %collective-permute-start.9 = (bf16[2,256,256]{2,1,0:T(8,128)(2,1)S(1)}, bf16[2,256,256]{2,1,0:T(8,128)(2,1)S(1)}, u32[]{:S(2)}, u32[]{:S(2)}) collective-permute-start(bf16[2,256,256]{2,1,0:T(8,128)(2,1)S(1)} %maximum_select_fusion.refs_4_.refs_3_), channel_id=1, source_target_pairs={{0,8},{4,12},{8,0},{12,4},{1,9},{5,13},{9,1},{13,5},{2,10},{6,14},... | collective-permute-start | bytes 786440 | tf_op jit(solution)/shard_map/ppermute | solution.py:21
  68.6 2.0 %shard_map.113.refs_3_ = f32[2,256,256]{2,1,0:T(8,128)S(1)} custom-call(s32[11]{0:T(128)S(1)} %pad_add_fusion.refs_0_, f32[3,9]{1,0:T(4,128)S(1)} %pad_maximum_fusion.1.refs_1_, bf16[12,256,256]{2,1,0:T(8,128)(2,1)S(1)} %copy-done, bf16[2,256,256]{2,1,0:T(8,128)(2,1)S(1)} %copy-done.1, bf16[2,256,256]{2,1,0:T(8,128)(2,1)S(1)} %maximum_select_fusion.refs_4_.refs_3_, ...), custom_call_target="tpu_custom_call" | custom-call | flops 671088640 | bytes 3932312 | tf_op jit(solution)/shard_map/pallas_call | solution.py:178
  71.7 5.2 %collective-permute-done.9.refs_6_ = bf16[2,256,256]{2,1,0:T(8,128)(2,1)S(1)} collective-permute-done((bf16[2,256,256]{2,1,0:T(8,128)(2,1)S(1)}, bf16[2,256,256]{2,1,0:T(8,128)(2,1)S(1)}, u32[]{:S(2)}, u32[]{:S(2)}) %collective-permute-start.9) | collective-permute-done | bytes 262176 | tf_op jit(solution)/shard_map/ppermute | solution.py:21
  78.1 1.9 %collective-permute-start.10 = (bf16[2,256,256]{2,1,0:T(8,128)(2,1)S(1)}, bf16[2,256,256]{2,1,0:T(8,128)(2,1)S(1)}, u32[]{:S(2)}, u32[]{:S(2)}) collective-permute-start(bf16[2,256,256]{2,1,0:T(8,128)(2,1)S(1)} %get-tuple-element.19.refs_4_), channel_id=1, source_target_pairs={{0,32},{16,48},{32,0},{48,16},{64,96},{80,112},{96,64},{112,80},{1... | collective-permute-start | bytes 786440 | tf_op jit(solution)/shard_map/ppermute | solution.py:21
  80.0 1.9 %collective-permute-start.15 = (bf16[2,256,256]{2,1,0:T(8,128)(2,1)S(1)}, bf16[2,256,256]{2,1,0:T(8,128)(2,1)S(1)}, u32[]{:S(2)}, u32[]{:S(2)}) collective-permute-start(bf16[2,256,256]{2,1,0:T(8,128)(2,1)S(1)} %get-tuple-element.19.refs_4_), channel_id=1, source_target_pairs={{0,64},{2,130},{16,80},{18,146},{32,96},{34,162},{48,112},{50,178}... | collective-permute-start | bytes 786440 | tf_op jit(solution)/shard_map/ppermute | solution.py:31
  81.9 1.9 %collective-permute-start.11 = (bf16[2,256,256]{2,1,0:T(8,128)(2,1)S(1)}, bf16[2,256,256]{2,1,0:T(8,128)(2,1)S(1)}, u32[]{:S(2)}, u32[]{:S(2)}) collective-permute-start(bf16[2,256,256]{2,1,0:T(8,128)(2,1)S(1)} %get-tuple-element.19.refs_4_), channel_id=1, source_target_pairs={{0,16},{16,0},{32,48},{48,32},{64,80},{80,64},{96,112},{112,96},{1... | collective-permute-start | bytes 786440 | tf_op jit(solution)/shard_map/ppermute | solution.py:21
  83.8 2.9 %collective-permute-start.12 = (bf16[2,256,256]{2,1,0:T(8,128)(2,1)S(1)}, bf16[2,256,256]{2,1,0:T(8,128)(2,1)S(1)}, u32[]{:S(2)}, u32[]{:S(2)}) collective-permute-start(bf16[2,256,256]{2,1,0:T(8,128)(2,1)S(1)} %get-tuple-element.19.refs_4_), channel_id=1, source_target_pairs={{0,2},{2,0},{1,3},{3,1},{4,6},{6,4},{5,7},{7,5},{8,10},{10,8},{9,1... | collective-permute-start | bytes 786440 | tf_op jit(solution)/shard_map/ppermute | solution.py:21
  86.8 2.1 %collective-permute-start.13 = (bf16[2,256,256]{2,1,0:T(8,128)(2,1)S(1)}, bf16[2,256,256]{2,1,0:T(8,128)(2,1)S(1)}, u32[]{:S(2)}, u32[]{:S(2)}) collective-permute-start(bf16[2,256,256]{2,1,0:T(8,128)(2,1)S(1)} %get-tuple-element.19.refs_4_), channel_id=1, source_target_pairs={{0,256},{256,0},{1,257},{257,1},{2,258},{258,2},{3,259},{259,3},{4... | collective-permute-start | bytes 786440 | tf_op jit(solution)/shard_map/ppermute | solution.py:21
  88.9 16.6 %collective-permute-done.10.refs_6_ = bf16[2,256,256]{2,1,0:T(8,128)(2,1)S(1)} collective-permute-done((bf16[2,256,256]{2,1,0:T(8,128)(2,1)S(1)}, bf16[2,256,256]{2,1,0:T(8,128)(2,1)S(1)}, u32[]{:S(2)}, u32[]{:S(2)}) %collective-permute-start.10) | collective-permute-done | bytes 262176 | tf_op jit(solution)/shard_map/ppermute | solution.py:21
  105.5 1.9 %collective-permute-start.14 = (bf16[2,256,256]{2,1,0:T(8,128)(2,1)S(1)}, bf16[2,256,256]{2,1,0:T(8,128)(2,1)S(1)}, u32[]{:S(2)}, u32[]{:S(2)}) collective-permute-start(bf16[2,256,256]{2,1,0:T(8,128)(2,1)S(1)} %get-tuple-element.19.refs_4_), channel_id=1, source_target_pairs={{0,1},{1,0},{2,3},{3,2},{4,5},{5,4},{6,7},{7,6},{8,9},{9,8},{10,11... | collective-permute-start | bytes 786440 | tf_op jit(solution)/shard_map/ppermute | solution.py:21
  107.4 1.9 %collective-permute-start.16 = (bf16[2,256,256]{2,1,0:T(8,128)(2,1)S(1)}, bf16[2,256,256]{2,1,0:T(8,128)(2,1)S(1)}, u32[]{:S(2)}, u32[]{:S(2)}) collective-permute-start(bf16[2,256,256]{2,1,0:T(8,128)(2,1)S(1)} %broadcast_select_fusion), channel_id=1, source_target_pairs={{0,192},{2,66},{16,208},{18,82},{32,224},{34,98},{48,240},{50,114}... | collective-permute-start | bytes 786440 | tf_op jit(solution)/shard_map/ppermute | solution.py:31
  109.4 10.9 %collective-permute-done.11.refs_7_ = bf16[2,256,256]{2,1,0:T(8,128)(2,1)S(1)} collective-permute-done((bf16[2,256,256]{2,1,0:T(8,128)(2,1)S(1)}, bf16[2,256,256]{2,1,0:T(8,128)(2,1)S(1)}, u32[]{:S(2)}, u32[]{:S(2)}) %collective-permute-start.11) | collective-permute-done | bytes 262176 | tf_op jit(solution)/shard_map/ppermute | solution.py:21
  120.3 1.9 %collective-permute-start.17 = (bf16[2,256,256]{2,1,0:T(8,128)(2,1)S(1)}, bf16[2,256,256]{2,1,0:T(8,128)(2,1)S(1)}, u32[]{:S(2)}, u32[]{:S(2)}) collective-permute-start(bf16[2,256,256]{2,1,0:T(8,128)(2,1)S(1)} %get-tuple-element.19.refs_4_), channel_id=1, source_target_pairs={{0,4},{4,0},{8,12},{12,8},{1,5},{5,1},{9,13},{13,9},{2,6},{6,2},{1... | collective-permute-start | bytes 786440 | tf_op jit(solution)/shard_map/ppermute | solution.py:21
  122.2 3.1 %collective-permute-start.18 = (bf16[2,256,256]{2,1,0:T(8,128)(2,1)S(1)}, bf16[2,256,256]{2,1,0:T(8,128)(2,1)S(1)}, u32[]{:S(2)}, u32[]{:S(2)}) collective-permute-start(bf16[2,256,256]{2,1,0:T(8,128)(2,1)S(1)} %get-tuple-element.19.refs_4_), channel_id=1, source_target_pairs={{0,8},{4,12},{8,0},{12,4},{1,9},{5,13},{9,1},{13,5},{2,10},{6,14},... | collective-permute-start | bytes 786440 | tf_op jit(solution)/shard_map/ppermute | solution.py:21
  125.4 2.0 %shard_map.116.refs_3_ = f32[2,256,256]{2,1,0:T(8,128)S(1)} custom-call(s32[11]{0:T(128)S(1)} %pad_add_fusion.refs_0_, f32[3,9]{1,0:T(4,128)S(1)} %pad_maximum_fusion.1.refs_1_, bf16[12,256,256]{2,1,0:T(8,128)(2,1)S(1)} %copy-done, bf16[2,256,256]{2,1,0:T(8,128)(2,1)S(1)} %copy-done.1, bf16[2,256,256]{2,1,0:T(8,128)(2,1)S(1)} %get-tuple-element.19.refs_4_, ...), custom_call_target="tpu_custom_call" | custom-call | flops 671088640 | bytes 4456600 | tf_op jit(solution)/shard_map/pallas_call | solution.py:178
  128.6 2.7 %collective-permute-done.17.refs_4_ = bf16[2,256,256]{2,1,0:T(8,128)(2,1)S(1)} collective-permute-done((bf16[2,256,256]{2,1,0:T(8,128)(2,1)S(1)}, bf16[2,256,256]{2,1,0:T(8,128)(2,1)S(1)}, u32[]{:S(2)}, u32[]{:S(2)}) %collective-permute-start.17) | collective-permute-done | bytes 262176 | tf_op jit(solution)/shard_map/ppermute | solution.py:21
  131.3 4.5 %collective-permute-done.18.refs_5_ = bf16[2,256,256]{2,1,0:T(8,128)(2,1)S(1)} collective-permute-done((bf16[2,256,256]{2,1,0:T(8,128)(2,1)S(1)}, bf16[2,256,256]{2,1,0:T(8,128)(2,1)S(1)}, u32[]{:S(2)}, u32[]{:S(2)}) %collective-permute-start.18) | collective-permute-done | bytes 262176 | tf_op jit(solution)/shard_map/ppermute | solution.py:21
  136.9 1.9 %collective-permute-start.19 = (bf16[2,128,256]{2,1,0:T(8,128)(2,1)S(1)}, bf16[2,128,256]{2,1,0:T(8,128)(2,1)S(1)}, u32[]{:S(2)}, u32[]{:S(2)}) collective-permute-start(bf16[2,128,256]{2,1,0:T(8,128)(2,1)S(1)} %get-tuple-element.21), channel_id=1, source_target_pairs={{0,1},{1,0},{2,3},{3,2},{4,5},{5,4},{6,7},{7,6},{8,9},{9,8},{10,11... | collective-permute-start | bytes 393224 | tf_op jit(solution)/shard_map/ppermute | solution.py:21
  138.9 7.0 %collective-permute-done.19 = bf16[2,128,256]{2,1,0:T(8,128)(2,1)S(1)} collective-permute-done((bf16[2,128,256]{2,1,0:T(8,128)(2,1)S(1)}, bf16[2,128,256]{2,1,0:T(8,128)(2,1)S(1)}, u32[]{:S(2)}, u32[]{:S(2)}) %collective-permute-start.19) | collective-permute-done | bytes 131104 | tf_op jit(solution)/shard_map/ppermute | solution.py:21
  (44 shorter events, 9.8 us)
Async XLA Ops:
  0.6 67.9 %copy-start = (bf16[12,256,256]{2,1,0:T(8,128)(2,1)S(1)}, bf16[12,256,256]{2,1,0:T(8,128)(2,1)}, u32[]{:S(2)}) copy-start(bf16[12,256,256]{2,1,0:T(8,128)(2,1)} %refs_2_.11) | copy-start | bytes 4718596
  0.6 67.9 %copy-start.1 = (bf16[2,256,256]{2,1,0:T(8,128)(2,1)S(1)}, bf16[2,256,256]{2,1,0:T(8,128)(2,1)}, u32[]{:S(2)}) copy-start(bf16[2,256,256]{2,1,0:T(8,128)(2,1)} %refs_3_.3) | copy-start | bytes 786436
  1.9 8.6 %collective-permute-start = (bf16[2,128,256]{2,1,0:T(8,128)(2,1)S(1)}, bf16[2,128,256]{2,1,0:T(8,128)(2,1)S(1)}, u32[]{:S(2)}, u32[]{:S(2)}) collective-permute-start(bf16[2,128,256]{2,1,0:T(8,128)(2,1)S(1)} %get-tuple-element.29), channel_id=1, source_target_pairs={{0,1},{1,0},{2,3},{3,2},{4,5},{5,4},{6,7},{7,6},{8,9},{9,8},{10,11... | collective-permute-start | bytes 393224 | tf_op jit(solution)/shard_map/ppermute | solution.py:21
  10.6 27.2 %collective-permute-start.1 = (bf16[2,256,256]{2,1,0:T(8,128)(2,1)S(1)}, bf16[2,256,256]{2,1,0:T(8,128)(2,1)S(1)}, u32[]{:S(2)}, u32[]{:S(2)}) collective-permute-start(bf16[2,256,256]{2,1,0:T(8,128)(2,1)S(1)} %maximum_select_fusion.refs_4_.refs_3_), channel_id=1, source_target_pairs={{0,32},{16,48},{32,0},{48,16},{64,96},{80,112},{96,64},{112,80},{1... | collective-permute-start | bytes 786440 | tf_op jit(solution)/shard_map/ppermute | solution.py:21
  14.0 25.8 %collective-permute-start.6 = (bf16[2,256,256]{2,1,0:T(8,128)(2,1)S(1)}, bf16[2,256,256]{2,1,0:T(8,128)(2,1)S(1)}, u32[]{:S(2)}, u32[]{:S(2)}) collective-permute-start(bf16[2,256,256]{2,1,0:T(8,128)(2,1)S(1)} %maximum_select_fusion.refs_4_.refs_3_), channel_id=1, source_target_pairs={{0,64},{2,130},{16,80},{18,146},{32,96},{34,162},{48,112},{50,178}... | collective-permute-start | bytes 786440 | tf_op jit(solution)/shard_map/ppermute | solution.py:31
  21.6 38.6 %collective-permute-start.2 = (bf16[2,256,256]{2,1,0:T(8,128)(2,1)S(1)}, bf16[2,256,256]{2,1,0:T(8,128)(2,1)S(1)}, u32[]{:S(2)}, u32[]{:S(2)}) collective-permute-start(bf16[2,256,256]{2,1,0:T(8,128)(2,1)S(1)} %maximum_select_fusion.refs_4_.refs_3_), channel_id=1, source_target_pairs={{0,16},{16,0},{32,48},{48,32},{64,80},{80,64},{96,112},{112,96},{1... | collective-permute-start | bytes 786440 | tf_op jit(solution)/shard_map/ppermute | solution.py:21
  24.5 39.1 %collective-permute-start.3 = (bf16[2,256,256]{2,1,0:T(8,128)(2,1)S(1)}, bf16[2,256,256]{2,1,0:T(8,128)(2,1)S(1)}, u32[]{:S(2)}, u32[]{:S(2)}) collective-permute-start(bf16[2,256,256]{2,1,0:T(8,128)(2,1)S(1)} %maximum_select_fusion.refs_4_.refs_3_), channel_id=1, source_target_pairs={{0,2},{2,0},{1,3},{3,1},{4,6},{6,4},{5,7},{7,5},{8,10},{10,8},{9,1... | collective-permute-start | bytes 786440 | tf_op jit(solution)/shard_map/ppermute | solution.py:21
  26.5 42.1 %collective-permute-start.4 = (bf16[2,256,256]{2,1,0:T(8,128)(2,1)S(1)}, bf16[2,256,256]{2,1,0:T(8,128)(2,1)S(1)}, u32[]{:S(2)}, u32[]{:S(2)}) collective-permute-start(bf16[2,256,256]{2,1,0:T(8,128)(2,1)S(1)} %maximum_select_fusion.refs_4_.refs_3_), channel_id=1, source_target_pairs={{0,256},{256,0},{1,257},{257,1},{2,258},{258,2},{3,259},{259,3},{4... | collective-permute-start | bytes 786440 | tf_op jit(solution)/shard_map/ppermute | solution.py:21
  37.9 30.7 %collective-permute-start.5 = (bf16[2,256,256]{2,1,0:T(8,128)(2,1)S(1)}, bf16[2,256,256]{2,1,0:T(8,128)(2,1)S(1)}, u32[]{:S(2)}, u32[]{:S(2)}) collective-permute-start(bf16[2,256,256]{2,1,0:T(8,128)(2,1)S(1)} %maximum_select_fusion.refs_4_.refs_3_), channel_id=1, source_target_pairs={{0,1},{1,0},{2,3},{3,2},{4,5},{5,4},{6,7},{7,6},{8,9},{9,8},{10,11... | collective-permute-start | bytes 786440 | tf_op jit(solution)/shard_map/ppermute | solution.py:21
  39.8 30.8 %collective-permute-start.7 = (bf16[2,256,256]{2,1,0:T(8,128)(2,1)S(1)}, bf16[2,256,256]{2,1,0:T(8,128)(2,1)S(1)}, u32[]{:S(2)}, u32[]{:S(2)}) collective-permute-start(bf16[2,256,256]{2,1,0:T(8,128)(2,1)S(1)} %broadcast_select_fusion.1), channel_id=1, source_target_pairs={{0,192},{2,66},{16,208},{18,82},{32,224},{34,98},{48,240},{50,114}... | collective-permute-start | bytes 786440 | tf_op jit(solution)/shard_map/ppermute | solution.py:31
  60.2 11.6 %collective-permute-start.8 = (bf16[2,256,256]{2,1,0:T(8,128)(2,1)S(1)}, bf16[2,256,256]{2,1,0:T(8,128)(2,1)S(1)}, u32[]{:S(2)}, u32[]{:S(2)}) collective-permute-start(bf16[2,256,256]{2,1,0:T(8,128)(2,1)S(1)} %maximum_select_fusion.refs_4_.refs_3_), channel_id=1, source_target_pairs={{0,4},{4,0},{8,12},{12,8},{1,5},{5,1},{9,13},{13,9},{2,6},{6,2},{1... | collective-permute-start | bytes 786440 | tf_op jit(solution)/shard_map/ppermute | solution.py:21
  63.6 13.3 %collective-permute-start.9 = (bf16[2,256,256]{2,1,0:T(8,128)(2,1)S(1)}, bf16[2,256,256]{2,1,0:T(8,128)(2,1)S(1)}, u32[]{:S(2)}, u32[]{:S(2)}) collective-permute-start(bf16[2,256,256]{2,1,0:T(8,128)(2,1)S(1)} %maximum_select_fusion.refs_4_.refs_3_), channel_id=1, source_target_pairs={{0,8},{4,12},{8,0},{12,4},{1,9},{5,13},{9,1},{13,5},{2,10},{6,14},... | collective-permute-start | bytes 786440 | tf_op jit(solution)/shard_map/ppermute | solution.py:21
  78.1 27.4 %collective-permute-start.10 = (bf16[2,256,256]{2,1,0:T(8,128)(2,1)S(1)}, bf16[2,256,256]{2,1,0:T(8,128)(2,1)S(1)}, u32[]{:S(2)}, u32[]{:S(2)}) collective-permute-start(bf16[2,256,256]{2,1,0:T(8,128)(2,1)S(1)} %get-tuple-element.19.refs_4_), channel_id=1, source_target_pairs={{0,32},{16,48},{32,0},{48,16},{64,96},{80,112},{96,64},{112,80},{1... | collective-permute-start | bytes 786440 | tf_op jit(solution)/shard_map/ppermute | solution.py:21
  80.0 27.4 %collective-permute-start.15 = (bf16[2,256,256]{2,1,0:T(8,128)(2,1)S(1)}, bf16[2,256,256]{2,1,0:T(8,128)(2,1)S(1)}, u32[]{:S(2)}, u32[]{:S(2)}) collective-permute-start(bf16[2,256,256]{2,1,0:T(8,128)(2,1)S(1)} %get-tuple-element.19.refs_4_), channel_id=1, source_target_pairs={{0,64},{2,130},{16,80},{18,146},{32,96},{34,162},{48,112},{50,178}... | collective-permute-start | bytes 786440 | tf_op jit(solution)/shard_map/ppermute | solution.py:31
  81.9 38.4 %collective-permute-start.11 = (bf16[2,256,256]{2,1,0:T(8,128)(2,1)S(1)}, bf16[2,256,256]{2,1,0:T(8,128)(2,1)S(1)}, u32[]{:S(2)}, u32[]{:S(2)}) collective-permute-start(bf16[2,256,256]{2,1,0:T(8,128)(2,1)S(1)} %get-tuple-element.19.refs_4_), channel_id=1, source_target_pairs={{0,16},{16,0},{32,48},{48,32},{64,80},{80,64},{96,112},{112,96},{1... | collective-permute-start | bytes 786440 | tf_op jit(solution)/shard_map/ppermute | solution.py:21
  83.8 38.4 %collective-permute-start.12 = (bf16[2,256,256]{2,1,0:T(8,128)(2,1)S(1)}, bf16[2,256,256]{2,1,0:T(8,128)(2,1)S(1)}, u32[]{:S(2)}, u32[]{:S(2)}) collective-permute-start(bf16[2,256,256]{2,1,0:T(8,128)(2,1)S(1)} %get-tuple-element.19.refs_4_), channel_id=1, source_target_pairs={{0,2},{2,0},{1,3},{3,1},{4,6},{6,4},{5,7},{7,5},{8,10},{10,8},{9,1... | collective-permute-start | bytes 786440 | tf_op jit(solution)/shard_map/ppermute | solution.py:21
  86.8 38.6 %collective-permute-start.13 = (bf16[2,256,256]{2,1,0:T(8,128)(2,1)S(1)}, bf16[2,256,256]{2,1,0:T(8,128)(2,1)S(1)}, u32[]{:S(2)}, u32[]{:S(2)}) collective-permute-start(bf16[2,256,256]{2,1,0:T(8,128)(2,1)S(1)} %get-tuple-element.19.refs_4_), channel_id=1, source_target_pairs={{0,256},{256,0},{1,257},{257,1},{2,258},{258,2},{3,259},{259,3},{4... | collective-permute-start | bytes 786440 | tf_op jit(solution)/shard_map/ppermute | solution.py:21
  105.5 19.9 %collective-permute-start.14 = (bf16[2,256,256]{2,1,0:T(8,128)(2,1)S(1)}, bf16[2,256,256]{2,1,0:T(8,128)(2,1)S(1)}, u32[]{:S(2)}, u32[]{:S(2)}) collective-permute-start(bf16[2,256,256]{2,1,0:T(8,128)(2,1)S(1)} %get-tuple-element.19.refs_4_), channel_id=1, source_target_pairs={{0,1},{1,0},{2,3},{3,2},{4,5},{5,4},{6,7},{7,6},{8,9},{9,8},{10,11... | collective-permute-start | bytes 786440 | tf_op jit(solution)/shard_map/ppermute | solution.py:21
  107.4 20.0 %collective-permute-start.16 = (bf16[2,256,256]{2,1,0:T(8,128)(2,1)S(1)}, bf16[2,256,256]{2,1,0:T(8,128)(2,1)S(1)}, u32[]{:S(2)}, u32[]{:S(2)}) collective-permute-start(bf16[2,256,256]{2,1,0:T(8,128)(2,1)S(1)} %broadcast_select_fusion), channel_id=1, source_target_pairs={{0,192},{2,66},{16,208},{18,82},{32,224},{34,98},{48,240},{50,114}... | collective-permute-start | bytes 786440 | tf_op jit(solution)/shard_map/ppermute | solution.py:31
  120.3 11.0 %collective-permute-start.17 = (bf16[2,256,256]{2,1,0:T(8,128)(2,1)S(1)}, bf16[2,256,256]{2,1,0:T(8,128)(2,1)S(1)}, u32[]{:S(2)}, u32[]{:S(2)}) collective-permute-start(bf16[2,256,256]{2,1,0:T(8,128)(2,1)S(1)} %get-tuple-element.19.refs_4_), channel_id=1, source_target_pairs={{0,4},{4,0},{8,12},{12,8},{1,5},{5,1},{9,13},{13,9},{2,6},{6,2},{1... | collective-permute-start | bytes 786440 | tf_op jit(solution)/shard_map/ppermute | solution.py:21
  122.2 13.6 %collective-permute-start.18 = (bf16[2,256,256]{2,1,0:T(8,128)(2,1)S(1)}, bf16[2,256,256]{2,1,0:T(8,128)(2,1)S(1)}, u32[]{:S(2)}, u32[]{:S(2)}) collective-permute-start(bf16[2,256,256]{2,1,0:T(8,128)(2,1)S(1)} %get-tuple-element.19.refs_4_), channel_id=1, source_target_pairs={{0,8},{4,12},{8,0},{12,4},{1,9},{5,13},{9,1},{13,5},{2,10},{6,14},... | collective-permute-start | bytes 786440 | tf_op jit(solution)/shard_map/ppermute | solution.py:21
  128.5 17.4 %copy-start.2 = (f32[2,128,256]{2,1,0:T(8,128)S(1)}, f32[2,128,256]{2,1,0:T(8,128)}, u32[]{:S(2)}) copy-start(f32[2,128,256]{2,1,0:T(8,128)} %param.11) | copy-start | bytes 786436
  128.6 17.4 %copy-start.3 = (f32[2,128,256]{2,1,0:T(8,128)S(1)}, f32[2,128,256]{2,1,0:T(8,128)}, u32[]{:S(2)}) copy-start(f32[2,128,256]{2,1,0:T(8,128)} %param.10) | copy-start | bytes 786436
  136.9 9.0 %collective-permute-start.19 = (bf16[2,128,256]{2,1,0:T(8,128)(2,1)S(1)}, bf16[2,128,256]{2,1,0:T(8,128)(2,1)S(1)}, u32[]{:S(2)}, u32[]{:S(2)}) collective-permute-start(bf16[2,128,256]{2,1,0:T(8,128)(2,1)S(1)} %get-tuple-element.21), channel_id=1, source_target_pairs={{0,1},{1,0},{2,3},{3,2},{4,5},{5,4},{6,7},{7,6},{8,9},{9,8},{10,11... | collective-permute-start | bytes 393224 | tf_op jit(solution)/shard_map/ppermute | solution.py:21

commit v5 on v4

--- a/solution.py
+++ b/solution.py
@@ -153,16 +153,16 @@
     half_float = shaped(float32, 2, rows, levels)
 
     def exchange(full):
+        first = across(full, inward, opposite)
+        core = swapped(full, "core", 1)
         z2 = swapped(full, "z", 2)
-        first = across(full, inward, opposite)
-        z1 = swapped(full, "z", 1)
-        core = swapped(full, "core", 1)
-        x1 = swapped(full, "x_lo", 1)
-        x2 = swapped(after(full, z2), "rep", 1)
-        y1 = swapped(after(full, first, z1), "y", 1)
-        y2 = swapped(after(full, first, core), "y", 2)
+        x2 = swapped(full, "rep", 1)
+        y2 = swapped(full, "y", 2)
+        z1 = swapped(after(full, first, core), "z", 1)
+        x1 = swapped(after(full, first, x2), "x_lo", 1)
+        y1 = swapped(after(full, first, z2), "y", 1)
         second = across(jnp.where(on_first, first, full), outward, inward)
-        return {5: [z2], 4: [z1], 1: [core], 8: [x1], 0: [x2]}, {6: [first, second], 7: [second, first]}, {2: [y1], 3: [y2]}
+        return {1: [core], 5: [z2], 0: [x2], 3: [y2]}, {6: [first, second], 7: [second, first]}, {4: [z1], 8: [x1], 2: [y1]}
 
     def call(body, parts, outs, scratch, *operands):
         held = []

time: 148 us -> 141 us (0.953)
  the two profiles are of different devices: /device:TPU:388 before, /device:TPU:2 now
where the time goes in v5:
time: 141 us; the launch traced here: 140 us
  starting transfers between devices  106 us (75%)
  waiting for transfers between devices  16.8 us (12%)
  Pallas kernels  8.55 us (6%)
  other arithmetic  5.74 us (4%)
  between operations  2.36 us (2%)
    ppermute x16, starting transfers between devices, swapped(): return lax.ppermute(value, axis, pairs)  88.5 us
    ppermute x4, starting transfers between devices, across(): return lax.ppermute(value, ('z', 'core'), pairs)  17.8 us
    ppermute x16, waiting for transfers between devices, swapped(): return lax.ppermute(value, axis, pairs)  12.5 us
    pallas_call x6, Pallas kernels, call(): pl.pallas_call(lambda *refs: body(counts, *refs), out_shape=outs, in_spec...  8.55 us
    ppermute x4, waiting for transfers between devices, across(): return lax.ppermute(value, ('z', 'core'), pairs)  4.31 us
  transfers between devices with their start and end apart: 20, of which 6 were waited for; matrix products, arithmetic and copies ran while one was open for 3% of the time, Pallas kernels for 4%

profile of v5, /device:TPU:2, one launch (start us, length us, event | category | flops | bytes accessed | tf_op | source)
XLA Modules:
  0.0 140.4 jit_solution(6176510292690102421)
XLA Ops:
  0.7 1.2 convert_bitcast_fusion
  1.9 4.0 %collective-permute-start = (bf16[2,128,256]{2,1,0:T(8,128)(2,1)S(1)}, bf16[2,128,256]{2,1,0:T(8,128)(2,1)S(1)}, u32[]{:S(2)}, u32[]{:S(2)}) collective-permute-start(bf16[2,128,256]{2,1,0:T(8,128)(2,1)S(1)} %get-tuple-element.29), channel_id=1, source_target_pairs={{0,1},{1,0},{2,3},{3,2},{4,5},{5,4},{6,7},{7,6},{8,9},{9,8},{10,11... | collective-permute-start | bytes 393224 | tf_op jit(solution)/shard_map/ppermute | solution.py:21
  9.1 1.4 %collective-permute-done = bf16[2,128,256]{2,1,0:T(8,128)(2,1)S(1)} collective-permute-done((bf16[2,128,256]{2,1,0:T(8,128)(2,1)S(1)}, bf16[2,128,256]{2,1,0:T(8,128)(2,1)S(1)}, u32[]{:S(2)}, u32[]{:S(2)}) %collective-permute-start) | collective-permute-done | bytes 131104 | tf_op jit(solution)/shard_map/ppermute | solution.py:21
  10.6 9.1 %collective-permute-start.5 = (bf16[2,256,256]{2,1,0:T(8,128)(2,1)S(1)}, bf16[2,256,256]{2,1,0:T(8,128)(2,1)S(1)}, u32[]{:S(2)}, u32[]{:S(2)}) collective-permute-start(bf16[2,256,256]{2,1,0:T(8,128)(2,1)S(1)} %maximum_select_fusion.refs_4_.refs_3_), channel_id=1, source_target_pairs={{0,64},{2,130},{16,80},{18,146},{32,96},{34,162},{48,112},{50,178}... | collective-permute-start | bytes 786440 | tf_op jit(solution)/shard_map/ppermute | solution.py:31
  21.8 7.2 %collective-permute-start.1 = (bf16[2,256,256]{2,1,0:T(8,128)(2,1)S(1)}, bf16[2,256,256]{2,1,0:T(8,128)(2,1)S(1)}, u32[]{:S(2)}, u32[]{:S(2)}) collective-permute-start(bf16[2,256,256]{2,1,0:T(8,128)(2,1)S(1)} %maximum_select_fusion.refs_4_.refs_3_), channel_id=1, source_target_pairs={{0,2},{2,0},{1,3},{3,1},{4,6},{6,4},{5,7},{7,5},{8,10},{10,8},{9,1... | collective-permute-start | bytes 786440 | tf_op jit(solution)/shard_map/ppermute | solution.py:21
  29.0 3.4 %collective-permute-start.2 = (bf16[2,256,256]{2,1,0:T(8,128)(2,1)S(1)}, bf16[2,256,256]{2,1,0:T(8,128)(2,1)S(1)}, u32[]{:S(2)}, u32[]{:S(2)}) collective-permute-start(bf16[2,256,256]{2,1,0:T(8,128)(2,1)S(1)} %maximum_select_fusion.refs_4_.refs_3_), channel_id=1, source_target_pairs={{0,32},{16,48},{32,0},{48,16},{64,96},{80,112},{96,64},{112,80},{1... | collective-permute-start | bytes 786440 | tf_op jit(solution)/shard_map/ppermute | solution.py:21
  32.4 4.0 %collective-permute-start.3 = (bf16[2,256,256]{2,1,0:T(8,128)(2,1)S(1)}, bf16[2,256,256]{2,1,0:T(8,128)(2,1)S(1)}, u32[]{:S(2)}, u32[]{:S(2)}) collective-permute-start(bf16[2,256,256]{2,1,0:T(8,128)(2,1)S(1)} %maximum_select_fusion.refs_4_.refs_3_), channel_id=1, source_target_pairs={{0,1},{1,0},{2,3},{3,2},{4,5},{5,4},{6,7},{7,6},{8,9},{9,8},{10,11... | collective-permute-start | bytes 786440 | tf_op jit(solution)/shard_map/ppermute | solution.py:21
  36.5 5.1 %collective-permute-start.4 = (bf16[2,256,256]{2,1,0:T(8,128)(2,1)S(1)}, bf16[2,256,256]{2,1,0:T(8,128)(2,1)S(1)}, u32[]{:S(2)}, u32[]{:S(2)}) collective-permute-start(bf16[2,256,256]{2,1,0:T(8,128)(2,1)S(1)} %maximum_select_fusion.refs_4_.refs_3_), channel_id=1, source_target_pairs={{0,8},{4,12},{8,0},{12,4},{1,9},{5,13},{9,1},{13,5},{2,10},{6,14},... | collective-permute-start | bytes 786440 | tf_op jit(solution)/shard_map/ppermute | solution.py:21
  42.4 4.9 %collective-permute-start.6 = (bf16[2,256,256]{2,1,0:T(8,128)(2,1)S(1)}, bf16[2,256,256]{2,1,0:T(8,128)(2,1)S(1)}, u32[]{:S(2)}, u32[]{:S(2)}) collective-permute-start(bf16[2,256,256]{2,1,0:T(8,128)(2,1)S(1)} %broadcast_select_fusion.1), channel_id=1, source_target_pairs={{0,192},{2,66},{16,208},{18,82},{32,224},{34,98},{48,240},{50,114}... | collective-permute-start | bytes 786440 | tf_op jit(solution)/shard_map/ppermute | solution.py:31
  47.3 13.5 %collective-permute-start.7 = (bf16[2,256,256]{2,1,0:T(8,128)(2,1)S(1)}, bf16[2,256,256]{2,1,0:T(8,128)(2,1)S(1)}, u32[]{:S(2)}, u32[]{:S(2)}) collective-permute-start(bf16[2,256,256]{2,1,0:T(8,128)(2,1)S(1)} %maximum_select_fusion.refs_4_.refs_3_), channel_id=1, source_target_pairs={{0,16},{16,0},{32,48},{48,32},{64,80},{80,64},{96,112},{112,96},{1... | collective-permute-start | bytes 786440 | tf_op jit(solution)/shard_map/ppermute | solution.py:21
  60.8 1.9 %collective-permute-start.8 = (bf16[2,256,256]{2,1,0:T(8,128)(2,1)S(1)}, bf16[2,256,256]{2,1,0:T(8,128)(2,1)S(1)}, u32[]{:S(2)}, u32[]{:S(2)}) collective-permute-start(bf16[2,256,256]{2,1,0:T(8,128)(2,1)S(1)} %maximum_select_fusion.refs_4_.refs_3_), channel_id=1, source_target_pairs={{0,256},{256,0},{1,257},{257,1},{2,258},{258,2},{3,259},{259,3},{4... | collective-permute-start | bytes 786440 | tf_op jit(solution)/shard_map/ppermute | solution.py:21
  62.7 4.0 %collective-permute-start.9 = (bf16[2,256,256]{2,1,0:T(8,128)(2,1)S(1)}, bf16[2,256,256]{2,1,0:T(8,128)(2,1)S(1)}, u32[]{:S(2)}, u32[]{:S(2)}) collective-permute-start(bf16[2,256,256]{2,1,0:T(8,128)(2,1)S(1)} %maximum_select_fusion.refs_4_.refs_3_), channel_id=1, source_target_pairs={{0,4},{4,0},{8,12},{12,8},{1,5},{5,1},{9,13},{13,9},{2,6},{6,2},{1... | collective-permute-start | bytes 786440 | tf_op jit(solution)/shard_map/ppermute | solution.py:21
  66.8 1.8 %shard_map.113.refs_3_ = f32[2,256,256]{2,1,0:T(8,128)S(1)} custom-call(s32[11]{0:T(128)S(1)} %pad_add_fusion.refs_0_, f32[3,9]{1,0:T(4,128)S(1)} %pad_maximum_fusion.1.refs_1_, bf16[12,256,256]{2,1,0:T(8,128)(2,1)S(1)} %copy-done, bf16[2,256,256]{2,1,0:T(8,128)(2,1)S(1)} %copy-done.1, bf16[2,256,256]{2,1,0:T(8,128)(2,1)S(1)} %maximum_select_fusion.refs_4_.refs_3_, ...), custom_call_target="tpu_custom_call" | custom-call | flops 536870912 | bytes 3670168 | tf_op jit(solution)/shard_map/pallas_call | solution.py:178
  68.7 1.1 shard_map.114.refs_4_
  69.8 1.3 collective-permute-done.9.refs_7_
  71.1 1.4 shard_map.115
  72.4 1.9 %collective-permute-start.14 = (bf16[2,256,256]{2,1,0:T(8,128)(2,1)S(1)}, bf16[2,256,256]{2,1,0:T(8,128)(2,1)S(1)}, u32[]{:S(2)}, u32[]{:S(2)}) collective-permute-start(bf16[2,256,256]{2,1,0:T(8,128)(2,1)S(1)} %get-tuple-element.19.refs_4_), channel_id=1, source_target_pairs={{0,64},{2,130},{16,80},{18,146},{32,96},{34,162},{48,112},{50,178}... | collective-permute-start | bytes 786440 | tf_op jit(solution)/shard_map/ppermute | solution.py:31
  74.4 1.9 %collective-permute-start.10 = (bf16[2,256,256]{2,1,0:T(8,128)(2,1)S(1)}, bf16[2,256,256]{2,1,0:T(8,128)(2,1)S(1)}, u32[]{:S(2)}, u32[]{:S(2)}) collective-permute-start(bf16[2,256,256]{2,1,0:T(8,128)(2,1)S(1)} %get-tuple-element.19.refs_4_), channel_id=1, source_target_pairs={{0,2},{2,0},{1,3},{3,1},{4,6},{6,4},{5,7},{7,5},{8,10},{10,8},{9,1... | collective-permute-start | bytes 786440 | tf_op jit(solution)/shard_map/ppermute | solution.py:21
  76.3 11.7 %collective-permute-start.11 = (bf16[2,256,256]{2,1,0:T(8,128)(2,1)S(1)}, bf16[2,256,256]{2,1,0:T(8,128)(2,1)S(1)}, u32[]{:S(2)}, u32[]{:S(2)}) collective-permute-start(bf16[2,256,256]{2,1,0:T(8,128)(2,1)S(1)} %get-tuple-element.19.refs_4_), channel_id=1, source_target_pairs={{0,32},{16,48},{32,0},{48,16},{64,96},{80,112},{96,64},{112,80},{1... | collective-permute-start | bytes 786440 | tf_op jit(solution)/shard_map/ppermute | solution.py:21
  88.0 4.3 %collective-permute-start.12 = (bf16[2,256,256]{2,1,0:T(8,128)(2,1)S(1)}, bf16[2,256,256]{2,1,0:T(8,128)(2,1)S(1)}, u32[]{:S(2)}, u32[]{:S(2)}) collective-permute-start(bf16[2,256,256]{2,1,0:T(8,128)(2,1)S(1)} %get-tuple-element.19.refs_4_), channel_id=1, source_target_pairs={{0,1},{1,0},{2,3},{3,2},{4,5},{5,4},{6,7},{7,6},{8,9},{9,8},{10,11... | collective-permute-start | bytes 786440 | tf_op jit(solution)/shard_map/ppermute | solution.py:21
  92.3 5.1 %collective-permute-start.13 = (bf16[2,256,256]{2,1,0:T(8,128)(2,1)S(1)}, bf16[2,256,256]{2,1,0:T(8,128)(2,1)S(1)}, u32[]{:S(2)}, u32[]{:S(2)}) collective-permute-start(bf16[2,256,256]{2,1,0:T(8,128)(2,1)S(1)} %get-tuple-element.19.refs_4_), channel_id=1, source_target_pairs={{0,8},{4,12},{8,0},{12,4},{1,9},{5,13},{9,1},{13,5},{2,10},{6,14},... | collective-permute-start | bytes 786440 | tf_op jit(solution)/shard_map/ppermute | solution.py:21
  97.4 3.6 %collective-permute-done.14.refs_4_ = bf16[2,256,256]{2,1,0:T(8,128)(2,1)S(1)} collective-permute-done((bf16[2,256,256]{2,1,0:T(8,128)(2,1)S(1)}, bf16[2,256,256]{2,1,0:T(8,128)(2,1)S(1)}, u32[]{:S(2)}, u32[]{:S(2)}) %collective-permute-start.14) | collective-permute-done | bytes 262176 | tf_op jit(solution)/shard_map/ppermute | solution.py:31
  101.0 1.9 %collective-permute-start.15 = (bf16[2,256,256]{2,1,0:T(8,128)(2,1)S(1)}, bf16[2,256,256]{2,1,0:T(8,128)(2,1)S(1)}, u32[]{:S(2)}, u32[]{:S(2)}) collective-permute-start(bf16[2,256,256]{2,1,0:T(8,128)(2,1)S(1)} %broadcast_select_fusion), channel_id=1, source_target_pairs={{0,192},{2,66},{16,208},{18,82},{32,224},{34,98},{48,240},{50,114}... | collective-permute-start | bytes 786440 | tf_op jit(solution)/shard_map/ppermute | solution.py:31
  102.9 1.9 %collective-permute-start.16 = (bf16[2,256,256]{2,1,0:T(8,128)(2,1)S(1)}, bf16[2,256,256]{2,1,0:T(8,128)(2,1)S(1)}, u32[]{:S(2)}, u32[]{:S(2)}) collective-permute-start(bf16[2,256,256]{2,1,0:T(8,128)(2,1)S(1)} %get-tuple-element.19.refs_4_), channel_id=1, source_target_pairs={{0,16},{16,0},{32,48},{48,32},{64,80},{80,64},{96,112},{112,96},{1... | collective-permute-start | bytes 786440 | tf_op jit(solution)/shard_map/ppermute | solution.py:21
  104.9 16.6 %collective-permute-start.17 = (bf16[2,256,256]{2,1,0:T(8,128)(2,1)S(1)}, bf16[2,256,256]{2,1,0:T(8,128)(2,1)S(1)}, u32[]{:S(2)}, u32[]{:S(2)}) collective-permute-start(bf16[2,256,256]{2,1,0:T(8,128)(2,1)S(1)} %get-tuple-element.19.refs_4_), channel_id=1, source_target_pairs={{0,256},{256,0},{1,257},{257,1},{2,258},{258,2},{3,259},{259,3},{4... | collective-permute-start | bytes 786440 | tf_op jit(solution)/shard_map/ppermute | solution.py:21
  121.5 1.9 %collective-permute-start.18 = (bf16[2,256,256]{2,1,0:T(8,128)(2,1)S(1)}, bf16[2,256,256]{2,1,0:T(8,128)(2,1)S(1)}, u32[]{:S(2)}, u32[]{:S(2)}) collective-permute-start(bf16[2,256,256]{2,1,0:T(8,128)(2,1)S(1)} %get-tuple-element.19.refs_4_), channel_id=1, source_target_pairs={{0,4},{4,0},{8,12},{12,8},{1,5},{5,1},{9,13},{13,9},{2,6},{6,2},{1... | collective-permute-start | bytes 786440 | tf_op jit(solution)/shard_map/ppermute | solution.py:21
  123.4 1.8 %shard_map.116.refs_3_ = f32[2,256,256]{2,1,0:T(8,128)S(1)} custom-call(s32[11]{0:T(128)S(1)} %pad_add_fusion.refs_0_, f32[3,9]{1,0:T(4,128)S(1)} %pad_maximum_fusion.1.refs_1_, bf16[12,256,256]{2,1,0:T(8,128)(2,1)S(1)} %copy-done, bf16[2,256,256]{2,1,0:T(8,128)(2,1)S(1)} %copy-done.1, bf16[2,256,256]{2,1,0:T(8,128)(2,1)S(1)} %get-tuple-element.19.refs_4_, ...), custom_call_target="tpu_custom_call" | custom-call | flops 536870912 | bytes 4194456 | tf_op jit(solution)/shard_map/pallas_call | solution.py:178
  125.3 1.1 shard_map.117.refs_3_
  126.4 3.3 %collective-permute-done.18.refs_6_ = bf16[2,256,256]{2,1,0:T(8,128)(2,1)S(1)} collective-permute-done((bf16[2,256,256]{2,1,0:T(8,128)(2,1)S(1)}, bf16[2,256,256]{2,1,0:T(8,128)(2,1)S(1)}, u32[]{:S(2)}, u32[]{:S(2)}) %collective-permute-start.18) | collective-permute-done | bytes 262176 | tf_op jit(solution)/shard_map/ppermute | solution.py:21
  129.7 1.3 shard_map.118
  131.1 1.9 %collective-permute-start.19 = (bf16[2,128,256]{2,1,0:T(8,128)(2,1)S(1)}, bf16[2,128,256]{2,1,0:T(8,128)(2,1)S(1)}, u32[]{:S(2)}, u32[]{:S(2)}) collective-permute-start(bf16[2,128,256]{2,1,0:T(8,128)(2,1)S(1)} %get-tuple-element.21), channel_id=1, source_target_pairs={{0,1},{1,0},{2,3},{3,2},{4,5},{5,4},{6,7},{7,6},{8,9},{9,8},{10,11... | collective-permute-start | bytes 393224 | tf_op jit(solution)/shard_map/ppermute | solution.py:21
  133.0 6.4 %collective-permute-done.19 = bf16[2,128,256]{2,1,0:T(8,128)(2,1)S(1)} collective-permute-done((bf16[2,128,256]{2,1,0:T(8,128)(2,1)S(1)}, bf16[2,128,256]{2,1,0:T(8,128)(2,1)S(1)}, u32[]{:S(2)}, u32[]{:S(2)}) %collective-permute-start.19) | collective-permute-done | bytes 131104 | tf_op jit(solution)/shard_map/ppermute | solution.py:21
  (44 shorter events, 6.0 us)
Async XLA Ops:
  0.6 66.2 %copy-start = (bf16[12,256,256]{2,1,0:T(8,128)(2,1)S(1)}, bf16[12,256,256]{2,1,0:T(8,128)(2,1)}, u32[]{:S(2)}) copy-start(bf16[12,256,256]{2,1,0:T(8,128)(2,1)} %refs_2_.11) | copy-start | bytes 4718596
  0.6 66.2 %copy-start.1 = (bf16[2,256,256]{2,1,0:T(8,128)(2,1)S(1)}, bf16[2,256,256]{2,1,0:T(8,128)(2,1)}, u32[]{:S(2)}) copy-start(bf16[2,256,256]{2,1,0:T(8,128)(2,1)} %refs_3_.3) | copy-start | bytes 786436
  1.9 8.6 %collective-permute-start = (bf16[2,128,256]{2,1,0:T(8,128)(2,1)S(1)}, bf16[2,128,256]{2,1,0:T(8,128)(2,1)S(1)}, u32[]{:S(2)}, u32[]{:S(2)}) collective-permute-start(bf16[2,128,256]{2,1,0:T(8,128)(2,1)S(1)} %get-tuple-element.29), channel_id=1, source_target_pairs={{0,1},{1,0},{2,3},{3,2},{4,5},{5,4},{6,7},{7,6},{8,9},{9,8},{10,11... | collective-permute-start | bytes 393224 | tf_op jit(solution)/shard_map/ppermute | solution.py:21
  10.6 31.7 %collective-permute-start.5 = (bf16[2,256,256]{2,1,0:T(8,128)(2,1)S(1)}, bf16[2,256,256]{2,1,0:T(8,128)(2,1)S(1)}, u32[]{:S(2)}, u32[]{:S(2)}) collective-permute-start(bf16[2,256,256]{2,1,0:T(8,128)(2,1)S(1)} %maximum_select_fusion.refs_4_.refs_3_), channel_id=1, source_target_pairs={{0,64},{2,130},{16,80},{18,146},{32,96},{34,162},{48,112},{50,178}... | collective-permute-start | bytes 786440 | tf_op jit(solution)/shard_map/ppermute | solution.py:31
  21.8 25.4 %collective-permute-start.1 = (bf16[2,256,256]{2,1,0:T(8,128)(2,1)S(1)}, bf16[2,256,256]{2,1,0:T(8,128)(2,1)S(1)}, u32[]{:S(2)}, u32[]{:S(2)}) collective-permute-start(bf16[2,256,256]{2,1,0:T(8,128)(2,1)S(1)} %maximum_select_fusion.refs_4_.refs_3_), channel_id=1, source_target_pairs={{0,2},{2,0},{1,3},{3,1},{4,6},{6,4},{5,7},{7,5},{8,10},{10,8},{9,1... | collective-permute-start | bytes 786440 | tf_op jit(solution)/shard_map/ppermute | solution.py:21
  29.0 33.7 %collective-permute-start.2 = (bf16[2,256,256]{2,1,0:T(8,128)(2,1)S(1)}, bf16[2,256,256]{2,1,0:T(8,128)(2,1)S(1)}, u32[]{:S(2)}, u32[]{:S(2)}) collective-permute-start(bf16[2,256,256]{2,1,0:T(8,128)(2,1)S(1)} %maximum_select_fusion.refs_4_.refs_3_), channel_id=1, source_target_pairs={{0,32},{16,48},{32,0},{48,16},{64,96},{80,112},{96,64},{112,80},{1... | collective-permute-start | bytes 786440 | tf_op jit(solution)/shard_map/ppermute | solution.py:21
  32.4 28.3 %collective-permute-start.3 = (bf16[2,256,256]{2,1,0:T(8,128)(2,1)S(1)}, bf16[2,256,256]{2,1,0:T(8,128)(2,1)S(1)}, u32[]{:S(2)}, u32[]{:S(2)}) collective-permute-start(bf16[2,256,256]{2,1,0:T(8,128)(2,1)S(1)} %maximum_select_fusion.refs_4_.refs_3_), channel_id=1, source_target_pairs={{0,1},{1,0},{2,3},{3,2},{4,5},{5,4},{6,7},{7,6},{8,9},{9,8},{10,11... | collective-permute-start | bytes 786440 | tf_op jit(solution)/shard_map/ppermute | solution.py:21
  36.5 30.3 %collective-permute-start.4 = (bf16[2,256,256]{2,1,0:T(8,128)(2,1)S(1)}, bf16[2,256,256]{2,1,0:T(8,128)(2,1)S(1)}, u32[]{:S(2)}, u32[]{:S(2)}) collective-permute-start(bf16[2,256,256]{2,1,0:T(8,128)(2,1)S(1)} %maximum_select_fusion.refs_4_.refs_3_), channel_id=1, source_target_pairs={{0,8},{4,12},{8,0},{12,4},{1,9},{5,13},{9,1},{13,5},{2,10},{6,14},... | collective-permute-start | bytes 786440 | tf_op jit(solution)/shard_map/ppermute | solution.py:21
  42.4 26.3 %collective-permute-start.6 = (bf16[2,256,256]{2,1,0:T(8,128)(2,1)S(1)}, bf16[2,256,256]{2,1,0:T(8,128)(2,1)S(1)}, u32[]{:S(2)}, u32[]{:S(2)}) collective-permute-start(bf16[2,256,256]{2,1,0:T(8,128)(2,1)S(1)} %broadcast_select_fusion.1), channel_id=1, source_target_pairs={{0,192},{2,66},{16,208},{18,82},{32,224},{34,98},{48,240},{50,114}... | collective-permute-start | bytes 786440 | tf_op jit(solution)/shard_map/ppermute | solution.py:31
  47.3 22.5 %collective-permute-start.7 = (bf16[2,256,256]{2,1,0:T(8,128)(2,1)S(1)}, bf16[2,256,256]{2,1,0:T(8,128)(2,1)S(1)}, u32[]{:S(2)}, u32[]{:S(2)}) collective-permute-start(bf16[2,256,256]{2,1,0:T(8,128)(2,1)S(1)} %maximum_select_fusion.refs_4_.refs_3_), channel_id=1, source_target_pairs={{0,16},{16,0},{32,48},{48,32},{64,80},{80,64},{96,112},{112,96},{1... | collective-permute-start | bytes 786440 | tf_op jit(solution)/shard_map/ppermute | solution.py:21
  60.8 9.0 %collective-permute-start.8 = (bf16[2,256,256]{2,1,0:T(8,128)(2,1)S(1)}, bf16[2,256,256]{2,1,0:T(8,128)(2,1)S(1)}, u32[]{:S(2)}, u32[]{:S(2)}) collective-permute-start(bf16[2,256,256]{2,1,0:T(8,128)(2,1)S(1)} %maximum_select_fusion.refs_4_.refs_3_), channel_id=1, source_target_pairs={{0,256},{256,0},{1,257},{257,1},{2,258},{258,2},{3,259},{259,3},{4... | collective-permute-start | bytes 786440 | tf_op jit(solution)/shard_map/ppermute | solution.py:21
  62.7 8.4 %collective-permute-start.9 = (bf16[2,256,256]{2,1,0:T(8,128)(2,1)S(1)}, bf16[2,256,256]{2,1,0:T(8,128)(2,1)S(1)}, u32[]{:S(2)}, u32[]{:S(2)}) collective-permute-start(bf16[2,256,256]{2,1,0:T(8,128)(2,1)S(1)} %maximum_select_fusion.refs_4_.refs_3_), channel_id=1, source_target_pairs={{0,4},{4,0},{8,12},{12,8},{1,5},{5,1},{9,13},{13,9},{2,6},{6,2},{1... | collective-permute-start | bytes 786440 | tf_op jit(solution)/shard_map/ppermute | solution.py:21
  72.4 28.5 %collective-permute-start.14 = (bf16[2,256,256]{2,1,0:T(8,128)(2,1)S(1)}, bf16[2,256,256]{2,1,0:T(8,128)(2,1)S(1)}, u32[]{:S(2)}, u32[]{:S(2)}) collective-permute-start(bf16[2,256,256]{2,1,0:T(8,128)(2,1)S(1)} %get-tuple-element.19.refs_4_), channel_id=1, source_target_pairs={{0,64},{2,130},{16,80},{18,146},{32,96},{34,162},{48,112},{50,178}... | collective-permute-start | bytes 786440 | tf_op jit(solution)/shard_map/ppermute | solution.py:31
  74.4 28.6 %collective-permute-start.10 = (bf16[2,256,256]{2,1,0:T(8,128)(2,1)S(1)}, bf16[2,256,256]{2,1,0:T(8,128)(2,1)S(1)}, u32[]{:S(2)}, u32[]{:S(2)}) collective-permute-start(bf16[2,256,256]{2,1,0:T(8,128)(2,1)S(1)} %get-tuple-element.19.refs_4_), channel_id=1, source_target_pairs={{0,2},{2,0},{1,3},{3,1},{4,6},{6,4},{5,7},{7,5},{8,10},{10,8},{9,1... | collective-permute-start | bytes 786440 | tf_op jit(solution)/shard_map/ppermute | solution.py:21
  76.3 45.2 %collective-permute-start.11 = (bf16[2,256,256]{2,1,0:T(8,128)(2,1)S(1)}, bf16[2,256,256]{2,1,0:T(8,128)(2,1)S(1)}, u32[]{:S(2)}, u32[]{:S(2)}) collective-permute-start(bf16[2,256,256]{2,1,0:T(8,128)(2,1)S(1)} %get-tuple-element.19.refs_4_), channel_id=1, source_target_pairs={{0,32},{16,48},{32,0},{48,16},{64,96},{80,112},{96,64},{112,80},{1... | collective-permute-start | bytes 786440 | tf_op jit(solution)/shard_map/ppermute | solution.py:21
  88.0 16.9 %collective-permute-start.12 = (bf16[2,256,256]{2,1,0:T(8,128)(2,1)S(1)}, bf16[2,256,256]{2,1,0:T(8,128)(2,1)S(1)}, u32[]{:S(2)}, u32[]{:S(2)}) collective-permute-start(bf16[2,256,256]{2,1,0:T(8,128)(2,1)S(1)} %get-tuple-element.19.refs_4_), channel_id=1, source_target_pairs={{0,1},{1,0},{2,3},{3,2},{4,5},{5,4},{6,7},{7,6},{8,9},{9,8},{10,11... | collective-permute-start | bytes 786440 | tf_op jit(solution)/shard_map/ppermute | solution.py:21
  92.3 31.1 %collective-permute-start.13 = (bf16[2,256,256]{2,1,0:T(8,128)(2,1)S(1)}, bf16[2,256,256]{2,1,0:T(8,128)(2,1)S(1)}, u32[]{:S(2)}, u32[]{:S(2)}) collective-permute-start(bf16[2,256,256]{2,1,0:T(8,128)(2,1)S(1)} %get-tuple-element.19.refs_4_), channel_id=1, source_target_pairs={{0,8},{4,12},{8,0},{12,4},{1,9},{5,13},{9,1},{13,5},{2,10},{6,14},... | collective-permute-start | bytes 786440 | tf_op jit(solution)/shard_map/ppermute | solution.py:21
  101.0 24.3 %collective-permute-start.15 = (bf16[2,256,256]{2,1,0:T(8,128)(2,1)S(1)}, bf16[2,256,256]{2,1,0:T(8,128)(2,1)S(1)}, u32[]{:S(2)}, u32[]{:S(2)}) collective-permute-start(bf16[2,256,256]{2,1,0:T(8,128)(2,1)S(1)} %broadcast_select_fusion), channel_id=1, source_target_pairs={{0,192},{2,66},{16,208},{18,82},{32,224},{34,98},{48,240},{50,114}... | collective-permute-start | bytes 786440 | tf_op jit(solution)/shard_map/ppermute | solution.py:31
  102.9 23.5 %collective-permute-start.16 = (bf16[2,256,256]{2,1,0:T(8,128)(2,1)S(1)}, bf16[2,256,256]{2,1,0:T(8,128)(2,1)S(1)}, u32[]{:S(2)}, u32[]{:S(2)}) collective-permute-start(bf16[2,256,256]{2,1,0:T(8,128)(2,1)S(1)} %get-tuple-element.19.refs_4_), channel_id=1, source_target_pairs={{0,16},{16,0},{32,48},{48,32},{64,80},{80,64},{96,112},{112,96},{1... | collective-permute-start | bytes 786440 | tf_op jit(solution)/shard_map/ppermute | solution.py:21
  104.9 21.6 %collective-permute-start.17 = (bf16[2,256,256]{2,1,0:T(8,128)(2,1)S(1)}, bf16[2,256,256]{2,1,0:T(8,128)(2,1)S(1)}, u32[]{:S(2)}, u32[]{:S(2)}) collective-permute-start(bf16[2,256,256]{2,1,0:T(8,128)(2,1)S(1)} %get-tuple-element.19.refs_4_), channel_id=1, source_target_pairs={{0,256},{256,0},{1,257},{257,1},{2,258},{258,2},{3,259},{259,3},{4... | collective-permute-start | bytes 786440 | tf_op jit(solution)/shard_map/ppermute | solution.py:21
  121.5 8.3 %collective-permute-start.18 = (bf16[2,256,256]{2,1,0:T(8,128)(2,1)S(1)}, bf16[2,256,256]{2,1,0:T(8,128)(2,1)S(1)}, u32[]{:S(2)}, u32[]{:S(2)}) collective-permute-start(bf16[2,256,256]{2,1,0:T(8,128)(2,1)S(1)} %get-tuple-element.19.refs_4_), channel_id=1, source_target_pairs={{0,4},{4,0},{8,12},{12,8},{1,5},{5,1},{9,13},{13,9},{2,6},{6,2},{1... | collective-permute-start | bytes 786440 | tf_op jit(solution)/shard_map/ppermute | solution.py:21
  126.4 13.1 %copy-start.2 = (f32[2,128,256]{2,1,0:T(8,128)S(1)}, f32[2,128,256]{2,1,0:T(8,128)}, u32[]{:S(2)}) copy-start(f32[2,128,256]{2,1,0:T(8,128)} %param.11) | copy-start | bytes 786436
  126.4 13.1 %copy-start.3 = (f32[2,128,256]{2,1,0:T(8,128)S(1)}, f32[2,128,256]{2,1,0:T(8,128)}, u32[]{:S(2)}) copy-start(f32[2,128,256]{2,1,0:T(8,128)} %param.10) | copy-start | bytes 786436
  131.1 8.4 %collective-permute-start.19 = (bf16[2,128,256]{2,1,0:T(8,128)(2,1)S(1)}, bf16[2,128,256]{2,1,0:T(8,128)(2,1)S(1)}, u32[]{:S(2)}, u32[]{:S(2)}) collective-permute-start(bf16[2,128,256]{2,1,0:T(8,128)(2,1)S(1)} %get-tuple-element.21), channel_id=1, source_target_pairs={{0,1},{1,0},{2,3},{3,2},{4,5},{5,4},{6,7},{7,6},{8,9},{9,8},{10,11... | collective-permute-start | bytes 393224 | tf_op jit(solution)/shard_map/ppermute | solution.py:21

commit v6 on v5

--- a/solution.py
+++ b/solution.py
@@ -35,8 +35,8 @@
     return source ^ 4
 
 
-def opposite(source):
-    return source ^ 8
+def next_pair(source):
+    return source ^ 2
 
 
 def outward(source):
@@ -153,16 +153,16 @@
     half_float = shaped(float32, 2, rows, levels)
 
     def exchange(full):
-        first = across(full, inward, opposite)
+        p1 = across(full, inward, next_pair)
         core = swapped(full, "core", 1)
-        z2 = swapped(full, "z", 2)
-        x2 = swapped(full, "rep", 1)
-        y2 = swapped(full, "y", 2)
-        z1 = swapped(after(full, first, core), "z", 1)
-        x1 = swapped(after(full, first, x2), "x_lo", 1)
-        y1 = swapped(after(full, first, z2), "y", 1)
-        second = across(jnp.where(on_first, first, full), outward, inward)
-        return {1: [core], 5: [z2], 0: [x2], 3: [y2]}, {6: [first, second], 7: [second, first]}, {4: [z1], 8: [x1], 2: [y1]}
+        z1 = swapped(full, "z", 1)
+        p2 = across(jnp.where(on_first, p1, full), outward, inward)
+        x2 = swapped(after(full, p1, core), "rep", 1)
+        x1 = swapped(after(full, p1, z1), "x_lo", 1)
+        p3 = across(jnp.where(on_first, full, p2), next_pair, outward)
+        y2 = swapped(after(full, p2, x2), "y", 2)
+        y1 = swapped(after(full, p2, x1), "y", 1)
+        return {1: [core], 4: [z1], 8: [x1], 0: [x2]}, {5: [p3, p1], 6: [p1, p2], 7: [p2, p3]}, {3: [y2], 2: [y1]}
 
     def call(body, parts, outs, scratch, *operands):
         held = []

time: 141 us -> 161 us (1.14)
  the two profiles are of different devices: /device:TPU:2 before, /device:TPU:64 now
where the time goes in v6:
time: 161 us; the launch traced here: 160 us
  starting transfers between devices  98.5 us (61%)
  waiting for transfers between devices  45.8 us (28%)
  Pallas kernels  8.54 us (5%)
  other arithmetic  3.78 us (2%)
  between operations  2.53 us (2%)
    ppermute x14, starting transfers between devices, swapped(): return lax.ppermute(value, axis, pairs)  61.6 us
    ppermute x14, waiting for transfers between devices, swapped(): return lax.ppermute(value, axis, pairs)  38 us
    ppermute x6, starting transfers between devices, across(): return lax.ppermute(value, ('z', 'core'), pairs)  36.9 us
    pallas_call x6, Pallas kernels, call(): pl.pallas_call(lambda *refs: body(counts, *refs), out_shape=outs, in_spec...  8.54 us
    ppermute x6, waiting for transfers between devices, across(): return lax.ppermute(value, ('z', 'core'), pairs)  7.73 us
  transfers between devices with their start and end apart: 20, of which 10 were waited for; matrix products, arithmetic and copies ran while one was open for 1% of the time, Pallas kernels for 4%

profile of v6, /device:TPU:64, one launch (start us, length us, event | category | flops | bytes accessed | tf_op | source)
XLA Modules:
  0.0 159.8 jit_solution(16693659962308205800)
XLA Ops:
  1.9 4.9 %collective-permute-start = (bf16[2,128,256]{2,1,0:T(8,128)(2,1)S(1)}, bf16[2,128,256]{2,1,0:T(8,128)(2,1)S(1)}, u32[]{:S(2)}, u32[]{:S(2)}) collective-permute-start(bf16[2,128,256]{2,1,0:T(8,128)(2,1)S(1)} %get-tuple-element.33), channel_id=1, source_target_pairs={{0,1},{1,0},{2,3},{3,2},{4,5},{5,4},{6,7},{7,6},{8,9},{9,8},{10,11... | collective-permute-start | bytes 393224 | tf_op jit(solution)/shard_map/ppermute | solution.py:21
  7.8 2.7 %collective-permute-done = bf16[2,128,256]{2,1,0:T(8,128)(2,1)S(1)} collective-permute-done((bf16[2,128,256]{2,1,0:T(8,128)(2,1)S(1)}, bf16[2,128,256]{2,1,0:T(8,128)(2,1)S(1)}, u32[]{:S(2)}, u32[]{:S(2)}) %collective-permute-start) | collective-permute-done | bytes 131104 | tf_op jit(solution)/shard_map/ppermute | solution.py:21
  10.7 9.1 %collective-permute-start.3 = (bf16[2,256,256]{2,1,0:T(8,128)(2,1)S(1)}, bf16[2,256,256]{2,1,0:T(8,128)(2,1)S(1)}, u32[]{:S(2)}, u32[]{:S(2)}) collective-permute-start(bf16[2,256,256]{2,1,0:T(8,128)(2,1)S(1)} %maximum_select_fusion.refs_4_.refs_3_), channel_id=1, source_target_pairs={{0,64},{2,34},{16,80},{18,50},{32,96},{34,2},{48,112},{50,18},{64,... | collective-permute-start | bytes 786440 | tf_op jit(solution)/shard_map/ppermute | solution.py:31
  20.0 1.9 %collective-permute-start.1 = (bf16[2,256,256]{2,1,0:T(8,128)(2,1)S(1)}, bf16[2,256,256]{2,1,0:T(8,128)(2,1)S(1)}, u32[]{:S(2)}, u32[]{:S(2)}) collective-permute-start(bf16[2,256,256]{2,1,0:T(8,128)(2,1)S(1)} %maximum_select_fusion.refs_4_.refs_3_), channel_id=1, source_target_pairs={{0,2},{2,0},{1,3},{3,1},{4,6},{6,4},{5,7},{7,5},{8,10},{10,8},{9,1... | collective-permute-start | bytes 786440 | tf_op jit(solution)/shard_map/ppermute | solution.py:21
  21.9 3.8 %collective-permute-start.2 = (bf16[2,256,256]{2,1,0:T(8,128)(2,1)S(1)}, bf16[2,256,256]{2,1,0:T(8,128)(2,1)S(1)}, u32[]{:S(2)}, u32[]{:S(2)}) collective-permute-start(bf16[2,256,256]{2,1,0:T(8,128)(2,1)S(1)} %maximum_select_fusion.refs_4_.refs_3_), channel_id=1, source_target_pairs={{0,16},{16,0},{32,48},{48,32},{64,80},{80,64},{96,112},{112,96},{1... | collective-permute-start | bytes 786440 | tf_op jit(solution)/shard_map/ppermute | solution.py:21
  25.7 7.6 %collective-permute-done.3.refs_5_ = bf16[2,256,256]{2,1,0:T(8,128)(2,1)S(1)} collective-permute-done((bf16[2,256,256]{2,1,0:T(8,128)(2,1)S(1)}, bf16[2,256,256]{2,1,0:T(8,128)(2,1)S(1)}, u32[]{:S(2)}, u32[]{:S(2)}) %collective-permute-start.3) | collective-permute-done | bytes 262176 | tf_op jit(solution)/shard_map/ppermute | solution.py:31
  33.4 15.9 %collective-permute-start.6 = (bf16[2,256,256]{2,1,0:T(8,128)(2,1)S(1)}, bf16[2,256,256]{2,1,0:T(8,128)(2,1)S(1)}, u32[]{:S(2)}, u32[]{:S(2)}) collective-permute-start(bf16[2,256,256]{2,1,0:T(8,128)(2,1)S(1)} %broadcast_select_fusion.3), channel_id=1, source_target_pairs={{0,192},{2,66},{16,208},{18,82},{32,224},{34,98},{48,240},{50,114}... | collective-permute-start | bytes 786440 | tf_op jit(solution)/shard_map/ppermute | solution.py:31
  51.4 3.4 %collective-permute-start.4 = (bf16[2,256,256]{2,1,0:T(8,128)(2,1)S(1)}, bf16[2,256,256]{2,1,0:T(8,128)(2,1)S(1)}, u32[]{:S(2)}, u32[]{:S(2)}) collective-permute-start(bf16[2,256,256]{2,1,0:T(8,128)(2,1)S(1)} %maximum_select_fusion.refs_4_.refs_3_), channel_id=1, source_target_pairs={{0,256},{256,0},{1,257},{257,1},{2,258},{258,2},{3,259},{259,3},{4... | collective-permute-start | bytes 786440 | tf_op jit(solution)/shard_map/ppermute | solution.py:21
  54.9 4.6 %collective-permute-start.5 = (bf16[2,256,256]{2,1,0:T(8,128)(2,1)S(1)}, bf16[2,256,256]{2,1,0:T(8,128)(2,1)S(1)}, u32[]{:S(2)}, u32[]{:S(2)}) collective-permute-start(bf16[2,256,256]{2,1,0:T(8,128)(2,1)S(1)} %maximum_select_fusion.refs_4_.refs_3_), channel_id=1, source_target_pairs={{0,1},{1,0},{2,3},{3,2},{4,5},{5,4},{6,7},{7,6},{8,9},{9,8},{10,11... | collective-permute-start | bytes 786440 | tf_op jit(solution)/shard_map/ppermute | solution.py:21
  59.7 1.9 %collective-permute-start.7 = (bf16[2,256,256]{2,1,0:T(8,128)(2,1)S(1)}, bf16[2,256,256]{2,1,0:T(8,128)(2,1)S(1)}, u32[]{:S(2)}, u32[]{:S(2)}) collective-permute-start(bf16[2,256,256]{2,1,0:T(8,128)(2,1)S(1)} %broadcast_select_fusion.2), channel_id=1, source_target_pairs={{0,32},{2,194},{16,48},{18,210},{32,0},{34,226},{48,16},{50,242},{... | collective-permute-start | bytes 786440 | tf_op jit(solution)/shard_map/ppermute | solution.py:31
  61.6 3.1 %collective-permute-done.5.refs_8_ = bf16[2,256,256]{2,1,0:T(8,128)(2,1)S(1)} collective-permute-done((bf16[2,256,256]{2,1,0:T(8,128)(2,1)S(1)}, bf16[2,256,256]{2,1,0:T(8,128)(2,1)S(1)}, u32[]{:S(2)}, u32[]{:S(2)}) %collective-permute-start.5) | collective-permute-done | bytes 262176 | tf_op jit(solution)/shard_map/ppermute | solution.py:21
  64.7 5.1 %collective-permute-start.8 = (bf16[2,256,256]{2,1,0:T(8,128)(2,1)S(1)}, bf16[2,256,256]{2,1,0:T(8,128)(2,1)S(1)}, u32[]{:S(2)}, u32[]{:S(2)}) collective-permute-start(bf16[2,256,256]{2,1,0:T(8,128)(2,1)S(1)} %maximum_select_fusion.refs_4_.refs_3_), channel_id=1, source_target_pairs={{0,8},{4,12},{8,0},{12,4},{1,9},{5,13},{9,1},{13,5},{2,10},{6,14},... | collective-permute-start | bytes 786440 | tf_op jit(solution)/shard_map/ppermute | solution.py:21
  69.8 2.6 %collective-permute-start.9 = (bf16[2,256,256]{2,1,0:T(8,128)(2,1)S(1)}, bf16[2,256,256]{2,1,0:T(8,128)(2,1)S(1)}, u32[]{:S(2)}, u32[]{:S(2)}) collective-permute-start(bf16[2,256,256]{2,1,0:T(8,128)(2,1)S(1)} %maximum_select_fusion.refs_4_.refs_3_), channel_id=1, source_target_pairs={{0,4},{4,0},{8,12},{12,8},{1,5},{5,1},{9,13},{13,9},{2,6},{6,2},{1... | collective-permute-start | bytes 786440 | tf_op jit(solution)/shard_map/ppermute | solution.py:21
  72.5 1.8 %shard_map.113.refs_3_ = f32[2,256,256]{2,1,0:T(8,128)S(1)} custom-call(s32[11]{0:T(128)S(1)} %pad_add_fusion.refs_0_, f32[3,9]{1,0:T(4,128)S(1)} %pad_maximum_fusion.1.refs_1_, bf16[12,256,256]{2,1,0:T(8,128)(2,1)S(1)} %copy-done, bf16[2,256,256]{2,1,0:T(8,128)(2,1)S(1)} %copy-done.1, bf16[2,256,256]{2,1,0:T(8,128)(2,1)S(1)} %maximum_select_fusion.refs_4_.refs_3_, ...), custom_call_target="tpu_custom_call" | custom-call | flops 536870912 | bytes 3670168 | tf_op jit(solution)/shard_map/pallas_call | solution.py:178
  75.7 2.4 %collective-permute-done.9.refs_6_ = bf16[2,256,256]{2,1,0:T(8,128)(2,1)S(1)} collective-permute-done((bf16[2,256,256]{2,1,0:T(8,128)(2,1)S(1)}, bf16[2,256,256]{2,1,0:T(8,128)(2,1)S(1)}, u32[]{:S(2)}, u32[]{:S(2)}) %collective-permute-start.9) | collective-permute-done | bytes 262176 | tf_op jit(solution)/shard_map/ppermute | solution.py:21
  79.2 2.8 %collective-permute-start.12 = (bf16[2,256,256]{2,1,0:T(8,128)(2,1)S(1)}, bf16[2,256,256]{2,1,0:T(8,128)(2,1)S(1)}, u32[]{:S(2)}, u32[]{:S(2)}) collective-permute-start(bf16[2,256,256]{2,1,0:T(8,128)(2,1)S(1)} %get-tuple-element.23.refs_4_), channel_id=1, source_target_pairs={{0,64},{2,34},{16,80},{18,50},{32,96},{34,2},{48,112},{50,18},{64,... | collective-permute-start | bytes 786440 | tf_op jit(solution)/shard_map/ppermute | solution.py:31
  82.0 1.9 %collective-permute-start.10 = (bf16[2,256,256]{2,1,0:T(8,128)(2,1)S(1)}, bf16[2,256,256]{2,1,0:T(8,128)(2,1)S(1)}, u32[]{:S(2)}, u32[]{:S(2)}) collective-permute-start(bf16[2,256,256]{2,1,0:T(8,128)(2,1)S(1)} %get-tuple-element.23.refs_4_), channel_id=1, source_target_pairs={{0,2},{2,0},{1,3},{3,1},{4,6},{6,4},{5,7},{7,5},{8,10},{10,8},{9,1... | collective-permute-start | bytes 786440 | tf_op jit(solution)/shard_map/ppermute | solution.py:21
  84.0 12.0 %collective-permute-start.11 = (bf16[2,256,256]{2,1,0:T(8,128)(2,1)S(1)}, bf16[2,256,256]{2,1,0:T(8,128)(2,1)S(1)}, u32[]{:S(2)}, u32[]{:S(2)}) collective-permute-start(bf16[2,256,256]{2,1,0:T(8,128)(2,1)S(1)} %get-tuple-element.23.refs_4_), channel_id=1, source_target_pairs={{0,16},{16,0},{32,48},{48,32},{64,80},{80,64},{96,112},{112,96},{1... | collective-permute-start | bytes 786440 | tf_op jit(solution)/shard_map/ppermute | solution.py:21
  96.1 5.3 %collective-permute-start.15 = (bf16[2,256,256]{2,1,0:T(8,128)(2,1)S(1)}, bf16[2,256,256]{2,1,0:T(8,128)(2,1)S(1)}, u32[]{:S(2)}, u32[]{:S(2)}) collective-permute-start(bf16[2,256,256]{2,1,0:T(8,128)(2,1)S(1)} %broadcast_select_fusion.1), channel_id=1, source_target_pairs={{0,192},{2,66},{16,208},{18,82},{32,224},{34,98},{48,240},{50,114}... | collective-permute-start | bytes 786440 | tf_op jit(solution)/shard_map/ppermute | solution.py:31
  101.4 9.5 %collective-permute-done.11.refs_7_ = bf16[2,256,256]{2,1,0:T(8,128)(2,1)S(1)} collective-permute-done((bf16[2,256,256]{2,1,0:T(8,128)(2,1)S(1)}, bf16[2,256,256]{2,1,0:T(8,128)(2,1)S(1)}, u32[]{:S(2)}, u32[]{:S(2)}) %collective-permute-start.11) | collective-permute-done | bytes 262176 | tf_op jit(solution)/shard_map/ppermute | solution.py:21
  110.9 2.8 %collective-permute-start.13 = (bf16[2,256,256]{2,1,0:T(8,128)(2,1)S(1)}, bf16[2,256,256]{2,1,0:T(8,128)(2,1)S(1)}, u32[]{:S(2)}, u32[]{:S(2)}) collective-permute-start(bf16[2,256,256]{2,1,0:T(8,128)(2,1)S(1)} %get-tuple-element.23.refs_4_), channel_id=1, source_target_pairs={{0,256},{256,0},{1,257},{257,1},{2,258},{258,2},{3,259},{259,3},{4... | collective-permute-start | bytes 786440 | tf_op jit(solution)/shard_map/ppermute | solution.py:21
  113.8 10.7 %collective-permute-start.14 = (bf16[2,256,256]{2,1,0:T(8,128)(2,1)S(1)}, bf16[2,256,256]{2,1,0:T(8,128)(2,1)S(1)}, u32[]{:S(2)}, u32[]{:S(2)}) collective-permute-start(bf16[2,256,256]{2,1,0:T(8,128)(2,1)S(1)} %get-tuple-element.23.refs_4_), channel_id=1, source_target_pairs={{0,1},{1,0},{2,3},{3,2},{4,5},{5,4},{6,7},{7,6},{8,9},{9,8},{10,11... | collective-permute-start | bytes 786440 | tf_op jit(solution)/shard_map/ppermute | solution.py:21
  124.6 1.9 %collective-permute-start.16 = (bf16[2,256,256]{2,1,0:T(8,128)(2,1)S(1)}, bf16[2,256,256]{2,1,0:T(8,128)(2,1)S(1)}, u32[]{:S(2)}, u32[]{:S(2)}) collective-permute-start(bf16[2,256,256]{2,1,0:T(8,128)(2,1)S(1)} %broadcast_select_fusion), channel_id=1, source_target_pairs={{0,32},{2,194},{16,48},{18,210},{32,0},{34,226},{48,16},{50,242},{... | collective-permute-start | bytes 786440 | tf_op jit(solution)/shard_map/ppermute | solution.py:31
  126.5 8.0 %collective-permute-done.14.refs_9_ = bf16[2,256,256]{2,1,0:T(8,128)(2,1)S(1)} collective-permute-done((bf16[2,256,256]{2,1,0:T(8,128)(2,1)S(1)}, bf16[2,256,256]{2,1,0:T(8,128)(2,1)S(1)}, u32[]{:S(2)}, u32[]{:S(2)}) %collective-permute-start.14) | collective-permute-done | bytes 262176 | tf_op jit(solution)/shard_map/ppermute | solution.py:21
  134.5 3.3 %collective-permute-start.17 = (bf16[2,256,256]{2,1,0:T(8,128)(2,1)S(1)}, bf16[2,256,256]{2,1,0:T(8,128)(2,1)S(1)}, u32[]{:S(2)}, u32[]{:S(2)}) collective-permute-start(bf16[2,256,256]{2,1,0:T(8,128)(2,1)S(1)} %get-tuple-element.23.refs_4_), channel_id=1, source_target_pairs={{0,8},{4,12},{8,0},{12,4},{1,9},{5,13},{9,1},{13,5},{2,10},{6,14},... | collective-permute-start | bytes 786440 | tf_op jit(solution)/shard_map/ppermute | solution.py:21
  137.7 2.4 %collective-permute-start.18 = (bf16[2,256,256]{2,1,0:T(8,128)(2,1)S(1)}, bf16[2,256,256]{2,1,0:T(8,128)(2,1)S(1)}, u32[]{:S(2)}, u32[]{:S(2)}) collective-permute-start(bf16[2,256,256]{2,1,0:T(8,128)(2,1)S(1)} %get-tuple-element.23.refs_4_), channel_id=1, source_target_pairs={{0,4},{4,0},{8,12},{12,8},{1,5},{5,1},{9,13},{13,9},{2,6},{6,2},{1... | collective-permute-start | bytes 786440 | tf_op jit(solution)/shard_map/ppermute | solution.py:21
  140.2 1.8 %shard_map.116.refs_3_ = f32[2,256,256]{2,1,0:T(8,128)S(1)} custom-call(s32[11]{0:T(128)S(1)} %pad_add_fusion.refs_0_, f32[3,9]{1,0:T(4,128)S(1)} %pad_maximum_fusion.1.refs_1_, bf16[12,256,256]{2,1,0:T(8,128)(2,1)S(1)} %copy-done, bf16[2,256,256]{2,1,0:T(8,128)(2,1)S(1)} %copy-done.1, bf16[2,256,256]{2,1,0:T(8,128)(2,1)S(1)} %get-tuple-element.23.refs_4_, ...), custom_call_target="tpu_custom_call" | custom-call | flops 536870912 | bytes 4194456 | tf_op jit(solution)/shard_map/pallas_call | solution.py:178
  142.0 1.3 shard_map.117.refs_3_
  143.4 3.7 %collective-permute-done.17.refs_4_ = bf16[2,256,256]{2,1,0:T(8,128)(2,1)S(1)} collective-permute-done((bf16[2,256,256]{2,1,0:T(8,128)(2,1)S(1)}, bf16[2,256,256]{2,1,0:T(8,128)(2,1)S(1)}, u32[]{:S(2)}, u32[]{:S(2)}) %collective-permute-start.17) | collective-permute-done | bytes 262176 | tf_op jit(solution)/shard_map/ppermute | solution.py:21
  147.1 2.2 %collective-permute-done.18.refs_5_ = bf16[2,256,256]{2,1,0:T(8,128)(2,1)S(1)} collective-permute-done((bf16[2,256,256]{2,1,0:T(8,128)(2,1)S(1)}, bf16[2,256,256]{2,1,0:T(8,128)(2,1)S(1)}, u32[]{:S(2)}, u32[]{:S(2)}) %collective-permute-start.18) | collective-permute-done | bytes 262176 | tf_op jit(solution)/shard_map/ppermute | solution.py:21
  150.5 1.9 %collective-permute-start.19 = (bf16[2,128,256]{2,1,0:T(8,128)(2,1)S(1)}, bf16[2,128,256]{2,1,0:T(8,128)(2,1)S(1)}, u32[]{:S(2)}, u32[]{:S(2)}) collective-permute-start(bf16[2,128,256]{2,1,0:T(8,128)(2,1)S(1)} %get-tuple-element.25), channel_id=1, source_target_pairs={{0,1},{1,0},{2,3},{3,2},{4,5},{5,4},{6,7},{7,6},{8,9},{9,8},{10,11... | collective-permute-start | bytes 393224 | tf_op jit(solution)/shard_map/ppermute | solution.py:21
  152.4 6.4 %collective-permute-done.19 = bf16[2,128,256]{2,1,0:T(8,128)(2,1)S(1)} collective-permute-done((bf16[2,128,256]{2,1,0:T(8,128)(2,1)S(1)}, bf16[2,128,256]{2,1,0:T(8,128)(2,1)S(1)}, u32[]{:S(2)}, u32[]{:S(2)}) %collective-permute-start.19) | collective-permute-done | bytes 131104 | tf_op jit(solution)/shard_map/ppermute | solution.py:21
  (54 shorter events, 8.2 us)
Async XLA Ops:
  0.6 19.1 %copy-start.7 = (f32[12]{0:T(128)S(1)}, f32[12]{0:T(128)}, u32[]{:S(2)}) copy-start(f32[12]{0:T(128)} %param.14) | copy-start | bytes 148
  0.6 19.1 %copy-start.4 = (s32[2,12]{1,0:T(2,128)S(1)}, s32[2,12]{1,0:T(2,128)}, u32[]{:S(2)}) copy-start(s32[2,12]{1,0:T(2,128)} %param.17) | copy-start | bytes 292
  0.7 19.3 %copy-start.5 = (f32[12]{0:T(128)S(1)}, f32[12]{0:T(128)}, u32[]{:S(2)}) copy-start(f32[12]{0:T(128)} %param.16) | copy-start | bytes 148
  0.7 19.3 %copy-start.6 = (f32[12]{0:T(128)S(1)}, f32[12]{0:T(128)}, u32[]{:S(2)}) copy-start(f32[12]{0:T(128)} %param.15) | copy-start | bytes 148
  0.7 71.8 %copy-start = (bf16[12,256,256]{2,1,0:T(8,128)(2,1)S(1)}, bf16[12,256,256]{2,1,0:T(8,128)(2,1)}, u32[]{:S(2)}) copy-start(bf16[12,256,256]{2,1,0:T(8,128)(2,1)} %refs_2_.11) | copy-start | bytes 4718596
  0.7 71.8 %copy-start.1 = (bf16[2,256,256]{2,1,0:T(8,128)(2,1)S(1)}, bf16[2,256,256]{2,1,0:T(8,128)(2,1)}, u32[]{:S(2)}) copy-start(bf16[2,256,256]{2,1,0:T(8,128)(2,1)} %refs_3_.3) | copy-start | bytes 786436
  1.9 8.6 %collective-permute-start = (bf16[2,128,256]{2,1,0:T(8,128)(2,1)S(1)}, bf16[2,128,256]{2,1,0:T(8,128)(2,1)S(1)}, u32[]{:S(2)}, u32[]{:S(2)}) collective-permute-start(bf16[2,128,256]{2,1,0:T(8,128)(2,1)S(1)} %get-tuple-element.33), channel_id=1, source_target_pairs={{0,1},{1,0},{2,3},{3,2},{4,5},{5,4},{6,7},{7,6},{8,9},{9,8},{10,11... | collective-permute-start | bytes 393224 | tf_op jit(solution)/shard_map/ppermute | solution.py:21
  10.7 22.6 %collective-permute-start.3 = (bf16[2,256,256]{2,1,0:T(8,128)(2,1)S(1)}, bf16[2,256,256]{2,1,0:T(8,128)(2,1)S(1)}, u32[]{:S(2)}, u32[]{:S(2)}) collective-permute-start(bf16[2,256,256]{2,1,0:T(8,128)(2,1)S(1)} %maximum_select_fusion.refs_4_.refs_3_), channel_id=1, source_target_pairs={{0,64},{2,34},{16,80},{18,50},{32,96},{34,2},{48,112},{50,18},{64,... | collective-permute-start | bytes 786440 | tf_op jit(solution)/shard_map/ppermute | solution.py:31
  20.0 34.9 %collective-permute-start.1 = (bf16[2,256,256]{2,1,0:T(8,128)(2,1)S(1)}, bf16[2,256,256]{2,1,0:T(8,128)(2,1)S(1)}, u32[]{:S(2)}, u32[]{:S(2)}) collective-permute-start(bf16[2,256,256]{2,1,0:T(8,128)(2,1)S(1)} %maximum_select_fusion.refs_4_.refs_3_), channel_id=1, source_target_pairs={{0,2},{2,0},{1,3},{3,1},{4,6},{6,4},{5,7},{7,5},{8,10},{10,8},{9,1... | collective-permute-start | bytes 786440 | tf_op jit(solution)/shard_map/ppermute | solution.py:21
  21.9 29.5 %collective-permute-start.2 = (bf16[2,256,256]{2,1,0:T(8,128)(2,1)S(1)}, bf16[2,256,256]{2,1,0:T(8,128)(2,1)S(1)}, u32[]{:S(2)}, u32[]{:S(2)}) collective-permute-start(bf16[2,256,256]{2,1,0:T(8,128)(2,1)S(1)} %maximum_select_fusion.refs_4_.refs_3_), channel_id=1, source_target_pairs={{0,16},{16,0},{32,48},{48,32},{64,80},{80,64},{96,112},{112,96},{1... | collective-permute-start | bytes 786440 | tf_op jit(solution)/shard_map/ppermute | solution.py:21
  33.4 26.3 %collective-permute-start.6 = (bf16[2,256,256]{2,1,0:T(8,128)(2,1)S(1)}, bf16[2,256,256]{2,1,0:T(8,128)(2,1)S(1)}, u32[]{:S(2)}, u32[]{:S(2)}) collective-permute-start(bf16[2,256,256]{2,1,0:T(8,128)(2,1)S(1)} %broadcast_select_fusion.3), channel_id=1, source_target_pairs={{0,192},{2,66},{16,208},{18,82},{32,224},{34,98},{48,240},{50,114}... | collective-permute-start | bytes 786440 | tf_op jit(solution)/shard_map/ppermute | solution.py:31
  51.4 18.4 %collective-permute-start.4 = (bf16[2,256,256]{2,1,0:T(8,128)(2,1)S(1)}, bf16[2,256,256]{2,1,0:T(8,128)(2,1)S(1)}, u32[]{:S(2)}, u32[]{:S(2)}) collective-permute-start(bf16[2,256,256]{2,1,0:T(8,128)(2,1)S(1)} %maximum_select_fusion.refs_4_.refs_3_), channel_id=1, source_target_pairs={{0,256},{256,0},{1,257},{257,1},{2,258},{258,2},{3,259},{259,3},{4... | collective-permute-start | bytes 786440 | tf_op jit(solution)/shard_map/ppermute | solution.py:21
  54.9 9.9 %collective-permute-start.5 = (bf16[2,256,256]{2,1,0:T(8,128)(2,1)S(1)}, bf16[2,256,256]{2,1,0:T(8,128)(2,1)S(1)}, u32[]{:S(2)}, u32[]{:S(2)}) collective-permute-start(bf16[2,256,256]{2,1,0:T(8,128)(2,1)S(1)} %maximum_select_fusion.refs_4_.refs_3_), channel_id=1, source_target_pairs={{0,1},{1,0},{2,3},{3,2},{4,5},{5,4},{6,7},{7,6},{8,9},{9,8},{10,11... | collective-permute-start | bytes 786440 | tf_op jit(solution)/shard_map/ppermute | solution.py:21
  59.7 14.7 %collective-permute-start.7 = (bf16[2,256,256]{2,1,0:T(8,128)(2,1)S(1)}, bf16[2,256,256]{2,1,0:T(8,128)(2,1)S(1)}, u32[]{:S(2)}, u32[]{:S(2)}) collective-permute-start(bf16[2,256,256]{2,1,0:T(8,128)(2,1)S(1)} %broadcast_select_fusion.2), channel_id=1, source_target_pairs={{0,32},{2,194},{16,48},{18,210},{32,0},{34,226},{48,16},{50,242},{... | collective-permute-start | bytes 786440 | tf_op jit(solution)/shard_map/ppermute | solution.py:31
  64.7 11.0 %collective-permute-start.8 = (bf16[2,256,256]{2,1,0:T(8,128)(2,1)S(1)}, bf16[2,256,256]{2,1,0:T(8,128)(2,1)S(1)}, u32[]{:S(2)}, u32[]{:S(2)}) collective-permute-start(bf16[2,256,256]{2,1,0:T(8,128)(2,1)S(1)} %maximum_select_fusion.refs_4_.refs_3_), channel_id=1, source_target_pairs={{0,8},{4,12},{8,0},{12,4},{1,9},{5,13},{9,1},{13,5},{2,10},{6,14},... | collective-permute-start | bytes 786440 | tf_op jit(solution)/shard_map/ppermute | solution.py:21
  69.8 8.3 %collective-permute-start.9 = (bf16[2,256,256]{2,1,0:T(8,128)(2,1)S(1)}, bf16[2,256,256]{2,1,0:T(8,128)(2,1)S(1)}, u32[]{:S(2)}, u32[]{:S(2)}) collective-permute-start(bf16[2,256,256]{2,1,0:T(8,128)(2,1)S(1)} %maximum_select_fusion.refs_4_.refs_3_), channel_id=1, source_target_pairs={{0,4},{4,0},{8,12},{12,8},{1,5},{5,1},{9,13},{13,9},{2,6},{6,2},{1... | collective-permute-start | bytes 786440 | tf_op jit(solution)/shard_map/ppermute | solution.py:21
  79.2 16.8 %collective-permute-start.12 = (bf16[2,256,256]{2,1,0:T(8,128)(2,1)S(1)}, bf16[2,256,256]{2,1,0:T(8,128)(2,1)S(1)}, u32[]{:S(2)}, u32[]{:S(2)}) collective-permute-start(bf16[2,256,256]{2,1,0:T(8,128)(2,1)S(1)} %get-tuple-element.23.refs_4_), channel_id=1, source_target_pairs={{0,64},{2,34},{16,80},{18,50},{32,96},{34,2},{48,112},{50,18},{64,... | collective-permute-start | bytes 786440 | tf_op jit(solution)/shard_map/ppermute | solution.py:31
  82.0 31.7 %collective-permute-start.10 = (bf16[2,256,256]{2,1,0:T(8,128)(2,1)S(1)}, bf16[2,256,256]{2,1,0:T(8,128)(2,1)S(1)}, u32[]{:S(2)}, u32[]{:S(2)}) collective-permute-start(bf16[2,256,256]{2,1,0:T(8,128)(2,1)S(1)} %get-tuple-element.23.refs_4_), channel_id=1, source_target_pairs={{0,2},{2,0},{1,3},{3,1},{4,6},{6,4},{5,7},{7,5},{8,10},{10,8},{9,1... | collective-permute-start | bytes 786440 | tf_op jit(solution)/shard_map/ppermute | solution.py:21
  84.0 27.0 %collective-permute-start.11 = (bf16[2,256,256]{2,1,0:T(8,128)(2,1)S(1)}, bf16[2,256,256]{2,1,0:T(8,128)(2,1)S(1)}, u32[]{:S(2)}, u32[]{:S(2)}) collective-permute-start(bf16[2,256,256]{2,1,0:T(8,128)(2,1)S(1)} %get-tuple-element.23.refs_4_), channel_id=1, source_target_pairs={{0,16},{16,0},{32,48},{48,32},{64,80},{80,64},{96,112},{112,96},{1... | collective-permute-start | bytes 786440 | tf_op jit(solution)/shard_map/ppermute | solution.py:21
  96.1 28.4 %collective-permute-start.15 = (bf16[2,256,256]{2,1,0:T(8,128)(2,1)S(1)}, bf16[2,256,256]{2,1,0:T(8,128)(2,1)S(1)}, u32[]{:S(2)}, u32[]{:S(2)}) collective-permute-start(bf16[2,256,256]{2,1,0:T(8,128)(2,1)S(1)} %broadcast_select_fusion.1), channel_id=1, source_target_pairs={{0,192},{2,66},{16,208},{18,82},{32,224},{34,98},{48,240},{50,114}... | collective-permute-start | bytes 786440 | tf_op jit(solution)/shard_map/ppermute | solution.py:31
  110.9 26.8 %collective-permute-start.13 = (bf16[2,256,256]{2,1,0:T(8,128)(2,1)S(1)}, bf16[2,256,256]{2,1,0:T(8,128)(2,1)S(1)}, u32[]{:S(2)}, u32[]{:S(2)}) collective-permute-start(bf16[2,256,256]{2,1,0:T(8,128)(2,1)S(1)} %get-tuple-element.23.refs_4_), channel_id=1, source_target_pairs={{0,256},{256,0},{1,257},{257,1},{2,258},{258,2},{3,259},{259,3},{4... | collective-permute-start | bytes 786440 | tf_op jit(solution)/shard_map/ppermute | solution.py:21
  113.8 20.7 %collective-permute-start.14 = (bf16[2,256,256]{2,1,0:T(8,128)(2,1)S(1)}, bf16[2,256,256]{2,1,0:T(8,128)(2,1)S(1)}, u32[]{:S(2)}, u32[]{:S(2)}) collective-permute-start(bf16[2,256,256]{2,1,0:T(8,128)(2,1)S(1)} %get-tuple-element.23.refs_4_), channel_id=1, source_target_pairs={{0,1},{1,0},{2,3},{3,2},{4,5},{5,4},{6,7},{7,6},{8,9},{9,8},{10,11... | collective-permute-start | bytes 786440 | tf_op jit(solution)/shard_map/ppermute | solution.py:21
  124.6 17.5 %collective-permute-start.16 = (bf16[2,256,256]{2,1,0:T(8,128)(2,1)S(1)}, bf16[2,256,256]{2,1,0:T(8,128)(2,1)S(1)}, u32[]{:S(2)}, u32[]{:S(2)}) collective-permute-start(bf16[2,256,256]{2,1,0:T(8,128)(2,1)S(1)} %broadcast_select_fusion), channel_id=1, source_target_pairs={{0,32},{2,194},{16,48},{18,210},{32,0},{34,226},{48,16},{50,242},{... | collective-permute-start | bytes 786440 | tf_op jit(solution)/shard_map/ppermute | solution.py:31
  134.5 12.6 %collective-permute-start.17 = (bf16[2,256,256]{2,1,0:T(8,128)(2,1)S(1)}, bf16[2,256,256]{2,1,0:T(8,128)(2,1)S(1)}, u32[]{:S(2)}, u32[]{:S(2)}) collective-permute-start(bf16[2,256,256]{2,1,0:T(8,128)(2,1)S(1)} %get-tuple-element.23.refs_4_), channel_id=1, source_target_pairs={{0,8},{4,12},{8,0},{12,4},{1,9},{5,13},{9,1},{13,5},{2,10},{6,14},... | collective-permute-start | bytes 786440 | tf_op jit(solution)/shard_map/ppermute | solution.py:21
  137.7 11.6 %collective-permute-start.18 = (bf16[2,256,256]{2,1,0:T(8,128)(2,1)S(1)}, bf16[2,256,256]{2,1,0:T(8,128)(2,1)S(1)}, u32[]{:S(2)}, u32[]{:S(2)}) collective-permute-start(bf16[2,256,256]{2,1,0:T(8,128)(2,1)S(1)} %get-tuple-element.23.refs_4_), channel_id=1, source_target_pairs={{0,4},{4,0},{8,12},{12,8},{1,5},{5,1},{9,13},{13,9},{2,6},{6,2},{1... | collective-permute-start | bytes 786440 | tf_op jit(solution)/shard_map/ppermute | solution.py:21
  143.4 15.5 %copy-start.2 = (f32[2,128,256]{2,1,0:T(8,128)S(1)}, f32[2,128,256]{2,1,0:T(8,128)}, u32[]{:S(2)}) copy-start(f32[2,128,256]{2,1,0:T(8,128)} %param.11) | copy-start | bytes 786436
  143.4 15.5 %copy-start.3 = (f32[2,128,256]{2,1,0:T(8,128)S(1)}, f32[2,128,256]{2,1,0:T(8,128)}, u32[]{:S(2)}) copy-start(f32[2,128,256]{2,1,0:T(8,128)} %param.10) | copy-start | bytes 786436
  150.5 8.4 %collective-permute-start.19 = (bf16[2,128,256]{2,1,0:T(8,128)(2,1)S(1)}, bf16[2,128,256]{2,1,0:T(8,128)(2,1)S(1)}, u32[]{:S(2)}, u32[]{:S(2)}) collective-permute-start(bf16[2,128,256]{2,1,0:T(8,128)(2,1)S(1)} %get-tuple-element.25), channel_id=1, source_target_pairs={{0,1},{1,0},{2,3},{3,2},{4,5},{5,4},{6,7},{7,6},{8,9},{9,8},{10,11... | collective-permute-start | bytes 393224 | tf_op jit(solution)/shard_map/ppermute | solution.py:21

commit v7 on v5

--- a/solution.py
+++ b/solution.py
@@ -33,10 +33,6 @@
 
 def inward(source):
     return source ^ 4
-
-
-def opposite(source):
-    return source ^ 8
 
 
 def outward(source):
@@ -146,23 +142,23 @@
     keeps = jnp.where(jnp.arange(bit_count) < 2, keep, 0.0)
     coef = jnp.stack([weight_a, weight_b, keeps]).astype(float32)
 
-    on_first = lax.axis_index("core") == 0
     whole = shaped(bfloat16, 2, levels, levels)
     slope = shaped(float32, 2, levels, levels)
     half = shaped(bfloat16, 2, rows, levels)
     half_float = shaped(float32, 2, rows, levels)
 
     def exchange(full):
-        first = across(full, inward, opposite)
+        first = across(full, inward, outward)
+        own = across(full, None, inward)
         core = swapped(full, "core", 1)
         z2 = swapped(full, "z", 2)
-        x2 = swapped(full, "rep", 1)
-        y2 = swapped(full, "y", 2)
+        second = across(first, outward, inward)
         z1 = swapped(after(full, first, core), "z", 1)
-        x1 = swapped(after(full, first, x2), "x_lo", 1)
-        y1 = swapped(after(full, first, z2), "y", 1)
-        second = across(jnp.where(on_first, first, full), outward, inward)
-        return {1: [core], 5: [z2], 0: [x2], 3: [y2]}, {6: [first, second], 7: [second, first]}, {4: [z1], 8: [x1], 2: [y1]}
+        x2 = swapped(after(full, first, core), "rep", 1)
+        x1 = swapped(after(full, first, own), "x_lo", 1)
+        y2 = swapped(after(full, first, own), "y", 2)
+        y1 = swapped(after(full, first, z2, z1), "y", 1)
+        return {1: [core], 5: [z2]}, {6: [first, own], 7: [second], 4: [z1]}, {0: [x2], 8: [x1], 3: [y2], 2: [y1]}
 
     def call(body, parts, outs, scratch, *operands):
         held = []

time: 141 us -> 158 us (1.12)
  the two profiles are of different devices: /device:TPU:2 before, /device:TPU:1 now
where the time goes in v7:
time: 158 us; the launch traced here: 157 us
  starting transfers between devices  112 us (71%)
  waiting for transfers between devices  30.7 us (19%)
  Pallas kernels  8.48 us (5%)
  other arithmetic  3.67 us (2%)
  between operations  2.45 us (2%)
    ppermute x16, starting transfers between devices, swapped(): return lax.ppermute(value, axis, pairs)  84.1 us
    ppermute x6, starting transfers between devices, across(): return lax.ppermute(value, ('z', 'core'), pairs)  27.4 us
    ppermute x16, waiting for transfers between devices, swapped(): return lax.ppermute(value, axis, pairs)  18.4 us
    ppermute x6, waiting for transfers between devices, across(): return lax.ppermute(value, ('z', 'core'), pairs)  12.3 us
    pallas_call x6, Pallas kernels, call(): pl.pallas_call(lambda *refs: body(counts, *refs), out_shape=outs, in_spec...  8.48 us
  transfers between devices with their start and end apart: 22, of which 6 were waited for; matrix products, arithmetic and copies ran while one was open for 1% of the time, Pallas kernels for 3%

profile of v7, /device:TPU:1, one launch (start us, length us, event | category | flops | bytes accessed | tf_op | source)
XLA Modules:
  0.0 157.5 jit_solution(18112452219585194621)
XLA Ops:
  1.9 5.5 %collective-permute-start = (bf16[2,128,256]{2,1,0:T(8,128)(2,1)S(1)}, bf16[2,128,256]{2,1,0:T(8,128)(2,1)S(1)}, u32[]{:S(2)}, u32[]{:S(2)}) collective-permute-start(bf16[2,128,256]{2,1,0:T(8,128)(2,1)S(1)} %get-tuple-element.29), channel_id=1, source_target_pairs={{0,1},{1,0},{2,3},{3,2},{4,5},{5,4},{6,7},{7,6},{8,9},{9,8},{10,11... | collective-permute-start | bytes 393224 | tf_op jit(solution)/shard_map/ppermute | solution.py:21
  8.4 1.4 collective-permute-done
  9.9 9.3 %collective-permute-start.1 = (bf16[2,256,256]{2,1,0:T(8,128)(2,1)S(1)}, bf16[2,256,256]{2,1,0:T(8,128)(2,1)S(1)}, u32[]{:S(2)}, u32[]{:S(2)}) collective-permute-start(bf16[2,256,256]{2,1,0:T(8,128)(2,1)S(1)} %maximum_select_fusion.refs_4_.refs_3_), channel_id=1, source_target_pairs={{0,2},{2,0},{1,3},{3,1},{4,6},{6,4},{5,7},{7,5},{8,10},{10,8},{9,1... | collective-permute-start | bytes 786440 | tf_op jit(solution)/shard_map/ppermute | solution.py:21
  19.2 7.4 %collective-permute-start.3 = (bf16[2,256,256]{2,1,0:T(8,128)(2,1)S(1)}, bf16[2,256,256]{2,1,0:T(8,128)(2,1)S(1)}, u32[]{:S(2)}, u32[]{:S(2)}) collective-permute-start(bf16[2,256,256]{2,1,0:T(8,128)(2,1)S(1)} %maximum_select_fusion.refs_4_.refs_3_), channel_id=1, source_target_pairs={{0,64},{2,194},{16,80},{18,210},{32,96},{34,226},{48,112},{50,242}... | collective-permute-start | bytes 786440 | tf_op jit(solution)/shard_map/ppermute | solution.py:31
  26.7 3.1 %collective-permute-start.2 = (bf16[2,256,256]{2,1,0:T(8,128)(2,1)S(1)}, bf16[2,256,256]{2,1,0:T(8,128)(2,1)S(1)}, u32[]{:S(2)}, u32[]{:S(2)}) collective-permute-start(bf16[2,256,256]{2,1,0:T(8,128)(2,1)S(1)} %maximum_select_fusion.refs_4_.refs_3_), channel_id=1, source_target_pairs={{0,32},{16,48},{32,0},{48,16},{64,96},{80,112},{96,64},{112,80},{1... | collective-permute-start | bytes 786440 | tf_op jit(solution)/shard_map/ppermute | solution.py:21
  29.8 5.2 %collective-permute-start.4 = (bf16[2,256,256]{2,1,0:T(8,128)(2,1)S(1)}, bf16[2,256,256]{2,1,0:T(8,128)(2,1)S(1)}, u32[]{:S(2)}, u32[]{:S(2)}) collective-permute-start(bf16[2,256,256]{2,1,0:T(8,128)(2,1)S(1)} %maximum_select_fusion.refs_4_.refs_3_), channel_id=1, source_target_pairs={{2,66},{18,82},{34,98},{50,114},{66,2},{82,18},{98,34},{114,50},{1... | collective-permute-start | bytes 786440 | tf_op jit(solution)/shard_map/ppermute | solution.py:31
  35.1 18.9 %collective-permute-start.6 = (bf16[2,256,256]{2,1,0:T(8,128)(2,1)S(1)}, bf16[2,256,256]{2,1,0:T(8,128)(2,1)S(1)}, u32[]{:S(2)}, u32[]{:S(2)}) collective-permute-start(bf16[2,256,256]{2,1,0:T(8,128)(2,1)S(1)} %maximum_select_fusion.refs_4_.refs_3_), channel_id=1, source_target_pairs={{0,16},{16,0},{32,48},{48,32},{64,80},{80,64},{96,112},{112,96},{1... | collective-permute-start | bytes 786440 | tf_op jit(solution)/shard_map/ppermute | solution.py:21
  56.0 5.7 %collective-permute-start.5 = (bf16[2,256,256]{2,1,0:T(8,128)(2,1)S(1)}, bf16[2,256,256]{2,1,0:T(8,128)(2,1)S(1)}, u32[]{:S(2)}, u32[]{:S(2)}) collective-permute-start(bf16[2,256,256]{2,1,0:T(8,128)(2,1)S(1)} %collective-permute-done.3.refs_4_), channel_id=1, source_target_pairs={{0,192},{2,66},{16,208},{18,82},{32,224},{34,98},{48,240},{50,114}... | collective-permute-start | bytes 786440 | tf_op jit(solution)/shard_map/ppermute | solution.py:31
  61.8 4.2 %collective-permute-start.7 = (bf16[2,256,256]{2,1,0:T(8,128)(2,1)S(1)}, bf16[2,256,256]{2,1,0:T(8,128)(2,1)S(1)}, u32[]{:S(2)}, u32[]{:S(2)}) collective-permute-start(bf16[2,256,256]{2,1,0:T(8,128)(2,1)S(1)} %maximum_select_fusion.refs_4_.refs_3_), channel_id=1, source_target_pairs={{0,1},{1,0},{2,3},{3,2},{4,5},{5,4},{6,7},{7,6},{8,9},{9,8},{10,11... | collective-permute-start | bytes 786440 | tf_op jit(solution)/shard_map/ppermute | solution.py:21
  66.0 2.2 %collective-permute-start.8 = (bf16[2,256,256]{2,1,0:T(8,128)(2,1)S(1)}, bf16[2,256,256]{2,1,0:T(8,128)(2,1)S(1)}, u32[]{:S(2)}, u32[]{:S(2)}) collective-permute-start(bf16[2,256,256]{2,1,0:T(8,128)(2,1)S(1)} %maximum_select_fusion.refs_4_.refs_3_), channel_id=1, source_target_pairs={{0,256},{256,0},{1,257},{257,1},{2,258},{258,2},{3,259},{259,3},{4... | collective-permute-start | bytes 786440 | tf_op jit(solution)/shard_map/ppermute | solution.py:21
  68.3 4.8 %collective-permute-start.9 = (bf16[2,256,256]{2,1,0:T(8,128)(2,1)S(1)}, bf16[2,256,256]{2,1,0:T(8,128)(2,1)S(1)}, u32[]{:S(2)}, u32[]{:S(2)}) collective-permute-start(bf16[2,256,256]{2,1,0:T(8,128)(2,1)S(1)} %maximum_select_fusion.refs_4_.refs_3_), channel_id=1, source_target_pairs={{0,8},{4,12},{8,0},{12,4},{1,9},{5,13},{9,1},{13,5},{2,10},{6,14},... | collective-permute-start | bytes 786440 | tf_op jit(solution)/shard_map/ppermute | solution.py:21
  73.1 2.3 %collective-permute-start.10 = (bf16[2,256,256]{2,1,0:T(8,128)(2,1)S(1)}, bf16[2,256,256]{2,1,0:T(8,128)(2,1)S(1)}, u32[]{:S(2)}, u32[]{:S(2)}) collective-permute-start(bf16[2,256,256]{2,1,0:T(8,128)(2,1)S(1)} %maximum_select_fusion.refs_4_.refs_3_), channel_id=1, source_target_pairs={{0,4},{4,0},{8,12},{12,8},{1,5},{5,1},{9,13},{13,9},{2,6},{6,2},{1... | collective-permute-start | bytes 786440 | tf_op jit(solution)/shard_map/ppermute | solution.py:21
  75.5 1.4 shard_map.113.refs_3_
  78.2 5.1 %collective-permute-done.10.refs_8_ = bf16[2,256,256]{2,1,0:T(8,128)(2,1)S(1)} collective-permute-done((bf16[2,256,256]{2,1,0:T(8,128)(2,1)S(1)}, bf16[2,256,256]{2,1,0:T(8,128)(2,1)S(1)}, u32[]{:S(2)}, u32[]{:S(2)}) %collective-permute-start.10) | collective-permute-done | bytes 262176 | tf_op jit(solution)/shard_map/ppermute | solution.py:21
  83.3 1.6 %shard_map.115 = (f32[2,256,256]{2,1,0:T(8,128)S(1)}, bf16[2,256,256]{2,1,0:T(8,128)(2,1)S(1)}) custom-call(s32[11]{0:T(128)S(1)} %pad_add_fusion.refs_0_, f32[3,9]{1,0:T(4,128)S(1)} %pad_maximum_fusion.1.refs_1_, bf16[12,256,256]{2,1,0:T(8,128)(2,1)S(1)} %copy-done, bf16[2,256,256]{2,1,0:T(8,128)(2,1)S(1)} %maximum_select_fusion.refs_4_.refs_3_, ...), custom_call_target="tpu_custom_call" | custom-call | flops 536870912 | bytes 4194456 | tf_op jit(solution)/shard_map/pallas_call | solution.py:174
  84.9 4.9 %collective-permute-start.11 = (bf16[2,256,256]{2,1,0:T(8,128)(2,1)S(1)}, bf16[2,256,256]{2,1,0:T(8,128)(2,1)S(1)}, u32[]{:S(2)}, u32[]{:S(2)}) collective-permute-start(bf16[2,256,256]{2,1,0:T(8,128)(2,1)S(1)} %get-tuple-element.19.refs_4_), channel_id=1, source_target_pairs={{0,2},{2,0},{1,3},{3,1},{4,6},{6,4},{5,7},{7,5},{8,10},{10,8},{9,1... | collective-permute-start | bytes 786440 | tf_op jit(solution)/shard_map/ppermute | solution.py:21
  89.9 4.2 %collective-permute-start.13 = (bf16[2,256,256]{2,1,0:T(8,128)(2,1)S(1)}, bf16[2,256,256]{2,1,0:T(8,128)(2,1)S(1)}, u32[]{:S(2)}, u32[]{:S(2)}) collective-permute-start(bf16[2,256,256]{2,1,0:T(8,128)(2,1)S(1)} %get-tuple-element.19.refs_4_), channel_id=1, source_target_pairs={{0,64},{2,194},{16,80},{18,210},{32,96},{34,226},{48,112},{50,242}... | collective-permute-start | bytes 786440 | tf_op jit(solution)/shard_map/ppermute | solution.py:31
  94.1 3.0 %collective-permute-start.14 = (bf16[2,256,256]{2,1,0:T(8,128)(2,1)S(1)}, bf16[2,256,256]{2,1,0:T(8,128)(2,1)S(1)}, u32[]{:S(2)}, u32[]{:S(2)}) collective-permute-start(bf16[2,256,256]{2,1,0:T(8,128)(2,1)S(1)} %get-tuple-element.19.refs_4_), channel_id=1, source_target_pairs={{2,66},{18,82},{34,98},{50,114},{66,2},{82,18},{98,34},{114,50},{1... | collective-permute-start | bytes 786440 | tf_op jit(solution)/shard_map/ppermute | solution.py:31
  97.1 4.6 %collective-permute-start.12 = (bf16[2,256,256]{2,1,0:T(8,128)(2,1)S(1)}, bf16[2,256,256]{2,1,0:T(8,128)(2,1)S(1)}, u32[]{:S(2)}, u32[]{:S(2)}) collective-permute-start(bf16[2,256,256]{2,1,0:T(8,128)(2,1)S(1)} %get-tuple-element.19.refs_4_), channel_id=1, source_target_pairs={{0,32},{16,48},{32,0},{48,16},{64,96},{80,112},{96,64},{112,80},{1... | collective-permute-start | bytes 786440 | tf_op jit(solution)/shard_map/ppermute | solution.py:21
  101.7 12.2 %collective-permute-done.13.refs_4_ = bf16[2,256,256]{2,1,0:T(8,128)(2,1)S(1)} collective-permute-done((bf16[2,256,256]{2,1,0:T(8,128)(2,1)S(1)}, bf16[2,256,256]{2,1,0:T(8,128)(2,1)S(1)}, u32[]{:S(2)}, u32[]{:S(2)}) %collective-permute-start.13) | collective-permute-done | bytes 262176 | tf_op jit(solution)/shard_map/ppermute | solution.py:31
  113.9 9.6 %collective-permute-start.16 = (bf16[2,256,256]{2,1,0:T(8,128)(2,1)S(1)}, bf16[2,256,256]{2,1,0:T(8,128)(2,1)S(1)}, u32[]{:S(2)}, u32[]{:S(2)}) collective-permute-start(bf16[2,256,256]{2,1,0:T(8,128)(2,1)S(1)} %get-tuple-element.19.refs_4_), channel_id=1, source_target_pairs={{0,16},{16,0},{32,48},{48,32},{64,80},{80,64},{96,112},{112,96},{1... | collective-permute-start | bytes 786440 | tf_op jit(solution)/shard_map/ppermute | solution.py:21
  123.5 1.9 %collective-permute-start.15 = (bf16[2,256,256]{2,1,0:T(8,128)(2,1)S(1)}, bf16[2,256,256]{2,1,0:T(8,128)(2,1)S(1)}, u32[]{:S(2)}, u32[]{:S(2)}) collective-permute-start(bf16[2,256,256]{2,1,0:T(8,128)(2,1)S(1)} %collective-permute-done.13.refs_4_), channel_id=1, source_target_pairs={{0,192},{2,66},{16,208},{18,82},{32,224},{34,98},{48,240},{50,114}... | collective-permute-start | bytes 786440 | tf_op jit(solution)/shard_map/ppermute | solution.py:31
  125.5 3.6 %collective-permute-start.17 = (bf16[2,256,256]{2,1,0:T(8,128)(2,1)S(1)}, bf16[2,256,256]{2,1,0:T(8,128)(2,1)S(1)}, u32[]{:S(2)}, u32[]{:S(2)}) collective-permute-start(bf16[2,256,256]{2,1,0:T(8,128)(2,1)S(1)} %get-tuple-element.19.refs_4_), channel_id=1, source_target_pairs={{0,1},{1,0},{2,3},{3,2},{4,5},{5,4},{6,7},{7,6},{8,9},{9,8},{10,11... | collective-permute-start | bytes 786440 | tf_op jit(solution)/shard_map/ppermute | solution.py:21
  129.1 1.9 %collective-permute-start.18 = (bf16[2,256,256]{2,1,0:T(8,128)(2,1)S(1)}, bf16[2,256,256]{2,1,0:T(8,128)(2,1)S(1)}, u32[]{:S(2)}, u32[]{:S(2)}) collective-permute-start(bf16[2,256,256]{2,1,0:T(8,128)(2,1)S(1)} %get-tuple-element.19.refs_4_), channel_id=1, source_target_pairs={{0,256},{256,0},{1,257},{257,1},{2,258},{258,2},{3,259},{259,3},{4... | collective-permute-start | bytes 786440 | tf_op jit(solution)/shard_map/ppermute | solution.py:21
  131.1 2.8 %collective-permute-start.19 = (bf16[2,256,256]{2,1,0:T(8,128)(2,1)S(1)}, bf16[2,256,256]{2,1,0:T(8,128)(2,1)S(1)}, u32[]{:S(2)}, u32[]{:S(2)}) collective-permute-start(bf16[2,256,256]{2,1,0:T(8,128)(2,1)S(1)} %get-tuple-element.19.refs_4_), channel_id=1, source_target_pairs={{0,8},{4,12},{8,0},{12,4},{1,9},{5,13},{9,1},{13,5},{2,10},{6,14},... | collective-permute-start | bytes 786440 | tf_op jit(solution)/shard_map/ppermute | solution.py:21
  133.8 3.8 %collective-permute-done.16.refs_7_ = bf16[2,256,256]{2,1,0:T(8,128)(2,1)S(1)} collective-permute-done((bf16[2,256,256]{2,1,0:T(8,128)(2,1)S(1)}, bf16[2,256,256]{2,1,0:T(8,128)(2,1)S(1)}, u32[]{:S(2)}, u32[]{:S(2)}) %collective-permute-start.16) | collective-permute-done | bytes 262176 | tf_op jit(solution)/shard_map/ppermute | solution.py:21
  137.7 1.9 %collective-permute-start.20 = (bf16[2,256,256]{2,1,0:T(8,128)(2,1)S(1)}, bf16[2,256,256]{2,1,0:T(8,128)(2,1)S(1)}, u32[]{:S(2)}, u32[]{:S(2)}) collective-permute-start(bf16[2,256,256]{2,1,0:T(8,128)(2,1)S(1)} %get-tuple-element.19.refs_4_), channel_id=1, source_target_pairs={{0,4},{4,0},{8,12},{12,8},{1,5},{5,1},{9,13},{13,9},{2,6},{6,2},{1... | collective-permute-start | bytes 786440 | tf_op jit(solution)/shard_map/ppermute | solution.py:21
  139.6 1.4 shard_map.116.refs_3_
  142.4 4.2 %collective-permute-done.20.refs_7_ = bf16[2,256,256]{2,1,0:T(8,128)(2,1)S(1)} collective-permute-done((bf16[2,256,256]{2,1,0:T(8,128)(2,1)S(1)}, bf16[2,256,256]{2,1,0:T(8,128)(2,1)S(1)}, u32[]{:S(2)}, u32[]{:S(2)}) %collective-permute-start.20) | collective-permute-done | bytes 262176 | tf_op jit(solution)/shard_map/ppermute | solution.py:21
  146.6 1.5 shard_map.118
  148.1 4.4 %collective-permute-start.21 = (bf16[2,128,256]{2,1,0:T(8,128)(2,1)S(1)}, bf16[2,128,256]{2,1,0:T(8,128)(2,1)S(1)}, u32[]{:S(2)}, u32[]{:S(2)}) collective-permute-start(bf16[2,128,256]{2,1,0:T(8,128)(2,1)S(1)} %get-tuple-element.21), channel_id=1, source_target_pairs={{0,1},{1,0},{2,3},{3,2},{4,5},{5,4},{6,7},{7,6},{8,9},{9,8},{10,11... | collective-permute-start | bytes 393224 | tf_op jit(solution)/shard_map/ppermute | solution.py:21
  152.5 3.9 %collective-permute-done.21 = bf16[2,128,256]{2,1,0:T(8,128)(2,1)S(1)} collective-permute-done((bf16[2,128,256]{2,1,0:T(8,128)(2,1)S(1)}, bf16[2,128,256]{2,1,0:T(8,128)(2,1)S(1)}, u32[]{:S(2)}, u32[]{:S(2)}) %collective-permute-start.21) | collective-permute-done | bytes 131104 | tf_op jit(solution)/shard_map/ppermute | solution.py:21
  (54 shorter events, 7.0 us)
Async XLA Ops:
  0.6 25.9 %copy-start.7 = (f32[12]{0:T(128)S(1)}, f32[12]{0:T(128)}, u32[]{:S(2)}) copy-start(f32[12]{0:T(128)} %param.14) | copy-start | bytes 148
  0.6 25.9 %copy-start.4 = (s32[2,12]{1,0:T(2,128)S(1)}, s32[2,12]{1,0:T(2,128)}, u32[]{:S(2)}) copy-start(s32[2,12]{1,0:T(2,128)} %param.17) | copy-start | bytes 292
  0.7 26.0 %copy-start.5 = (f32[12]{0:T(128)S(1)}, f32[12]{0:T(128)}, u32[]{:S(2)}) copy-start(f32[12]{0:T(128)} %param.16) | copy-start | bytes 148
  0.7 26.0 %copy-start.6 = (f32[12]{0:T(128)S(1)}, f32[12]{0:T(128)}, u32[]{:S(2)}) copy-start(f32[12]{0:T(128)} %param.15) | copy-start | bytes 148
  0.7 74.8 %copy-start = (bf16[12,256,256]{2,1,0:T(8,128)(2,1)S(1)}, bf16[12,256,256]{2,1,0:T(8,128)(2,1)}, u32[]{:S(2)}) copy-start(bf16[12,256,256]{2,1,0:T(8,128)(2,1)} %refs_2_.11) | copy-start | bytes 4718596
  0.7 74.8 %copy-start.1 = (bf16[2,256,256]{2,1,0:T(8,128)(2,1)S(1)}, bf16[2,256,256]{2,1,0:T(8,128)(2,1)}, u32[]{:S(2)}) copy-start(bf16[2,256,256]{2,1,0:T(8,128)(2,1)} %refs_3_.3) | copy-start | bytes 786436
  1.9 7.8 %collective-permute-start = (bf16[2,128,256]{2,1,0:T(8,128)(2,1)S(1)}, bf16[2,128,256]{2,1,0:T(8,128)(2,1)S(1)}, u32[]{:S(2)}, u32[]{:S(2)}) collective-permute-start(bf16[2,128,256]{2,1,0:T(8,128)(2,1)S(1)} %get-tuple-element.29), channel_id=1, source_target_pairs={{0,1},{1,0},{2,3},{3,2},{4,5},{5,4},{6,7},{7,6},{8,9},{9,8},{10,11... | collective-permute-start | bytes 393224 | tf_op jit(solution)/shard_map/ppermute | solution.py:21
  9.9 25.2 %collective-permute-start.1 = (bf16[2,256,256]{2,1,0:T(8,128)(2,1)S(1)}, bf16[2,256,256]{2,1,0:T(8,128)(2,1)S(1)}, u32[]{:S(2)}, u32[]{:S(2)}) collective-permute-start(bf16[2,256,256]{2,1,0:T(8,128)(2,1)S(1)} %maximum_select_fusion.refs_4_.refs_3_), channel_id=1, source_target_pairs={{0,2},{2,0},{1,3},{3,1},{4,6},{6,4},{5,7},{7,5},{8,10},{10,8},{9,1... | collective-permute-start | bytes 786440 | tf_op jit(solution)/shard_map/ppermute | solution.py:21
  19.2 15.9 %collective-permute-start.3 = (bf16[2,256,256]{2,1,0:T(8,128)(2,1)S(1)}, bf16[2,256,256]{2,1,0:T(8,128)(2,1)S(1)}, u32[]{:S(2)}, u32[]{:S(2)}) collective-permute-start(bf16[2,256,256]{2,1,0:T(8,128)(2,1)S(1)} %maximum_select_fusion.refs_4_.refs_3_), channel_id=1, source_target_pairs={{0,64},{2,194},{16,80},{18,210},{32,96},{34,226},{48,112},{50,242}... | collective-permute-start | bytes 786440 | tf_op jit(solution)/shard_map/ppermute | solution.py:31
  26.7 41.5 %collective-permute-start.2 = (bf16[2,256,256]{2,1,0:T(8,128)(2,1)S(1)}, bf16[2,256,256]{2,1,0:T(8,128)(2,1)S(1)}, u32[]{:S(2)}, u32[]{:S(2)}) collective-permute-start(bf16[2,256,256]{2,1,0:T(8,128)(2,1)S(1)} %maximum_select_fusion.refs_4_.refs_3_), channel_id=1, source_target_pairs={{0,32},{16,48},{32,0},{48,16},{64,96},{80,112},{96,64},{112,80},{1... | collective-permute-start | bytes 786440 | tf_op jit(solution)/shard_map/ppermute | solution.py:21
  29.8 36.2 %collective-permute-start.4 = (bf16[2,256,256]{2,1,0:T(8,128)(2,1)S(1)}, bf16[2,256,256]{2,1,0:T(8,128)(2,1)S(1)}, u32[]{:S(2)}, u32[]{:S(2)}) collective-permute-start(bf16[2,256,256]{2,1,0:T(8,128)(2,1)S(1)} %maximum_select_fusion.refs_4_.refs_3_), channel_id=1, source_target_pairs={{2,66},{18,82},{34,98},{50,114},{66,2},{82,18},{98,34},{114,50},{1... | collective-permute-start | bytes 786440 | tf_op jit(solution)/shard_map/ppermute | solution.py:31
  35.1 38.0 %collective-permute-start.6 = (bf16[2,256,256]{2,1,0:T(8,128)(2,1)S(1)}, bf16[2,256,256]{2,1,0:T(8,128)(2,1)S(1)}, u32[]{:S(2)}, u32[]{:S(2)}) collective-permute-start(bf16[2,256,256]{2,1,0:T(8,128)(2,1)S(1)} %maximum_select_fusion.refs_4_.refs_3_), channel_id=1, source_target_pairs={{0,16},{16,0},{32,48},{48,32},{64,80},{80,64},{96,112},{112,96},{1... | collective-permute-start | bytes 786440 | tf_op jit(solution)/shard_map/ppermute | solution.py:21
  56.0 20.9 %collective-permute-start.5 = (bf16[2,256,256]{2,1,0:T(8,128)(2,1)S(1)}, bf16[2,256,256]{2,1,0:T(8,128)(2,1)S(1)}, u32[]{:S(2)}, u32[]{:S(2)}) collective-permute-start(bf16[2,256,256]{2,1,0:T(8,128)(2,1)S(1)} %collective-permute-done.3.refs_4_), channel_id=1, source_target_pairs={{0,192},{2,66},{16,208},{18,82},{32,224},{34,98},{48,240},{50,114}... | collective-permute-start | bytes 786440 | tf_op jit(solution)/shard_map/ppermute | solution.py:31
  61.8 16.4 %collective-permute-start.7 = (bf16[2,256,256]{2,1,0:T(8,128)(2,1)S(1)}, bf16[2,256,256]{2,1,0:T(8,128)(2,1)S(1)}, u32[]{:S(2)}, u32[]{:S(2)}) collective-permute-start(bf16[2,256,256]{2,1,0:T(8,128)(2,1)S(1)} %maximum_select_fusion.refs_4_.refs_3_), channel_id=1, source_target_pairs={{0,1},{1,0},{2,3},{3,2},{4,5},{5,4},{6,7},{7,6},{8,9},{9,8},{10,11... | collective-permute-start | bytes 786440 | tf_op jit(solution)/shard_map/ppermute | solution.py:21
  66.0 12.2 %collective-permute-start.8 = (bf16[2,256,256]{2,1,0:T(8,128)(2,1)S(1)}, bf16[2,256,256]{2,1,0:T(8,128)(2,1)S(1)}, u32[]{:S(2)}, u32[]{:S(2)}) collective-permute-start(bf16[2,256,256]{2,1,0:T(8,128)(2,1)S(1)} %maximum_select_fusion.refs_4_.refs_3_), channel_id=1, source_target_pairs={{0,256},{256,0},{1,257},{257,1},{2,258},{258,2},{3,259},{259,3},{4... | collective-permute-start | bytes 786440 | tf_op jit(solution)/shard_map/ppermute | solution.py:21
  68.3 10.0 %collective-permute-start.9 = (bf16[2,256,256]{2,1,0:T(8,128)(2,1)S(1)}, bf16[2,256,256]{2,1,0:T(8,128)(2,1)S(1)}, u32[]{:S(2)}, u32[]{:S(2)}) collective-permute-start(bf16[2,256,256]{2,1,0:T(8,128)(2,1)S(1)} %maximum_select_fusion.refs_4_.refs_3_), channel_id=1, source_target_pairs={{0,8},{4,12},{8,0},{12,4},{1,9},{5,13},{9,1},{13,5},{2,10},{6,14},... | collective-permute-start | bytes 786440 | tf_op jit(solution)/shard_map/ppermute | solution.py:21
  73.1 10.2 %collective-permute-start.10 = (bf16[2,256,256]{2,1,0:T(8,128)(2,1)S(1)}, bf16[2,256,256]{2,1,0:T(8,128)(2,1)S(1)}, u32[]{:S(2)}, u32[]{:S(2)}) collective-permute-start(bf16[2,256,256]{2,1,0:T(8,128)(2,1)S(1)} %maximum_select_fusion.refs_4_.refs_3_), channel_id=1, source_target_pairs={{0,4},{4,0},{8,12},{12,8},{1,5},{5,1},{9,13},{13,9},{2,6},{6,2},{1... | collective-permute-start | bytes 786440 | tf_op jit(solution)/shard_map/ppermute | solution.py:21
  84.9 16.8 %collective-permute-start.11 = (bf16[2,256,256]{2,1,0:T(8,128)(2,1)S(1)}, bf16[2,256,256]{2,1,0:T(8,128)(2,1)S(1)}, u32[]{:S(2)}, u32[]{:S(2)}) collective-permute-start(bf16[2,256,256]{2,1,0:T(8,128)(2,1)S(1)} %get-tuple-element.19.refs_4_), channel_id=1, source_target_pairs={{0,2},{2,0},{1,3},{3,1},{4,6},{6,4},{5,7},{7,5},{8,10},{10,8},{9,1... | collective-permute-start | bytes 786440 | tf_op jit(solution)/shard_map/ppermute | solution.py:21
  89.9 24.1 %collective-permute-start.13 = (bf16[2,256,256]{2,1,0:T(8,128)(2,1)S(1)}, bf16[2,256,256]{2,1,0:T(8,128)(2,1)S(1)}, u32[]{:S(2)}, u32[]{:S(2)}) collective-permute-start(bf16[2,256,256]{2,1,0:T(8,128)(2,1)S(1)} %get-tuple-element.19.refs_4_), channel_id=1, source_target_pairs={{0,64},{2,194},{16,80},{18,210},{32,96},{34,226},{48,112},{50,242}... | collective-permute-start | bytes 786440 | tf_op jit(solution)/shard_map/ppermute | solution.py:31
  94.1 35.0 %collective-permute-start.14 = (bf16[2,256,256]{2,1,0:T(8,128)(2,1)S(1)}, bf16[2,256,256]{2,1,0:T(8,128)(2,1)S(1)}, u32[]{:S(2)}, u32[]{:S(2)}) collective-permute-start(bf16[2,256,256]{2,1,0:T(8,128)(2,1)S(1)} %get-tuple-element.19.refs_4_), channel_id=1, source_target_pairs={{2,66},{18,82},{34,98},{50,114},{66,2},{82,18},{98,34},{114,50},{1... | collective-permute-start | bytes 786440 | tf_op jit(solution)/shard_map/ppermute | solution.py:31
  97.1 34.0 %collective-permute-start.12 = (bf16[2,256,256]{2,1,0:T(8,128)(2,1)S(1)}, bf16[2,256,256]{2,1,0:T(8,128)(2,1)S(1)}, u32[]{:S(2)}, u32[]{:S(2)}) collective-permute-start(bf16[2,256,256]{2,1,0:T(8,128)(2,1)S(1)} %get-tuple-element.19.refs_4_), channel_id=1, source_target_pairs={{0,32},{16,48},{32,0},{48,16},{64,96},{80,112},{96,64},{112,80},{1... | collective-permute-start | bytes 786440 | tf_op jit(solution)/shard_map/ppermute | solution.py:21
  113.9 23.7 %collective-permute-start.16 = (bf16[2,256,256]{2,1,0:T(8,128)(2,1)S(1)}, bf16[2,256,256]{2,1,0:T(8,128)(2,1)S(1)}, u32[]{:S(2)}, u32[]{:S(2)}) collective-permute-start(bf16[2,256,256]{2,1,0:T(8,128)(2,1)S(1)} %get-tuple-element.19.refs_4_), channel_id=1, source_target_pairs={{0,16},{16,0},{32,48},{48,32},{64,80},{80,64},{96,112},{112,96},{1... | collective-permute-start | bytes 786440 | tf_op jit(solution)/shard_map/ppermute | solution.py:21
  123.5 17.5 %collective-permute-start.15 = (bf16[2,256,256]{2,1,0:T(8,128)(2,1)S(1)}, bf16[2,256,256]{2,1,0:T(8,128)(2,1)S(1)}, u32[]{:S(2)}, u32[]{:S(2)}) collective-permute-start(bf16[2,256,256]{2,1,0:T(8,128)(2,1)S(1)} %collective-permute-done.13.refs_4_), channel_id=1, source_target_pairs={{0,192},{2,66},{16,208},{18,82},{32,224},{34,98},{48,240},{50,114}... | collective-permute-start | bytes 786440 | tf_op jit(solution)/shard_map/ppermute | solution.py:31
  125.5 16.9 %collective-permute-start.17 = (bf16[2,256,256]{2,1,0:T(8,128)(2,1)S(1)}, bf16[2,256,256]{2,1,0:T(8,128)(2,1)S(1)}, u32[]{:S(2)}, u32[]{:S(2)}) collective-permute-start(bf16[2,256,256]{2,1,0:T(8,128)(2,1)S(1)} %get-tuple-element.19.refs_4_), channel_id=1, source_target_pairs={{0,1},{1,0},{2,3},{3,2},{4,5},{5,4},{6,7},{7,6},{8,9},{9,8},{10,11... | collective-permute-start | bytes 786440 | tf_op jit(solution)/shard_map/ppermute | solution.py:21
  129.1 13.3 %collective-permute-start.18 = (bf16[2,256,256]{2,1,0:T(8,128)(2,1)S(1)}, bf16[2,256,256]{2,1,0:T(8,128)(2,1)S(1)}, u32[]{:S(2)}, u32[]{:S(2)}) collective-permute-start(bf16[2,256,256]{2,1,0:T(8,128)(2,1)S(1)} %get-tuple-element.19.refs_4_), channel_id=1, source_target_pairs={{0,256},{256,0},{1,257},{257,1},{2,258},{258,2},{3,259},{259,3},{4... | collective-permute-start | bytes 786440 | tf_op jit(solution)/shard_map/ppermute | solution.py:21
  131.1 11.3 %collective-permute-start.19 = (bf16[2,256,256]{2,1,0:T(8,128)(2,1)S(1)}, bf16[2,256,256]{2,1,0:T(8,128)(2,1)S(1)}, u32[]{:S(2)}, u32[]{:S(2)}) collective-permute-start(bf16[2,256,256]{2,1,0:T(8,128)(2,1)S(1)} %get-tuple-element.19.refs_4_), channel_id=1, source_target_pairs={{0,8},{4,12},{8,0},{12,4},{1,9},{5,13},{9,1},{13,5},{2,10},{6,14},... | collective-permute-start | bytes 786440 | tf_op jit(solution)/shard_map/ppermute | solution.py:21
  137.7 8.9 %collective-permute-start.20 = (bf16[2,256,256]{2,1,0:T(8,128)(2,1)S(1)}, bf16[2,256,256]{2,1,0:T(8,128)(2,1)S(1)}, u32[]{:S(2)}, u32[]{:S(2)}) collective-permute-start(bf16[2,256,256]{2,1,0:T(8,128)(2,1)S(1)} %get-tuple-element.19.refs_4_), channel_id=1, source_target_pairs={{0,4},{4,0},{8,12},{12,8},{1,5},{5,1},{9,13},{13,9},{2,6},{6,2},{1... | collective-permute-start | bytes 786440 | tf_op jit(solution)/shard_map/ppermute | solution.py:21
  142.3 14.2 %copy-start.2 = (f32[2,128,256]{2,1,0:T(8,128)S(1)}, f32[2,128,256]{2,1,0:T(8,128)}, u32[]{:S(2)}) copy-start(f32[2,128,256]{2,1,0:T(8,128)} %param.11) | copy-start | bytes 786436
  142.3 14.2 %copy-start.3 = (f32[2,128,256]{2,1,0:T(8,128)S(1)}, f32[2,128,256]{2,1,0:T(8,128)}, u32[]{:S(2)}) copy-start(f32[2,128,256]{2,1,0:T(8,128)} %param.10) | copy-start | bytes 786436
  148.1 8.3 %collective-permute-start.21 = (bf16[2,128,256]{2,1,0:T(8,128)(2,1)S(1)}, bf16[2,128,256]{2,1,0:T(8,128)(2,1)S(1)}, u32[]{:S(2)}, u32[]{:S(2)}) collective-permute-start(bf16[2,128,256]{2,1,0:T(8,128)(2,1)S(1)} %get-tuple-element.21), channel_id=1, source_target_pairs={{0,1},{1,0},{2,3},{3,2},{4,5},{5,4},{6,7},{7,6},{8,9},{9,8},{10,11... | collective-permute-start | bytes 393224 | tf_op jit(solution)/shard_map/ppermute | solution.py:21

commit v8 on v5

--- a/solution.py
+++ b/solution.py
@@ -155,14 +155,14 @@
     def exchange(full):
         first = across(full, inward, opposite)
         core = swapped(full, "core", 1)
-        z2 = swapped(full, "z", 2)
         x2 = swapped(full, "rep", 1)
         y2 = swapped(full, "y", 2)
-        z1 = swapped(after(full, first, core), "z", 1)
-        x1 = swapped(after(full, first, x2), "x_lo", 1)
-        y1 = swapped(after(full, first, z2), "y", 1)
+        x1 = swapped(full, "x_lo", 1)
         second = across(jnp.where(on_first, first, full), outward, inward)
-        return {1: [core], 5: [z2], 0: [x2], 3: [y2]}, {6: [first, second], 7: [second, first]}, {4: [z1], 8: [x1], 2: [y1]}
+        z2 = swapped(after(full, first, core), "z", 2)
+        z1 = swapped(after(full, first, x2), "z", 1)
+        y1 = swapped(after(full, first, y2), "y", 1)
+        return {1: [core], 0: [x2], 3: [y2], 8: [x1]}, {6: [first, second], 7: [second, first]}, {5: [z2], 4: [z1], 2: [y1]}
 
     def call(body, parts, outs, scratch, *operands):
         held = []

time: 141 us -> 145 us (1.028)
  the two profiles are of different devices: /device:TPU:2 before, /device:TPU:4 now
where the time goes in v8:
time: 145 us; the launch traced here: 144 us
  starting transfers between devices  94.9 us (65%)
  waiting for transfers between devices  31.8 us (22%)
  Pallas kernels  8.55 us (6%)
  other arithmetic  5.74 us (4%)
  between operations  2.33 us (2%)
    ppermute x16, starting transfers between devices, swapped(): return lax.ppermute(value, axis, pairs)  69.3 us
    ppermute x4, starting transfers between devices, across(): return lax.ppermute(value, ('z', 'core'), pairs)  25.6 us
    ppermute x16, waiting for transfers between devices, swapped(): return lax.ppermute(value, axis, pairs)  16.7 us
    ppermute x4, waiting for transfers between devices, across(): return lax.ppermute(value, ('z', 'core'), pairs)  15 us
    pallas_call x6, Pallas kernels, call(): pl.pallas_call(lambda *refs: body(counts, *refs), out_shape=outs, in_spec...  8.55 us
  transfers between devices with their start and end apart: 20, of which 7 were waited for; matrix products, arithmetic and copies ran while one was open for 3% of the time, Pallas kernels for 4%

profile of v8, /device:TPU:4, one launch (start us, length us, event | category | flops | bytes accessed | tf_op | source)
XLA Modules:
  0.0 143.9 jit_solution(5205145812039923773)
XLA Ops:
  0.7 1.2 convert_bitcast_fusion
  1.9 7.8 %collective-permute-start = (bf16[2,128,256]{2,1,0:T(8,128)(2,1)S(1)}, bf16[2,128,256]{2,1,0:T(8,128)(2,1)S(1)}, u32[]{:S(2)}, u32[]{:S(2)}) collective-permute-start(bf16[2,128,256]{2,1,0:T(8,128)(2,1)S(1)} %get-tuple-element.29), channel_id=1, source_target_pairs={{0,1},{1,0},{2,3},{3,2},{4,5},{5,4},{6,7},{7,6},{8,9},{9,8},{10,11... | collective-permute-start | bytes 393224 | tf_op jit(solution)/shard_map/ppermute | solution.py:21
  12.9 6.8 %collective-permute-start.5 = (bf16[2,256,256]{2,1,0:T(8,128)(2,1)S(1)}, bf16[2,256,256]{2,1,0:T(8,128)(2,1)S(1)}, u32[]{:S(2)}, u32[]{:S(2)}) collective-permute-start(bf16[2,256,256]{2,1,0:T(8,128)(2,1)S(1)} %maximum_select_fusion.refs_4_.refs_3_), channel_id=1, source_target_pairs={{0,64},{2,130},{16,80},{18,146},{32,96},{34,162},{48,112},{50,178}... | collective-permute-start | bytes 786440 | tf_op jit(solution)/shard_map/ppermute | solution.py:31
  21.8 7.2 %collective-permute-start.1 = (bf16[2,256,256]{2,1,0:T(8,128)(2,1)S(1)}, bf16[2,256,256]{2,1,0:T(8,128)(2,1)S(1)}, u32[]{:S(2)}, u32[]{:S(2)}) collective-permute-start(bf16[2,256,256]{2,1,0:T(8,128)(2,1)S(1)} %maximum_select_fusion.refs_4_.refs_3_), channel_id=1, source_target_pairs={{0,2},{2,0},{1,3},{3,1},{4,6},{6,4},{5,7},{7,5},{8,10},{10,8},{9,1... | collective-permute-start | bytes 786440 | tf_op jit(solution)/shard_map/ppermute | solution.py:21
  29.0 2.5 %collective-permute-start.2 = (bf16[2,256,256]{2,1,0:T(8,128)(2,1)S(1)}, bf16[2,256,256]{2,1,0:T(8,128)(2,1)S(1)}, u32[]{:S(2)}, u32[]{:S(2)}) collective-permute-start(bf16[2,256,256]{2,1,0:T(8,128)(2,1)S(1)} %maximum_select_fusion.refs_4_.refs_3_), channel_id=1, source_target_pairs={{0,1},{1,0},{2,3},{3,2},{4,5},{5,4},{6,7},{7,6},{8,9},{9,8},{10,11... | collective-permute-start | bytes 786440 | tf_op jit(solution)/shard_map/ppermute | solution.py:21
  31.5 5.1 %collective-permute-start.3 = (bf16[2,256,256]{2,1,0:T(8,128)(2,1)S(1)}, bf16[2,256,256]{2,1,0:T(8,128)(2,1)S(1)}, u32[]{:S(2)}, u32[]{:S(2)}) collective-permute-start(bf16[2,256,256]{2,1,0:T(8,128)(2,1)S(1)} %maximum_select_fusion.refs_4_.refs_3_), channel_id=1, source_target_pairs={{0,8},{4,12},{8,0},{12,4},{1,9},{5,13},{9,1},{13,5},{2,10},{6,14},... | collective-permute-start | bytes 786440 | tf_op jit(solution)/shard_map/ppermute | solution.py:21
  36.6 4.0 %collective-permute-start.4 = (bf16[2,256,256]{2,1,0:T(8,128)(2,1)S(1)}, bf16[2,256,256]{2,1,0:T(8,128)(2,1)S(1)}, u32[]{:S(2)}, u32[]{:S(2)}) collective-permute-start(bf16[2,256,256]{2,1,0:T(8,128)(2,1)S(1)} %maximum_select_fusion.refs_4_.refs_3_), channel_id=1, source_target_pairs={{0,256},{256,0},{1,257},{257,1},{2,258},{258,2},{3,259},{259,3},{4... | collective-permute-start | bytes 786440 | tf_op jit(solution)/shard_map/ppermute | solution.py:21
  40.6 4.2 %collective-permute-done.5.refs_4_ = bf16[2,256,256]{2,1,0:T(8,128)(2,1)S(1)} collective-permute-done((bf16[2,256,256]{2,1,0:T(8,128)(2,1)S(1)}, bf16[2,256,256]{2,1,0:T(8,128)(2,1)S(1)}, u32[]{:S(2)}, u32[]{:S(2)}) %collective-permute-start.5) | collective-permute-done | bytes 262176 | tf_op jit(solution)/shard_map/ppermute | solution.py:31
  44.8 11.9 %collective-permute-start.6 = (bf16[2,256,256]{2,1,0:T(8,128)(2,1)S(1)}, bf16[2,256,256]{2,1,0:T(8,128)(2,1)S(1)}, u32[]{:S(2)}, u32[]{:S(2)}) collective-permute-start(bf16[2,256,256]{2,1,0:T(8,128)(2,1)S(1)} %broadcast_select_fusion.1), channel_id=1, source_target_pairs={{0,192},{2,66},{16,208},{18,82},{32,224},{34,98},{48,240},{50,114}... | collective-permute-start | bytes 786440 | tf_op jit(solution)/shard_map/ppermute | solution.py:31
  56.7 1.9 %collective-permute-start.7 = (bf16[2,256,256]{2,1,0:T(8,128)(2,1)S(1)}, bf16[2,256,256]{2,1,0:T(8,128)(2,1)S(1)}, u32[]{:S(2)}, u32[]{:S(2)}) collective-permute-start(bf16[2,256,256]{2,1,0:T(8,128)(2,1)S(1)} %maximum_select_fusion.refs_4_.refs_3_), channel_id=1, source_target_pairs={{0,32},{16,48},{32,0},{48,16},{64,96},{80,112},{96,64},{112,80},{1... | collective-permute-start | bytes 786440 | tf_op jit(solution)/shard_map/ppermute | solution.py:21
  58.7 1.9 %collective-permute-start.8 = (bf16[2,256,256]{2,1,0:T(8,128)(2,1)S(1)}, bf16[2,256,256]{2,1,0:T(8,128)(2,1)S(1)}, u32[]{:S(2)}, u32[]{:S(2)}) collective-permute-start(bf16[2,256,256]{2,1,0:T(8,128)(2,1)S(1)} %maximum_select_fusion.refs_4_.refs_3_), channel_id=1, source_target_pairs={{0,16},{16,0},{32,48},{48,32},{64,80},{80,64},{96,112},{112,96},{1... | collective-permute-start | bytes 786440 | tf_op jit(solution)/shard_map/ppermute | solution.py:21
  60.6 4.5 %collective-permute-start.9 = (bf16[2,256,256]{2,1,0:T(8,128)(2,1)S(1)}, bf16[2,256,256]{2,1,0:T(8,128)(2,1)S(1)}, u32[]{:S(2)}, u32[]{:S(2)}) collective-permute-start(bf16[2,256,256]{2,1,0:T(8,128)(2,1)S(1)} %maximum_select_fusion.refs_4_.refs_3_), channel_id=1, source_target_pairs={{0,4},{4,0},{8,12},{12,8},{1,5},{5,1},{9,13},{13,9},{2,6},{6,2},{1... | collective-permute-start | bytes 786440 | tf_op jit(solution)/shard_map/ppermute | solution.py:21
  65.3 1.8 %shard_map.113.refs_3_ = f32[2,256,256]{2,1,0:T(8,128)S(1)} custom-call(s32[11]{0:T(128)S(1)} %pad_add_fusion.refs_0_, f32[3,9]{1,0:T(4,128)S(1)} %pad_maximum_fusion.1.refs_1_, bf16[12,256,256]{2,1,0:T(8,128)(2,1)S(1)} %copy-done, bf16[2,256,256]{2,1,0:T(8,128)(2,1)S(1)} %copy-done.1, bf16[2,256,256]{2,1,0:T(8,128)(2,1)S(1)} %maximum_select_fusion.refs_4_.refs_3_, ...), custom_call_target="tpu_custom_call" | custom-call | flops 536870912 | bytes 3670168 | tf_op jit(solution)/shard_map/pallas_call | solution.py:178
  68.2 3.5 %collective-permute-done.7.refs_5_ = bf16[2,256,256]{2,1,0:T(8,128)(2,1)S(1)} collective-permute-done((bf16[2,256,256]{2,1,0:T(8,128)(2,1)S(1)}, bf16[2,256,256]{2,1,0:T(8,128)(2,1)S(1)}, u32[]{:S(2)}, u32[]{:S(2)}) %collective-permute-start.7) | collective-permute-done | bytes 262176 | tf_op jit(solution)/shard_map/ppermute | solution.py:21
  71.7 1.3 collective-permute-done.8.refs_6_
  73.0 1.4 shard_map.115
  74.4 5.0 %collective-permute-start.14 = (bf16[2,256,256]{2,1,0:T(8,128)(2,1)S(1)}, bf16[2,256,256]{2,1,0:T(8,128)(2,1)S(1)}, u32[]{:S(2)}, u32[]{:S(2)}) collective-permute-start(bf16[2,256,256]{2,1,0:T(8,128)(2,1)S(1)} %get-tuple-element.19.refs_4_), channel_id=1, source_target_pairs={{0,64},{2,130},{16,80},{18,146},{32,96},{34,162},{48,112},{50,178}... | collective-permute-start | bytes 786440 | tf_op jit(solution)/shard_map/ppermute | solution.py:31
  79.4 2.0 %collective-permute-start.10 = (bf16[2,256,256]{2,1,0:T(8,128)(2,1)S(1)}, bf16[2,256,256]{2,1,0:T(8,128)(2,1)S(1)}, u32[]{:S(2)}, u32[]{:S(2)}) collective-permute-start(bf16[2,256,256]{2,1,0:T(8,128)(2,1)S(1)} %get-tuple-element.19.refs_4_), channel_id=1, source_target_pairs={{0,2},{2,0},{1,3},{3,1},{4,6},{6,4},{5,7},{7,5},{8,10},{10,8},{9,1... | collective-permute-start | bytes 786440 | tf_op jit(solution)/shard_map/ppermute | solution.py:21
  81.4 3.1 %collective-permute-start.11 = (bf16[2,256,256]{2,1,0:T(8,128)(2,1)S(1)}, bf16[2,256,256]{2,1,0:T(8,128)(2,1)S(1)}, u32[]{:S(2)}, u32[]{:S(2)}) collective-permute-start(bf16[2,256,256]{2,1,0:T(8,128)(2,1)S(1)} %get-tuple-element.19.refs_4_), channel_id=1, source_target_pairs={{0,1},{1,0},{2,3},{3,2},{4,5},{5,4},{6,7},{7,6},{8,9},{9,8},{10,11... | collective-permute-start | bytes 786440 | tf_op jit(solution)/shard_map/ppermute | solution.py:21
  84.5 6.3 %collective-permute-start.12 = (bf16[2,256,256]{2,1,0:T(8,128)(2,1)S(1)}, bf16[2,256,256]{2,1,0:T(8,128)(2,1)S(1)}, u32[]{:S(2)}, u32[]{:S(2)}) collective-permute-start(bf16[2,256,256]{2,1,0:T(8,128)(2,1)S(1)} %get-tuple-element.19.refs_4_), channel_id=1, source_target_pairs={{0,8},{4,12},{8,0},{12,4},{1,9},{5,13},{9,1},{13,5},{2,10},{6,14},... | collective-permute-start | bytes 786440 | tf_op jit(solution)/shard_map/ppermute | solution.py:21
  90.7 7.6 %collective-permute-start.13 = (bf16[2,256,256]{2,1,0:T(8,128)(2,1)S(1)}, bf16[2,256,256]{2,1,0:T(8,128)(2,1)S(1)}, u32[]{:S(2)}, u32[]{:S(2)}) collective-permute-start(bf16[2,256,256]{2,1,0:T(8,128)(2,1)S(1)} %get-tuple-element.19.refs_4_), channel_id=1, source_target_pairs={{0,256},{256,0},{1,257},{257,1},{2,258},{258,2},{3,259},{259,3},{4... | collective-permute-start | bytes 786440 | tf_op jit(solution)/shard_map/ppermute | solution.py:21
  98.3 5.4 %collective-permute-done.14.refs_4_ = bf16[2,256,256]{2,1,0:T(8,128)(2,1)S(1)} collective-permute-done((bf16[2,256,256]{2,1,0:T(8,128)(2,1)S(1)}, bf16[2,256,256]{2,1,0:T(8,128)(2,1)S(1)}, u32[]{:S(2)}, u32[]{:S(2)}) %collective-permute-start.14) | collective-permute-done | bytes 262176 | tf_op jit(solution)/shard_map/ppermute | solution.py:31
  103.8 1.9 %collective-permute-start.15 = (bf16[2,256,256]{2,1,0:T(8,128)(2,1)S(1)}, bf16[2,256,256]{2,1,0:T(8,128)(2,1)S(1)}, u32[]{:S(2)}, u32[]{:S(2)}) collective-permute-start(bf16[2,256,256]{2,1,0:T(8,128)(2,1)S(1)} %broadcast_select_fusion), channel_id=1, source_target_pairs={{0,192},{2,66},{16,208},{18,82},{32,224},{34,98},{48,240},{50,114}... | collective-permute-start | bytes 786440 | tf_op jit(solution)/shard_map/ppermute | solution.py:31
  105.7 6.0 %collective-permute-start.16 = (bf16[2,256,256]{2,1,0:T(8,128)(2,1)S(1)}, bf16[2,256,256]{2,1,0:T(8,128)(2,1)S(1)}, u32[]{:S(2)}, u32[]{:S(2)}) collective-permute-start(bf16[2,256,256]{2,1,0:T(8,128)(2,1)S(1)} %get-tuple-element.19.refs_4_), channel_id=1, source_target_pairs={{0,32},{16,48},{32,0},{48,16},{64,96},{80,112},{96,64},{112,80},{1... | collective-permute-start | bytes 786440 | tf_op jit(solution)/shard_map/ppermute | solution.py:21
  111.8 4.4 %collective-permute-start.17 = (bf16[2,256,256]{2,1,0:T(8,128)(2,1)S(1)}, bf16[2,256,256]{2,1,0:T(8,128)(2,1)S(1)}, u32[]{:S(2)}, u32[]{:S(2)}) collective-permute-start(bf16[2,256,256]{2,1,0:T(8,128)(2,1)S(1)} %get-tuple-element.19.refs_4_), channel_id=1, source_target_pairs={{0,16},{16,0},{32,48},{48,32},{64,80},{80,64},{96,112},{112,96},{1... | collective-permute-start | bytes 786440 | tf_op jit(solution)/shard_map/ppermute | solution.py:21
  116.2 3.1 %collective-permute-start.18 = (bf16[2,256,256]{2,1,0:T(8,128)(2,1)S(1)}, bf16[2,256,256]{2,1,0:T(8,128)(2,1)S(1)}, u32[]{:S(2)}, u32[]{:S(2)}) collective-permute-start(bf16[2,256,256]{2,1,0:T(8,128)(2,1)S(1)} %get-tuple-element.19.refs_4_), channel_id=1, source_target_pairs={{0,4},{4,0},{8,12},{12,8},{1,5},{5,1},{9,13},{13,9},{2,6},{6,2},{1... | collective-permute-start | bytes 786440 | tf_op jit(solution)/shard_map/ppermute | solution.py:21
  119.3 1.8 %shard_map.116.refs_3_ = f32[2,256,256]{2,1,0:T(8,128)S(1)} custom-call(s32[11]{0:T(128)S(1)} %pad_add_fusion.refs_0_, f32[3,9]{1,0:T(4,128)S(1)} %pad_maximum_fusion.1.refs_1_, bf16[12,256,256]{2,1,0:T(8,128)(2,1)S(1)} %copy-done, bf16[2,256,256]{2,1,0:T(8,128)(2,1)S(1)} %copy-done.1, bf16[2,256,256]{2,1,0:T(8,128)(2,1)S(1)} %get-tuple-element.19.refs_4_, ...), custom_call_target="tpu_custom_call" | custom-call | flops 536870912 | bytes 4194456 | tf_op jit(solution)/shard_map/pallas_call | solution.py:178
  121.2 5.5 %collective-permute-done.15.refs_5_ = bf16[2,256,256]{2,1,0:T(8,128)(2,1)S(1)} collective-permute-done((bf16[2,256,256]{2,1,0:T(8,128)(2,1)S(1)}, bf16[2,256,256]{2,1,0:T(8,128)(2,1)S(1)}, u32[]{:S(2)}, u32[]{:S(2)}) %collective-permute-start.15) | collective-permute-done | bytes 262176 | tf_op jit(solution)/shard_map/ppermute | solution.py:31
  127.7 5.5 %collective-permute-done.16.refs_4_ = bf16[2,256,256]{2,1,0:T(8,128)(2,1)S(1)} collective-permute-done((bf16[2,256,256]{2,1,0:T(8,128)(2,1)S(1)}, bf16[2,256,256]{2,1,0:T(8,128)(2,1)S(1)}, u32[]{:S(2)}, u32[]{:S(2)}) %collective-permute-start.16) | collective-permute-done | bytes 262176 | tf_op jit(solution)/shard_map/ppermute | solution.py:21
  133.2 1.3 shard_map.118
  134.6 1.9 %collective-permute-start.19 = (bf16[2,128,256]{2,1,0:T(8,128)(2,1)S(1)}, bf16[2,128,256]{2,1,0:T(8,128)(2,1)S(1)}, u32[]{:S(2)}, u32[]{:S(2)}) collective-permute-start(bf16[2,128,256]{2,1,0:T(8,128)(2,1)S(1)} %get-tuple-element.21), channel_id=1, source_target_pairs={{0,1},{1,0},{2,3},{3,2},{4,5},{5,4},{6,7},{7,6},{8,9},{9,8},{10,11... | collective-permute-start | bytes 393224 | tf_op jit(solution)/shard_map/ppermute | solution.py:21
  136.5 6.4 %collective-permute-done.19 = bf16[2,128,256]{2,1,0:T(8,128)(2,1)S(1)} collective-permute-done((bf16[2,128,256]{2,1,0:T(8,128)(2,1)S(1)}, bf16[2,128,256]{2,1,0:T(8,128)(2,1)S(1)}, u32[]{:S(2)}, u32[]{:S(2)}) %collective-permute-start.19) | collective-permute-done | bytes 131104 | tf_op jit(solution)/shard_map/ppermute | solution.py:21
  (44 shorter events, 7.5 us)
Async XLA Ops:
  0.6 64.6 %copy-start = (bf16[12,256,256]{2,1,0:T(8,128)(2,1)S(1)}, bf16[12,256,256]{2,1,0:T(8,128)(2,1)}, u32[]{:S(2)}) copy-start(bf16[12,256,256]{2,1,0:T(8,128)(2,1)} %refs_2_.11) | copy-start | bytes 4718596
  0.6 64.6 %copy-start.1 = (bf16[2,256,256]{2,1,0:T(8,128)(2,1)S(1)}, bf16[2,256,256]{2,1,0:T(8,128)(2,1)}, u32[]{:S(2)}) copy-start(bf16[2,256,256]{2,1,0:T(8,128)(2,1)} %refs_3_.3) | copy-start | bytes 786436
  1.9 10.9 %collective-permute-start = (bf16[2,128,256]{2,1,0:T(8,128)(2,1)S(1)}, bf16[2,128,256]{2,1,0:T(8,128)(2,1)S(1)}, u32[]{:S(2)}, u32[]{:S(2)}) collective-permute-start(bf16[2,128,256]{2,1,0:T(8,128)(2,1)S(1)} %get-tuple-element.29), channel_id=1, source_target_pairs={{0,1},{1,0},{2,3},{3,2},{4,5},{5,4},{6,7},{7,6},{8,9},{9,8},{10,11... | collective-permute-start | bytes 393224 | tf_op jit(solution)/shard_map/ppermute | solution.py:21
  12.9 31.8 %collective-permute-start.5 = (bf16[2,256,256]{2,1,0:T(8,128)(2,1)S(1)}, bf16[2,256,256]{2,1,0:T(8,128)(2,1)S(1)}, u32[]{:S(2)}, u32[]{:S(2)}) collective-permute-start(bf16[2,256,256]{2,1,0:T(8,128)(2,1)S(1)} %maximum_select_fusion.refs_4_.refs_3_), channel_id=1, source_target_pairs={{0,64},{2,130},{16,80},{18,146},{32,96},{34,162},{48,112},{50,178}... | collective-permute-start | bytes 786440 | tf_op jit(solution)/shard_map/ppermute | solution.py:31
  21.8 34.9 %collective-permute-start.1 = (bf16[2,256,256]{2,1,0:T(8,128)(2,1)S(1)}, bf16[2,256,256]{2,1,0:T(8,128)(2,1)S(1)}, u32[]{:S(2)}, u32[]{:S(2)}) collective-permute-start(bf16[2,256,256]{2,1,0:T(8,128)(2,1)S(1)} %maximum_select_fusion.refs_4_.refs_3_), channel_id=1, source_target_pairs={{0,2},{2,0},{1,3},{3,1},{4,6},{6,4},{5,7},{7,5},{8,10},{10,8},{9,1... | collective-permute-start | bytes 786440 | tf_op jit(solution)/shard_map/ppermute | solution.py:21
  29.0 29.6 %collective-permute-start.2 = (bf16[2,256,256]{2,1,0:T(8,128)(2,1)S(1)}, bf16[2,256,256]{2,1,0:T(8,128)(2,1)S(1)}, u32[]{:S(2)}, u32[]{:S(2)}) collective-permute-start(bf16[2,256,256]{2,1,0:T(8,128)(2,1)S(1)} %maximum_select_fusion.refs_4_.refs_3_), channel_id=1, source_target_pairs={{0,1},{1,0},{2,3},{3,2},{4,5},{5,4},{6,7},{7,6},{8,9},{9,8},{10,11... | collective-permute-start | bytes 786440 | tf_op jit(solution)/shard_map/ppermute | solution.py:21
  31.5 29.1 %collective-permute-start.3 = (bf16[2,256,256]{2,1,0:T(8,128)(2,1)S(1)}, bf16[2,256,256]{2,1,0:T(8,128)(2,1)S(1)}, u32[]{:S(2)}, u32[]{:S(2)}) collective-permute-start(bf16[2,256,256]{2,1,0:T(8,128)(2,1)S(1)} %maximum_select_fusion.refs_4_.refs_3_), channel_id=1, source_target_pairs={{0,8},{4,12},{8,0},{12,4},{1,9},{5,13},{9,1},{13,5},{2,10},{6,14},... | collective-permute-start | bytes 786440 | tf_op jit(solution)/shard_map/ppermute | solution.py:21
  36.6 28.6 %collective-permute-start.4 = (bf16[2,256,256]{2,1,0:T(8,128)(2,1)S(1)}, bf16[2,256,256]{2,1,0:T(8,128)(2,1)S(1)}, u32[]{:S(2)}, u32[]{:S(2)}) collective-permute-start(bf16[2,256,256]{2,1,0:T(8,128)(2,1)S(1)} %maximum_select_fusion.refs_4_.refs_3_), channel_id=1, source_target_pairs={{0,256},{256,0},{1,257},{257,1},{2,258},{258,2},{3,259},{259,3},{4... | collective-permute-start | bytes 786440 | tf_op jit(solution)/shard_map/ppermute | solution.py:21
  44.8 22.3 %collective-permute-start.6 = (bf16[2,256,256]{2,1,0:T(8,128)(2,1)S(1)}, bf16[2,256,256]{2,1,0:T(8,128)(2,1)S(1)}, u32[]{:S(2)}, u32[]{:S(2)}) collective-permute-start(bf16[2,256,256]{2,1,0:T(8,128)(2,1)S(1)} %broadcast_select_fusion.1), channel_id=1, source_target_pairs={{0,192},{2,66},{16,208},{18,82},{32,224},{34,98},{48,240},{50,114}... | collective-permute-start | bytes 786440 | tf_op jit(solution)/shard_map/ppermute | solution.py:31
  56.7 15.0 %collective-permute-start.7 = (bf16[2,256,256]{2,1,0:T(8,128)(2,1)S(1)}, bf16[2,256,256]{2,1,0:T(8,128)(2,1)S(1)}, u32[]{:S(2)}, u32[]{:S(2)}) collective-permute-start(bf16[2,256,256]{2,1,0:T(8,128)(2,1)S(1)} %maximum_select_fusion.refs_4_.refs_3_), channel_id=1, source_target_pairs={{0,32},{16,48},{32,0},{48,16},{64,96},{80,112},{96,64},{112,80},{1... | collective-permute-start | bytes 786440 | tf_op jit(solution)/shard_map/ppermute | solution.py:21
  58.7 14.3 %collective-permute-start.8 = (bf16[2,256,256]{2,1,0:T(8,128)(2,1)S(1)}, bf16[2,256,256]{2,1,0:T(8,128)(2,1)S(1)}, u32[]{:S(2)}, u32[]{:S(2)}) collective-permute-start(bf16[2,256,256]{2,1,0:T(8,128)(2,1)S(1)} %maximum_select_fusion.refs_4_.refs_3_), channel_id=1, source_target_pairs={{0,16},{16,0},{32,48},{48,32},{64,80},{80,64},{96,112},{112,96},{1... | collective-permute-start | bytes 786440 | tf_op jit(solution)/shard_map/ppermute | solution.py:21
  60.6 12.4 %collective-permute-start.9 = (bf16[2,256,256]{2,1,0:T(8,128)(2,1)S(1)}, bf16[2,256,256]{2,1,0:T(8,128)(2,1)S(1)}, u32[]{:S(2)}, u32[]{:S(2)}) collective-permute-start(bf16[2,256,256]{2,1,0:T(8,128)(2,1)S(1)} %maximum_select_fusion.refs_4_.refs_3_), channel_id=1, source_target_pairs={{0,4},{4,0},{8,12},{12,8},{1,5},{5,1},{9,13},{13,9},{2,6},{6,2},{1... | collective-permute-start | bytes 786440 | tf_op jit(solution)/shard_map/ppermute | solution.py:21
  74.4 29.3 %collective-permute-start.14 = (bf16[2,256,256]{2,1,0:T(8,128)(2,1)S(1)}, bf16[2,256,256]{2,1,0:T(8,128)(2,1)S(1)}, u32[]{:S(2)}, u32[]{:S(2)}) collective-permute-start(bf16[2,256,256]{2,1,0:T(8,128)(2,1)S(1)} %get-tuple-element.19.refs_4_), channel_id=1, source_target_pairs={{0,64},{2,130},{16,80},{18,146},{32,96},{34,162},{48,112},{50,178}... | collective-permute-start | bytes 786440 | tf_op jit(solution)/shard_map/ppermute | solution.py:31
  79.4 26.3 %collective-permute-start.10 = (bf16[2,256,256]{2,1,0:T(8,128)(2,1)S(1)}, bf16[2,256,256]{2,1,0:T(8,128)(2,1)S(1)}, u32[]{:S(2)}, u32[]{:S(2)}) collective-permute-start(bf16[2,256,256]{2,1,0:T(8,128)(2,1)S(1)} %get-tuple-element.19.refs_4_), channel_id=1, source_target_pairs={{0,2},{2,0},{1,3},{3,1},{4,6},{6,4},{5,7},{7,5},{8,10},{10,8},{9,1... | collective-permute-start | bytes 786440 | tf_op jit(solution)/shard_map/ppermute | solution.py:21
  81.4 30.4 %collective-permute-start.11 = (bf16[2,256,256]{2,1,0:T(8,128)(2,1)S(1)}, bf16[2,256,256]{2,1,0:T(8,128)(2,1)S(1)}, u32[]{:S(2)}, u32[]{:S(2)}) collective-permute-start(bf16[2,256,256]{2,1,0:T(8,128)(2,1)S(1)} %get-tuple-element.19.refs_4_), channel_id=1, source_target_pairs={{0,1},{1,0},{2,3},{3,2},{4,5},{5,4},{6,7},{7,6},{8,9},{9,8},{10,11... | collective-permute-start | bytes 786440 | tf_op jit(solution)/shard_map/ppermute | solution.py:21
  84.5 31.7 %collective-permute-start.12 = (bf16[2,256,256]{2,1,0:T(8,128)(2,1)S(1)}, bf16[2,256,256]{2,1,0:T(8,128)(2,1)S(1)}, u32[]{:S(2)}, u32[]{:S(2)}) collective-permute-start(bf16[2,256,256]{2,1,0:T(8,128)(2,1)S(1)} %get-tuple-element.19.refs_4_), channel_id=1, source_target_pairs={{0,8},{4,12},{8,0},{12,4},{1,9},{5,13},{9,1},{13,5},{2,10},{6,14},... | collective-permute-start | bytes 786440 | tf_op jit(solution)/shard_map/ppermute | solution.py:21
  90.7 28.5 %collective-permute-start.13 = (bf16[2,256,256]{2,1,0:T(8,128)(2,1)S(1)}, bf16[2,256,256]{2,1,0:T(8,128)(2,1)S(1)}, u32[]{:S(2)}, u32[]{:S(2)}) collective-permute-start(bf16[2,256,256]{2,1,0:T(8,128)(2,1)S(1)} %get-tuple-element.19.refs_4_), channel_id=1, source_target_pairs={{0,256},{256,0},{1,257},{257,1},{2,258},{258,2},{3,259},{259,3},{4... | collective-permute-start | bytes 786440 | tf_op jit(solution)/shard_map/ppermute | solution.py:21
  103.8 22.8 %collective-permute-start.15 = (bf16[2,256,256]{2,1,0:T(8,128)(2,1)S(1)}, bf16[2,256,256]{2,1,0:T(8,128)(2,1)S(1)}, u32[]{:S(2)}, u32[]{:S(2)}) collective-permute-start(bf16[2,256,256]{2,1,0:T(8,128)(2,1)S(1)} %broadcast_select_fusion), channel_id=1, source_target_pairs={{0,192},{2,66},{16,208},{18,82},{32,224},{34,98},{48,240},{50,114}... | collective-permute-start | bytes 786440 | tf_op jit(solution)/shard_map/ppermute | solution.py:31
  105.7 27.5 %collective-permute-start.16 = (bf16[2,256,256]{2,1,0:T(8,128)(2,1)S(1)}, bf16[2,256,256]{2,1,0:T(8,128)(2,1)S(1)}, u32[]{:S(2)}, u32[]{:S(2)}) collective-permute-start(bf16[2,256,256]{2,1,0:T(8,128)(2,1)S(1)} %get-tuple-element.19.refs_4_), channel_id=1, source_target_pairs={{0,32},{16,48},{32,0},{48,16},{64,96},{80,112},{96,64},{112,80},{1... | collective-permute-start | bytes 786440 | tf_op jit(solution)/shard_map/ppermute | solution.py:21
  111.8 21.5 %collective-permute-start.17 = (bf16[2,256,256]{2,1,0:T(8,128)(2,1)S(1)}, bf16[2,256,256]{2,1,0:T(8,128)(2,1)S(1)}, u32[]{:S(2)}, u32[]{:S(2)}) collective-permute-start(bf16[2,256,256]{2,1,0:T(8,128)(2,1)S(1)} %get-tuple-element.19.refs_4_), channel_id=1, source_target_pairs={{0,16},{16,0},{32,48},{48,32},{64,80},{80,64},{96,112},{112,96},{1... | collective-permute-start | bytes 786440 | tf_op jit(solution)/shard_map/ppermute | solution.py:21
  116.2 17.1 %collective-permute-start.18 = (bf16[2,256,256]{2,1,0:T(8,128)(2,1)S(1)}, bf16[2,256,256]{2,1,0:T(8,128)(2,1)S(1)}, u32[]{:S(2)}, u32[]{:S(2)}) collective-permute-start(bf16[2,256,256]{2,1,0:T(8,128)(2,1)S(1)} %get-tuple-element.19.refs_4_), channel_id=1, source_target_pairs={{0,4},{4,0},{8,12},{12,8},{1,5},{5,1},{9,13},{13,9},{2,6},{6,2},{1... | collective-permute-start | bytes 786440 | tf_op jit(solution)/shard_map/ppermute | solution.py:21
  127.7 15.3 %copy-start.2 = (f32[2,128,256]{2,1,0:T(8,128)S(1)}, f32[2,128,256]{2,1,0:T(8,128)}, u32[]{:S(2)}) copy-start(f32[2,128,256]{2,1,0:T(8,128)} %param.11) | copy-start | bytes 786436
  127.7 15.3 %copy-start.3 = (f32[2,128,256]{2,1,0:T(8,128)S(1)}, f32[2,128,256]{2,1,0:T(8,128)}, u32[]{:S(2)}) copy-start(f32[2,128,256]{2,1,0:T(8,128)} %param.10) | copy-start | bytes 786436
  134.6 8.4 %collective-permute-start.19 = (bf16[2,128,256]{2,1,0:T(8,128)(2,1)S(1)}, bf16[2,128,256]{2,1,0:T(8,128)(2,1)S(1)}, u32[]{:S(2)}, u32[]{:S(2)}) collective-permute-start(bf16[2,128,256]{2,1,0:T(8,128)(2,1)S(1)} %get-tuple-element.21), channel_id=1, source_target_pairs={{0,1},{1,0},{2,3},{3,2},{4,5},{5,4},{6,7},{7,6},{8,9},{9,8},{10,11... | collective-permute-start | bytes 393224 | tf_op jit(solution)/shard_map/ppermute | solution.py:21

commit v9 on v7

--- a/solution.py
+++ b/solution.py
@@ -149,16 +149,16 @@
 
     def exchange(full):
         first = across(full, inward, outward)
-        own = across(full, None, inward)
+        z1 = swapped(full, "z", 1)
         core = swapped(full, "core", 1)
         z2 = swapped(full, "z", 2)
+        own = across(full, None, inward)
+        x2 = swapped(after(full, z1), "rep", 1)
+        x1 = swapped(after(full, core), "x_lo", 1)
         second = across(first, outward, inward)
-        z1 = swapped(after(full, first, core), "z", 1)
-        x2 = swapped(after(full, first, core), "rep", 1)
-        x1 = swapped(after(full, first, own), "x_lo", 1)
-        y2 = swapped(after(full, first, own), "y", 2)
-        y1 = swapped(after(full, first, z2, z1), "y", 1)
-        return {1: [core], 5: [z2]}, {6: [first, own], 7: [second], 4: [z1]}, {0: [x2], 8: [x1], 3: [y2], 2: [y1]}
+        y2 = swapped(after(full, first, x2), "y", 2)
+        y1 = swapped(after(full, first, x1), "y", 1)
+        return {1: [core], 4: [z1], 5: [z2], 8: [x1], 0: [x2], 6: [first, own]}, {7: [second]}, {3: [y2], 2: [y1]}
 
     def call(body, parts, outs, scratch, *operands):
         held = []

time: 158 us -> 149 us (0.943)
  the two profiles are of different devices: /device:TPU:1 before, /device:TPU:32 now
where the time goes in v9:
time: 149 us
  starting transfers between devices  104 us (70%)
  waiting for transfers between devices  28.8 us (19%)
  Pallas kernels  8.56 us (6%)
  other arithmetic  3.64 us (2%)
  between operations  2.42 us (2%)
    ppermute x16, starting transfers between devices, swapped(): return lax.ppermute(value, axis, pairs)  65.5 us
    ppermute x6, starting transfers between devices, across(): return lax.ppermute(value, ('z', 'core'), pairs)  38.9 us
    ppermute x16, waiting for transfers between devices, swapped(): return lax.ppermute(value, axis, pairs)  18.8 us
    ppermute x6, waiting for transfers between devices, across(): return lax.ppermute(value, ('z', 'core'), pairs)  9.94 us
    pallas_call x6, Pallas kernels, call(): pl.pallas_call(lambda *refs: body(counts, *refs), out_shape=outs, in_spec...  8.56 us
  transfers between devices with their start and end apart: 22, of which 7 were waited for; matrix products, arithmetic and copies ran while one was open for 1% of the time, Pallas kernels for 4%

profile of v9, /device:TPU:32, one launch (start us, length us, event | category | flops | bytes accessed | tf_op | source)
XLA Modules:
  0.0 148.5 jit_solution(9693651470741660102)
XLA Ops:
  0.7 1.2 convert_bitcast_fusion
  1.9 4.9 %collective-permute-start = (bf16[2,128,256]{2,1,0:T(8,128)(2,1)S(1)}, bf16[2,128,256]{2,1,0:T(8,128)(2,1)S(1)}, u32[]{:S(2)}, u32[]{:S(2)}) collective-permute-start(bf16[2,128,256]{2,1,0:T(8,128)(2,1)S(1)} %get-tuple-element.33), channel_id=1, source_target_pairs={{0,1},{1,0},{2,3},{3,2},{4,5},{5,4},{6,7},{7,6},{8,9},{9,8},{10,11... | collective-permute-start | bytes 393224 | tf_op jit(solution)/shard_map/ppermute | solution.py:21
  7.8 2.7 %collective-permute-done = bf16[2,128,256]{2,1,0:T(8,128)(2,1)S(1)} collective-permute-done((bf16[2,128,256]{2,1,0:T(8,128)(2,1)S(1)}, bf16[2,128,256]{2,1,0:T(8,128)(2,1)S(1)}, u32[]{:S(2)}, u32[]{:S(2)}) %collective-permute-start) | collective-permute-done | bytes 131104 | tf_op jit(solution)/shard_map/ppermute | solution.py:21
  10.7 1.9 %collective-permute-start.1 = (bf16[2,256,256]{2,1,0:T(8,128)(2,1)S(1)}, bf16[2,256,256]{2,1,0:T(8,128)(2,1)S(1)}, u32[]{:S(2)}, u32[]{:S(2)}) collective-permute-start(bf16[2,256,256]{2,1,0:T(8,128)(2,1)S(1)} %maximum_select_fusion.refs_4_.refs_3_), channel_id=1, source_target_pairs={{0,2},{2,0},{1,3},{3,1},{4,6},{6,4},{5,7},{7,5},{8,10},{10,8},{9,1... | collective-permute-start | bytes 786440 | tf_op jit(solution)/shard_map/ppermute | solution.py:21
  12.6 7.1 %collective-permute-start.2 = (bf16[2,256,256]{2,1,0:T(8,128)(2,1)S(1)}, bf16[2,256,256]{2,1,0:T(8,128)(2,1)S(1)}, u32[]{:S(2)}, u32[]{:S(2)}) collective-permute-start(bf16[2,256,256]{2,1,0:T(8,128)(2,1)S(1)} %maximum_select_fusion.refs_4_.refs_3_), channel_id=1, source_target_pairs={{0,16},{16,0},{32,48},{48,32},{64,80},{80,64},{96,112},{112,96},{1... | collective-permute-start | bytes 786440 | tf_op jit(solution)/shard_map/ppermute | solution.py:21
  19.9 4.0 %collective-permute-start.6 = (bf16[2,256,256]{2,1,0:T(8,128)(2,1)S(1)}, bf16[2,256,256]{2,1,0:T(8,128)(2,1)S(1)}, u32[]{:S(2)}, u32[]{:S(2)}) collective-permute-start(bf16[2,256,256]{2,1,0:T(8,128)(2,1)S(1)} %maximum_select_fusion.refs_4_.refs_3_), channel_id=1, source_target_pairs={{0,64},{2,194},{16,80},{18,210},{32,96},{34,226},{48,112},{50,242}... | collective-permute-start | bytes 786440 | tf_op jit(solution)/shard_map/ppermute | solution.py:31
  23.9 3.4 %collective-permute-start.4 = (bf16[2,256,256]{2,1,0:T(8,128)(2,1)S(1)}, bf16[2,256,256]{2,1,0:T(8,128)(2,1)S(1)}, u32[]{:S(2)}, u32[]{:S(2)}) collective-permute-start(bf16[2,256,256]{2,1,0:T(8,128)(2,1)S(1)} %maximum_select_fusion.refs_4_.refs_3_), channel_id=1, source_target_pairs={{0,256},{256,0},{1,257},{257,1},{2,258},{258,2},{3,259},{259,3},{4... | collective-permute-start | bytes 786440 | tf_op jit(solution)/shard_map/ppermute | solution.py:21
  27.3 4.6 %collective-permute-start.5 = (bf16[2,256,256]{2,1,0:T(8,128)(2,1)S(1)}, bf16[2,256,256]{2,1,0:T(8,128)(2,1)S(1)}, u32[]{:S(2)}, u32[]{:S(2)}) collective-permute-start(bf16[2,256,256]{2,1,0:T(8,128)(2,1)S(1)} %maximum_select_fusion.refs_4_.refs_3_), channel_id=1, source_target_pairs={{0,1},{1,0},{2,3},{3,2},{4,5},{5,4},{6,7},{7,6},{8,9},{9,8},{10,11... | collective-permute-start | bytes 786440 | tf_op jit(solution)/shard_map/ppermute | solution.py:21
  34.0 5.2 %collective-permute-start.3 = (bf16[2,256,256]{2,1,0:T(8,128)(2,1)S(1)}, bf16[2,256,256]{2,1,0:T(8,128)(2,1)S(1)}, u32[]{:S(2)}, u32[]{:S(2)}) collective-permute-start(bf16[2,256,256]{2,1,0:T(8,128)(2,1)S(1)} %maximum_select_fusion.refs_4_.refs_3_), channel_id=1, source_target_pairs={{0,32},{16,48},{32,0},{48,16},{64,96},{80,112},{96,64},{112,80},{1... | collective-permute-start | bytes 786440 | tf_op jit(solution)/shard_map/ppermute | solution.py:21
  39.9 13.7 %collective-permute-start.8 = (bf16[2,256,256]{2,1,0:T(8,128)(2,1)S(1)}, bf16[2,256,256]{2,1,0:T(8,128)(2,1)S(1)}, u32[]{:S(2)}, u32[]{:S(2)}) collective-permute-start(bf16[2,256,256]{2,1,0:T(8,128)(2,1)S(1)} %collective-permute-done.6.refs_10_), channel_id=1, source_target_pairs={{0,192},{2,66},{16,208},{18,82},{32,224},{34,98},{48,240},{50,114}... | collective-permute-start | bytes 786440 | tf_op jit(solution)/shard_map/ppermute | solution.py:31
  53.7 5.1 %collective-permute-start.9 = (bf16[2,256,256]{2,1,0:T(8,128)(2,1)S(1)}, bf16[2,256,256]{2,1,0:T(8,128)(2,1)S(1)}, u32[]{:S(2)}, u32[]{:S(2)}) collective-permute-start(bf16[2,256,256]{2,1,0:T(8,128)(2,1)S(1)} %maximum_select_fusion.refs_4_.refs_3_), channel_id=1, source_target_pairs={{0,8},{4,12},{8,0},{12,4},{1,9},{5,13},{9,1},{13,5},{2,10},{6,14},... | collective-permute-start | bytes 786440 | tf_op jit(solution)/shard_map/ppermute | solution.py:21
  58.8 2.6 %collective-permute-start.10 = (bf16[2,256,256]{2,1,0:T(8,128)(2,1)S(1)}, bf16[2,256,256]{2,1,0:T(8,128)(2,1)S(1)}, u32[]{:S(2)}, u32[]{:S(2)}) collective-permute-start(bf16[2,256,256]{2,1,0:T(8,128)(2,1)S(1)} %maximum_select_fusion.refs_4_.refs_3_), channel_id=1, source_target_pairs={{0,4},{4,0},{8,12},{12,8},{1,5},{5,1},{9,13},{13,9},{2,6},{6,2},{1... | collective-permute-start | bytes 786440 | tf_op jit(solution)/shard_map/ppermute | solution.py:21
  61.5 1.7 %collective-permute-done.3.refs_7_ = bf16[2,256,256]{2,1,0:T(8,128)(2,1)S(1)} collective-permute-done((bf16[2,256,256]{2,1,0:T(8,128)(2,1)S(1)}, bf16[2,256,256]{2,1,0:T(8,128)(2,1)S(1)}, u32[]{:S(2)}, u32[]{:S(2)}) %collective-permute-start.3) | collective-permute-done | bytes 262176 | tf_op jit(solution)/shard_map/ppermute | solution.py:21
  63.2 2.2 %shard_map.113.refs_3_ = f32[2,256,256]{2,1,0:T(8,128)S(1)} custom-call(s32[11]{0:T(128)S(1)} %pad_add_fusion.refs_0_, f32[3,9]{1,0:T(4,128)S(1)} %pad_maximum_fusion.1.refs_1_, bf16[12,256,256]{2,1,0:T(8,128)(2,1)S(1)} %copy-done, bf16[2,256,256]{2,1,0:T(8,128)(2,1)S(1)} %copy-done.1, bf16[2,256,256]{2,1,0:T(8,128)(2,1)S(1)} %maximum_select_fusion.refs_4_.refs_3_, ...), custom_call_target="tpu_custom_call" | custom-call | flops 805306368 | bytes 4456600 | tf_op jit(solution)/shard_map/pallas_call | solution.py:174
  65.4 9.9 %collective-permute-done.8.refs_4_ = bf16[2,256,256]{2,1,0:T(8,128)(2,1)S(1)} collective-permute-done((bf16[2,256,256]{2,1,0:T(8,128)(2,1)S(1)}, bf16[2,256,256]{2,1,0:T(8,128)(2,1)S(1)}, u32[]{:S(2)}, u32[]{:S(2)}) %collective-permute-start.8) | collective-permute-done | bytes 262176 | tf_op jit(solution)/shard_map/ppermute | solution.py:31
  76.2 1.2 shard_map.115
  77.4 1.9 %collective-permute-start.12 = (bf16[2,256,256]{2,1,0:T(8,128)(2,1)S(1)}, bf16[2,256,256]{2,1,0:T(8,128)(2,1)S(1)}, u32[]{:S(2)}, u32[]{:S(2)}) collective-permute-start(bf16[2,256,256]{2,1,0:T(8,128)(2,1)S(1)} %get-tuple-element.23.refs_4_), channel_id=1, source_target_pairs={{0,16},{16,0},{32,48},{48,32},{64,80},{80,64},{96,112},{112,96},{1... | collective-permute-start | bytes 786440 | tf_op jit(solution)/shard_map/ppermute | solution.py:21
  79.3 1.9 %collective-permute-start.11 = (bf16[2,256,256]{2,1,0:T(8,128)(2,1)S(1)}, bf16[2,256,256]{2,1,0:T(8,128)(2,1)S(1)}, u32[]{:S(2)}, u32[]{:S(2)}) collective-permute-start(bf16[2,256,256]{2,1,0:T(8,128)(2,1)S(1)} %get-tuple-element.23.refs_4_), channel_id=1, source_target_pairs={{0,2},{2,0},{1,3},{3,1},{4,6},{6,4},{5,7},{7,5},{8,10},{10,8},{9,1... | collective-permute-start | bytes 786440 | tf_op jit(solution)/shard_map/ppermute | solution.py:21
  81.2 1.9 %collective-permute-start.16 = (bf16[2,256,256]{2,1,0:T(8,128)(2,1)S(1)}, bf16[2,256,256]{2,1,0:T(8,128)(2,1)S(1)}, u32[]{:S(2)}, u32[]{:S(2)}) collective-permute-start(bf16[2,256,256]{2,1,0:T(8,128)(2,1)S(1)} %get-tuple-element.23.refs_4_), channel_id=1, source_target_pairs={{0,64},{2,194},{16,80},{18,210},{32,96},{34,226},{48,112},{50,242}... | collective-permute-start | bytes 786440 | tf_op jit(solution)/shard_map/ppermute | solution.py:31
  83.2 3.0 %collective-permute-done.12.refs_7_ = bf16[2,256,256]{2,1,0:T(8,128)(2,1)S(1)} collective-permute-done((bf16[2,256,256]{2,1,0:T(8,128)(2,1)S(1)}, bf16[2,256,256]{2,1,0:T(8,128)(2,1)S(1)}, u32[]{:S(2)}, u32[]{:S(2)}) %collective-permute-start.12) | collective-permute-done | bytes 262176 | tf_op jit(solution)/shard_map/ppermute | solution.py:21
  86.1 13.1 %collective-permute-start.15 = (bf16[2,256,256]{2,1,0:T(8,128)(2,1)S(1)}, bf16[2,256,256]{2,1,0:T(8,128)(2,1)S(1)}, u32[]{:S(2)}, u32[]{:S(2)}) collective-permute-start(bf16[2,256,256]{2,1,0:T(8,128)(2,1)S(1)} %get-tuple-element.23.refs_4_), channel_id=1, source_target_pairs={{0,1},{1,0},{2,3},{3,2},{4,5},{5,4},{6,7},{7,6},{8,9},{9,8},{10,11... | collective-permute-start | bytes 786440 | tf_op jit(solution)/shard_map/ppermute | solution.py:21
  99.2 1.9 %collective-permute-start.14 = (bf16[2,256,256]{2,1,0:T(8,128)(2,1)S(1)}, bf16[2,256,256]{2,1,0:T(8,128)(2,1)S(1)}, u32[]{:S(2)}, u32[]{:S(2)}) collective-permute-start(bf16[2,256,256]{2,1,0:T(8,128)(2,1)S(1)} %get-tuple-element.23.refs_4_), channel_id=1, source_target_pairs={{0,256},{256,0},{1,257},{257,1},{2,258},{258,2},{3,259},{259,3},{4... | collective-permute-start | bytes 786440 | tf_op jit(solution)/shard_map/ppermute | solution.py:21
  101.1 1.9 %collective-permute-start.13 = (bf16[2,256,256]{2,1,0:T(8,128)(2,1)S(1)}, bf16[2,256,256]{2,1,0:T(8,128)(2,1)S(1)}, u32[]{:S(2)}, u32[]{:S(2)}) collective-permute-start(bf16[2,256,256]{2,1,0:T(8,128)(2,1)S(1)} %get-tuple-element.23.refs_4_), channel_id=1, source_target_pairs={{0,32},{16,48},{32,0},{48,16},{64,96},{80,112},{96,64},{112,80},{1... | collective-permute-start | bytes 786440 | tf_op jit(solution)/shard_map/ppermute | solution.py:21
  103.8 17.9 %collective-permute-start.18 = (bf16[2,256,256]{2,1,0:T(8,128)(2,1)S(1)}, bf16[2,256,256]{2,1,0:T(8,128)(2,1)S(1)}, u32[]{:S(2)}, u32[]{:S(2)}) collective-permute-start(bf16[2,256,256]{2,1,0:T(8,128)(2,1)S(1)} %collective-permute-done.16.refs_11_), channel_id=1, source_target_pairs={{0,192},{2,66},{16,208},{18,82},{32,224},{34,98},{48,240},{50,114}... | collective-permute-start | bytes 786440 | tf_op jit(solution)/shard_map/ppermute | solution.py:31
  121.7 5.4 %collective-permute-start.19 = (bf16[2,256,256]{2,1,0:T(8,128)(2,1)S(1)}, bf16[2,256,256]{2,1,0:T(8,128)(2,1)S(1)}, u32[]{:S(2)}, u32[]{:S(2)}) collective-permute-start(bf16[2,256,256]{2,1,0:T(8,128)(2,1)S(1)} %get-tuple-element.23.refs_4_), channel_id=1, source_target_pairs={{0,8},{4,12},{8,0},{12,4},{1,9},{5,13},{9,1},{13,5},{2,10},{6,14},... | collective-permute-start | bytes 786440 | tf_op jit(solution)/shard_map/ppermute | solution.py:21
  127.2 2.6 %collective-permute-start.20 = (bf16[2,256,256]{2,1,0:T(8,128)(2,1)S(1)}, bf16[2,256,256]{2,1,0:T(8,128)(2,1)S(1)}, u32[]{:S(2)}, u32[]{:S(2)}) collective-permute-start(bf16[2,256,256]{2,1,0:T(8,128)(2,1)S(1)} %get-tuple-element.23.refs_4_), channel_id=1, source_target_pairs={{0,4},{4,0},{8,12},{12,8},{1,5},{5,1},{9,13},{13,9},{2,6},{6,2},{1... | collective-permute-start | bytes 786440 | tf_op jit(solution)/shard_map/ppermute | solution.py:21
  129.8 2.3 %shard_map.116.refs_3_ = f32[2,256,256]{2,1,0:T(8,128)S(1)} custom-call(s32[11]{0:T(128)S(1)} %pad_add_fusion.refs_0_, f32[3,9]{1,0:T(4,128)S(1)} %pad_maximum_fusion.1.refs_1_, bf16[12,256,256]{2,1,0:T(8,128)(2,1)S(1)} %copy-done, bf16[2,256,256]{2,1,0:T(8,128)(2,1)S(1)} %copy-done.1, bf16[2,256,256]{2,1,0:T(8,128)(2,1)S(1)} %get-tuple-element.23.refs_4_, ...), custom_call_target="tpu_custom_call" | custom-call | flops 805306368 | bytes 4980888 | tf_op jit(solution)/shard_map/pallas_call | solution.py:174
  133.9 4.1 %collective-permute-done.20.refs_5_ = bf16[2,256,256]{2,1,0:T(8,128)(2,1)S(1)} collective-permute-done((bf16[2,256,256]{2,1,0:T(8,128)(2,1)S(1)}, bf16[2,256,256]{2,1,0:T(8,128)(2,1)S(1)}, u32[]{:S(2)}, u32[]{:S(2)}) %collective-permute-start.20) | collective-permute-done | bytes 262176 | tf_op jit(solution)/shard_map/ppermute | solution.py:21
  138.0 1.1 shard_map.118
  139.2 1.9 %collective-permute-start.21 = (bf16[2,128,256]{2,1,0:T(8,128)(2,1)S(1)}, bf16[2,128,256]{2,1,0:T(8,128)(2,1)S(1)}, u32[]{:S(2)}, u32[]{:S(2)}) collective-permute-start(bf16[2,128,256]{2,1,0:T(8,128)(2,1)S(1)} %get-tuple-element.25), channel_id=1, source_target_pairs={{0,1},{1,0},{2,3},{3,2},{4,5},{5,4},{6,7},{7,6},{8,9},{9,8},{10,11... | collective-permute-start | bytes 393224 | tf_op jit(solution)/shard_map/ppermute | solution.py:21
  141.1 6.4 %collective-permute-done.21 = bf16[2,128,256]{2,1,0:T(8,128)(2,1)S(1)} collective-permute-done((bf16[2,128,256]{2,1,0:T(8,128)(2,1)S(1)}, bf16[2,128,256]{2,1,0:T(8,128)(2,1)S(1)}, u32[]{:S(2)}, u32[]{:S(2)}) %collective-permute-start.21) | collective-permute-done | bytes 131104 | tf_op jit(solution)/shard_map/ppermute | solution.py:21
  147.6 0.9 select_add_fusion
  (54 shorter events, 6.3 us)
Async XLA Ops:
  0.6 19.1 %copy-start.7 = (f32[12]{0:T(128)S(1)}, f32[12]{0:T(128)}, u32[]{:S(2)}) copy-start(f32[12]{0:T(128)} %param.14) | copy-start | bytes 148
  0.6 19.1 %copy-start.4 = (s32[2,12]{1,0:T(2,128)S(1)}, s32[2,12]{1,0:T(2,128)}, u32[]{:S(2)}) copy-start(s32[2,12]{1,0:T(2,128)} %param.17) | copy-start | bytes 292
  0.7 19.2 %copy-start.5 = (f32[12]{0:T(128)S(1)}, f32[12]{0:T(128)}, u32[]{:S(2)}) copy-start(f32[12]{0:T(128)} %param.16) | copy-start | bytes 148
  0.7 19.2 %copy-start.6 = (f32[12]{0:T(128)S(1)}, f32[12]{0:T(128)}, u32[]{:S(2)}) copy-start(f32[12]{0:T(128)} %param.15) | copy-start | bytes 148
  0.7 62.5 %copy-start = (bf16[12,256,256]{2,1,0:T(8,128)(2,1)S(1)}, bf16[12,256,256]{2,1,0:T(8,128)(2,1)}, u32[]{:S(2)}) copy-start(bf16[12,256,256]{2,1,0:T(8,128)(2,1)} %refs_2_.11) | copy-start | bytes 4718596
  0.7 62.5 %copy-start.1 = (bf16[2,256,256]{2,1,0:T(8,128)(2,1)S(1)}, bf16[2,256,256]{2,1,0:T(8,128)(2,1)}, u32[]{:S(2)}) copy-start(bf16[2,256,256]{2,1,0:T(8,128)(2,1)} %refs_3_.3) | copy-start | bytes 786436
  1.9 8.6 %collective-permute-start = (bf16[2,128,256]{2,1,0:T(8,128)(2,1)S(1)}, bf16[2,128,256]{2,1,0:T(8,128)(2,1)S(1)}, u32[]{:S(2)}, u32[]{:S(2)}) collective-permute-start(bf16[2,128,256]{2,1,0:T(8,128)(2,1)S(1)} %get-tuple-element.33), channel_id=1, source_target_pairs={{0,1},{1,0},{2,3},{3,2},{4,5},{5,4},{6,7},{7,6},{8,9},{9,8},{10,11... | collective-permute-start | bytes 393224 | tf_op jit(solution)/shard_map/ppermute | solution.py:21
  10.7 13.2 %collective-permute-start.1 = (bf16[2,256,256]{2,1,0:T(8,128)(2,1)S(1)}, bf16[2,256,256]{2,1,0:T(8,128)(2,1)S(1)}, u32[]{:S(2)}, u32[]{:S(2)}) collective-permute-start(bf16[2,256,256]{2,1,0:T(8,128)(2,1)S(1)} %maximum_select_fusion.refs_4_.refs_3_), channel_id=1, source_target_pairs={{0,2},{2,0},{1,3},{3,1},{4,6},{6,4},{5,7},{7,5},{8,10},{10,8},{9,1... | collective-permute-start | bytes 786440 | tf_op jit(solution)/shard_map/ppermute | solution.py:21
  12.6 14.7 %collective-permute-start.2 = (bf16[2,256,256]{2,1,0:T(8,128)(2,1)S(1)}, bf16[2,256,256]{2,1,0:T(8,128)(2,1)S(1)}, u32[]{:S(2)}, u32[]{:S(2)}) collective-permute-start(bf16[2,256,256]{2,1,0:T(8,128)(2,1)S(1)} %maximum_select_fusion.refs_4_.refs_3_), channel_id=1, source_target_pairs={{0,16},{16,0},{32,48},{48,32},{64,80},{80,64},{96,112},{112,96},{1... | collective-permute-start | bytes 786440 | tf_op jit(solution)/shard_map/ppermute | solution.py:21
  19.9 20.0 %collective-permute-start.6 = (bf16[2,256,256]{2,1,0:T(8,128)(2,1)S(1)}, bf16[2,256,256]{2,1,0:T(8,128)(2,1)S(1)}, u32[]{:S(2)}, u32[]{:S(2)}) collective-permute-start(bf16[2,256,256]{2,1,0:T(8,128)(2,1)S(1)} %maximum_select_fusion.refs_4_.refs_3_), channel_id=1, source_target_pairs={{0,64},{2,194},{16,80},{18,210},{32,96},{34,226},{48,112},{50,242}... | collective-permute-start | bytes 786440 | tf_op jit(solution)/shard_map/ppermute | solution.py:31
  23.9 34.9 %collective-permute-start.4 = (bf16[2,256,256]{2,1,0:T(8,128)(2,1)S(1)}, bf16[2,256,256]{2,1,0:T(8,128)(2,1)S(1)}, u32[]{:S(2)}, u32[]{:S(2)}) collective-permute-start(bf16[2,256,256]{2,1,0:T(8,128)(2,1)S(1)} %maximum_select_fusion.refs_4_.refs_3_), channel_id=1, source_target_pairs={{0,256},{256,0},{1,257},{257,1},{2,258},{258,2},{3,259},{259,3},{4... | collective-permute-start | bytes 786440 | tf_op jit(solution)/shard_map/ppermute | solution.py:21
  27.3 26.3 %collective-permute-start.5 = (bf16[2,256,256]{2,1,0:T(8,128)(2,1)S(1)}, bf16[2,256,256]{2,1,0:T(8,128)(2,1)S(1)}, u32[]{:S(2)}, u32[]{:S(2)}) collective-permute-start(bf16[2,256,256]{2,1,0:T(8,128)(2,1)S(1)} %maximum_select_fusion.refs_4_.refs_3_), channel_id=1, source_target_pairs={{0,1},{1,0},{2,3},{3,2},{4,5},{5,4},{6,7},{7,6},{8,9},{9,8},{10,11... | collective-permute-start | bytes 786440 | tf_op jit(solution)/shard_map/ppermute | solution.py:21
  34.0 29.1 %collective-permute-start.3 = (bf16[2,256,256]{2,1,0:T(8,128)(2,1)S(1)}, bf16[2,256,256]{2,1,0:T(8,128)(2,1)S(1)}, u32[]{:S(2)}, u32[]{:S(2)}) collective-permute-start(bf16[2,256,256]{2,1,0:T(8,128)(2,1)S(1)} %maximum_select_fusion.refs_4_.refs_3_), channel_id=1, source_target_pairs={{0,32},{16,48},{32,0},{48,16},{64,96},{80,112},{96,64},{112,80},{1... | collective-permute-start | bytes 786440 | tf_op jit(solution)/shard_map/ppermute | solution.py:21
  39.2 23.9 %collective-permute-start.7 = (bf16[2,256,256]{2,1,0:T(8,128)(2,1)S(1)}, bf16[2,256,256]{2,1,0:T(8,128)(2,1)S(1)}, u32[]{:S(2)}, u32[]{:S(2)}) collective-permute-start(bf16[2,256,256]{2,1,0:T(8,128)(2,1)S(1)} %maximum_select_fusion.refs_4_.refs_3_), channel_id=1, source_target_pairs={{2,66},{18,82},{34,98},{50,114},{66,2},{82,18},{98,34},{114,50},{1... | collective-permute-start | bytes 786440 | tf_op jit(solution)/shard_map/ppermute | solution.py:31
  39.9 35.4 %collective-permute-start.8 = (bf16[2,256,256]{2,1,0:T(8,128)(2,1)S(1)}, bf16[2,256,256]{2,1,0:T(8,128)(2,1)S(1)}, u32[]{:S(2)}, u32[]{:S(2)}) collective-permute-start(bf16[2,256,256]{2,1,0:T(8,128)(2,1)S(1)} %collective-permute-done.6.refs_10_), channel_id=1, source_target_pairs={{0,192},{2,66},{16,208},{18,82},{32,224},{34,98},{48,240},{50,114}... | collective-permute-start | bytes 786440 | tf_op jit(solution)/shard_map/ppermute | solution.py:31
  53.7 22.5 %collective-permute-start.9 = (bf16[2,256,256]{2,1,0:T(8,128)(2,1)S(1)}, bf16[2,256,256]{2,1,0:T(8,128)(2,1)S(1)}, u32[]{:S(2)}, u32[]{:S(2)}) collective-permute-start(bf16[2,256,256]{2,1,0:T(8,128)(2,1)S(1)} %maximum_select_fusion.refs_4_.refs_3_), channel_id=1, source_target_pairs={{0,8},{4,12},{8,0},{12,4},{1,9},{5,13},{9,1},{13,5},{2,10},{6,14},... | collective-permute-start | bytes 786440 | tf_op jit(solution)/shard_map/ppermute | solution.py:21
  58.8 17.4 %collective-permute-start.10 = (bf16[2,256,256]{2,1,0:T(8,128)(2,1)S(1)}, bf16[2,256,256]{2,1,0:T(8,128)(2,1)S(1)}, u32[]{:S(2)}, u32[]{:S(2)}) collective-permute-start(bf16[2,256,256]{2,1,0:T(8,128)(2,1)S(1)} %maximum_select_fusion.refs_4_.refs_3_), channel_id=1, source_target_pairs={{0,4},{4,0},{8,12},{12,8},{1,5},{5,1},{9,13},{13,9},{2,6},{6,2},{1... | collective-permute-start | bytes 786440 | tf_op jit(solution)/shard_map/ppermute | solution.py:21
  77.4 8.7 %collective-permute-start.12 = (bf16[2,256,256]{2,1,0:T(8,128)(2,1)S(1)}, bf16[2,256,256]{2,1,0:T(8,128)(2,1)S(1)}, u32[]{:S(2)}, u32[]{:S(2)}) collective-permute-start(bf16[2,256,256]{2,1,0:T(8,128)(2,1)S(1)} %get-tuple-element.23.refs_4_), channel_id=1, source_target_pairs={{0,16},{16,0},{32,48},{48,32},{64,80},{80,64},{96,112},{112,96},{1... | collective-permute-start | bytes 786440 | tf_op jit(solution)/shard_map/ppermute | solution.py:21
  79.3 19.9 %collective-permute-start.11 = (bf16[2,256,256]{2,1,0:T(8,128)(2,1)S(1)}, bf16[2,256,256]{2,1,0:T(8,128)(2,1)S(1)}, u32[]{:S(2)}, u32[]{:S(2)}) collective-permute-start(bf16[2,256,256]{2,1,0:T(8,128)(2,1)S(1)} %get-tuple-element.23.refs_4_), channel_id=1, source_target_pairs={{0,2},{2,0},{1,3},{3,1},{4,6},{6,4},{5,7},{7,5},{8,10},{10,8},{9,1... | collective-permute-start | bytes 786440 | tf_op jit(solution)/shard_map/ppermute | solution.py:21
  81.2 22.5 %collective-permute-start.16 = (bf16[2,256,256]{2,1,0:T(8,128)(2,1)S(1)}, bf16[2,256,256]{2,1,0:T(8,128)(2,1)S(1)}, u32[]{:S(2)}, u32[]{:S(2)}) collective-permute-start(bf16[2,256,256]{2,1,0:T(8,128)(2,1)S(1)} %get-tuple-element.23.refs_4_), channel_id=1, source_target_pairs={{0,64},{2,194},{16,80},{18,210},{32,96},{34,226},{48,112},{50,242}... | collective-permute-start | bytes 786440 | tf_op jit(solution)/shard_map/ppermute | solution.py:31
  86.1 35.6 %collective-permute-start.15 = (bf16[2,256,256]{2,1,0:T(8,128)(2,1)S(1)}, bf16[2,256,256]{2,1,0:T(8,128)(2,1)S(1)}, u32[]{:S(2)}, u32[]{:S(2)}) collective-permute-start(bf16[2,256,256]{2,1,0:T(8,128)(2,1)S(1)} %get-tuple-element.23.refs_4_), channel_id=1, source_target_pairs={{0,1},{1,0},{2,3},{3,2},{4,5},{5,4},{6,7},{7,6},{8,9},{9,8},{10,11... | collective-permute-start | bytes 786440 | tf_op jit(solution)/shard_map/ppermute | solution.py:21
  99.2 27.9 %collective-permute-start.14 = (bf16[2,256,256]{2,1,0:T(8,128)(2,1)S(1)}, bf16[2,256,256]{2,1,0:T(8,128)(2,1)S(1)}, u32[]{:S(2)}, u32[]{:S(2)}) collective-permute-start(bf16[2,256,256]{2,1,0:T(8,128)(2,1)S(1)} %get-tuple-element.23.refs_4_), channel_id=1, source_target_pairs={{0,256},{256,0},{1,257},{257,1},{2,258},{258,2},{3,259},{259,3},{4... | collective-permute-start | bytes 786440 | tf_op jit(solution)/shard_map/ppermute | solution.py:21
  101.1 28.6 %collective-permute-start.13 = (bf16[2,256,256]{2,1,0:T(8,128)(2,1)S(1)}, bf16[2,256,256]{2,1,0:T(8,128)(2,1)S(1)}, u32[]{:S(2)}, u32[]{:S(2)}) collective-permute-start(bf16[2,256,256]{2,1,0:T(8,128)(2,1)S(1)} %get-tuple-element.23.refs_4_), channel_id=1, source_target_pairs={{0,32},{16,48},{32,0},{48,16},{64,96},{80,112},{96,64},{112,80},{1... | collective-permute-start | bytes 786440 | tf_op jit(solution)/shard_map/ppermute | solution.py:21
  103.1 26.7 %collective-permute-start.17 = (bf16[2,256,256]{2,1,0:T(8,128)(2,1)S(1)}, bf16[2,256,256]{2,1,0:T(8,128)(2,1)S(1)}, u32[]{:S(2)}, u32[]{:S(2)}) collective-permute-start(bf16[2,256,256]{2,1,0:T(8,128)(2,1)S(1)} %get-tuple-element.23.refs_4_), channel_id=1, source_target_pairs={{2,66},{18,82},{34,98},{50,114},{66,2},{82,18},{98,34},{114,50},{1... | collective-permute-start | bytes 786440 | tf_op jit(solution)/shard_map/ppermute | solution.py:31
  103.8 28.3 %collective-permute-start.18 = (bf16[2,256,256]{2,1,0:T(8,128)(2,1)S(1)}, bf16[2,256,256]{2,1,0:T(8,128)(2,1)S(1)}, u32[]{:S(2)}, u32[]{:S(2)}) collective-permute-start(bf16[2,256,256]{2,1,0:T(8,128)(2,1)S(1)} %collective-permute-done.16.refs_11_), channel_id=1, source_target_pairs={{0,192},{2,66},{16,208},{18,82},{32,224},{34,98},{48,240},{50,114}... | collective-permute-start | bytes 786440 | tf_op jit(solution)/shard_map/ppermute | solution.py:31
  121.7 12.2 %collective-permute-start.19 = (bf16[2,256,256]{2,1,0:T(8,128)(2,1)S(1)}, bf16[2,256,256]{2,1,0:T(8,128)(2,1)S(1)}, u32[]{:S(2)}, u32[]{:S(2)}) collective-permute-start(bf16[2,256,256]{2,1,0:T(8,128)(2,1)S(1)} %get-tuple-element.23.refs_4_), channel_id=1, source_target_pairs={{0,8},{4,12},{8,0},{12,4},{1,9},{5,13},{9,1},{13,5},{2,10},{6,14},... | collective-permute-start | bytes 786440 | tf_op jit(solution)/shard_map/ppermute | solution.py:21
  127.2 10.9 %collective-permute-start.20 = (bf16[2,256,256]{2,1,0:T(8,128)(2,1)S(1)}, bf16[2,256,256]{2,1,0:T(8,128)(2,1)S(1)}, u32[]{:S(2)}, u32[]{:S(2)}) collective-permute-start(bf16[2,256,256]{2,1,0:T(8,128)(2,1)S(1)} %get-tuple-element.23.refs_4_), channel_id=1, source_target_pairs={{0,4},{4,0},{8,12},{12,8},{1,5},{5,1},{9,13},{13,9},{2,6},{6,2},{1... | collective-permute-start | bytes 786440 | tf_op jit(solution)/shard_map/ppermute | solution.py:21
  133.0 14.6 %copy-start.2 = (f32[2,128,256]{2,1,0:T(8,128)S(1)}, f32[2,128,256]{2,1,0:T(8,128)}, u32[]{:S(2)}) copy-start(f32[2,128,256]{2,1,0:T(8,128)} %param.11) | copy-start | bytes 786436
  133.0 14.6 %copy-start.3 = (f32[2,128,256]{2,1,0:T(8,128)S(1)}, f32[2,128,256]{2,1,0:T(8,128)}, u32[]{:S(2)}) copy-start(f32[2,128,256]{2,1,0:T(8,128)} %param.10) | copy-start | bytes 786436
  139.2 8.4 %collective-permute-start.21 = (bf16[2,128,256]{2,1,0:T(8,128)(2,1)S(1)}, bf16[2,128,256]{2,1,0:T(8,128)(2,1)S(1)}, u32[]{:S(2)}, u32[]{:S(2)}) collective-permute-start(bf16[2,128,256]{2,1,0:T(8,128)(2,1)S(1)} %get-tuple-element.25), channel_id=1, source_target_pairs={{0,1},{1,0},{2,3},{3,2},{4,5},{5,4},{6,7},{7,6},{8,9},{9,8},{10,11... | collective-permute-start | bytes 393224 | tf_op jit(solution)/shard_map/ppermute | solution.py:21

commit v10 on v5

--- a/solution.py
+++ b/solution.py
@@ -158,11 +158,11 @@
         z2 = swapped(full, "z", 2)
         x2 = swapped(full, "rep", 1)
         y2 = swapped(full, "y", 2)
-        z1 = swapped(after(full, first, core), "z", 1)
-        x1 = swapped(after(full, first, x2), "x_lo", 1)
-        y1 = swapped(after(full, first, z2), "y", 1)
         second = across(jnp.where(on_first, first, full), outward, inward)
-        return {1: [core], 5: [z2], 0: [x2], 3: [y2]}, {6: [first, second], 7: [second, first]}, {4: [z1], 8: [x1], 2: [y1]}
+        x1 = swapped(after(full, first, core), "x_lo", 1)
+        y1 = swapped(after(full, first, x2), "y", 1)
+        z1 = swapped(after(full, first, y2), "z", 1)
+        return {1: [core], 0: [x2], 3: [y2]}, {6: [first, second], 7: [second, first]}, {5: [z2], 8: [x1], 2: [y1], 4: [z1]}
 
     def call(body, parts, outs, scratch, *operands):
         held = []

time: 141 us -> 153 us (1.085)
  waiting for transfers between devices: 16.8 us -> 33.6 us
  starting transfers between devices: 106 us -> 101 us
    ppermute x16, starting transfers between devices: 88.5 us -> 74.1 us  [swapped(): return lax.ppermute(value, axis, pairs)]
    ppermute x4, waiting for transfers between devices: 4.31 us -> 13.7 us  [across(): return lax.ppermute(value, ('z', 'core'), pairs)]
    ppermute x4, starting transfers between devices: 17.8 us -> 27.2 us  [across(): return lax.ppermute(value, ('z', 'core'), pairs)]
    ppermute x16, waiting for transfers between devices: 12.5 us -> 19.9 us  [swapped(): return lax.ppermute(value, axis, pairs)]
  transfers between devices with their start and end apart: 20 -> 20, of which waited for: 6 -> 7; matrix products, arithmetic and copies ran while one was open for 3% -> 3% of each run, Pallas kernels for 4% -> 4%
where the time goes in v10:
time: 153 us; the launch traced here: 152 us
  starting transfers between devices  101 us (66%)
  waiting for transfers between devices  33.6 us (22%)
  Pallas kernels  8.49 us (6%)
  other arithmetic  5.77 us (4%)
  between operations  2.35 us (2%)
    ppermute x16, starting transfers between devices, swapped(): return lax.ppermute(value, axis, pairs)  74.1 us
    ppermute x4, starting transfers between devices, across(): return lax.ppermute(value, ('z', 'core'), pairs)  27.2 us
    ppermute x16, waiting for transfers between devices, swapped(): return lax.ppermute(value, axis, pairs)  19.9 us
    ppermute x4, waiting for transfers between devices, across(): return lax.ppermute(value, ('z', 'core'), pairs)  13.7 us
    pallas_call x6, Pallas kernels, call(): pl.pallas_call(lambda *refs: body(counts, *refs), out_shape=outs, in_spec...  8.49 us
  transfers between devices with their start and end apart: 20, of which 7 were waited for; matrix products, arithmetic and copies ran while one was open for 3% of the time, Pallas kernels for 4%

profile of v10, /device:TPU:2, one launch (start us, length us, event | category | flops | bytes accessed | tf_op | source)
XLA Modules:
  0.0 152.3 jit_solution(6005349939398300605)
XLA Ops:
  0.7 1.2 convert_bitcast_fusion
  1.9 4.0 %collective-permute-start = (bf16[2,128,256]{2,1,0:T(8,128)(2,1)S(1)}, bf16[2,128,256]{2,1,0:T(8,128)(2,1)S(1)}, u32[]{:S(2)}, u32[]{:S(2)}) collective-permute-start(bf16[2,128,256]{2,1,0:T(8,128)(2,1)S(1)} %get-tuple-element.29), channel_id=1, source_target_pairs={{0,1},{1,0},{2,3},{3,2},{4,5},{5,4},{6,7},{7,6},{8,9},{9,8},{10,11... | collective-permute-start | bytes 393224 | tf_op jit(solution)/shard_map/ppermute | solution.py:21
  9.1 1.4 collective-permute-done
  10.6 9.1 %collective-permute-start.4 = (bf16[2,256,256]{2,1,0:T(8,128)(2,1)S(1)}, bf16[2,256,256]{2,1,0:T(8,128)(2,1)S(1)}, u32[]{:S(2)}, u32[]{:S(2)}) collective-permute-start(bf16[2,256,256]{2,1,0:T(8,128)(2,1)S(1)} %maximum_select_fusion.refs_4_.refs_3_), channel_id=1, source_target_pairs={{0,64},{2,130},{16,80},{18,146},{32,96},{34,162},{48,112},{50,178}... | collective-permute-start | bytes 786440 | tf_op jit(solution)/shard_map/ppermute | solution.py:31
  21.8 7.2 %collective-permute-start.1 = (bf16[2,256,256]{2,1,0:T(8,128)(2,1)S(1)}, bf16[2,256,256]{2,1,0:T(8,128)(2,1)S(1)}, u32[]{:S(2)}, u32[]{:S(2)}) collective-permute-start(bf16[2,256,256]{2,1,0:T(8,128)(2,1)S(1)} %maximum_select_fusion.refs_4_.refs_3_), channel_id=1, source_target_pairs={{0,2},{2,0},{1,3},{3,1},{4,6},{6,4},{5,7},{7,5},{8,10},{10,8},{9,1... | collective-permute-start | bytes 786440 | tf_op jit(solution)/shard_map/ppermute | solution.py:21
  29.0 4.0 %collective-permute-start.2 = (bf16[2,256,256]{2,1,0:T(8,128)(2,1)S(1)}, bf16[2,256,256]{2,1,0:T(8,128)(2,1)S(1)}, u32[]{:S(2)}, u32[]{:S(2)}) collective-permute-start(bf16[2,256,256]{2,1,0:T(8,128)(2,1)S(1)} %maximum_select_fusion.refs_4_.refs_3_), channel_id=1, source_target_pairs={{0,1},{1,0},{2,3},{3,2},{4,5},{5,4},{6,7},{7,6},{8,9},{9,8},{10,11... | collective-permute-start | bytes 786440 | tf_op jit(solution)/shard_map/ppermute | solution.py:21
  33.1 5.1 %collective-permute-start.3 = (bf16[2,256,256]{2,1,0:T(8,128)(2,1)S(1)}, bf16[2,256,256]{2,1,0:T(8,128)(2,1)S(1)}, u32[]{:S(2)}, u32[]{:S(2)}) collective-permute-start(bf16[2,256,256]{2,1,0:T(8,128)(2,1)S(1)} %maximum_select_fusion.refs_4_.refs_3_), channel_id=1, source_target_pairs={{0,8},{4,12},{8,0},{12,4},{1,9},{5,13},{9,1},{13,5},{2,10},{6,14},... | collective-permute-start | bytes 786440 | tf_op jit(solution)/shard_map/ppermute | solution.py:21
  38.2 3.4 %collective-permute-start.6 = (bf16[2,256,256]{2,1,0:T(8,128)(2,1)S(1)}, bf16[2,256,256]{2,1,0:T(8,128)(2,1)S(1)}, u32[]{:S(2)}, u32[]{:S(2)}) collective-permute-start(bf16[2,256,256]{2,1,0:T(8,128)(2,1)S(1)} %maximum_select_fusion.refs_4_.refs_3_), channel_id=1, source_target_pairs={{0,32},{16,48},{32,0},{48,16},{64,96},{80,112},{96,64},{112,80},{1... | collective-permute-start | bytes 786440 | tf_op jit(solution)/shard_map/ppermute | solution.py:21
  41.6 2.2 %collective-permute-done.4.refs_4_ = bf16[2,256,256]{2,1,0:T(8,128)(2,1)S(1)} collective-permute-done((bf16[2,256,256]{2,1,0:T(8,128)(2,1)S(1)}, bf16[2,256,256]{2,1,0:T(8,128)(2,1)S(1)}, u32[]{:S(2)}, u32[]{:S(2)}) %collective-permute-start.4) | collective-permute-done | bytes 262176 | tf_op jit(solution)/shard_map/ppermute | solution.py:31
  43.9 6.6 %collective-permute-start.5 = (bf16[2,256,256]{2,1,0:T(8,128)(2,1)S(1)}, bf16[2,256,256]{2,1,0:T(8,128)(2,1)S(1)}, u32[]{:S(2)}, u32[]{:S(2)}) collective-permute-start(bf16[2,256,256]{2,1,0:T(8,128)(2,1)S(1)} %broadcast_select_fusion.1), channel_id=1, source_target_pairs={{0,192},{2,66},{16,208},{18,82},{32,224},{34,98},{48,240},{50,114}... | collective-permute-start | bytes 786440 | tf_op jit(solution)/shard_map/ppermute | solution.py:31
  50.4 2.1 %collective-permute-start.7 = (bf16[2,256,256]{2,1,0:T(8,128)(2,1)S(1)}, bf16[2,256,256]{2,1,0:T(8,128)(2,1)S(1)}, u32[]{:S(2)}, u32[]{:S(2)}) collective-permute-start(bf16[2,256,256]{2,1,0:T(8,128)(2,1)S(1)} %maximum_select_fusion.refs_4_.refs_3_), channel_id=1, source_target_pairs={{0,256},{256,0},{1,257},{257,1},{2,258},{258,2},{3,259},{259,3},{4... | collective-permute-start | bytes 786440 | tf_op jit(solution)/shard_map/ppermute | solution.py:21
  52.5 4.1 %collective-permute-start.8 = (bf16[2,256,256]{2,1,0:T(8,128)(2,1)S(1)}, bf16[2,256,256]{2,1,0:T(8,128)(2,1)S(1)}, u32[]{:S(2)}, u32[]{:S(2)}) collective-permute-start(bf16[2,256,256]{2,1,0:T(8,128)(2,1)S(1)} %maximum_select_fusion.refs_4_.refs_3_), channel_id=1, source_target_pairs={{0,4},{4,0},{8,12},{12,8},{1,5},{5,1},{9,13},{13,9},{2,6},{6,2},{1... | collective-permute-start | bytes 786440 | tf_op jit(solution)/shard_map/ppermute | solution.py:21
  56.7 1.9 %collective-permute-start.9 = (bf16[2,256,256]{2,1,0:T(8,128)(2,1)S(1)}, bf16[2,256,256]{2,1,0:T(8,128)(2,1)S(1)}, u32[]{:S(2)}, u32[]{:S(2)}) collective-permute-start(bf16[2,256,256]{2,1,0:T(8,128)(2,1)S(1)} %maximum_select_fusion.refs_4_.refs_3_), channel_id=1, source_target_pairs={{0,16},{16,0},{32,48},{48,32},{64,80},{80,64},{96,112},{112,96},{1... | collective-permute-start | bytes 786440 | tf_op jit(solution)/shard_map/ppermute | solution.py:21
  58.7 1.6 %shard_map.113.refs_3_ = f32[2,256,256]{2,1,0:T(8,128)S(1)} custom-call(s32[11]{0:T(128)S(1)} %pad_add_fusion.refs_0_, f32[3,9]{1,0:T(4,128)S(1)} %pad_maximum_fusion.1.refs_1_, bf16[12,256,256]{2,1,0:T(8,128)(2,1)S(1)} %copy-done, bf16[2,256,256]{2,1,0:T(8,128)(2,1)S(1)} %copy-done.1, bf16[2,256,256]{2,1,0:T(8,128)(2,1)S(1)} %maximum_select_fusion.refs_4_.refs_3_, ...), custom_call_target="tpu_custom_call" | custom-call | flops 402653184 | bytes 3408024 | tf_op jit(solution)/shard_map/pallas_call | solution.py:178
  60.3 3.7 %collective-permute-done.5.refs_5_ = bf16[2,256,256]{2,1,0:T(8,128)(2,1)S(1)} collective-permute-done((bf16[2,256,256]{2,1,0:T(8,128)(2,1)S(1)}, bf16[2,256,256]{2,1,0:T(8,128)(2,1)S(1)}, u32[]{:S(2)}, u32[]{:S(2)}) %collective-permute-start.5) | collective-permute-done | bytes 262176 | tf_op jit(solution)/shard_map/ppermute | solution.py:31
  65.2 6.6 %collective-permute-done.9.refs_8_ = bf16[2,256,256]{2,1,0:T(8,128)(2,1)S(1)} collective-permute-done((bf16[2,256,256]{2,1,0:T(8,128)(2,1)S(1)}, bf16[2,256,256]{2,1,0:T(8,128)(2,1)S(1)}, u32[]{:S(2)}, u32[]{:S(2)}) %collective-permute-start.9) | collective-permute-done | bytes 262176 | tf_op jit(solution)/shard_map/ppermute | solution.py:21
  71.7 1.6 %shard_map.115 = (f32[2,256,256]{2,1,0:T(8,128)S(1)}, bf16[2,256,256]{2,1,0:T(8,128)(2,1)S(1)}) custom-call(s32[11]{0:T(128)S(1)} %pad_add_fusion.refs_0_, f32[3,9]{1,0:T(4,128)S(1)} %pad_maximum_fusion.1.refs_1_, bf16[12,256,256]{2,1,0:T(8,128)(2,1)S(1)} %copy-done, bf16[2,256,256]{2,1,0:T(8,128)(2,1)S(1)} %maximum_select_fusion.refs_4_.refs_3_, ...), custom_call_target="tpu_custom_call" | custom-call | flops 536870912 | bytes 4194456 | tf_op jit(solution)/shard_map/pallas_call | solution.py:178
  73.3 3.0 %collective-permute-start.13 = (bf16[2,256,256]{2,1,0:T(8,128)(2,1)S(1)}, bf16[2,256,256]{2,1,0:T(8,128)(2,1)S(1)}, u32[]{:S(2)}, u32[]{:S(2)}) collective-permute-start(bf16[2,256,256]{2,1,0:T(8,128)(2,1)S(1)} %get-tuple-element.19.refs_4_), channel_id=1, source_target_pairs={{0,64},{2,130},{16,80},{18,146},{32,96},{34,162},{48,112},{50,178}... | collective-permute-start | bytes 786440 | tf_op jit(solution)/shard_map/ppermute | solution.py:31
  76.3 5.0 %collective-permute-start.10 = (bf16[2,256,256]{2,1,0:T(8,128)(2,1)S(1)}, bf16[2,256,256]{2,1,0:T(8,128)(2,1)S(1)}, u32[]{:S(2)}, u32[]{:S(2)}) collective-permute-start(bf16[2,256,256]{2,1,0:T(8,128)(2,1)S(1)} %get-tuple-element.19.refs_4_), channel_id=1, source_target_pairs={{0,2},{2,0},{1,3},{3,1},{4,6},{6,4},{5,7},{7,5},{8,10},{10,8},{9,1... | collective-permute-start | bytes 786440 | tf_op jit(solution)/shard_map/ppermute | solution.py:21
  81.3 4.0 %collective-permute-start.11 = (bf16[2,256,256]{2,1,0:T(8,128)(2,1)S(1)}, bf16[2,256,256]{2,1,0:T(8,128)(2,1)S(1)}, u32[]{:S(2)}, u32[]{:S(2)}) collective-permute-start(bf16[2,256,256]{2,1,0:T(8,128)(2,1)S(1)} %get-tuple-element.19.refs_4_), channel_id=1, source_target_pairs={{0,1},{1,0},{2,3},{3,2},{4,5},{5,4},{6,7},{7,6},{8,9},{9,8},{10,11... | collective-permute-start | bytes 786440 | tf_op jit(solution)/shard_map/ppermute | solution.py:21
  85.4 5.2 %collective-permute-start.12 = (bf16[2,256,256]{2,1,0:T(8,128)(2,1)S(1)}, bf16[2,256,256]{2,1,0:T(8,128)(2,1)S(1)}, u32[]{:S(2)}, u32[]{:S(2)}) collective-permute-start(bf16[2,256,256]{2,1,0:T(8,128)(2,1)S(1)} %get-tuple-element.19.refs_4_), channel_id=1, source_target_pairs={{0,8},{4,12},{8,0},{12,4},{1,9},{5,13},{9,1},{13,5},{2,10},{6,14},... | collective-permute-start | bytes 786440 | tf_op jit(solution)/shard_map/ppermute | solution.py:21
  90.6 20.1 %collective-permute-start.15 = (bf16[2,256,256]{2,1,0:T(8,128)(2,1)S(1)}, bf16[2,256,256]{2,1,0:T(8,128)(2,1)S(1)}, u32[]{:S(2)}, u32[]{:S(2)}) collective-permute-start(bf16[2,256,256]{2,1,0:T(8,128)(2,1)S(1)} %get-tuple-element.19.refs_4_), channel_id=1, source_target_pairs={{0,32},{16,48},{32,0},{48,16},{64,96},{80,112},{96,64},{112,80},{1... | collective-permute-start | bytes 786440 | tf_op jit(solution)/shard_map/ppermute | solution.py:21
  110.8 8.6 %collective-permute-start.14 = (bf16[2,256,256]{2,1,0:T(8,128)(2,1)S(1)}, bf16[2,256,256]{2,1,0:T(8,128)(2,1)S(1)}, u32[]{:S(2)}, u32[]{:S(2)}) collective-permute-start(bf16[2,256,256]{2,1,0:T(8,128)(2,1)S(1)} %broadcast_select_fusion), channel_id=1, source_target_pairs={{0,192},{2,66},{16,208},{18,82},{32,224},{34,98},{48,240},{50,114}... | collective-permute-start | bytes 786440 | tf_op jit(solution)/shard_map/ppermute | solution.py:31
  119.4 1.9 %collective-permute-start.16 = (bf16[2,256,256]{2,1,0:T(8,128)(2,1)S(1)}, bf16[2,256,256]{2,1,0:T(8,128)(2,1)S(1)}, u32[]{:S(2)}, u32[]{:S(2)}) collective-permute-start(bf16[2,256,256]{2,1,0:T(8,128)(2,1)S(1)} %get-tuple-element.19.refs_4_), channel_id=1, source_target_pairs={{0,256},{256,0},{1,257},{257,1},{2,258},{258,2},{3,259},{259,3},{4... | collective-permute-start | bytes 786440 | tf_op jit(solution)/shard_map/ppermute | solution.py:21
  121.3 1.9 %collective-permute-start.17 = (bf16[2,256,256]{2,1,0:T(8,128)(2,1)S(1)}, bf16[2,256,256]{2,1,0:T(8,128)(2,1)S(1)}, u32[]{:S(2)}, u32[]{:S(2)}) collective-permute-start(bf16[2,256,256]{2,1,0:T(8,128)(2,1)S(1)} %get-tuple-element.19.refs_4_), channel_id=1, source_target_pairs={{0,4},{4,0},{8,12},{12,8},{1,5},{5,1},{9,13},{13,9},{2,6},{6,2},{1... | collective-permute-start | bytes 786440 | tf_op jit(solution)/shard_map/ppermute | solution.py:21
  123.2 2.1 %collective-permute-start.18 = (bf16[2,256,256]{2,1,0:T(8,128)(2,1)S(1)}, bf16[2,256,256]{2,1,0:T(8,128)(2,1)S(1)}, u32[]{:S(2)}, u32[]{:S(2)}) collective-permute-start(bf16[2,256,256]{2,1,0:T(8,128)(2,1)S(1)} %get-tuple-element.19.refs_4_), channel_id=1, source_target_pairs={{0,16},{16,0},{32,48},{48,32},{64,80},{80,64},{96,112},{112,96},{1... | collective-permute-start | bytes 786440 | tf_op jit(solution)/shard_map/ppermute | solution.py:21
  125.4 1.6 %shard_map.116.refs_3_ = f32[2,256,256]{2,1,0:T(8,128)S(1)} custom-call(s32[11]{0:T(128)S(1)} %pad_add_fusion.refs_0_, f32[3,9]{1,0:T(4,128)S(1)} %pad_maximum_fusion.1.refs_1_, bf16[12,256,256]{2,1,0:T(8,128)(2,1)S(1)} %copy-done, bf16[2,256,256]{2,1,0:T(8,128)(2,1)S(1)} %copy-done.1, bf16[2,256,256]{2,1,0:T(8,128)(2,1)S(1)} %get-tuple-element.19.refs_4_, ...), custom_call_target="tpu_custom_call" | custom-call | flops 402653184 | bytes 3932312 | tf_op jit(solution)/shard_map/pallas_call | solution.py:178
  127.0 7.8 %collective-permute-done.14.refs_5_ = bf16[2,256,256]{2,1,0:T(8,128)(2,1)S(1)} collective-permute-done((bf16[2,256,256]{2,1,0:T(8,128)(2,1)S(1)}, bf16[2,256,256]{2,1,0:T(8,128)(2,1)S(1)}, u32[]{:S(2)}, u32[]{:S(2)}) %collective-permute-start.14) | collective-permute-done | bytes 262176 | tf_op jit(solution)/shard_map/ppermute | solution.py:31
  136.0 5.4 %collective-permute-done.18.refs_7_ = bf16[2,256,256]{2,1,0:T(8,128)(2,1)S(1)} collective-permute-done((bf16[2,256,256]{2,1,0:T(8,128)(2,1)S(1)}, bf16[2,256,256]{2,1,0:T(8,128)(2,1)S(1)}, u32[]{:S(2)}, u32[]{:S(2)}) %collective-permute-start.18) | collective-permute-done | bytes 262176 | tf_op jit(solution)/shard_map/ppermute | solution.py:21
  141.4 1.5 shard_map.118
  142.9 1.9 %collective-permute-start.19 = (bf16[2,128,256]{2,1,0:T(8,128)(2,1)S(1)}, bf16[2,128,256]{2,1,0:T(8,128)(2,1)S(1)}, u32[]{:S(2)}, u32[]{:S(2)}) collective-permute-start(bf16[2,128,256]{2,1,0:T(8,128)(2,1)S(1)} %get-tuple-element.21), channel_id=1, source_target_pairs={{0,1},{1,0},{2,3},{3,2},{4,5},{5,4},{6,7},{7,6},{8,9},{9,8},{10,11... | collective-permute-start | bytes 393224 | tf_op jit(solution)/shard_map/ppermute | solution.py:21
  144.8 6.4 %collective-permute-done.19 = bf16[2,128,256]{2,1,0:T(8,128)(2,1)S(1)} collective-permute-done((bf16[2,128,256]{2,1,0:T(8,128)(2,1)S(1)}, bf16[2,128,256]{2,1,0:T(8,128)(2,1)S(1)}, u32[]{:S(2)}, u32[]{:S(2)}) %collective-permute-start.19) | collective-permute-done | bytes 131104 | tf_op jit(solution)/shard_map/ppermute | solution.py:21
  (44 shorter events, 7.5 us)
Async XLA Ops:
  0.6 58.1 %copy-start = (bf16[12,256,256]{2,1,0:T(8,128)(2,1)S(1)}, bf16[12,256,256]{2,1,0:T(8,128)(2,1)}, u32[]{:S(2)}) copy-start(bf16[12,256,256]{2,1,0:T(8,128)(2,1)} %refs_2_.11) | copy-start | bytes 4718596
  0.6 58.1 %copy-start.1 = (bf16[2,256,256]{2,1,0:T(8,128)(2,1)S(1)}, bf16[2,256,256]{2,1,0:T(8,128)(2,1)}, u32[]{:S(2)}) copy-start(bf16[2,256,256]{2,1,0:T(8,128)(2,1)} %refs_3_.3) | copy-start | bytes 786436
  1.9 8.6 %collective-permute-start = (bf16[2,128,256]{2,1,0:T(8,128)(2,1)S(1)}, bf16[2,128,256]{2,1,0:T(8,128)(2,1)S(1)}, u32[]{:S(2)}, u32[]{:S(2)}) collective-permute-start(bf16[2,128,256]{2,1,0:T(8,128)(2,1)S(1)} %get-tuple-element.29), channel_id=1, source_target_pairs={{0,1},{1,0},{2,3},{3,2},{4,5},{5,4},{6,7},{7,6},{8,9},{9,8},{10,11... | collective-permute-start | bytes 393224 | tf_op jit(solution)/shard_map/ppermute | solution.py:21
  10.6 33.2 %collective-permute-start.4 = (bf16[2,256,256]{2,1,0:T(8,128)(2,1)S(1)}, bf16[2,256,256]{2,1,0:T(8,128)(2,1)S(1)}, u32[]{:S(2)}, u32[]{:S(2)}) collective-permute-start(bf16[2,256,256]{2,1,0:T(8,128)(2,1)S(1)} %maximum_select_fusion.refs_4_.refs_3_), channel_id=1, source_target_pairs={{0,64},{2,130},{16,80},{18,146},{32,96},{34,162},{48,112},{50,178}... | collective-permute-start | bytes 786440 | tf_op jit(solution)/shard_map/ppermute | solution.py:31
  21.8 28.6 %collective-permute-start.1 = (bf16[2,256,256]{2,1,0:T(8,128)(2,1)S(1)}, bf16[2,256,256]{2,1,0:T(8,128)(2,1)S(1)}, u32[]{:S(2)}, u32[]{:S(2)}) collective-permute-start(bf16[2,256,256]{2,1,0:T(8,128)(2,1)S(1)} %maximum_select_fusion.refs_4_.refs_3_), channel_id=1, source_target_pairs={{0,2},{2,0},{1,3},{3,1},{4,6},{6,4},{5,7},{7,5},{8,10},{10,8},{9,1... | collective-permute-start | bytes 786440 | tf_op jit(solution)/shard_map/ppermute | solution.py:21
  29.0 23.5 %collective-permute-start.2 = (bf16[2,256,256]{2,1,0:T(8,128)(2,1)S(1)}, bf16[2,256,256]{2,1,0:T(8,128)(2,1)S(1)}, u32[]{:S(2)}, u32[]{:S(2)}) collective-permute-start(bf16[2,256,256]{2,1,0:T(8,128)(2,1)S(1)} %maximum_select_fusion.refs_4_.refs_3_), channel_id=1, source_target_pairs={{0,1},{1,0},{2,3},{3,2},{4,5},{5,4},{6,7},{7,6},{8,9},{9,8},{10,11... | collective-permute-start | bytes 786440 | tf_op jit(solution)/shard_map/ppermute | solution.py:21
  33.1 23.6 %collective-permute-start.3 = (bf16[2,256,256]{2,1,0:T(8,128)(2,1)S(1)}, bf16[2,256,256]{2,1,0:T(8,128)(2,1)S(1)}, u32[]{:S(2)}, u32[]{:S(2)}) collective-permute-start(bf16[2,256,256]{2,1,0:T(8,128)(2,1)S(1)} %maximum_select_fusion.refs_4_.refs_3_), channel_id=1, source_target_pairs={{0,8},{4,12},{8,0},{12,4},{1,9},{5,13},{9,1},{13,5},{2,10},{6,14},... | collective-permute-start | bytes 786440 | tf_op jit(solution)/shard_map/ppermute | solution.py:21
  38.2 26.9 %collective-permute-start.6 = (bf16[2,256,256]{2,1,0:T(8,128)(2,1)S(1)}, bf16[2,256,256]{2,1,0:T(8,128)(2,1)S(1)}, u32[]{:S(2)}, u32[]{:S(2)}) collective-permute-start(bf16[2,256,256]{2,1,0:T(8,128)(2,1)S(1)} %maximum_select_fusion.refs_4_.refs_3_), channel_id=1, source_target_pairs={{0,32},{16,48},{32,0},{48,16},{64,96},{80,112},{96,64},{112,80},{1... | collective-permute-start | bytes 786440 | tf_op jit(solution)/shard_map/ppermute | solution.py:21
  43.9 20.2 %collective-permute-start.5 = (bf16[2,256,256]{2,1,0:T(8,128)(2,1)S(1)}, bf16[2,256,256]{2,1,0:T(8,128)(2,1)S(1)}, u32[]{:S(2)}, u32[]{:S(2)}) collective-permute-start(bf16[2,256,256]{2,1,0:T(8,128)(2,1)S(1)} %broadcast_select_fusion.1), channel_id=1, source_target_pairs={{0,192},{2,66},{16,208},{18,82},{32,224},{34,98},{48,240},{50,114}... | collective-permute-start | bytes 786440 | tf_op jit(solution)/shard_map/ppermute | solution.py:31
  50.4 14.7 %collective-permute-start.7 = (bf16[2,256,256]{2,1,0:T(8,128)(2,1)S(1)}, bf16[2,256,256]{2,1,0:T(8,128)(2,1)S(1)}, u32[]{:S(2)}, u32[]{:S(2)}) collective-permute-start(bf16[2,256,256]{2,1,0:T(8,128)(2,1)S(1)} %maximum_select_fusion.refs_4_.refs_3_), channel_id=1, source_target_pairs={{0,256},{256,0},{1,257},{257,1},{2,258},{258,2},{3,259},{259,3},{4... | collective-permute-start | bytes 786440 | tf_op jit(solution)/shard_map/ppermute | solution.py:21
  52.5 12.6 %collective-permute-start.8 = (bf16[2,256,256]{2,1,0:T(8,128)(2,1)S(1)}, bf16[2,256,256]{2,1,0:T(8,128)(2,1)S(1)}, u32[]{:S(2)}, u32[]{:S(2)}) collective-permute-start(bf16[2,256,256]{2,1,0:T(8,128)(2,1)S(1)} %maximum_select_fusion.refs_4_.refs_3_), channel_id=1, source_target_pairs={{0,4},{4,0},{8,12},{12,8},{1,5},{5,1},{9,13},{13,9},{2,6},{6,2},{1... | collective-permute-start | bytes 786440 | tf_op jit(solution)/shard_map/ppermute | solution.py:21
  56.7 15.0 %collective-permute-start.9 = (bf16[2,256,256]{2,1,0:T(8,128)(2,1)S(1)}, bf16[2,256,256]{2,1,0:T(8,128)(2,1)S(1)}, u32[]{:S(2)}, u32[]{:S(2)}) collective-permute-start(bf16[2,256,256]{2,1,0:T(8,128)(2,1)S(1)} %maximum_select_fusion.refs_4_.refs_3_), channel_id=1, source_target_pairs={{0,16},{16,0},{32,48},{48,32},{64,80},{80,64},{96,112},{112,96},{1... | collective-permute-start | bytes 786440 | tf_op jit(solution)/shard_map/ppermute | solution.py:21
  73.3 37.4 %collective-permute-start.13 = (bf16[2,256,256]{2,1,0:T(8,128)(2,1)S(1)}, bf16[2,256,256]{2,1,0:T(8,128)(2,1)S(1)}, u32[]{:S(2)}, u32[]{:S(2)}) collective-permute-start(bf16[2,256,256]{2,1,0:T(8,128)(2,1)S(1)} %get-tuple-element.19.refs_4_), channel_id=1, source_target_pairs={{0,64},{2,130},{16,80},{18,146},{32,96},{34,162},{48,112},{50,178}... | collective-permute-start | bytes 786440 | tf_op jit(solution)/shard_map/ppermute | solution.py:31
  76.3 43.0 %collective-permute-start.10 = (bf16[2,256,256]{2,1,0:T(8,128)(2,1)S(1)}, bf16[2,256,256]{2,1,0:T(8,128)(2,1)S(1)}, u32[]{:S(2)}, u32[]{:S(2)}) collective-permute-start(bf16[2,256,256]{2,1,0:T(8,128)(2,1)S(1)} %get-tuple-element.19.refs_4_), channel_id=1, source_target_pairs={{0,2},{2,0},{1,3},{3,1},{4,6},{6,4},{5,7},{7,5},{8,10},{10,8},{9,1... | collective-permute-start | bytes 786440 | tf_op jit(solution)/shard_map/ppermute | solution.py:21
  81.3 39.9 %collective-permute-start.11 = (bf16[2,256,256]{2,1,0:T(8,128)(2,1)S(1)}, bf16[2,256,256]{2,1,0:T(8,128)(2,1)S(1)}, u32[]{:S(2)}, u32[]{:S(2)}) collective-permute-start(bf16[2,256,256]{2,1,0:T(8,128)(2,1)S(1)} %get-tuple-element.19.refs_4_), channel_id=1, source_target_pairs={{0,1},{1,0},{2,3},{3,2},{4,5},{5,4},{6,7},{7,6},{8,9},{9,8},{10,11... | collective-permute-start | bytes 786440 | tf_op jit(solution)/shard_map/ppermute | solution.py:21
  85.4 37.9 %collective-permute-start.12 = (bf16[2,256,256]{2,1,0:T(8,128)(2,1)S(1)}, bf16[2,256,256]{2,1,0:T(8,128)(2,1)S(1)}, u32[]{:S(2)}, u32[]{:S(2)}) collective-permute-start(bf16[2,256,256]{2,1,0:T(8,128)(2,1)S(1)} %get-tuple-element.19.refs_4_), channel_id=1, source_target_pairs={{0,8},{4,12},{8,0},{12,4},{1,9},{5,13},{9,1},{13,5},{2,10},{6,14},... | collective-permute-start | bytes 786440 | tf_op jit(solution)/shard_map/ppermute | solution.py:21
  90.6 45.3 %collective-permute-start.15 = (bf16[2,256,256]{2,1,0:T(8,128)(2,1)S(1)}, bf16[2,256,256]{2,1,0:T(8,128)(2,1)S(1)}, u32[]{:S(2)}, u32[]{:S(2)}) collective-permute-start(bf16[2,256,256]{2,1,0:T(8,128)(2,1)S(1)} %get-tuple-element.19.refs_4_), channel_id=1, source_target_pairs={{0,32},{16,48},{32,0},{48,16},{64,96},{80,112},{96,64},{112,80},{1... | collective-permute-start | bytes 786440 | tf_op jit(solution)/shard_map/ppermute | solution.py:21
  110.8 24.0 %collective-permute-start.14 = (bf16[2,256,256]{2,1,0:T(8,128)(2,1)S(1)}, bf16[2,256,256]{2,1,0:T(8,128)(2,1)S(1)}, u32[]{:S(2)}, u32[]{:S(2)}) collective-permute-start(bf16[2,256,256]{2,1,0:T(8,128)(2,1)S(1)} %broadcast_select_fusion), channel_id=1, source_target_pairs={{0,192},{2,66},{16,208},{18,82},{32,224},{34,98},{48,240},{50,114}... | collective-permute-start | bytes 786440 | tf_op jit(solution)/shard_map/ppermute | solution.py:31
  119.4 16.6 %collective-permute-start.16 = (bf16[2,256,256]{2,1,0:T(8,128)(2,1)S(1)}, bf16[2,256,256]{2,1,0:T(8,128)(2,1)S(1)}, u32[]{:S(2)}, u32[]{:S(2)}) collective-permute-start(bf16[2,256,256]{2,1,0:T(8,128)(2,1)S(1)} %get-tuple-element.19.refs_4_), channel_id=1, source_target_pairs={{0,256},{256,0},{1,257},{257,1},{2,258},{258,2},{3,259},{259,3},{4... | collective-permute-start | bytes 786440 | tf_op jit(solution)/shard_map/ppermute | solution.py:21
  121.3 14.7 %collective-permute-start.17 = (bf16[2,256,256]{2,1,0:T(8,128)(2,1)S(1)}, bf16[2,256,256]{2,1,0:T(8,128)(2,1)S(1)}, u32[]{:S(2)}, u32[]{:S(2)}) collective-permute-start(bf16[2,256,256]{2,1,0:T(8,128)(2,1)S(1)} %get-tuple-element.19.refs_4_), channel_id=1, source_target_pairs={{0,4},{4,0},{8,12},{12,8},{1,5},{5,1},{9,13},{13,9},{2,6},{6,2},{1... | collective-permute-start | bytes 786440 | tf_op jit(solution)/shard_map/ppermute | solution.py:21
  123.2 18.1 %collective-permute-start.18 = (bf16[2,256,256]{2,1,0:T(8,128)(2,1)S(1)}, bf16[2,256,256]{2,1,0:T(8,128)(2,1)S(1)}, u32[]{:S(2)}, u32[]{:S(2)}) collective-permute-start(bf16[2,256,256]{2,1,0:T(8,128)(2,1)S(1)} %get-tuple-element.19.refs_4_), channel_id=1, source_target_pairs={{0,16},{16,0},{32,48},{48,32},{64,80},{80,64},{96,112},{112,96},{1... | collective-permute-start | bytes 786440 | tf_op jit(solution)/shard_map/ppermute | solution.py:21
  135.9 15.4 %copy-start.2 = (f32[2,128,256]{2,1,0:T(8,128)S(1)}, f32[2,128,256]{2,1,0:T(8,128)}, u32[]{:S(2)}) copy-start(f32[2,128,256]{2,1,0:T(8,128)} %param.11) | copy-start | bytes 786436
  135.9 15.4 %copy-start.3 = (f32[2,128,256]{2,1,0:T(8,128)S(1)}, f32[2,128,256]{2,1,0:T(8,128)}, u32[]{:S(2)}) copy-start(f32[2,128,256]{2,1,0:T(8,128)} %param.10) | copy-start | bytes 786436
  142.9 8.4 %collective-permute-start.19 = (bf16[2,128,256]{2,1,0:T(8,128)(2,1)S(1)}, bf16[2,128,256]{2,1,0:T(8,128)(2,1)S(1)}, u32[]{:S(2)}, u32[]{:S(2)}) collective-permute-start(bf16[2,128,256]{2,1,0:T(8,128)(2,1)S(1)} %get-tuple-element.21), channel_id=1, source_target_pairs={{0,1},{1,0},{2,3},{3,2},{4,5},{5,4},{6,7},{7,6},{8,9},{9,8},{10,11... | collective-permute-start | bytes 393224 | tf_op jit(solution)/shard_map/ppermute | solution.py:21

commit v11 on v10

--- a/solution.py
+++ b/solution.py
@@ -154,15 +154,15 @@
 
     def exchange(full):
         first = across(full, inward, opposite)
-        core = swapped(full, "core", 1)
+        z1 = swapped(full, "z", 1)
         z2 = swapped(full, "z", 2)
         x2 = swapped(full, "rep", 1)
         y2 = swapped(full, "y", 2)
         second = across(jnp.where(on_first, first, full), outward, inward)
-        x1 = swapped(after(full, first, core), "x_lo", 1)
+        x1 = swapped(after(full, first, z1), "x_lo", 1)
         y1 = swapped(after(full, first, x2), "y", 1)
-        z1 = swapped(after(full, first, y2), "z", 1)
-        return {1: [core], 0: [x2], 3: [y2]}, {6: [first, second], 7: [second, first]}, {5: [z2], 8: [x1], 2: [y1], 4: [z1]}
+        core = swapped(after(full, first, z2), "core", 1)
+        return {4: [z1], 0: [x2], 3: [y2]}, {6: [first, second], 7: [second, first]}, {5: [z2], 8: [x1], 2: [y1], 1: [core]}
 
     def call(body, parts, outs, scratch, *operands):
         held = []

time: 153 us -> 139 us (0.908)
  the two profiles are of different devices: /device:TPU:2 before, /device:TPU:112 now
where the time goes in v11:
time: 139 us; the launch traced here: 138 us
  starting transfers between devices  82 us (59%)
  waiting for transfers between devices  39 us (28%)
  Pallas kernels  8.5 us (6%)
  other arithmetic  5.75 us (4%)
  between operations  2.33 us (2%)
    ppermute x16, starting transfers between devices, swapped(): return lax.ppermute(value, axis, pairs)  55.9 us
    ppermute x16, waiting for transfers between devices, swapped(): return lax.ppermute(value, axis, pairs)  29.9 us
    ppermute x4, starting transfers between devices, across(): return lax.ppermute(value, ('z', 'core'), pairs)  26.1 us
    ppermute x4, waiting for transfers between devices, across(): return lax.ppermute(value, ('z', 'core'), pairs)  9.1 us
    pallas_call x6, Pallas kernels, call(): pl.pallas_call(lambda *refs: body(counts, *refs), out_shape=outs, in_spec...  8.5 us
  transfers between devices with their start and end apart: 20, of which 8 were waited for; matrix products, arithmetic and copies ran while one was open for 3% of the time, Pallas kernels for 4%

profile of v11, /device:TPU:112, one launch (start us, length us, event | category | flops | bytes accessed | tf_op | source)
XLA Modules:
  0.0 138.2 jit_solution(1006604209325690430)
XLA Ops:
  0.7 1.2 convert_bitcast_fusion
  1.9 4.9 %collective-permute-start = (bf16[2,128,256]{2,1,0:T(8,128)(2,1)S(1)}, bf16[2,128,256]{2,1,0:T(8,128)(2,1)S(1)}, u32[]{:S(2)}, u32[]{:S(2)}) collective-permute-start(bf16[2,128,256]{2,1,0:T(8,128)(2,1)S(1)} %get-tuple-element.29), channel_id=1, source_target_pairs={{0,1},{1,0},{2,3},{3,2},{4,5},{5,4},{6,7},{7,6},{8,9},{9,8},{10,11... | collective-permute-start | bytes 393224 | tf_op jit(solution)/shard_map/ppermute | solution.py:21
  10.6 9.1 %collective-permute-start.4 = (bf16[2,256,256]{2,1,0:T(8,128)(2,1)S(1)}, bf16[2,256,256]{2,1,0:T(8,128)(2,1)S(1)}, u32[]{:S(2)}, u32[]{:S(2)}) collective-permute-start(bf16[2,256,256]{2,1,0:T(8,128)(2,1)S(1)} %maximum_select_fusion.refs_4_.refs_3_), channel_id=1, source_target_pairs={{0,64},{2,130},{16,80},{18,146},{32,96},{34,162},{48,112},{50,178}... | collective-permute-start | bytes 786440 | tf_op jit(solution)/shard_map/ppermute | solution.py:31
  21.8 2.0 %collective-permute-start.1 = (bf16[2,256,256]{2,1,0:T(8,128)(2,1)S(1)}, bf16[2,256,256]{2,1,0:T(8,128)(2,1)S(1)}, u32[]{:S(2)}, u32[]{:S(2)}) collective-permute-start(bf16[2,256,256]{2,1,0:T(8,128)(2,1)S(1)} %maximum_select_fusion.refs_4_.refs_3_), channel_id=1, source_target_pairs={{0,16},{16,0},{32,48},{48,32},{64,80},{80,64},{96,112},{112,96},{1... | collective-permute-start | bytes 786440 | tf_op jit(solution)/shard_map/ppermute | solution.py:21
  23.8 4.9 %collective-permute-start.2 = (bf16[2,256,256]{2,1,0:T(8,128)(2,1)S(1)}, bf16[2,256,256]{2,1,0:T(8,128)(2,1)S(1)}, u32[]{:S(2)}, u32[]{:S(2)}) collective-permute-start(bf16[2,256,256]{2,1,0:T(8,128)(2,1)S(1)} %maximum_select_fusion.refs_4_.refs_3_), channel_id=1, source_target_pairs={{0,1},{1,0},{2,3},{3,2},{4,5},{5,4},{6,7},{7,6},{8,9},{9,8},{10,11... | collective-permute-start | bytes 786440 | tf_op jit(solution)/shard_map/ppermute | solution.py:21
  28.8 1.9 %collective-permute-start.6 = (bf16[2,256,256]{2,1,0:T(8,128)(2,1)S(1)}, bf16[2,256,256]{2,1,0:T(8,128)(2,1)S(1)}, u32[]{:S(2)}, u32[]{:S(2)}) collective-permute-start(bf16[2,256,256]{2,1,0:T(8,128)(2,1)S(1)} %maximum_select_fusion.refs_4_.refs_3_), channel_id=1, source_target_pairs={{0,32},{16,48},{32,0},{48,16},{64,96},{80,112},{96,64},{112,80},{1... | collective-permute-start | bytes 786440 | tf_op jit(solution)/shard_map/ppermute | solution.py:21
  30.7 2.2 %collective-permute-start.3 = (bf16[2,256,256]{2,1,0:T(8,128)(2,1)S(1)}, bf16[2,256,256]{2,1,0:T(8,128)(2,1)S(1)}, u32[]{:S(2)}, u32[]{:S(2)}) collective-permute-start(bf16[2,256,256]{2,1,0:T(8,128)(2,1)S(1)} %maximum_select_fusion.refs_4_.refs_3_), channel_id=1, source_target_pairs={{0,8},{4,12},{8,0},{12,4},{1,9},{5,13},{9,1},{13,5},{2,10},{6,14},... | collective-permute-start | bytes 786440 | tf_op jit(solution)/shard_map/ppermute | solution.py:21
  33.0 6.6 %collective-permute-done.4.refs_4_ = bf16[2,256,256]{2,1,0:T(8,128)(2,1)S(1)} collective-permute-done((bf16[2,256,256]{2,1,0:T(8,128)(2,1)S(1)}, bf16[2,256,256]{2,1,0:T(8,128)(2,1)S(1)}, u32[]{:S(2)}, u32[]{:S(2)}) %collective-permute-start.4) | collective-permute-done | bytes 262176 | tf_op jit(solution)/shard_map/ppermute | solution.py:31
  39.6 7.4 %collective-permute-start.5 = (bf16[2,256,256]{2,1,0:T(8,128)(2,1)S(1)}, bf16[2,256,256]{2,1,0:T(8,128)(2,1)S(1)}, u32[]{:S(2)}, u32[]{:S(2)}) collective-permute-start(bf16[2,256,256]{2,1,0:T(8,128)(2,1)S(1)} %broadcast_select_fusion.1), channel_id=1, source_target_pairs={{0,192},{2,66},{16,208},{18,82},{32,224},{34,98},{48,240},{50,114}... | collective-permute-start | bytes 786440 | tf_op jit(solution)/shard_map/ppermute | solution.py:31
  47.0 8.9 %collective-permute-done.1.refs_5_ = bf16[2,256,256]{2,1,0:T(8,128)(2,1)S(1)} collective-permute-done((bf16[2,256,256]{2,1,0:T(8,128)(2,1)S(1)}, bf16[2,256,256]{2,1,0:T(8,128)(2,1)S(1)}, u32[]{:S(2)}, u32[]{:S(2)}) %collective-permute-start.1) | collective-permute-done | bytes 262176 | tf_op jit(solution)/shard_map/ppermute | solution.py:21
  55.9 3.3 %collective-permute-start.7 = (bf16[2,256,256]{2,1,0:T(8,128)(2,1)S(1)}, bf16[2,256,256]{2,1,0:T(8,128)(2,1)S(1)}, u32[]{:S(2)}, u32[]{:S(2)}) collective-permute-start(bf16[2,256,256]{2,1,0:T(8,128)(2,1)S(1)} %maximum_select_fusion.refs_4_.refs_3_), channel_id=1, source_target_pairs={{0,256},{256,0},{1,257},{257,1},{2,258},{258,2},{3,259},{259,3},{4... | collective-permute-start | bytes 786440 | tf_op jit(solution)/shard_map/ppermute | solution.py:21
  59.2 3.2 %collective-permute-start.8 = (bf16[2,256,256]{2,1,0:T(8,128)(2,1)S(1)}, bf16[2,256,256]{2,1,0:T(8,128)(2,1)S(1)}, u32[]{:S(2)}, u32[]{:S(2)}) collective-permute-start(bf16[2,256,256]{2,1,0:T(8,128)(2,1)S(1)} %maximum_select_fusion.refs_4_.refs_3_), channel_id=1, source_target_pairs={{0,4},{4,0},{8,12},{12,8},{1,5},{5,1},{9,13},{13,9},{2,6},{6,2},{1... | collective-permute-start | bytes 786440 | tf_op jit(solution)/shard_map/ppermute | solution.py:21
  62.5 1.9 %collective-permute-start.9 = (bf16[2,256,256]{2,1,0:T(8,128)(2,1)S(1)}, bf16[2,256,256]{2,1,0:T(8,128)(2,1)S(1)}, u32[]{:S(2)}, u32[]{:S(2)}) collective-permute-start(bf16[2,256,256]{2,1,0:T(8,128)(2,1)S(1)} %maximum_select_fusion.refs_4_.refs_3_), channel_id=1, source_target_pairs={{0,2},{2,0},{1,3},{3,1},{4,6},{6,4},{5,7},{7,5},{8,10},{10,8},{9,1... | collective-permute-start | bytes 786440 | tf_op jit(solution)/shard_map/ppermute | solution.py:21
  64.5 1.6 %shard_map.113.refs_3_ = f32[2,256,256]{2,1,0:T(8,128)S(1)} custom-call(s32[11]{0:T(128)S(1)} %pad_add_fusion.refs_0_, f32[3,9]{1,0:T(4,128)S(1)} %pad_maximum_fusion.1.refs_1_, bf16[12,256,256]{2,1,0:T(8,128)(2,1)S(1)} %copy-done, bf16[2,256,256]{2,1,0:T(8,128)(2,1)S(1)} %copy-done.1, bf16[2,256,256]{2,1,0:T(8,128)(2,1)S(1)} %maximum_select_fusion.refs_4_.refs_3_, ...), custom_call_target="tpu_custom_call" | custom-call | flops 402653184 | bytes 3408024 | tf_op jit(solution)/shard_map/pallas_call | solution.py:178
  66.1 1.1 shard_map.114.refs_4_
  67.2 2.0 %collective-permute-done.8.refs_7_ = bf16[2,256,256]{2,1,0:T(8,128)(2,1)S(1)} collective-permute-done((bf16[2,256,256]{2,1,0:T(8,128)(2,1)S(1)}, bf16[2,256,256]{2,1,0:T(8,128)(2,1)S(1)}, u32[]{:S(2)}, u32[]{:S(2)}) %collective-permute-start.8) | collective-permute-done | bytes 262176 | tf_op jit(solution)/shard_map/ppermute | solution.py:21
  69.2 1.6 %shard_map.115 = (f32[2,256,256]{2,1,0:T(8,128)S(1)}, bf16[2,256,256]{2,1,0:T(8,128)(2,1)S(1)}) custom-call(s32[11]{0:T(128)S(1)} %pad_add_fusion.refs_0_, f32[3,9]{1,0:T(4,128)S(1)} %pad_maximum_fusion.1.refs_1_, bf16[12,256,256]{2,1,0:T(8,128)(2,1)S(1)} %copy-done, bf16[2,256,256]{2,1,0:T(8,128)(2,1)S(1)} %maximum_select_fusion.refs_4_.refs_3_, ...), custom_call_target="tpu_custom_call" | custom-call | flops 536870912 | bytes 4194456 | tf_op jit(solution)/shard_map/pallas_call | solution.py:178
  70.8 1.9 %collective-permute-start.13 = (bf16[2,256,256]{2,1,0:T(8,128)(2,1)S(1)}, bf16[2,256,256]{2,1,0:T(8,128)(2,1)S(1)}, u32[]{:S(2)}, u32[]{:S(2)}) collective-permute-start(bf16[2,256,256]{2,1,0:T(8,128)(2,1)S(1)} %get-tuple-element.19.refs_4_), channel_id=1, source_target_pairs={{0,64},{2,130},{16,80},{18,146},{32,96},{34,162},{48,112},{50,178}... | collective-permute-start | bytes 786440 | tf_op jit(solution)/shard_map/ppermute | solution.py:31
  72.7 6.6 %collective-permute-start.10 = (bf16[2,256,256]{2,1,0:T(8,128)(2,1)S(1)}, bf16[2,256,256]{2,1,0:T(8,128)(2,1)S(1)}, u32[]{:S(2)}, u32[]{:S(2)}) collective-permute-start(bf16[2,256,256]{2,1,0:T(8,128)(2,1)S(1)} %get-tuple-element.19.refs_4_), channel_id=1, source_target_pairs={{0,16},{16,0},{32,48},{48,32},{64,80},{80,64},{96,112},{112,96},{1... | collective-permute-start | bytes 786440 | tf_op jit(solution)/shard_map/ppermute | solution.py:21
  79.3 4.9 %collective-permute-start.11 = (bf16[2,256,256]{2,1,0:T(8,128)(2,1)S(1)}, bf16[2,256,256]{2,1,0:T(8,128)(2,1)S(1)}, u32[]{:S(2)}, u32[]{:S(2)}) collective-permute-start(bf16[2,256,256]{2,1,0:T(8,128)(2,1)S(1)} %get-tuple-element.19.refs_4_), channel_id=1, source_target_pairs={{0,1},{1,0},{2,3},{3,2},{4,5},{5,4},{6,7},{7,6},{8,9},{9,8},{10,11... | collective-permute-start | bytes 786440 | tf_op jit(solution)/shard_map/ppermute | solution.py:21
  84.2 1.9 %collective-permute-start.15 = (bf16[2,256,256]{2,1,0:T(8,128)(2,1)S(1)}, bf16[2,256,256]{2,1,0:T(8,128)(2,1)S(1)}, u32[]{:S(2)}, u32[]{:S(2)}) collective-permute-start(bf16[2,256,256]{2,1,0:T(8,128)(2,1)S(1)} %get-tuple-element.19.refs_4_), channel_id=1, source_target_pairs={{0,32},{16,48},{32,0},{48,16},{64,96},{80,112},{96,64},{112,80},{1... | collective-permute-start | bytes 786440 | tf_op jit(solution)/shard_map/ppermute | solution.py:21
  86.1 2.2 %collective-permute-start.12 = (bf16[2,256,256]{2,1,0:T(8,128)(2,1)S(1)}, bf16[2,256,256]{2,1,0:T(8,128)(2,1)S(1)}, u32[]{:S(2)}, u32[]{:S(2)}) collective-permute-start(bf16[2,256,256]{2,1,0:T(8,128)(2,1)S(1)} %get-tuple-element.19.refs_4_), channel_id=1, source_target_pairs={{0,8},{4,12},{8,0},{12,4},{1,9},{5,13},{9,1},{13,5},{2,10},{6,14},... | collective-permute-start | bytes 786440 | tf_op jit(solution)/shard_map/ppermute | solution.py:21
  88.4 2.5 %collective-permute-done.13.refs_4_ = bf16[2,256,256]{2,1,0:T(8,128)(2,1)S(1)} collective-permute-done((bf16[2,256,256]{2,1,0:T(8,128)(2,1)S(1)}, bf16[2,256,256]{2,1,0:T(8,128)(2,1)S(1)}, u32[]{:S(2)}, u32[]{:S(2)}) %collective-permute-start.13) | collective-permute-done | bytes 262176 | tf_op jit(solution)/shard_map/ppermute | solution.py:31
  90.9 7.7 %collective-permute-start.14 = (bf16[2,256,256]{2,1,0:T(8,128)(2,1)S(1)}, bf16[2,256,256]{2,1,0:T(8,128)(2,1)S(1)}, u32[]{:S(2)}, u32[]{:S(2)}) collective-permute-start(bf16[2,256,256]{2,1,0:T(8,128)(2,1)S(1)} %broadcast_select_fusion), channel_id=1, source_target_pairs={{0,192},{2,66},{16,208},{18,82},{32,224},{34,98},{48,240},{50,114}... | collective-permute-start | bytes 786440 | tf_op jit(solution)/shard_map/ppermute | solution.py:31
  98.6 13.7 %collective-permute-done.10.refs_6_ = bf16[2,256,256]{2,1,0:T(8,128)(2,1)S(1)} collective-permute-done((bf16[2,256,256]{2,1,0:T(8,128)(2,1)S(1)}, bf16[2,256,256]{2,1,0:T(8,128)(2,1)S(1)}, u32[]{:S(2)}, u32[]{:S(2)}) %collective-permute-start.10) | collective-permute-done | bytes 262176 | tf_op jit(solution)/shard_map/ppermute | solution.py:21
  112.3 6.1 %collective-permute-start.16 = (bf16[2,256,256]{2,1,0:T(8,128)(2,1)S(1)}, bf16[2,256,256]{2,1,0:T(8,128)(2,1)S(1)}, u32[]{:S(2)}, u32[]{:S(2)}) collective-permute-start(bf16[2,256,256]{2,1,0:T(8,128)(2,1)S(1)} %get-tuple-element.19.refs_4_), channel_id=1, source_target_pairs={{0,256},{256,0},{1,257},{257,1},{2,258},{258,2},{3,259},{259,3},{4... | collective-permute-start | bytes 786440 | tf_op jit(solution)/shard_map/ppermute | solution.py:21
  118.5 3.2 %collective-permute-start.17 = (bf16[2,256,256]{2,1,0:T(8,128)(2,1)S(1)}, bf16[2,256,256]{2,1,0:T(8,128)(2,1)S(1)}, u32[]{:S(2)}, u32[]{:S(2)}) collective-permute-start(bf16[2,256,256]{2,1,0:T(8,128)(2,1)S(1)} %get-tuple-element.19.refs_4_), channel_id=1, source_target_pairs={{0,4},{4,0},{8,12},{12,8},{1,5},{5,1},{9,13},{13,9},{2,6},{6,2},{1... | collective-permute-start | bytes 786440 | tf_op jit(solution)/shard_map/ppermute | solution.py:21
  121.7 1.9 %collective-permute-start.18 = (bf16[2,256,256]{2,1,0:T(8,128)(2,1)S(1)}, bf16[2,256,256]{2,1,0:T(8,128)(2,1)S(1)}, u32[]{:S(2)}, u32[]{:S(2)}) collective-permute-start(bf16[2,256,256]{2,1,0:T(8,128)(2,1)S(1)} %get-tuple-element.19.refs_4_), channel_id=1, source_target_pairs={{0,2},{2,0},{1,3},{3,1},{4,6},{6,4},{5,7},{7,5},{8,10},{10,8},{9,1... | collective-permute-start | bytes 786440 | tf_op jit(solution)/shard_map/ppermute | solution.py:21
  123.6 1.6 %shard_map.116.refs_3_ = f32[2,256,256]{2,1,0:T(8,128)S(1)} custom-call(s32[11]{0:T(128)S(1)} %pad_add_fusion.refs_0_, f32[3,9]{1,0:T(4,128)S(1)} %pad_maximum_fusion.1.refs_1_, bf16[12,256,256]{2,1,0:T(8,128)(2,1)S(1)} %copy-done, bf16[2,256,256]{2,1,0:T(8,128)(2,1)S(1)} %copy-done.1, bf16[2,256,256]{2,1,0:T(8,128)(2,1)S(1)} %get-tuple-element.19.refs_4_, ...), custom_call_target="tpu_custom_call" | custom-call | flops 402653184 | bytes 3932312 | tf_op jit(solution)/shard_map/pallas_call | solution.py:178
  126.8 1.5 %shard_map.118 = (f32[2,128,256]{2,1,0:T(8,128)S(1)}, bf16[2,128,256]{2,1,0:T(8,128)(2,1)S(1)}) custom-call(s32[11]{0:T(128)S(1)} %pad_add_fusion.refs_0_, f32[3,9]{1,0:T(4,128)S(1)} %pad_maximum_fusion.1.refs_1_, bf16[12,256,256]{2,1,0:T(8,128)(2,1)S(1)} %copy-done, f32[2,256,256]{2,1,0:T(8,128)S(1)} %shard_map.117.refs_3_, ...), custom_call_target="tpu_custom_call" | custom-call | flops 536870912 | bytes 3539096 | tf_op jit(solution)/shard_map/pallas_call | solution.py:178
  128.3 4.6 %collective-permute-start.19 = (bf16[2,128,256]{2,1,0:T(8,128)(2,1)S(1)}, bf16[2,128,256]{2,1,0:T(8,128)(2,1)S(1)}, u32[]{:S(2)}, u32[]{:S(2)}) collective-permute-start(bf16[2,128,256]{2,1,0:T(8,128)(2,1)S(1)} %get-tuple-element.21), channel_id=1, source_target_pairs={{0,1},{1,0},{2,3},{3,2},{4,5},{5,4},{6,7},{7,6},{8,9},{9,8},{10,11... | collective-permute-start | bytes 393224 | tf_op jit(solution)/shard_map/ppermute | solution.py:21
  132.9 4.3 %collective-permute-done.19 = bf16[2,128,256]{2,1,0:T(8,128)(2,1)S(1)} collective-permute-done((bf16[2,128,256]{2,1,0:T(8,128)(2,1)S(1)}, bf16[2,128,256]{2,1,0:T(8,128)(2,1)S(1)}, u32[]{:S(2)}, u32[]{:S(2)}) %collective-permute-start.19) | collective-permute-done | bytes 131104 | tf_op jit(solution)/shard_map/ppermute | solution.py:21
  (44 shorter events, 7.3 us)
Async XLA Ops:
  0.6 63.9 %copy-start = (bf16[12,256,256]{2,1,0:T(8,128)(2,1)S(1)}, bf16[12,256,256]{2,1,0:T(8,128)(2,1)}, u32[]{:S(2)}) copy-start(bf16[12,256,256]{2,1,0:T(8,128)(2,1)} %refs_2_.11) | copy-start | bytes 4718596
  0.6 63.9 %copy-start.1 = (bf16[2,256,256]{2,1,0:T(8,128)(2,1)S(1)}, bf16[2,256,256]{2,1,0:T(8,128)(2,1)}, u32[]{:S(2)}) copy-start(bf16[2,256,256]{2,1,0:T(8,128)(2,1)} %refs_3_.3) | copy-start | bytes 786436
  1.9 8.6 %collective-permute-start = (bf16[2,128,256]{2,1,0:T(8,128)(2,1)S(1)}, bf16[2,128,256]{2,1,0:T(8,128)(2,1)S(1)}, u32[]{:S(2)}, u32[]{:S(2)}) collective-permute-start(bf16[2,128,256]{2,1,0:T(8,128)(2,1)S(1)} %get-tuple-element.29), channel_id=1, source_target_pairs={{0,1},{1,0},{2,3},{3,2},{4,5},{5,4},{6,7},{7,6},{8,9},{9,8},{10,11... | collective-permute-start | bytes 393224 | tf_op jit(solution)/shard_map/ppermute | solution.py:21
  10.6 29.0 %collective-permute-start.4 = (bf16[2,256,256]{2,1,0:T(8,128)(2,1)S(1)}, bf16[2,256,256]{2,1,0:T(8,128)(2,1)S(1)}, u32[]{:S(2)}, u32[]{:S(2)}) collective-permute-start(bf16[2,256,256]{2,1,0:T(8,128)(2,1)S(1)} %maximum_select_fusion.refs_4_.refs_3_), channel_id=1, source_target_pairs={{0,64},{2,130},{16,80},{18,146},{32,96},{34,162},{48,112},{50,178}... | collective-permute-start | bytes 786440 | tf_op jit(solution)/shard_map/ppermute | solution.py:31
  21.8 34.1 %collective-permute-start.1 = (bf16[2,256,256]{2,1,0:T(8,128)(2,1)S(1)}, bf16[2,256,256]{2,1,0:T(8,128)(2,1)S(1)}, u32[]{:S(2)}, u32[]{:S(2)}) collective-permute-start(bf16[2,256,256]{2,1,0:T(8,128)(2,1)S(1)} %maximum_select_fusion.refs_4_.refs_3_), channel_id=1, source_target_pairs={{0,16},{16,0},{32,48},{48,32},{64,80},{80,64},{96,112},{112,96},{1... | collective-permute-start | bytes 786440 | tf_op jit(solution)/shard_map/ppermute | solution.py:21
  23.8 35.4 %collective-permute-start.2 = (bf16[2,256,256]{2,1,0:T(8,128)(2,1)S(1)}, bf16[2,256,256]{2,1,0:T(8,128)(2,1)S(1)}, u32[]{:S(2)}, u32[]{:S(2)}) collective-permute-start(bf16[2,256,256]{2,1,0:T(8,128)(2,1)S(1)} %maximum_select_fusion.refs_4_.refs_3_), channel_id=1, source_target_pairs={{0,1},{1,0},{2,3},{3,2},{4,5},{5,4},{6,7},{7,6},{8,9},{9,8},{10,11... | collective-permute-start | bytes 786440 | tf_op jit(solution)/shard_map/ppermute | solution.py:21
  28.8 33.7 %collective-permute-start.6 = (bf16[2,256,256]{2,1,0:T(8,128)(2,1)S(1)}, bf16[2,256,256]{2,1,0:T(8,128)(2,1)S(1)}, u32[]{:S(2)}, u32[]{:S(2)}) collective-permute-start(bf16[2,256,256]{2,1,0:T(8,128)(2,1)S(1)} %maximum_select_fusion.refs_4_.refs_3_), channel_id=1, source_target_pairs={{0,32},{16,48},{32,0},{48,16},{64,96},{80,112},{96,64},{112,80},{1... | collective-permute-start | bytes 786440 | tf_op jit(solution)/shard_map/ppermute | solution.py:21
  30.7 33.7 %collective-permute-start.3 = (bf16[2,256,256]{2,1,0:T(8,128)(2,1)S(1)}, bf16[2,256,256]{2,1,0:T(8,128)(2,1)S(1)}, u32[]{:S(2)}, u32[]{:S(2)}) collective-permute-start(bf16[2,256,256]{2,1,0:T(8,128)(2,1)S(1)} %maximum_select_fusion.refs_4_.refs_3_), channel_id=1, source_target_pairs={{0,8},{4,12},{8,0},{12,4},{1,9},{5,13},{9,1},{13,5},{2,10},{6,14},... | collective-permute-start | bytes 786440 | tf_op jit(solution)/shard_map/ppermute | solution.py:21
  39.6 26.5 %collective-permute-start.5 = (bf16[2,256,256]{2,1,0:T(8,128)(2,1)S(1)}, bf16[2,256,256]{2,1,0:T(8,128)(2,1)S(1)}, u32[]{:S(2)}, u32[]{:S(2)}) collective-permute-start(bf16[2,256,256]{2,1,0:T(8,128)(2,1)S(1)} %broadcast_select_fusion.1), channel_id=1, source_target_pairs={{0,192},{2,66},{16,208},{18,82},{32,224},{34,98},{48,240},{50,114}... | collective-permute-start | bytes 786440 | tf_op jit(solution)/shard_map/ppermute | solution.py:31
  55.9 11.3 %collective-permute-start.7 = (bf16[2,256,256]{2,1,0:T(8,128)(2,1)S(1)}, bf16[2,256,256]{2,1,0:T(8,128)(2,1)S(1)}, u32[]{:S(2)}, u32[]{:S(2)}) collective-permute-start(bf16[2,256,256]{2,1,0:T(8,128)(2,1)S(1)} %maximum_select_fusion.refs_4_.refs_3_), channel_id=1, source_target_pairs={{0,256},{256,0},{1,257},{257,1},{2,258},{258,2},{3,259},{259,3},{4... | collective-permute-start | bytes 786440 | tf_op jit(solution)/shard_map/ppermute | solution.py:21
  59.2 9.9 %collective-permute-start.8 = (bf16[2,256,256]{2,1,0:T(8,128)(2,1)S(1)}, bf16[2,256,256]{2,1,0:T(8,128)(2,1)S(1)}, u32[]{:S(2)}, u32[]{:S(2)}) collective-permute-start(bf16[2,256,256]{2,1,0:T(8,128)(2,1)S(1)} %maximum_select_fusion.refs_4_.refs_3_), channel_id=1, source_target_pairs={{0,4},{4,0},{8,12},{12,8},{1,5},{5,1},{9,13},{13,9},{2,6},{6,2},{1... | collective-permute-start | bytes 786440 | tf_op jit(solution)/shard_map/ppermute | solution.py:21
  62.5 6.7 %collective-permute-start.9 = (bf16[2,256,256]{2,1,0:T(8,128)(2,1)S(1)}, bf16[2,256,256]{2,1,0:T(8,128)(2,1)S(1)}, u32[]{:S(2)}, u32[]{:S(2)}) collective-permute-start(bf16[2,256,256]{2,1,0:T(8,128)(2,1)S(1)} %maximum_select_fusion.refs_4_.refs_3_), channel_id=1, source_target_pairs={{0,2},{2,0},{1,3},{3,1},{4,6},{6,4},{5,7},{7,5},{8,10},{10,8},{9,1... | collective-permute-start | bytes 786440 | tf_op jit(solution)/shard_map/ppermute | solution.py:21
  70.8 20.1 %collective-permute-start.13 = (bf16[2,256,256]{2,1,0:T(8,128)(2,1)S(1)}, bf16[2,256,256]{2,1,0:T(8,128)(2,1)S(1)}, u32[]{:S(2)}, u32[]{:S(2)}) collective-permute-start(bf16[2,256,256]{2,1,0:T(8,128)(2,1)S(1)} %get-tuple-element.19.refs_4_), channel_id=1, source_target_pairs={{0,64},{2,130},{16,80},{18,146},{32,96},{34,162},{48,112},{50,178}... | collective-permute-start | bytes 786440 | tf_op jit(solution)/shard_map/ppermute | solution.py:31
  72.7 39.6 %collective-permute-start.10 = (bf16[2,256,256]{2,1,0:T(8,128)(2,1)S(1)}, bf16[2,256,256]{2,1,0:T(8,128)(2,1)S(1)}, u32[]{:S(2)}, u32[]{:S(2)}) collective-permute-start(bf16[2,256,256]{2,1,0:T(8,128)(2,1)S(1)} %get-tuple-element.19.refs_4_), channel_id=1, source_target_pairs={{0,16},{16,0},{32,48},{48,32},{64,80},{80,64},{96,112},{112,96},{1... | collective-permute-start | bytes 786440 | tf_op jit(solution)/shard_map/ppermute | solution.py:21
  79.3 39.2 %collective-permute-start.11 = (bf16[2,256,256]{2,1,0:T(8,128)(2,1)S(1)}, bf16[2,256,256]{2,1,0:T(8,128)(2,1)S(1)}, u32[]{:S(2)}, u32[]{:S(2)}) collective-permute-start(bf16[2,256,256]{2,1,0:T(8,128)(2,1)S(1)} %get-tuple-element.19.refs_4_), channel_id=1, source_target_pairs={{0,1},{1,0},{2,3},{3,2},{4,5},{5,4},{6,7},{7,6},{8,9},{9,8},{10,11... | collective-permute-start | bytes 786440 | tf_op jit(solution)/shard_map/ppermute | solution.py:21
  84.2 37.5 %collective-permute-start.15 = (bf16[2,256,256]{2,1,0:T(8,128)(2,1)S(1)}, bf16[2,256,256]{2,1,0:T(8,128)(2,1)S(1)}, u32[]{:S(2)}, u32[]{:S(2)}) collective-permute-start(bf16[2,256,256]{2,1,0:T(8,128)(2,1)S(1)} %get-tuple-element.19.refs_4_), channel_id=1, source_target_pairs={{0,32},{16,48},{32,0},{48,16},{64,96},{80,112},{96,64},{112,80},{1... | collective-permute-start | bytes 786440 | tf_op jit(solution)/shard_map/ppermute | solution.py:21
  86.1 37.5 %collective-permute-start.12 = (bf16[2,256,256]{2,1,0:T(8,128)(2,1)S(1)}, bf16[2,256,256]{2,1,0:T(8,128)(2,1)S(1)}, u32[]{:S(2)}, u32[]{:S(2)}) collective-permute-start(bf16[2,256,256]{2,1,0:T(8,128)(2,1)S(1)} %get-tuple-element.19.refs_4_), channel_id=1, source_target_pairs={{0,8},{4,12},{8,0},{12,4},{1,9},{5,13},{9,1},{13,5},{2,10},{6,14},... | collective-permute-start | bytes 786440 | tf_op jit(solution)/shard_map/ppermute | solution.py:21
  90.9 34.3 %collective-permute-start.14 = (bf16[2,256,256]{2,1,0:T(8,128)(2,1)S(1)}, bf16[2,256,256]{2,1,0:T(8,128)(2,1)S(1)}, u32[]{:S(2)}, u32[]{:S(2)}) collective-permute-start(bf16[2,256,256]{2,1,0:T(8,128)(2,1)S(1)} %broadcast_select_fusion), channel_id=1, source_target_pairs={{0,192},{2,66},{16,208},{18,82},{32,224},{34,98},{48,240},{50,114}... | collective-permute-start | bytes 786440 | tf_op jit(solution)/shard_map/ppermute | solution.py:31
  112.3 14.1 %collective-permute-start.16 = (bf16[2,256,256]{2,1,0:T(8,128)(2,1)S(1)}, bf16[2,256,256]{2,1,0:T(8,128)(2,1)S(1)}, u32[]{:S(2)}, u32[]{:S(2)}) collective-permute-start(bf16[2,256,256]{2,1,0:T(8,128)(2,1)S(1)} %get-tuple-element.19.refs_4_), channel_id=1, source_target_pairs={{0,256},{256,0},{1,257},{257,1},{2,258},{258,2},{3,259},{259,3},{4... | collective-permute-start | bytes 786440 | tf_op jit(solution)/shard_map/ppermute | solution.py:21
  118.5 8.3 %collective-permute-start.17 = (bf16[2,256,256]{2,1,0:T(8,128)(2,1)S(1)}, bf16[2,256,256]{2,1,0:T(8,128)(2,1)S(1)}, u32[]{:S(2)}, u32[]{:S(2)}) collective-permute-start(bf16[2,256,256]{2,1,0:T(8,128)(2,1)S(1)} %get-tuple-element.19.refs_4_), channel_id=1, source_target_pairs={{0,4},{4,0},{8,12},{12,8},{1,5},{5,1},{9,13},{13,9},{2,6},{6,2},{1... | collective-permute-start | bytes 786440 | tf_op jit(solution)/shard_map/ppermute | solution.py:21
  121.7 5.1 %collective-permute-start.18 = (bf16[2,256,256]{2,1,0:T(8,128)(2,1)S(1)}, bf16[2,256,256]{2,1,0:T(8,128)(2,1)S(1)}, u32[]{:S(2)}, u32[]{:S(2)}) collective-permute-start(bf16[2,256,256]{2,1,0:T(8,128)(2,1)S(1)} %get-tuple-element.19.refs_4_), channel_id=1, source_target_pairs={{0,2},{2,0},{1,3},{3,1},{4,6},{6,4},{5,7},{7,5},{8,10},{10,8},{9,1... | collective-permute-start | bytes 786440 | tf_op jit(solution)/shard_map/ppermute | solution.py:21
  126.4 10.9 %copy-start.2 = (f32[2,128,256]{2,1,0:T(8,128)S(1)}, f32[2,128,256]{2,1,0:T(8,128)}, u32[]{:S(2)}) copy-start(f32[2,128,256]{2,1,0:T(8,128)} %param.11) | copy-start | bytes 786436
  126.4 10.9 %copy-start.3 = (f32[2,128,256]{2,1,0:T(8,128)S(1)}, f32[2,128,256]{2,1,0:T(8,128)}, u32[]{:S(2)}) copy-start(f32[2,128,256]{2,1,0:T(8,128)} %param.10) | copy-start | bytes 786436
  128.3 9.0 %collective-permute-start.19 = (bf16[2,128,256]{2,1,0:T(8,128)(2,1)S(1)}, bf16[2,128,256]{2,1,0:T(8,128)(2,1)S(1)}, u32[]{:S(2)}, u32[]{:S(2)}) collective-permute-start(bf16[2,128,256]{2,1,0:T(8,128)(2,1)S(1)} %get-tuple-element.21), channel_id=1, source_target_pairs={{0,1},{1,0},{2,3},{3,2},{4,5},{5,4},{6,7},{7,6},{8,9},{9,8},{10,11... | collective-permute-start | bytes 393224 | tf_op jit(solution)/shard_map/ppermute | solution.py:21

commit v12 on v11

--- a/solution.py
+++ b/solution.py
@@ -159,8 +159,8 @@
         x2 = swapped(full, "rep", 1)
         y2 = swapped(full, "y", 2)
         second = across(jnp.where(on_first, first, full), outward, inward)
-        x1 = swapped(after(full, first, z1), "x_lo", 1)
-        y1 = swapped(after(full, first, x2), "y", 1)
+        x1 = swapped(after(full, first, x2), "x_lo", 1)
+        y1 = swapped(after(full, first, z1), "y", 1)
         core = swapped(after(full, first, z2), "core", 1)
         return {4: [z1], 0: [x2], 3: [y2]}, {6: [first, second], 7: [second, first]}, {5: [z2], 8: [x1], 2: [y1], 1: [core]}
 

time: 139 us -> 136 us (0.978)
  the two profiles are of different devices: /device:TPU:112 before, /device:TPU:102 now
where the time goes in v12:
time: 136 us; the launch traced here: 135 us
  starting transfers between devices  85.6 us (63%)
  waiting for transfers between devices  32.3 us (24%)
  Pallas kernels  8.5 us (6%)
  other arithmetic  5.76 us (4%)
  between operations  2.35 us (2%)
    ppermute x16, starting transfers between devices, swapped(): return lax.ppermute(value, axis, pairs)  58.7 us
    ppermute x4, starting transfers between devices, across(): return lax.ppermute(value, ('z', 'core'), pairs)  26.9 us
    ppermute x16, waiting for transfers between devices, swapped(): return lax.ppermute(value, axis, pairs)  26.9 us
    pallas_call x6, Pallas kernels, call(): pl.pallas_call(lambda *refs: body(counts, *refs), out_shape=outs, in_spec...  8.5 us
    ppermute x4, waiting for transfers between devices, across(): return lax.ppermute(value, ('z', 'core'), pairs)  5.45 us
  transfers between devices with their start and end apart: 20, of which 6 were waited for; matrix products, arithmetic and copies ran while one was open for 3% of the time, Pallas kernels for 4%

profile of v12, /device:TPU:102, one launch (start us, length us, event | category | flops | bytes accessed | tf_op | source)
XLA Modules:
  0.0 135.2 jit_solution(15232514721942514863)
XLA Ops:
  0.7 1.2 convert_bitcast_fusion
  1.9 3.3 %collective-permute-start = (bf16[2,128,256]{2,1,0:T(8,128)(2,1)S(1)}, bf16[2,128,256]{2,1,0:T(8,128)(2,1)S(1)}, u32[]{:S(2)}, u32[]{:S(2)}) collective-permute-start(bf16[2,128,256]{2,1,0:T(8,128)(2,1)S(1)} %get-tuple-element.29), channel_id=1, source_target_pairs={{0,1},{1,0},{2,3},{3,2},{4,5},{5,4},{6,7},{7,6},{8,9},{9,8},{10,11... | collective-permute-start | bytes 393224 | tf_op jit(solution)/shard_map/ppermute | solution.py:21
  8.3 2.2 %collective-permute-done = bf16[2,128,256]{2,1,0:T(8,128)(2,1)S(1)} collective-permute-done((bf16[2,128,256]{2,1,0:T(8,128)(2,1)S(1)}, bf16[2,128,256]{2,1,0:T(8,128)(2,1)S(1)}, u32[]{:S(2)}, u32[]{:S(2)}) %collective-permute-start) | collective-permute-done | bytes 131104 | tf_op jit(solution)/shard_map/ppermute | solution.py:21
  10.6 9.1 %collective-permute-start.4 = (bf16[2,256,256]{2,1,0:T(8,128)(2,1)S(1)}, bf16[2,256,256]{2,1,0:T(8,128)(2,1)S(1)}, u32[]{:S(2)}, u32[]{:S(2)}) collective-permute-start(bf16[2,256,256]{2,1,0:T(8,128)(2,1)S(1)} %maximum_select_fusion.refs_4_.refs_3_), channel_id=1, source_target_pairs={{0,64},{2,130},{16,80},{18,146},{32,96},{34,162},{48,112},{50,178}... | collective-permute-start | bytes 786440 | tf_op jit(solution)/shard_map/ppermute | solution.py:31
  21.8 2.0 %collective-permute-start.1 = (bf16[2,256,256]{2,1,0:T(8,128)(2,1)S(1)}, bf16[2,256,256]{2,1,0:T(8,128)(2,1)S(1)}, u32[]{:S(2)}, u32[]{:S(2)}) collective-permute-start(bf16[2,256,256]{2,1,0:T(8,128)(2,1)S(1)} %maximum_select_fusion.refs_4_.refs_3_), channel_id=1, source_target_pairs={{0,16},{16,0},{32,48},{48,32},{64,80},{80,64},{96,112},{112,96},{1... | collective-permute-start | bytes 786440 | tf_op jit(solution)/shard_map/ppermute | solution.py:21
  23.8 3.3 %collective-permute-start.2 = (bf16[2,256,256]{2,1,0:T(8,128)(2,1)S(1)}, bf16[2,256,256]{2,1,0:T(8,128)(2,1)S(1)}, u32[]{:S(2)}, u32[]{:S(2)}) collective-permute-start(bf16[2,256,256]{2,1,0:T(8,128)(2,1)S(1)} %maximum_select_fusion.refs_4_.refs_3_), channel_id=1, source_target_pairs={{0,1},{1,0},{2,3},{3,2},{4,5},{5,4},{6,7},{7,6},{8,9},{9,8},{10,11... | collective-permute-start | bytes 786440 | tf_op jit(solution)/shard_map/ppermute | solution.py:21
  27.2 1.9 %collective-permute-start.6 = (bf16[2,256,256]{2,1,0:T(8,128)(2,1)S(1)}, bf16[2,256,256]{2,1,0:T(8,128)(2,1)S(1)}, u32[]{:S(2)}, u32[]{:S(2)}) collective-permute-start(bf16[2,256,256]{2,1,0:T(8,128)(2,1)S(1)} %maximum_select_fusion.refs_4_.refs_3_), channel_id=1, source_target_pairs={{0,32},{16,48},{32,0},{48,16},{64,96},{80,112},{96,64},{112,80},{1... | collective-permute-start | bytes 786440 | tf_op jit(solution)/shard_map/ppermute | solution.py:21
  29.1 5.1 %collective-permute-start.3 = (bf16[2,256,256]{2,1,0:T(8,128)(2,1)S(1)}, bf16[2,256,256]{2,1,0:T(8,128)(2,1)S(1)}, u32[]{:S(2)}, u32[]{:S(2)}) collective-permute-start(bf16[2,256,256]{2,1,0:T(8,128)(2,1)S(1)} %maximum_select_fusion.refs_4_.refs_3_), channel_id=1, source_target_pairs={{0,8},{4,12},{8,0},{12,4},{1,9},{5,13},{9,1},{13,5},{2,10},{6,14},... | collective-permute-start | bytes 786440 | tf_op jit(solution)/shard_map/ppermute | solution.py:21
  34.2 5.4 %collective-permute-done.4.refs_4_ = bf16[2,256,256]{2,1,0:T(8,128)(2,1)S(1)} collective-permute-done((bf16[2,256,256]{2,1,0:T(8,128)(2,1)S(1)}, bf16[2,256,256]{2,1,0:T(8,128)(2,1)S(1)}, u32[]{:S(2)}, u32[]{:S(2)}) %collective-permute-start.4) | collective-permute-done | bytes 262176 | tf_op jit(solution)/shard_map/ppermute | solution.py:31
  39.7 7.3 %collective-permute-start.5 = (bf16[2,256,256]{2,1,0:T(8,128)(2,1)S(1)}, bf16[2,256,256]{2,1,0:T(8,128)(2,1)S(1)}, u32[]{:S(2)}, u32[]{:S(2)}) collective-permute-start(bf16[2,256,256]{2,1,0:T(8,128)(2,1)S(1)} %broadcast_select_fusion.1), channel_id=1, source_target_pairs={{0,192},{2,66},{16,208},{18,82},{32,224},{34,98},{48,240},{50,114}... | collective-permute-start | bytes 786440 | tf_op jit(solution)/shard_map/ppermute | solution.py:31
  47.0 2.7 %collective-permute-start.7 = (bf16[2,256,256]{2,1,0:T(8,128)(2,1)S(1)}, bf16[2,256,256]{2,1,0:T(8,128)(2,1)S(1)}, u32[]{:S(2)}, u32[]{:S(2)}) collective-permute-start(bf16[2,256,256]{2,1,0:T(8,128)(2,1)S(1)} %maximum_select_fusion.refs_4_.refs_3_), channel_id=1, source_target_pairs={{0,256},{256,0},{1,257},{257,1},{2,258},{258,2},{3,259},{259,3},{4... | collective-permute-start | bytes 786440 | tf_op jit(solution)/shard_map/ppermute | solution.py:21
  49.7 6.1 %collective-permute-done.1.refs_5_ = bf16[2,256,256]{2,1,0:T(8,128)(2,1)S(1)} collective-permute-done((bf16[2,256,256]{2,1,0:T(8,128)(2,1)S(1)}, bf16[2,256,256]{2,1,0:T(8,128)(2,1)S(1)}, u32[]{:S(2)}, u32[]{:S(2)}) %collective-permute-start.1) | collective-permute-done | bytes 262176 | tf_op jit(solution)/shard_map/ppermute | solution.py:21
  55.8 3.5 %collective-permute-start.8 = (bf16[2,256,256]{2,1,0:T(8,128)(2,1)S(1)}, bf16[2,256,256]{2,1,0:T(8,128)(2,1)S(1)}, u32[]{:S(2)}, u32[]{:S(2)}) collective-permute-start(bf16[2,256,256]{2,1,0:T(8,128)(2,1)S(1)} %maximum_select_fusion.refs_4_.refs_3_), channel_id=1, source_target_pairs={{0,4},{4,0},{8,12},{12,8},{1,5},{5,1},{9,13},{13,9},{2,6},{6,2},{1... | collective-permute-start | bytes 786440 | tf_op jit(solution)/shard_map/ppermute | solution.py:21
  59.3 1.9 %collective-permute-start.9 = (bf16[2,256,256]{2,1,0:T(8,128)(2,1)S(1)}, bf16[2,256,256]{2,1,0:T(8,128)(2,1)S(1)}, u32[]{:S(2)}, u32[]{:S(2)}) collective-permute-start(bf16[2,256,256]{2,1,0:T(8,128)(2,1)S(1)} %maximum_select_fusion.refs_4_.refs_3_), channel_id=1, source_target_pairs={{0,2},{2,0},{1,3},{3,1},{4,6},{6,4},{5,7},{7,5},{8,10},{10,8},{9,1... | collective-permute-start | bytes 786440 | tf_op jit(solution)/shard_map/ppermute | solution.py:21
  61.4 1.6 %shard_map.113.refs_3_ = f32[2,256,256]{2,1,0:T(8,128)S(1)} custom-call(s32[11]{0:T(128)S(1)} %pad_add_fusion.refs_0_, f32[3,9]{1,0:T(4,128)S(1)} %pad_maximum_fusion.1.refs_1_, bf16[12,256,256]{2,1,0:T(8,128)(2,1)S(1)} %copy-done, bf16[2,256,256]{2,1,0:T(8,128)(2,1)S(1)} %copy-done.1, bf16[2,256,256]{2,1,0:T(8,128)(2,1)S(1)} %maximum_select_fusion.refs_4_.refs_3_, ...), custom_call_target="tpu_custom_call" | custom-call | flops 402653184 | bytes 3408024 | tf_op jit(solution)/shard_map/pallas_call | solution.py:178
  63.0 1.1 shard_map.114.refs_4_
  64.1 1.9 %collective-permute-done.8.refs_7_ = bf16[2,256,256]{2,1,0:T(8,128)(2,1)S(1)} collective-permute-done((bf16[2,256,256]{2,1,0:T(8,128)(2,1)S(1)}, bf16[2,256,256]{2,1,0:T(8,128)(2,1)S(1)}, u32[]{:S(2)}, u32[]{:S(2)}) %collective-permute-start.8) | collective-permute-done | bytes 262176 | tf_op jit(solution)/shard_map/ppermute | solution.py:21
  66.1 1.6 %shard_map.115 = (f32[2,256,256]{2,1,0:T(8,128)S(1)}, bf16[2,256,256]{2,1,0:T(8,128)(2,1)S(1)}) custom-call(s32[11]{0:T(128)S(1)} %pad_add_fusion.refs_0_, f32[3,9]{1,0:T(4,128)S(1)} %pad_maximum_fusion.1.refs_1_, bf16[12,256,256]{2,1,0:T(8,128)(2,1)S(1)} %copy-done, bf16[2,256,256]{2,1,0:T(8,128)(2,1)S(1)} %maximum_select_fusion.refs_4_.refs_3_, ...), custom_call_target="tpu_custom_call" | custom-call | flops 536870912 | bytes 4194456 | tf_op jit(solution)/shard_map/pallas_call | solution.py:178
  67.6 1.9 %collective-permute-start.13 = (bf16[2,256,256]{2,1,0:T(8,128)(2,1)S(1)}, bf16[2,256,256]{2,1,0:T(8,128)(2,1)S(1)}, u32[]{:S(2)}, u32[]{:S(2)}) collective-permute-start(bf16[2,256,256]{2,1,0:T(8,128)(2,1)S(1)} %get-tuple-element.19.refs_4_), channel_id=1, source_target_pairs={{0,64},{2,130},{16,80},{18,146},{32,96},{34,162},{48,112},{50,178}... | collective-permute-start | bytes 786440 | tf_op jit(solution)/shard_map/ppermute | solution.py:31
  69.6 9.8 %collective-permute-start.10 = (bf16[2,256,256]{2,1,0:T(8,128)(2,1)S(1)}, bf16[2,256,256]{2,1,0:T(8,128)(2,1)S(1)}, u32[]{:S(2)}, u32[]{:S(2)}) collective-permute-start(bf16[2,256,256]{2,1,0:T(8,128)(2,1)S(1)} %get-tuple-element.19.refs_4_), channel_id=1, source_target_pairs={{0,16},{16,0},{32,48},{48,32},{64,80},{80,64},{96,112},{112,96},{1... | collective-permute-start | bytes 786440 | tf_op jit(solution)/shard_map/ppermute | solution.py:21
  79.4 3.2 %collective-permute-start.11 = (bf16[2,256,256]{2,1,0:T(8,128)(2,1)S(1)}, bf16[2,256,256]{2,1,0:T(8,128)(2,1)S(1)}, u32[]{:S(2)}, u32[]{:S(2)}) collective-permute-start(bf16[2,256,256]{2,1,0:T(8,128)(2,1)S(1)} %get-tuple-element.19.refs_4_), channel_id=1, source_target_pairs={{0,1},{1,0},{2,3},{3,2},{4,5},{5,4},{6,7},{7,6},{8,9},{9,8},{10,11... | collective-permute-start | bytes 786440 | tf_op jit(solution)/shard_map/ppermute | solution.py:21
  82.6 1.9 %collective-permute-start.15 = (bf16[2,256,256]{2,1,0:T(8,128)(2,1)S(1)}, bf16[2,256,256]{2,1,0:T(8,128)(2,1)S(1)}, u32[]{:S(2)}, u32[]{:S(2)}) collective-permute-start(bf16[2,256,256]{2,1,0:T(8,128)(2,1)S(1)} %get-tuple-element.19.refs_4_), channel_id=1, source_target_pairs={{0,32},{16,48},{32,0},{48,16},{64,96},{80,112},{96,64},{112,80},{1... | collective-permute-start | bytes 786440 | tf_op jit(solution)/shard_map/ppermute | solution.py:21
  84.5 5.1 %collective-permute-start.12 = (bf16[2,256,256]{2,1,0:T(8,128)(2,1)S(1)}, bf16[2,256,256]{2,1,0:T(8,128)(2,1)S(1)}, u32[]{:S(2)}, u32[]{:S(2)}) collective-permute-start(bf16[2,256,256]{2,1,0:T(8,128)(2,1)S(1)} %get-tuple-element.19.refs_4_), channel_id=1, source_target_pairs={{0,8},{4,12},{8,0},{12,4},{1,9},{5,13},{9,1},{13,5},{2,10},{6,14},... | collective-permute-start | bytes 786440 | tf_op jit(solution)/shard_map/ppermute | solution.py:21
  89.7 8.6 %collective-permute-start.14 = (bf16[2,256,256]{2,1,0:T(8,128)(2,1)S(1)}, bf16[2,256,256]{2,1,0:T(8,128)(2,1)S(1)}, u32[]{:S(2)}, u32[]{:S(2)}) collective-permute-start(bf16[2,256,256]{2,1,0:T(8,128)(2,1)S(1)} %broadcast_select_fusion), channel_id=1, source_target_pairs={{0,192},{2,66},{16,208},{18,82},{32,224},{34,98},{48,240},{50,114}... | collective-permute-start | bytes 786440 | tf_op jit(solution)/shard_map/ppermute | solution.py:31
  98.3 3.7 %collective-permute-start.16 = (bf16[2,256,256]{2,1,0:T(8,128)(2,1)S(1)}, bf16[2,256,256]{2,1,0:T(8,128)(2,1)S(1)}, u32[]{:S(2)}, u32[]{:S(2)}) collective-permute-start(bf16[2,256,256]{2,1,0:T(8,128)(2,1)S(1)} %get-tuple-element.19.refs_4_), channel_id=1, source_target_pairs={{0,256},{256,0},{1,257},{257,1},{2,258},{258,2},{3,259},{259,3},{4... | collective-permute-start | bytes 786440 | tf_op jit(solution)/shard_map/ppermute | solution.py:21
  102.0 10.6 %collective-permute-done.10.refs_6_ = bf16[2,256,256]{2,1,0:T(8,128)(2,1)S(1)} collective-permute-done((bf16[2,256,256]{2,1,0:T(8,128)(2,1)S(1)}, bf16[2,256,256]{2,1,0:T(8,128)(2,1)S(1)}, u32[]{:S(2)}, u32[]{:S(2)}) %collective-permute-start.10) | collective-permute-done | bytes 262176 | tf_op jit(solution)/shard_map/ppermute | solution.py:21
  112.7 6.0 %collective-permute-start.17 = (bf16[2,256,256]{2,1,0:T(8,128)(2,1)S(1)}, bf16[2,256,256]{2,1,0:T(8,128)(2,1)S(1)}, u32[]{:S(2)}, u32[]{:S(2)}) collective-permute-start(bf16[2,256,256]{2,1,0:T(8,128)(2,1)S(1)} %get-tuple-element.19.refs_4_), channel_id=1, source_target_pairs={{0,4},{4,0},{8,12},{12,8},{1,5},{5,1},{9,13},{13,9},{2,6},{6,2},{1... | collective-permute-start | bytes 786440 | tf_op jit(solution)/shard_map/ppermute | solution.py:21
  118.7 1.9 %collective-permute-start.18 = (bf16[2,256,256]{2,1,0:T(8,128)(2,1)S(1)}, bf16[2,256,256]{2,1,0:T(8,128)(2,1)S(1)}, u32[]{:S(2)}, u32[]{:S(2)}) collective-permute-start(bf16[2,256,256]{2,1,0:T(8,128)(2,1)S(1)} %get-tuple-element.19.refs_4_), channel_id=1, source_target_pairs={{0,2},{2,0},{1,3},{3,1},{4,6},{6,4},{5,7},{7,5},{8,10},{10,8},{9,1... | collective-permute-start | bytes 786440 | tf_op jit(solution)/shard_map/ppermute | solution.py:21
  120.6 1.6 %shard_map.116.refs_3_ = f32[2,256,256]{2,1,0:T(8,128)S(1)} custom-call(s32[11]{0:T(128)S(1)} %pad_add_fusion.refs_0_, f32[3,9]{1,0:T(4,128)S(1)} %pad_maximum_fusion.1.refs_1_, bf16[12,256,256]{2,1,0:T(8,128)(2,1)S(1)} %copy-done, bf16[2,256,256]{2,1,0:T(8,128)(2,1)S(1)} %copy-done.1, bf16[2,256,256]{2,1,0:T(8,128)(2,1)S(1)} %get-tuple-element.19.refs_4_, ...), custom_call_target="tpu_custom_call" | custom-call | flops 402653184 | bytes 3932312 | tf_op jit(solution)/shard_map/pallas_call | solution.py:178
  123.4 1.5 %shard_map.118 = (f32[2,128,256]{2,1,0:T(8,128)S(1)}, bf16[2,128,256]{2,1,0:T(8,128)(2,1)S(1)}) custom-call(s32[11]{0:T(128)S(1)} %pad_add_fusion.refs_0_, f32[3,9]{1,0:T(4,128)S(1)} %pad_maximum_fusion.1.refs_1_, bf16[12,256,256]{2,1,0:T(8,128)(2,1)S(1)} %copy-done, f32[2,256,256]{2,1,0:T(8,128)S(1)} %shard_map.117.refs_3_, ...), custom_call_target="tpu_custom_call" | custom-call | flops 536870912 | bytes 3539096 | tf_op jit(solution)/shard_map/pallas_call | solution.py:178
  124.9 3.3 %collective-permute-start.19 = (bf16[2,128,256]{2,1,0:T(8,128)(2,1)S(1)}, bf16[2,128,256]{2,1,0:T(8,128)(2,1)S(1)}, u32[]{:S(2)}, u32[]{:S(2)}) collective-permute-start(bf16[2,128,256]{2,1,0:T(8,128)(2,1)S(1)} %get-tuple-element.21), channel_id=1, source_target_pairs={{0,1},{1,0},{2,3},{3,2},{4,5},{5,4},{6,7},{7,6},{8,9},{9,8},{10,11... | collective-permute-start | bytes 393224 | tf_op jit(solution)/shard_map/ppermute | solution.py:21
  128.3 6.0 %collective-permute-done.19 = bf16[2,128,256]{2,1,0:T(8,128)(2,1)S(1)} collective-permute-done((bf16[2,128,256]{2,1,0:T(8,128)(2,1)S(1)}, bf16[2,128,256]{2,1,0:T(8,128)(2,1)S(1)}, u32[]{:S(2)}, u32[]{:S(2)}) %collective-permute-start.19) | collective-permute-done | bytes 131104 | tf_op jit(solution)/shard_map/ppermute | solution.py:21
  (44 shorter events, 6.4 us)
Async XLA Ops:
  0.6 60.7 %copy-start = (bf16[12,256,256]{2,1,0:T(8,128)(2,1)S(1)}, bf16[12,256,256]{2,1,0:T(8,128)(2,1)}, u32[]{:S(2)}) copy-start(bf16[12,256,256]{2,1,0:T(8,128)(2,1)} %refs_2_.11) | copy-start | bytes 4718596
  0.6 60.7 %copy-start.1 = (bf16[2,256,256]{2,1,0:T(8,128)(2,1)S(1)}, bf16[2,256,256]{2,1,0:T(8,128)(2,1)}, u32[]{:S(2)}) copy-start(bf16[2,256,256]{2,1,0:T(8,128)(2,1)} %refs_3_.3) | copy-start | bytes 786436
  1.9 8.6 %collective-permute-start = (bf16[2,128,256]{2,1,0:T(8,128)(2,1)S(1)}, bf16[2,128,256]{2,1,0:T(8,128)(2,1)S(1)}, u32[]{:S(2)}, u32[]{:S(2)}) collective-permute-start(bf16[2,128,256]{2,1,0:T(8,128)(2,1)S(1)} %get-tuple-element.29), channel_id=1, source_target_pairs={{0,1},{1,0},{2,3},{3,2},{4,5},{5,4},{6,7},{7,6},{8,9},{9,8},{10,11... | collective-permute-start | bytes 393224 | tf_op jit(solution)/shard_map/ppermute | solution.py:21
  10.6 29.0 %collective-permute-start.4 = (bf16[2,256,256]{2,1,0:T(8,128)(2,1)S(1)}, bf16[2,256,256]{2,1,0:T(8,128)(2,1)S(1)}, u32[]{:S(2)}, u32[]{:S(2)}) collective-permute-start(bf16[2,256,256]{2,1,0:T(8,128)(2,1)S(1)} %maximum_select_fusion.refs_4_.refs_3_), channel_id=1, source_target_pairs={{0,64},{2,130},{16,80},{18,146},{32,96},{34,162},{48,112},{50,178}... | collective-permute-start | bytes 786440 | tf_op jit(solution)/shard_map/ppermute | solution.py:31
  21.8 34.0 %collective-permute-start.1 = (bf16[2,256,256]{2,1,0:T(8,128)(2,1)S(1)}, bf16[2,256,256]{2,1,0:T(8,128)(2,1)S(1)}, u32[]{:S(2)}, u32[]{:S(2)}) collective-permute-start(bf16[2,256,256]{2,1,0:T(8,128)(2,1)S(1)} %maximum_select_fusion.refs_4_.refs_3_), channel_id=1, source_target_pairs={{0,16},{16,0},{32,48},{48,32},{64,80},{80,64},{96,112},{112,96},{1... | collective-permute-start | bytes 786440 | tf_op jit(solution)/shard_map/ppermute | solution.py:21
  23.8 23.1 %collective-permute-start.2 = (bf16[2,256,256]{2,1,0:T(8,128)(2,1)S(1)}, bf16[2,256,256]{2,1,0:T(8,128)(2,1)S(1)}, u32[]{:S(2)}, u32[]{:S(2)}) collective-permute-start(bf16[2,256,256]{2,1,0:T(8,128)(2,1)S(1)} %maximum_select_fusion.refs_4_.refs_3_), channel_id=1, source_target_pairs={{0,1},{1,0},{2,3},{3,2},{4,5},{5,4},{6,7},{7,6},{8,9},{9,8},{10,11... | collective-permute-start | bytes 786440 | tf_op jit(solution)/shard_map/ppermute | solution.py:21
  27.2 32.2 %collective-permute-start.6 = (bf16[2,256,256]{2,1,0:T(8,128)(2,1)S(1)}, bf16[2,256,256]{2,1,0:T(8,128)(2,1)S(1)}, u32[]{:S(2)}, u32[]{:S(2)}) collective-permute-start(bf16[2,256,256]{2,1,0:T(8,128)(2,1)S(1)} %maximum_select_fusion.refs_4_.refs_3_), channel_id=1, source_target_pairs={{0,32},{16,48},{32,0},{48,16},{64,96},{80,112},{96,64},{112,80},{1... | collective-permute-start | bytes 786440 | tf_op jit(solution)/shard_map/ppermute | solution.py:21
  29.1 32.2 %collective-permute-start.3 = (bf16[2,256,256]{2,1,0:T(8,128)(2,1)S(1)}, bf16[2,256,256]{2,1,0:T(8,128)(2,1)S(1)}, u32[]{:S(2)}, u32[]{:S(2)}) collective-permute-start(bf16[2,256,256]{2,1,0:T(8,128)(2,1)S(1)} %maximum_select_fusion.refs_4_.refs_3_), channel_id=1, source_target_pairs={{0,8},{4,12},{8,0},{12,4},{1,9},{5,13},{9,1},{13,5},{2,10},{6,14},... | collective-permute-start | bytes 786440 | tf_op jit(solution)/shard_map/ppermute | solution.py:21
  39.7 23.3 %collective-permute-start.5 = (bf16[2,256,256]{2,1,0:T(8,128)(2,1)S(1)}, bf16[2,256,256]{2,1,0:T(8,128)(2,1)S(1)}, u32[]{:S(2)}, u32[]{:S(2)}) collective-permute-start(bf16[2,256,256]{2,1,0:T(8,128)(2,1)S(1)} %broadcast_select_fusion.1), channel_id=1, source_target_pairs={{0,192},{2,66},{16,208},{18,82},{32,224},{34,98},{48,240},{50,114}... | collective-permute-start | bytes 786440 | tf_op jit(solution)/shard_map/ppermute | solution.py:31
  47.0 17.1 %collective-permute-start.7 = (bf16[2,256,256]{2,1,0:T(8,128)(2,1)S(1)}, bf16[2,256,256]{2,1,0:T(8,128)(2,1)S(1)}, u32[]{:S(2)}, u32[]{:S(2)}) collective-permute-start(bf16[2,256,256]{2,1,0:T(8,128)(2,1)S(1)} %maximum_select_fusion.refs_4_.refs_3_), channel_id=1, source_target_pairs={{0,256},{256,0},{1,257},{257,1},{2,258},{258,2},{3,259},{259,3},{4... | collective-permute-start | bytes 786440 | tf_op jit(solution)/shard_map/ppermute | solution.py:21
  55.8 10.2 %collective-permute-start.8 = (bf16[2,256,256]{2,1,0:T(8,128)(2,1)S(1)}, bf16[2,256,256]{2,1,0:T(8,128)(2,1)S(1)}, u32[]{:S(2)}, u32[]{:S(2)}) collective-permute-start(bf16[2,256,256]{2,1,0:T(8,128)(2,1)S(1)} %maximum_select_fusion.refs_4_.refs_3_), channel_id=1, source_target_pairs={{0,4},{4,0},{8,12},{12,8},{1,5},{5,1},{9,13},{13,9},{2,6},{6,2},{1... | collective-permute-start | bytes 786440 | tf_op jit(solution)/shard_map/ppermute | solution.py:21
  59.3 6.7 %collective-permute-start.9 = (bf16[2,256,256]{2,1,0:T(8,128)(2,1)S(1)}, bf16[2,256,256]{2,1,0:T(8,128)(2,1)S(1)}, u32[]{:S(2)}, u32[]{:S(2)}) collective-permute-start(bf16[2,256,256]{2,1,0:T(8,128)(2,1)S(1)} %maximum_select_fusion.refs_4_.refs_3_), channel_id=1, source_target_pairs={{0,2},{2,0},{1,3},{3,1},{4,6},{6,4},{5,7},{7,5},{8,10},{10,8},{9,1... | collective-permute-start | bytes 786440 | tf_op jit(solution)/shard_map/ppermute | solution.py:21
  67.6 22.0 %collective-permute-start.13 = (bf16[2,256,256]{2,1,0:T(8,128)(2,1)S(1)}, bf16[2,256,256]{2,1,0:T(8,128)(2,1)S(1)}, u32[]{:S(2)}, u32[]{:S(2)}) collective-permute-start(bf16[2,256,256]{2,1,0:T(8,128)(2,1)S(1)} %get-tuple-element.19.refs_4_), channel_id=1, source_target_pairs={{0,64},{2,130},{16,80},{18,146},{32,96},{34,162},{48,112},{50,178}... | collective-permute-start | bytes 786440 | tf_op jit(solution)/shard_map/ppermute | solution.py:31
  69.6 43.1 %collective-permute-start.10 = (bf16[2,256,256]{2,1,0:T(8,128)(2,1)S(1)}, bf16[2,256,256]{2,1,0:T(8,128)(2,1)S(1)}, u32[]{:S(2)}, u32[]{:S(2)}) collective-permute-start(bf16[2,256,256]{2,1,0:T(8,128)(2,1)S(1)} %get-tuple-element.19.refs_4_), channel_id=1, source_target_pairs={{0,16},{16,0},{32,48},{48,32},{64,80},{80,64},{96,112},{112,96},{1... | collective-permute-start | bytes 786440 | tf_op jit(solution)/shard_map/ppermute | solution.py:21
  79.4 19.0 %collective-permute-start.11 = (bf16[2,256,256]{2,1,0:T(8,128)(2,1)S(1)}, bf16[2,256,256]{2,1,0:T(8,128)(2,1)S(1)}, u32[]{:S(2)}, u32[]{:S(2)}) collective-permute-start(bf16[2,256,256]{2,1,0:T(8,128)(2,1)S(1)} %get-tuple-element.19.refs_4_), channel_id=1, source_target_pairs={{0,1},{1,0},{2,3},{3,2},{4,5},{5,4},{6,7},{7,6},{8,9},{9,8},{10,11... | collective-permute-start | bytes 786440 | tf_op jit(solution)/shard_map/ppermute | solution.py:21
  82.6 36.1 %collective-permute-start.15 = (bf16[2,256,256]{2,1,0:T(8,128)(2,1)S(1)}, bf16[2,256,256]{2,1,0:T(8,128)(2,1)S(1)}, u32[]{:S(2)}, u32[]{:S(2)}) collective-permute-start(bf16[2,256,256]{2,1,0:T(8,128)(2,1)S(1)} %get-tuple-element.19.refs_4_), channel_id=1, source_target_pairs={{0,32},{16,48},{32,0},{48,16},{64,96},{80,112},{96,64},{112,80},{1... | collective-permute-start | bytes 786440 | tf_op jit(solution)/shard_map/ppermute | solution.py:21
  84.5 36.1 %collective-permute-start.12 = (bf16[2,256,256]{2,1,0:T(8,128)(2,1)S(1)}, bf16[2,256,256]{2,1,0:T(8,128)(2,1)S(1)}, u32[]{:S(2)}, u32[]{:S(2)}) collective-permute-start(bf16[2,256,256]{2,1,0:T(8,128)(2,1)S(1)} %get-tuple-element.19.refs_4_), channel_id=1, source_target_pairs={{0,8},{4,12},{8,0},{12,4},{1,9},{5,13},{9,1},{13,5},{2,10},{6,14},... | collective-permute-start | bytes 786440 | tf_op jit(solution)/shard_map/ppermute | solution.py:21
  89.7 32.5 %collective-permute-start.14 = (bf16[2,256,256]{2,1,0:T(8,128)(2,1)S(1)}, bf16[2,256,256]{2,1,0:T(8,128)(2,1)S(1)}, u32[]{:S(2)}, u32[]{:S(2)}) collective-permute-start(bf16[2,256,256]{2,1,0:T(8,128)(2,1)S(1)} %broadcast_select_fusion), channel_id=1, source_target_pairs={{0,192},{2,66},{16,208},{18,82},{32,224},{34,98},{48,240},{50,114}... | collective-permute-start | bytes 786440 | tf_op jit(solution)/shard_map/ppermute | solution.py:31
  98.3 25.1 %collective-permute-start.16 = (bf16[2,256,256]{2,1,0:T(8,128)(2,1)S(1)}, bf16[2,256,256]{2,1,0:T(8,128)(2,1)S(1)}, u32[]{:S(2)}, u32[]{:S(2)}) collective-permute-start(bf16[2,256,256]{2,1,0:T(8,128)(2,1)S(1)} %get-tuple-element.19.refs_4_), channel_id=1, source_target_pairs={{0,256},{256,0},{1,257},{257,1},{2,258},{258,2},{3,259},{259,3},{4... | collective-permute-start | bytes 786440 | tf_op jit(solution)/shard_map/ppermute | solution.py:21
  112.7 10.7 %collective-permute-start.17 = (bf16[2,256,256]{2,1,0:T(8,128)(2,1)S(1)}, bf16[2,256,256]{2,1,0:T(8,128)(2,1)S(1)}, u32[]{:S(2)}, u32[]{:S(2)}) collective-permute-start(bf16[2,256,256]{2,1,0:T(8,128)(2,1)S(1)} %get-tuple-element.19.refs_4_), channel_id=1, source_target_pairs={{0,4},{4,0},{8,12},{12,8},{1,5},{5,1},{9,13},{13,9},{2,6},{6,2},{1... | collective-permute-start | bytes 786440 | tf_op jit(solution)/shard_map/ppermute | solution.py:21
  118.7 4.7 %collective-permute-start.18 = (bf16[2,256,256]{2,1,0:T(8,128)(2,1)S(1)}, bf16[2,256,256]{2,1,0:T(8,128)(2,1)S(1)}, u32[]{:S(2)}, u32[]{:S(2)}) collective-permute-start(bf16[2,256,256]{2,1,0:T(8,128)(2,1)S(1)} %get-tuple-element.19.refs_4_), channel_id=1, source_target_pairs={{0,2},{2,0},{1,3},{3,1},{4,6},{6,4},{5,7},{7,5},{8,10},{10,8},{9,1... | collective-permute-start | bytes 786440 | tf_op jit(solution)/shard_map/ppermute | solution.py:21
  123.4 10.9 %copy-start.2 = (f32[2,128,256]{2,1,0:T(8,128)S(1)}, f32[2,128,256]{2,1,0:T(8,128)}, u32[]{:S(2)}) copy-start(f32[2,128,256]{2,1,0:T(8,128)} %param.11) | copy-start | bytes 786436
  123.4 10.9 %copy-start.3 = (f32[2,128,256]{2,1,0:T(8,128)S(1)}, f32[2,128,256]{2,1,0:T(8,128)}, u32[]{:S(2)}) copy-start(f32[2,128,256]{2,1,0:T(8,128)} %param.10) | copy-start | bytes 786436
  124.9 9.3 %collective-permute-start.19 = (bf16[2,128,256]{2,1,0:T(8,128)(2,1)S(1)}, bf16[2,128,256]{2,1,0:T(8,128)(2,1)S(1)}, u32[]{:S(2)}, u32[]{:S(2)}) collective-permute-start(bf16[2,128,256]{2,1,0:T(8,128)(2,1)S(1)} %get-tuple-element.21), channel_id=1, source_target_pairs={{0,1},{1,0},{2,3},{3,2},{4,5},{5,4},{6,7},{7,6},{8,9},{9,8},{10,11... | collective-permute-start | bytes 393224 | tf_op jit(solution)/shard_map/ppermute | solution.py:21

commit v13 on v12

--- a/solution.py
+++ b/solution.py
@@ -90,12 +90,6 @@
         total[...] = jnp.zeros_like(total)
     add_commutator(total, ham_ref, own_ref[0], own_ref[1])
     add_bits(total, parts, index_ref, coef_ref, couple_ref, partner_refs, whole)
-
-
-def add_kernel(parts, index_ref, coef_ref, couple_ref, total_ref, *refs):
-    *partner_refs, out_ref, whole = refs
-    out_ref[...] = total_ref[...]
-    add_bits(out_ref, parts, index_ref, coef_ref, couple_ref, partner_refs, whole)
 
 
 def middle_kernel(parts, index_ref, coef_ref, couple_ref, own_ref, total_ref, *refs):
@@ -162,7 +156,7 @@
         x1 = swapped(after(full, first, x2), "x_lo", 1)
         y1 = swapped(after(full, first, z1), "y", 1)
         core = swapped(after(full, first, z2), "core", 1)
-        return {4: [z1], 0: [x2], 3: [y2]}, {6: [first, second], 7: [second, first]}, {5: [z2], 8: [x1], 2: [y1], 1: [core]}
+        return {4: [z1], 0: [x2], 3: [y2]}, {6: [first, second], 7: [second, first], 5: [z2], 8: [x1], 2: [y1], 1: [core]}
 
     def call(body, parts, outs, scratch, *operands):
         held = []
@@ -191,14 +185,12 @@
     far = swapped(away, "rep", 1)
     full = jnp.where(rep == 0, jnp.concatenate([near, far], axis=1), jnp.concatenate([far, near], axis=1))
 
-    early, inner, late = exchange(full)
+    early, late = exchange(full)
     (total,) = call(functools.partial(early_kernel, with_prior=False), early, [slope], [], ham, full)
-    (total,) = call(add_kernel, inner, [slope], [], total)
     first, middle = call(middle_kernel, late, [slope, whole], [], full, total)
 
-    early, inner, late = exchange(middle)
+    early, late = exchange(middle)
     (total,) = call(functools.partial(early_kernel, with_prior=True), early, [slope], [], ham, middle, first)
-    (total,) = call(add_kernel, inner, [slope], [], total)
     near, away = call(last_kernel, late, [half_float, half], [pltpu.VMEM((2, levels, levels), float32)], total)
     far = swapped(away, "rep", 1).astype(float32)
     stay = 1.0 - step_size * decay + (0.5 * step_size * step_size) * decay * decay

time: 136 us -> 135 us (level)
  the two profiles are of different devices: /device:TPU:102 before, /device:TPU:71 now
where the time goes in v13:
time: 135 us; the launch traced here: 134 us
  starting transfers between devices  82.3 us (61%)
  waiting for transfers between devices  35.7 us (26%)
  Pallas kernels  7.1 us (5%)
  other arithmetic  5.74 us (4%)
  between operations  2.32 us (2%)
    ppermute x16, starting transfers between devices, swapped(): return lax.ppermute(value, axis, pairs)  55.6 us
    ppermute x4, starting transfers between devices, across(): return lax.ppermute(value, ('z', 'core'), pairs)  26.8 us
    ppermute x16, waiting for transfers between devices, swapped(): return lax.ppermute(value, axis, pairs)  18.3 us
    ppermute x4, waiting for transfers between devices, across(): return lax.ppermute(value, ('z', 'core'), pairs)  17.4 us
    pallas_call x4, Pallas kernels, call(): pl.pallas_call(lambda *refs: body(counts, *refs), out_shape=outs, in_spec...  7.1 us
  transfers between devices with their start and end apart: 20, of which 7 were waited for; matrix products, arithmetic and copies ran while one was open for 3% of the time, Pallas kernels for 2%

profile of v13, /device:TPU:71, one launch (start us, length us, event | category | flops | bytes accessed | tf_op | source)
XLA Modules:
  0.0 133.9 jit_solution(310826266962426231)
XLA Ops:
  0.7 1.2 convert_bitcast_fusion
  1.9 3.0 %collective-permute-start = (bf16[2,128,256]{2,1,0:T(8,128)(2,1)S(1)}, bf16[2,128,256]{2,1,0:T(8,128)(2,1)S(1)}, u32[]{:S(2)}, u32[]{:S(2)}) collective-permute-start(bf16[2,128,256]{2,1,0:T(8,128)(2,1)S(1)} %get-tuple-element.29), channel_id=1, source_target_pairs={{0,1},{1,0},{2,3},{3,2},{4,5},{5,4},{6,7},{7,6},{8,9},{9,8},{10,11... | collective-permute-start | bytes 393224 | tf_op jit(solution)/shard_map/ppermute | solution.py:21
  8.1 1.6 %collective-permute-done = bf16[2,128,256]{2,1,0:T(8,128)(2,1)S(1)} collective-permute-done((bf16[2,128,256]{2,1,0:T(8,128)(2,1)S(1)}, bf16[2,128,256]{2,1,0:T(8,128)(2,1)S(1)}, u32[]{:S(2)}, u32[]{:S(2)}) %collective-permute-start) | collective-permute-done | bytes 131104 | tf_op jit(solution)/shard_map/ppermute | solution.py:21
  9.8 13.6 %collective-permute-start.4 = (bf16[2,256,256]{2,1,0:T(8,128)(2,1)S(1)}, bf16[2,256,256]{2,1,0:T(8,128)(2,1)S(1)}, u32[]{:S(2)}, u32[]{:S(2)}) collective-permute-start(bf16[2,256,256]{2,1,0:T(8,128)(2,1)S(1)} %maximum_select_fusion.refs_4_.refs_3_), channel_id=1, source_target_pairs={{0,64},{2,130},{16,80},{18,146},{32,96},{34,162},{48,112},{50,178}... | collective-permute-start | bytes 786440 | tf_op jit(solution)/shard_map/ppermute | solution.py:31
  25.5 2.6 %collective-permute-start.1 = (bf16[2,256,256]{2,1,0:T(8,128)(2,1)S(1)}, bf16[2,256,256]{2,1,0:T(8,128)(2,1)S(1)}, u32[]{:S(2)}, u32[]{:S(2)}) collective-permute-start(bf16[2,256,256]{2,1,0:T(8,128)(2,1)S(1)} %maximum_select_fusion.refs_4_.refs_3_), channel_id=1, source_target_pairs={{0,16},{16,0},{32,48},{48,32},{64,80},{80,64},{96,112},{112,96},{1... | collective-permute-start | bytes 786440 | tf_op jit(solution)/shard_map/ppermute | solution.py:21
  28.1 3.0 %collective-permute-start.2 = (bf16[2,256,256]{2,1,0:T(8,128)(2,1)S(1)}, bf16[2,256,256]{2,1,0:T(8,128)(2,1)S(1)}, u32[]{:S(2)}, u32[]{:S(2)}) collective-permute-start(bf16[2,256,256]{2,1,0:T(8,128)(2,1)S(1)} %maximum_select_fusion.refs_4_.refs_3_), channel_id=1, source_target_pairs={{0,1},{1,0},{2,3},{3,2},{4,5},{5,4},{6,7},{7,6},{8,9},{9,8},{10,11... | collective-permute-start | bytes 786440 | tf_op jit(solution)/shard_map/ppermute | solution.py:21
  31.2 3.1 %collective-permute-start.6 = (bf16[2,256,256]{2,1,0:T(8,128)(2,1)S(1)}, bf16[2,256,256]{2,1,0:T(8,128)(2,1)S(1)}, u32[]{:S(2)}, u32[]{:S(2)}) collective-permute-start(bf16[2,256,256]{2,1,0:T(8,128)(2,1)S(1)} %maximum_select_fusion.refs_4_.refs_3_), channel_id=1, source_target_pairs={{0,32},{16,48},{32,0},{48,16},{64,96},{80,112},{96,64},{112,80},{1... | collective-permute-start | bytes 786440 | tf_op jit(solution)/shard_map/ppermute | solution.py:21
  34.3 4.8 %collective-permute-start.3 = (bf16[2,256,256]{2,1,0:T(8,128)(2,1)S(1)}, bf16[2,256,256]{2,1,0:T(8,128)(2,1)S(1)}, u32[]{:S(2)}, u32[]{:S(2)}) collective-permute-start(bf16[2,256,256]{2,1,0:T(8,128)(2,1)S(1)} %maximum_select_fusion.refs_4_.refs_3_), channel_id=1, source_target_pairs={{0,8},{4,12},{8,0},{12,4},{1,9},{5,13},{9,1},{13,5},{2,10},{6,14},... | collective-permute-start | bytes 786440 | tf_op jit(solution)/shard_map/ppermute | solution.py:21
  39.1 5.6 %collective-permute-done.4.refs_5_ = bf16[2,256,256]{2,1,0:T(8,128)(2,1)S(1)} collective-permute-done((bf16[2,256,256]{2,1,0:T(8,128)(2,1)S(1)}, bf16[2,256,256]{2,1,0:T(8,128)(2,1)S(1)}, u32[]{:S(2)}, u32[]{:S(2)}) %collective-permute-start.4) | collective-permute-done | bytes 262176 | tf_op jit(solution)/shard_map/ppermute | solution.py:31
  44.7 1.9 %collective-permute-start.5 = (bf16[2,256,256]{2,1,0:T(8,128)(2,1)S(1)}, bf16[2,256,256]{2,1,0:T(8,128)(2,1)S(1)}, u32[]{:S(2)}, u32[]{:S(2)}) collective-permute-start(bf16[2,256,256]{2,1,0:T(8,128)(2,1)S(1)} %broadcast_select_fusion.1), channel_id=1, source_target_pairs={{0,192},{2,66},{16,208},{18,82},{32,224},{34,98},{48,240},{50,114}... | collective-permute-start | bytes 786440 | tf_op jit(solution)/shard_map/ppermute | solution.py:31
  46.7 2.5 %collective-permute-start.7 = (bf16[2,256,256]{2,1,0:T(8,128)(2,1)S(1)}, bf16[2,256,256]{2,1,0:T(8,128)(2,1)S(1)}, u32[]{:S(2)}, u32[]{:S(2)}) collective-permute-start(bf16[2,256,256]{2,1,0:T(8,128)(2,1)S(1)} %maximum_select_fusion.refs_4_.refs_3_), channel_id=1, source_target_pairs={{0,256},{256,0},{1,257},{257,1},{2,258},{258,2},{3,259},{259,3},{4... | collective-permute-start | bytes 786440 | tf_op jit(solution)/shard_map/ppermute | solution.py:21
  49.1 6.5 %collective-permute-done.1.refs_5_ = bf16[2,256,256]{2,1,0:T(8,128)(2,1)S(1)} collective-permute-done((bf16[2,256,256]{2,1,0:T(8,128)(2,1)S(1)}, bf16[2,256,256]{2,1,0:T(8,128)(2,1)S(1)}, u32[]{:S(2)}, u32[]{:S(2)}) %collective-permute-start.1) | collective-permute-done | bytes 262176 | tf_op jit(solution)/shard_map/ppermute | solution.py:21
  55.7 3.2 %collective-permute-start.8 = (bf16[2,256,256]{2,1,0:T(8,128)(2,1)S(1)}, bf16[2,256,256]{2,1,0:T(8,128)(2,1)S(1)}, u32[]{:S(2)}, u32[]{:S(2)}) collective-permute-start(bf16[2,256,256]{2,1,0:T(8,128)(2,1)S(1)} %maximum_select_fusion.refs_4_.refs_3_), channel_id=1, source_target_pairs={{0,4},{4,0},{8,12},{12,8},{1,5},{5,1},{9,13},{13,9},{2,6},{6,2},{1... | collective-permute-start | bytes 786440 | tf_op jit(solution)/shard_map/ppermute | solution.py:21
  58.9 2.3 %collective-permute-start.9 = (bf16[2,256,256]{2,1,0:T(8,128)(2,1)S(1)}, bf16[2,256,256]{2,1,0:T(8,128)(2,1)S(1)}, u32[]{:S(2)}, u32[]{:S(2)}) collective-permute-start(bf16[2,256,256]{2,1,0:T(8,128)(2,1)S(1)} %maximum_select_fusion.refs_4_.refs_3_), channel_id=1, source_target_pairs={{0,2},{2,0},{1,3},{3,1},{4,6},{6,4},{5,7},{7,5},{8,10},{10,8},{9,1... | collective-permute-start | bytes 786440 | tf_op jit(solution)/shard_map/ppermute | solution.py:21
  61.3 1.6 %shard_map.113.refs_4_ = f32[2,256,256]{2,1,0:T(8,128)S(1)} custom-call(s32[11]{0:T(128)S(1)} %pad_add_fusion.refs_0_, f32[3,9]{1,0:T(4,128)S(1)} %pad_maximum_fusion.1.refs_1_, bf16[12,256,256]{2,1,0:T(8,128)(2,1)S(1)} %copy-done, bf16[2,256,256]{2,1,0:T(8,128)(2,1)S(1)} %copy-done.1, bf16[2,256,256]{2,1,0:T(8,128)(2,1)S(1)} %maximum_select_fusion.refs_4_.refs_3_, ...), custom_call_target="tpu_custom_call" | custom-call | flops 402653184 | bytes 3408024 | tf_op jit(solution)/shard_map/pallas_call | solution.py:172
  62.9 2.5 %collective-permute-done.8.refs_9_ = bf16[2,256,256]{2,1,0:T(8,128)(2,1)S(1)} collective-permute-done((bf16[2,256,256]{2,1,0:T(8,128)(2,1)S(1)}, bf16[2,256,256]{2,1,0:T(8,128)(2,1)S(1)}, u32[]{:S(2)}, u32[]{:S(2)}) %collective-permute-start.8) | collective-permute-done | bytes 262176 | tf_op jit(solution)/shard_map/ppermute | solution.py:21
  65.4 2.0 %shard_map.114 = (f32[2,256,256]{2,1,0:T(8,128)S(1)}, bf16[2,256,256]{2,1,0:T(8,128)(2,1)S(1)}) custom-call(s32[11]{0:T(128)S(1)} %pad_add_fusion.refs_0_, f32[3,9]{1,0:T(4,128)S(1)} %pad_maximum_fusion.1.refs_1_, bf16[12,256,256]{2,1,0:T(8,128)(2,1)S(1)} %copy-done, bf16[2,256,256]{2,1,0:T(8,128)(2,1)S(1)} %maximum_select_fusion.refs_4_.refs_3_, ...), custom_call_target="tpu_custom_call" | custom-call | flops 805306368 | bytes 4718744 | tf_op jit(solution)/shard_map/pallas_call | solution.py:172
  67.4 4.3 %collective-permute-start.13 = (bf16[2,256,256]{2,1,0:T(8,128)(2,1)S(1)}, bf16[2,256,256]{2,1,0:T(8,128)(2,1)S(1)}, u32[]{:S(2)}, u32[]{:S(2)}) collective-permute-start(bf16[2,256,256]{2,1,0:T(8,128)(2,1)S(1)} %get-tuple-element.19.refs_4_), channel_id=1, source_target_pairs={{0,64},{2,130},{16,80},{18,146},{32,96},{34,162},{48,112},{50,178}... | collective-permute-start | bytes 786440 | tf_op jit(solution)/shard_map/ppermute | solution.py:31
  71.8 3.0 %collective-permute-start.11 = (bf16[2,256,256]{2,1,0:T(8,128)(2,1)S(1)}, bf16[2,256,256]{2,1,0:T(8,128)(2,1)S(1)}, u32[]{:S(2)}, u32[]{:S(2)}) collective-permute-start(bf16[2,256,256]{2,1,0:T(8,128)(2,1)S(1)} %get-tuple-element.19.refs_4_), channel_id=1, source_target_pairs={{0,1},{1,0},{2,3},{3,2},{4,5},{5,4},{6,7},{7,6},{8,9},{9,8},{10,11... | collective-permute-start | bytes 786440 | tf_op jit(solution)/shard_map/ppermute | solution.py:21
  74.8 1.9 %collective-permute-start.10 = (bf16[2,256,256]{2,1,0:T(8,128)(2,1)S(1)}, bf16[2,256,256]{2,1,0:T(8,128)(2,1)S(1)}, u32[]{:S(2)}, u32[]{:S(2)}) collective-permute-start(bf16[2,256,256]{2,1,0:T(8,128)(2,1)S(1)} %get-tuple-element.19.refs_4_), channel_id=1, source_target_pairs={{0,16},{16,0},{32,48},{48,32},{64,80},{80,64},{96,112},{112,96},{1... | collective-permute-start | bytes 786440 | tf_op jit(solution)/shard_map/ppermute | solution.py:21
  76.7 8.3 %collective-permute-start.15 = (bf16[2,256,256]{2,1,0:T(8,128)(2,1)S(1)}, bf16[2,256,256]{2,1,0:T(8,128)(2,1)S(1)}, u32[]{:S(2)}, u32[]{:S(2)}) collective-permute-start(bf16[2,256,256]{2,1,0:T(8,128)(2,1)S(1)} %get-tuple-element.19.refs_4_), channel_id=1, source_target_pairs={{0,32},{16,48},{32,0},{48,16},{64,96},{80,112},{96,64},{112,80},{1... | collective-permute-start | bytes 786440 | tf_op jit(solution)/shard_map/ppermute | solution.py:21
  85.0 5.0 %collective-permute-start.12 = (bf16[2,256,256]{2,1,0:T(8,128)(2,1)S(1)}, bf16[2,256,256]{2,1,0:T(8,128)(2,1)S(1)}, u32[]{:S(2)}, u32[]{:S(2)}) collective-permute-start(bf16[2,256,256]{2,1,0:T(8,128)(2,1)S(1)} %get-tuple-element.19.refs_4_), channel_id=1, source_target_pairs={{0,8},{4,12},{8,0},{12,4},{1,9},{5,13},{9,1},{13,5},{2,10},{6,14},... | collective-permute-start | bytes 786440 | tf_op jit(solution)/shard_map/ppermute | solution.py:21
  90.0 11.8 %collective-permute-done.13.refs_4_ = bf16[2,256,256]{2,1,0:T(8,128)(2,1)S(1)} collective-permute-done((bf16[2,256,256]{2,1,0:T(8,128)(2,1)S(1)}, bf16[2,256,256]{2,1,0:T(8,128)(2,1)S(1)}, u32[]{:S(2)}, u32[]{:S(2)}) %collective-permute-start.13) | collective-permute-done | bytes 262176 | tf_op jit(solution)/shard_map/ppermute | solution.py:31
  101.9 6.9 %collective-permute-start.14 = (bf16[2,256,256]{2,1,0:T(8,128)(2,1)S(1)}, bf16[2,256,256]{2,1,0:T(8,128)(2,1)S(1)}, u32[]{:S(2)}, u32[]{:S(2)}) collective-permute-start(bf16[2,256,256]{2,1,0:T(8,128)(2,1)S(1)} %broadcast_select_fusion), channel_id=1, source_target_pairs={{0,192},{2,66},{16,208},{18,82},{32,224},{34,98},{48,240},{50,114}... | collective-permute-start | bytes 786440 | tf_op jit(solution)/shard_map/ppermute | solution.py:31
  108.7 6.9 %collective-permute-start.16 = (bf16[2,256,256]{2,1,0:T(8,128)(2,1)S(1)}, bf16[2,256,256]{2,1,0:T(8,128)(2,1)S(1)}, u32[]{:S(2)}, u32[]{:S(2)}) collective-permute-start(bf16[2,256,256]{2,1,0:T(8,128)(2,1)S(1)} %get-tuple-element.19.refs_4_), channel_id=1, source_target_pairs={{0,256},{256,0},{1,257},{257,1},{2,258},{258,2},{3,259},{259,3},{4... | collective-permute-start | bytes 786440 | tf_op jit(solution)/shard_map/ppermute | solution.py:21
  115.7 1.9 %collective-permute-start.17 = (bf16[2,256,256]{2,1,0:T(8,128)(2,1)S(1)}, bf16[2,256,256]{2,1,0:T(8,128)(2,1)S(1)}, u32[]{:S(2)}, u32[]{:S(2)}) collective-permute-start(bf16[2,256,256]{2,1,0:T(8,128)(2,1)S(1)} %get-tuple-element.19.refs_4_), channel_id=1, source_target_pairs={{0,4},{4,0},{8,12},{12,8},{1,5},{5,1},{9,13},{13,9},{2,6},{6,2},{1... | collective-permute-start | bytes 786440 | tf_op jit(solution)/shard_map/ppermute | solution.py:21
  117.6 1.9 %collective-permute-start.18 = (bf16[2,256,256]{2,1,0:T(8,128)(2,1)S(1)}, bf16[2,256,256]{2,1,0:T(8,128)(2,1)S(1)}, u32[]{:S(2)}, u32[]{:S(2)}) collective-permute-start(bf16[2,256,256]{2,1,0:T(8,128)(2,1)S(1)} %get-tuple-element.19.refs_4_), channel_id=1, source_target_pairs={{0,2},{2,0},{1,3},{3,1},{4,6},{6,4},{5,7},{7,5},{8,10},{10,8},{9,1... | collective-permute-start | bytes 786440 | tf_op jit(solution)/shard_map/ppermute | solution.py:21
  119.6 1.6 %shard_map.115.refs_3_ = f32[2,256,256]{2,1,0:T(8,128)S(1)} custom-call(s32[11]{0:T(128)S(1)} %pad_add_fusion.refs_0_, f32[3,9]{1,0:T(4,128)S(1)} %pad_maximum_fusion.1.refs_1_, bf16[12,256,256]{2,1,0:T(8,128)(2,1)S(1)} %copy-done, bf16[2,256,256]{2,1,0:T(8,128)(2,1)S(1)} %copy-done.1, bf16[2,256,256]{2,1,0:T(8,128)(2,1)S(1)} %get-tuple-element.19.refs_4_, ...), custom_call_target="tpu_custom_call" | custom-call | flops 402653184 | bytes 3932312 | tf_op jit(solution)/shard_map/pallas_call | solution.py:172
  121.2 1.6 %collective-permute-done.17.refs_8_ = bf16[2,256,256]{2,1,0:T(8,128)(2,1)S(1)} collective-permute-done((bf16[2,256,256]{2,1,0:T(8,128)(2,1)S(1)}, bf16[2,256,256]{2,1,0:T(8,128)(2,1)S(1)}, u32[]{:S(2)}, u32[]{:S(2)}) %collective-permute-start.17) | collective-permute-done | bytes 262176 | tf_op jit(solution)/shard_map/ppermute | solution.py:21
  122.8 1.9 %shard_map.116 = (f32[2,128,256]{2,1,0:T(8,128)S(1)}, bf16[2,128,256]{2,1,0:T(8,128)(2,1)S(1)}) custom-call(s32[11]{0:T(128)S(1)} %pad_add_fusion.refs_0_, f32[3,9]{1,0:T(4,128)S(1)} %pad_maximum_fusion.1.refs_1_, bf16[12,256,256]{2,1,0:T(8,128)(2,1)S(1)} %copy-done, f32[2,256,256]{2,1,0:T(8,128)S(1)} %shard_map.115.refs_3_, ...), custom_call_target="tpu_custom_call" | custom-call | flops 805306368 | bytes 4063384 | tf_op jit(solution)/shard_map/pallas_call | solution.py:172
  124.7 2.1 %collective-permute-start.19 = (bf16[2,128,256]{2,1,0:T(8,128)(2,1)S(1)}, bf16[2,128,256]{2,1,0:T(8,128)(2,1)S(1)}, u32[]{:S(2)}, u32[]{:S(2)}) collective-permute-start(bf16[2,128,256]{2,1,0:T(8,128)(2,1)S(1)} %get-tuple-element.21), channel_id=1, source_target_pairs={{0,1},{1,0},{2,3},{3,2},{4,5},{5,4},{6,7},{7,6},{8,9},{9,8},{10,11... | collective-permute-start | bytes 393224 | tf_op jit(solution)/shard_map/ppermute | solution.py:21
  126.8 6.1 %collective-permute-done.19 = bf16[2,128,256]{2,1,0:T(8,128)(2,1)S(1)} collective-permute-done((bf16[2,128,256]{2,1,0:T(8,128)(2,1)S(1)}, bf16[2,128,256]{2,1,0:T(8,128)(2,1)S(1)}, u32[]{:S(2)}, u32[]{:S(2)}) %collective-permute-start.19) | collective-permute-done | bytes 131104 | tf_op jit(solution)/shard_map/ppermute | solution.py:21
  (42 shorter events, 5.3 us)
Async XLA Ops:
  0.6 60.7 %copy-start = (bf16[12,256,256]{2,1,0:T(8,128)(2,1)S(1)}, bf16[12,256,256]{2,1,0:T(8,128)(2,1)}, u32[]{:S(2)}) copy-start(bf16[12,256,256]{2,1,0:T(8,128)(2,1)} %refs_2_.7) | copy-start | bytes 4718596
  0.6 60.7 %copy-start.1 = (bf16[2,256,256]{2,1,0:T(8,128)(2,1)S(1)}, bf16[2,256,256]{2,1,0:T(8,128)(2,1)}, u32[]{:S(2)}) copy-start(bf16[2,256,256]{2,1,0:T(8,128)(2,1)} %refs_3_.3) | copy-start | bytes 786436
  1.9 7.8 %collective-permute-start = (bf16[2,128,256]{2,1,0:T(8,128)(2,1)S(1)}, bf16[2,128,256]{2,1,0:T(8,128)(2,1)S(1)}, u32[]{:S(2)}, u32[]{:S(2)}) collective-permute-start(bf16[2,128,256]{2,1,0:T(8,128)(2,1)S(1)} %get-tuple-element.29), channel_id=1, source_target_pairs={{0,1},{1,0},{2,3},{3,2},{4,5},{5,4},{6,7},{7,6},{8,9},{9,8},{10,11... | collective-permute-start | bytes 393224 | tf_op jit(solution)/shard_map/ppermute | solution.py:21
  9.8 35.0 %collective-permute-start.4 = (bf16[2,256,256]{2,1,0:T(8,128)(2,1)S(1)}, bf16[2,256,256]{2,1,0:T(8,128)(2,1)S(1)}, u32[]{:S(2)}, u32[]{:S(2)}) collective-permute-start(bf16[2,256,256]{2,1,0:T(8,128)(2,1)S(1)} %maximum_select_fusion.refs_4_.refs_3_), channel_id=1, source_target_pairs={{0,64},{2,130},{16,80},{18,146},{32,96},{34,162},{48,112},{50,178}... | collective-permute-start | bytes 786440 | tf_op jit(solution)/shard_map/ppermute | solution.py:31
  25.5 30.2 %collective-permute-start.1 = (bf16[2,256,256]{2,1,0:T(8,128)(2,1)S(1)}, bf16[2,256,256]{2,1,0:T(8,128)(2,1)S(1)}, u32[]{:S(2)}, u32[]{:S(2)}) collective-permute-start(bf16[2,256,256]{2,1,0:T(8,128)(2,1)S(1)} %maximum_select_fusion.refs_4_.refs_3_), channel_id=1, source_target_pairs={{0,16},{16,0},{32,48},{48,32},{64,80},{80,64},{96,112},{112,96},{1... | collective-permute-start | bytes 786440 | tf_op jit(solution)/shard_map/ppermute | solution.py:21
  28.1 18.5 %collective-permute-start.2 = (bf16[2,256,256]{2,1,0:T(8,128)(2,1)S(1)}, bf16[2,256,256]{2,1,0:T(8,128)(2,1)S(1)}, u32[]{:S(2)}, u32[]{:S(2)}) collective-permute-start(bf16[2,256,256]{2,1,0:T(8,128)(2,1)S(1)} %maximum_select_fusion.refs_4_.refs_3_), channel_id=1, source_target_pairs={{0,1},{1,0},{2,3},{3,2},{4,5},{5,4},{6,7},{7,6},{8,9},{9,8},{10,11... | collective-permute-start | bytes 786440 | tf_op jit(solution)/shard_map/ppermute | solution.py:21
  31.2 27.7 %collective-permute-start.6 = (bf16[2,256,256]{2,1,0:T(8,128)(2,1)S(1)}, bf16[2,256,256]{2,1,0:T(8,128)(2,1)S(1)}, u32[]{:S(2)}, u32[]{:S(2)}) collective-permute-start(bf16[2,256,256]{2,1,0:T(8,128)(2,1)S(1)} %maximum_select_fusion.refs_4_.refs_3_), channel_id=1, source_target_pairs={{0,32},{16,48},{32,0},{48,16},{64,96},{80,112},{96,64},{112,80},{1... | collective-permute-start | bytes 786440 | tf_op jit(solution)/shard_map/ppermute | solution.py:21
  34.3 27.0 %collective-permute-start.3 = (bf16[2,256,256]{2,1,0:T(8,128)(2,1)S(1)}, bf16[2,256,256]{2,1,0:T(8,128)(2,1)S(1)}, u32[]{:S(2)}, u32[]{:S(2)}) collective-permute-start(bf16[2,256,256]{2,1,0:T(8,128)(2,1)S(1)} %maximum_select_fusion.refs_4_.refs_3_), channel_id=1, source_target_pairs={{0,8},{4,12},{8,0},{12,4},{1,9},{5,13},{9,1},{13,5},{2,10},{6,14},... | collective-permute-start | bytes 786440 | tf_op jit(solution)/shard_map/ppermute | solution.py:21
  44.7 18.2 %collective-permute-start.5 = (bf16[2,256,256]{2,1,0:T(8,128)(2,1)S(1)}, bf16[2,256,256]{2,1,0:T(8,128)(2,1)S(1)}, u32[]{:S(2)}, u32[]{:S(2)}) collective-permute-start(bf16[2,256,256]{2,1,0:T(8,128)(2,1)S(1)} %broadcast_select_fusion.1), channel_id=1, source_target_pairs={{0,192},{2,66},{16,208},{18,82},{32,224},{34,98},{48,240},{50,114}... | collective-permute-start | bytes 786440 | tf_op jit(solution)/shard_map/ppermute | solution.py:31
  46.7 16.2 %collective-permute-start.7 = (bf16[2,256,256]{2,1,0:T(8,128)(2,1)S(1)}, bf16[2,256,256]{2,1,0:T(8,128)(2,1)S(1)}, u32[]{:S(2)}, u32[]{:S(2)}) collective-permute-start(bf16[2,256,256]{2,1,0:T(8,128)(2,1)S(1)} %maximum_select_fusion.refs_4_.refs_3_), channel_id=1, source_target_pairs={{0,256},{256,0},{1,257},{257,1},{2,258},{258,2},{3,259},{259,3},{4... | collective-permute-start | bytes 786440 | tf_op jit(solution)/shard_map/ppermute | solution.py:21
  55.7 9.7 %collective-permute-start.8 = (bf16[2,256,256]{2,1,0:T(8,128)(2,1)S(1)}, bf16[2,256,256]{2,1,0:T(8,128)(2,1)S(1)}, u32[]{:S(2)}, u32[]{:S(2)}) collective-permute-start(bf16[2,256,256]{2,1,0:T(8,128)(2,1)S(1)} %maximum_select_fusion.refs_4_.refs_3_), channel_id=1, source_target_pairs={{0,4},{4,0},{8,12},{12,8},{1,5},{5,1},{9,13},{13,9},{2,6},{6,2},{1... | collective-permute-start | bytes 786440 | tf_op jit(solution)/shard_map/ppermute | solution.py:21
  58.9 6.5 %collective-permute-start.9 = (bf16[2,256,256]{2,1,0:T(8,128)(2,1)S(1)}, bf16[2,256,256]{2,1,0:T(8,128)(2,1)S(1)}, u32[]{:S(2)}, u32[]{:S(2)}) collective-permute-start(bf16[2,256,256]{2,1,0:T(8,128)(2,1)S(1)} %maximum_select_fusion.refs_4_.refs_3_), channel_id=1, source_target_pairs={{0,2},{2,0},{1,3},{3,1},{4,6},{6,4},{5,7},{7,5},{8,10},{10,8},{9,1... | collective-permute-start | bytes 786440 | tf_op jit(solution)/shard_map/ppermute | solution.py:21
  67.4 34.4 %collective-permute-start.13 = (bf16[2,256,256]{2,1,0:T(8,128)(2,1)S(1)}, bf16[2,256,256]{2,1,0:T(8,128)(2,1)S(1)}, u32[]{:S(2)}, u32[]{:S(2)}) collective-permute-start(bf16[2,256,256]{2,1,0:T(8,128)(2,1)S(1)} %get-tuple-element.19.refs_4_), channel_id=1, source_target_pairs={{0,64},{2,130},{16,80},{18,146},{32,96},{34,162},{48,112},{50,178}... | collective-permute-start | bytes 786440 | tf_op jit(solution)/shard_map/ppermute | solution.py:31
  71.8 37.0 %collective-permute-start.11 = (bf16[2,256,256]{2,1,0:T(8,128)(2,1)S(1)}, bf16[2,256,256]{2,1,0:T(8,128)(2,1)S(1)}, u32[]{:S(2)}, u32[]{:S(2)}) collective-permute-start(bf16[2,256,256]{2,1,0:T(8,128)(2,1)S(1)} %get-tuple-element.19.refs_4_), channel_id=1, source_target_pairs={{0,1},{1,0},{2,3},{3,2},{4,5},{5,4},{6,7},{7,6},{8,9},{9,8},{10,11... | collective-permute-start | bytes 786440 | tf_op jit(solution)/shard_map/ppermute | solution.py:21
  74.8 40.8 %collective-permute-start.10 = (bf16[2,256,256]{2,1,0:T(8,128)(2,1)S(1)}, bf16[2,256,256]{2,1,0:T(8,128)(2,1)S(1)}, u32[]{:S(2)}, u32[]{:S(2)}) collective-permute-start(bf16[2,256,256]{2,1,0:T(8,128)(2,1)S(1)} %get-tuple-element.19.refs_4_), channel_id=1, source_target_pairs={{0,16},{16,0},{32,48},{48,32},{64,80},{80,64},{96,112},{112,96},{1... | collective-permute-start | bytes 786440 | tf_op jit(solution)/shard_map/ppermute | solution.py:21
  76.7 40.8 %collective-permute-start.15 = (bf16[2,256,256]{2,1,0:T(8,128)(2,1)S(1)}, bf16[2,256,256]{2,1,0:T(8,128)(2,1)S(1)}, u32[]{:S(2)}, u32[]{:S(2)}) collective-permute-start(bf16[2,256,256]{2,1,0:T(8,128)(2,1)S(1)} %get-tuple-element.19.refs_4_), channel_id=1, source_target_pairs={{0,32},{16,48},{32,0},{48,16},{64,96},{80,112},{96,64},{112,80},{1... | collective-permute-start | bytes 786440 | tf_op jit(solution)/shard_map/ppermute | solution.py:21
  85.0 34.5 %collective-permute-start.12 = (bf16[2,256,256]{2,1,0:T(8,128)(2,1)S(1)}, bf16[2,256,256]{2,1,0:T(8,128)(2,1)S(1)}, u32[]{:S(2)}, u32[]{:S(2)}) collective-permute-start(bf16[2,256,256]{2,1,0:T(8,128)(2,1)S(1)} %get-tuple-element.19.refs_4_), channel_id=1, source_target_pairs={{0,8},{4,12},{8,0},{12,4},{1,9},{5,13},{9,1},{13,5},{2,10},{6,14},... | collective-permute-start | bytes 786440 | tf_op jit(solution)/shard_map/ppermute | solution.py:21
  101.9 19.3 %collective-permute-start.14 = (bf16[2,256,256]{2,1,0:T(8,128)(2,1)S(1)}, bf16[2,256,256]{2,1,0:T(8,128)(2,1)S(1)}, u32[]{:S(2)}, u32[]{:S(2)}) collective-permute-start(bf16[2,256,256]{2,1,0:T(8,128)(2,1)S(1)} %broadcast_select_fusion), channel_id=1, source_target_pairs={{0,192},{2,66},{16,208},{18,82},{32,224},{34,98},{48,240},{50,114}... | collective-permute-start | bytes 786440 | tf_op jit(solution)/shard_map/ppermute | solution.py:31
  108.7 12.5 %collective-permute-start.16 = (bf16[2,256,256]{2,1,0:T(8,128)(2,1)S(1)}, bf16[2,256,256]{2,1,0:T(8,128)(2,1)S(1)}, u32[]{:S(2)}, u32[]{:S(2)}) collective-permute-start(bf16[2,256,256]{2,1,0:T(8,128)(2,1)S(1)} %get-tuple-element.19.refs_4_), channel_id=1, source_target_pairs={{0,256},{256,0},{1,257},{257,1},{2,258},{258,2},{3,259},{259,3},{4... | collective-permute-start | bytes 786440 | tf_op jit(solution)/shard_map/ppermute | solution.py:21
  115.7 7.1 %collective-permute-start.17 = (bf16[2,256,256]{2,1,0:T(8,128)(2,1)S(1)}, bf16[2,256,256]{2,1,0:T(8,128)(2,1)S(1)}, u32[]{:S(2)}, u32[]{:S(2)}) collective-permute-start(bf16[2,256,256]{2,1,0:T(8,128)(2,1)S(1)} %get-tuple-element.19.refs_4_), channel_id=1, source_target_pairs={{0,4},{4,0},{8,12},{12,8},{1,5},{5,1},{9,13},{13,9},{2,6},{6,2},{1... | collective-permute-start | bytes 786440 | tf_op jit(solution)/shard_map/ppermute | solution.py:21
  117.6 5.2 %collective-permute-start.18 = (bf16[2,256,256]{2,1,0:T(8,128)(2,1)S(1)}, bf16[2,256,256]{2,1,0:T(8,128)(2,1)S(1)}, u32[]{:S(2)}, u32[]{:S(2)}) collective-permute-start(bf16[2,256,256]{2,1,0:T(8,128)(2,1)S(1)} %get-tuple-element.19.refs_4_), channel_id=1, source_target_pairs={{0,2},{2,0},{1,3},{3,1},{4,6},{6,4},{5,7},{7,5},{8,10},{10,8},{9,1... | collective-permute-start | bytes 786440 | tf_op jit(solution)/shard_map/ppermute | solution.py:21
  124.7 8.2 %copy-start.2 = (f32[2,128,256]{2,1,0:T(8,128)S(1)}, f32[2,128,256]{2,1,0:T(8,128)}, u32[]{:S(2)}) copy-start(f32[2,128,256]{2,1,0:T(8,128)} %param.11) | copy-start | bytes 786436
  124.7 8.2 %copy-start.3 = (f32[2,128,256]{2,1,0:T(8,128)S(1)}, f32[2,128,256]{2,1,0:T(8,128)}, u32[]{:S(2)}) copy-start(f32[2,128,256]{2,1,0:T(8,128)} %param.10) | copy-start | bytes 786436
  124.7 8.2 %collective-permute-start.19 = (bf16[2,128,256]{2,1,0:T(8,128)(2,1)S(1)}, bf16[2,128,256]{2,1,0:T(8,128)(2,1)S(1)}, u32[]{:S(2)}, u32[]{:S(2)}) collective-permute-start(bf16[2,128,256]{2,1,0:T(8,128)(2,1)S(1)} %get-tuple-element.21), channel_id=1, source_target_pairs={{0,1},{1,0},{2,3},{3,2},{4,5},{5,4},{6,7},{7,6},{8,9},{9,8},{10,11... | collective-permute-start | bytes 393224 | tf_op jit(solution)/shard_map/ppermute | solution.py:21

commit v14 on v13

--- a/solution.py
+++ b/solution.py
@@ -154,8 +154,8 @@
         y2 = swapped(full, "y", 2)
         second = across(jnp.where(on_first, first, full), outward, inward)
         x1 = swapped(after(full, first, x2), "x_lo", 1)
-        y1 = swapped(after(full, first, z1), "y", 1)
-        core = swapped(after(full, first, z2), "core", 1)
+        y1 = swapped(after(full, first, y2), "y", 1)
+        core = swapped(after(full, first, z2, z1), "core", 1)
         return {4: [z1], 0: [x2], 3: [y2]}, {6: [first, second], 7: [second, first], 5: [z2], 8: [x1], 2: [y1], 1: [core]}
 
     def call(body, parts, outs, scratch, *operands):

time: 135 us -> 135 us (level)
  the two profiles are of different devices: /device:TPU:71 before, /device:TPU:1 now
where the time goes in v14:
time: 135 us
  starting transfers between devices  97.7 us (72%)
  waiting for transfers between devices  21 us (16%)
  Pallas kernels  7.1 us (5%)
  other arithmetic  5.74 us (4%)
  between operations  2.35 us (2%)
    ppermute x16, starting transfers between devices, swapped(): return lax.ppermute(value, axis, pairs)  57.2 us
    ppermute x4, starting transfers between devices, across(): return lax.ppermute(value, ('z', 'core'), pairs)  40.5 us
    ppermute x16, waiting for transfers between devices, swapped(): return lax.ppermute(value, axis, pairs)  20.2 us
    pallas_call x4, Pallas kernels, call(): pl.pallas_call(lambda *refs: body(counts, *refs), out_shape=outs, in_spec...  7.1 us
  transfers between devices with their start and end apart: 20, of which 5 were waited for; matrix products, arithmetic and copies ran while one was open for 3% of the time, Pallas kernels for 2%

profile of v14, /device:TPU:1, one launch (start us, length us, event | category | flops | bytes accessed | tf_op | source)
XLA Modules:
  0.0 134.6 jit_solution(10757996289737260196)
XLA Ops:
  0.7 1.2 convert_bitcast_fusion
  1.9 5.5 %collective-permute-start = (bf16[2,128,256]{2,1,0:T(8,128)(2,1)S(1)}, bf16[2,128,256]{2,1,0:T(8,128)(2,1)S(1)}, u32[]{:S(2)}, u32[]{:S(2)}) collective-permute-start(bf16[2,128,256]{2,1,0:T(8,128)(2,1)S(1)} %get-tuple-element.29), channel_id=1, source_target_pairs={{0,1},{1,0},{2,3},{3,2},{4,5},{5,4},{6,7},{7,6},{8,9},{9,8},{10,11... | collective-permute-start | bytes 393224 | tf_op jit(solution)/shard_map/ppermute | solution.py:21
  8.1 0.8 multiply_reduce_fusion
  8.9 0.8 fusion.4
  10.6 15.4 %collective-permute-start.4 = (bf16[2,256,256]{2,1,0:T(8,128)(2,1)S(1)}, bf16[2,256,256]{2,1,0:T(8,128)(2,1)S(1)}, u32[]{:S(2)}, u32[]{:S(2)}) collective-permute-start(bf16[2,256,256]{2,1,0:T(8,128)(2,1)S(1)} %maximum_select_fusion.refs_4_.refs_3_), channel_id=1, source_target_pairs={{0,64},{2,130},{16,80},{18,146},{32,96},{34,162},{48,112},{50,178}... | collective-permute-start | bytes 786440 | tf_op jit(solution)/shard_map/ppermute | solution.py:31
  28.2 2.6 %collective-permute-start.1 = (bf16[2,256,256]{2,1,0:T(8,128)(2,1)S(1)}, bf16[2,256,256]{2,1,0:T(8,128)(2,1)S(1)}, u32[]{:S(2)}, u32[]{:S(2)}) collective-permute-start(bf16[2,256,256]{2,1,0:T(8,128)(2,1)S(1)} %maximum_select_fusion.refs_4_.refs_3_), channel_id=1, source_target_pairs={{0,16},{16,0},{32,48},{48,32},{64,80},{80,64},{96,112},{112,96},{1... | collective-permute-start | bytes 786440 | tf_op jit(solution)/shard_map/ppermute | solution.py:21
  30.8 4.6 %collective-permute-start.2 = (bf16[2,256,256]{2,1,0:T(8,128)(2,1)S(1)}, bf16[2,256,256]{2,1,0:T(8,128)(2,1)S(1)}, u32[]{:S(2)}, u32[]{:S(2)}) collective-permute-start(bf16[2,256,256]{2,1,0:T(8,128)(2,1)S(1)} %maximum_select_fusion.refs_4_.refs_3_), channel_id=1, source_target_pairs={{0,1},{1,0},{2,3},{3,2},{4,5},{5,4},{6,7},{7,6},{8,9},{9,8},{10,11... | collective-permute-start | bytes 786440 | tf_op jit(solution)/shard_map/ppermute | solution.py:21
  35.4 4.8 %collective-permute-start.3 = (bf16[2,256,256]{2,1,0:T(8,128)(2,1)S(1)}, bf16[2,256,256]{2,1,0:T(8,128)(2,1)S(1)}, u32[]{:S(2)}, u32[]{:S(2)}) collective-permute-start(bf16[2,256,256]{2,1,0:T(8,128)(2,1)S(1)} %maximum_select_fusion.refs_4_.refs_3_), channel_id=1, source_target_pairs={{0,8},{4,12},{8,0},{12,4},{1,9},{5,13},{9,1},{13,5},{2,10},{6,14},... | collective-permute-start | bytes 786440 | tf_op jit(solution)/shard_map/ppermute | solution.py:21
  40.3 3.1 %collective-permute-start.6 = (bf16[2,256,256]{2,1,0:T(8,128)(2,1)S(1)}, bf16[2,256,256]{2,1,0:T(8,128)(2,1)S(1)}, u32[]{:S(2)}, u32[]{:S(2)}) collective-permute-start(bf16[2,256,256]{2,1,0:T(8,128)(2,1)S(1)} %maximum_select_fusion.refs_4_.refs_3_), channel_id=1, source_target_pairs={{0,32},{16,48},{32,0},{48,16},{64,96},{80,112},{96,64},{112,80},{1... | collective-permute-start | bytes 786440 | tf_op jit(solution)/shard_map/ppermute | solution.py:21
  43.4 8.6 %collective-permute-start.5 = (bf16[2,256,256]{2,1,0:T(8,128)(2,1)S(1)}, bf16[2,256,256]{2,1,0:T(8,128)(2,1)S(1)}, u32[]{:S(2)}, u32[]{:S(2)}) collective-permute-start(bf16[2,256,256]{2,1,0:T(8,128)(2,1)S(1)} %broadcast_select_fusion.1), channel_id=1, source_target_pairs={{0,192},{2,66},{16,208},{18,82},{32,224},{34,98},{48,240},{50,114}... | collective-permute-start | bytes 786440 | tf_op jit(solution)/shard_map/ppermute | solution.py:31
  52.1 3.5 %collective-permute-start.7 = (bf16[2,256,256]{2,1,0:T(8,128)(2,1)S(1)}, bf16[2,256,256]{2,1,0:T(8,128)(2,1)S(1)}, u32[]{:S(2)}, u32[]{:S(2)}) collective-permute-start(bf16[2,256,256]{2,1,0:T(8,128)(2,1)S(1)} %maximum_select_fusion.refs_4_.refs_3_), channel_id=1, source_target_pairs={{0,256},{256,0},{1,257},{257,1},{2,258},{258,2},{3,259},{259,3},{4... | collective-permute-start | bytes 786440 | tf_op jit(solution)/shard_map/ppermute | solution.py:21
  55.6 5.9 %collective-permute-start.8 = (bf16[2,256,256]{2,1,0:T(8,128)(2,1)S(1)}, bf16[2,256,256]{2,1,0:T(8,128)(2,1)S(1)}, u32[]{:S(2)}, u32[]{:S(2)}) collective-permute-start(bf16[2,256,256]{2,1,0:T(8,128)(2,1)S(1)} %maximum_select_fusion.refs_4_.refs_3_), channel_id=1, source_target_pairs={{0,4},{4,0},{8,12},{12,8},{1,5},{5,1},{9,13},{13,9},{2,6},{6,2},{1... | collective-permute-start | bytes 786440 | tf_op jit(solution)/shard_map/ppermute | solution.py:21
  62.1 1.9 %collective-permute-start.9 = (bf16[2,256,256]{2,1,0:T(8,128)(2,1)S(1)}, bf16[2,256,256]{2,1,0:T(8,128)(2,1)S(1)}, u32[]{:S(2)}, u32[]{:S(2)}) collective-permute-start(bf16[2,256,256]{2,1,0:T(8,128)(2,1)S(1)} %maximum_select_fusion.refs_4_.refs_3_), channel_id=1, source_target_pairs={{0,2},{2,0},{1,3},{3,1},{4,6},{6,4},{5,7},{7,5},{8,10},{10,8},{9,1... | collective-permute-start | bytes 786440 | tf_op jit(solution)/shard_map/ppermute | solution.py:21
  64.1 1.6 %shard_map.113.refs_4_ = f32[2,256,256]{2,1,0:T(8,128)S(1)} custom-call(s32[11]{0:T(128)S(1)} %pad_add_fusion.refs_0_, f32[3,9]{1,0:T(4,128)S(1)} %pad_maximum_fusion.1.refs_1_, bf16[12,256,256]{2,1,0:T(8,128)(2,1)S(1)} %copy-done, bf16[2,256,256]{2,1,0:T(8,128)(2,1)S(1)} %copy-done.1, bf16[2,256,256]{2,1,0:T(8,128)(2,1)S(1)} %maximum_select_fusion.refs_4_.refs_3_, ...), custom_call_target="tpu_custom_call" | custom-call | flops 402653184 | bytes 3408024 | tf_op jit(solution)/shard_map/pallas_call | solution.py:172
  65.7 2.0 %shard_map.114 = (f32[2,256,256]{2,1,0:T(8,128)S(1)}, bf16[2,256,256]{2,1,0:T(8,128)(2,1)S(1)}) custom-call(s32[11]{0:T(128)S(1)} %pad_add_fusion.refs_0_, f32[3,9]{1,0:T(4,128)S(1)} %pad_maximum_fusion.1.refs_1_, bf16[12,256,256]{2,1,0:T(8,128)(2,1)S(1)} %copy-done, bf16[2,256,256]{2,1,0:T(8,128)(2,1)S(1)} %maximum_select_fusion.refs_4_.refs_3_, ...), custom_call_target="tpu_custom_call" | custom-call | flops 805306368 | bytes 4718744 | tf_op jit(solution)/shard_map/pallas_call | solution.py:172
  67.7 12.5 %collective-permute-start.13 = (bf16[2,256,256]{2,1,0:T(8,128)(2,1)S(1)}, bf16[2,256,256]{2,1,0:T(8,128)(2,1)S(1)}, u32[]{:S(2)}, u32[]{:S(2)}) collective-permute-start(bf16[2,256,256]{2,1,0:T(8,128)(2,1)S(1)} %get-tuple-element.19.refs_4_), channel_id=1, source_target_pairs={{0,64},{2,130},{16,80},{18,146},{32,96},{34,162},{48,112},{50,178}... | collective-permute-start | bytes 786440 | tf_op jit(solution)/shard_map/ppermute | solution.py:31
  80.3 4.2 %collective-permute-start.11 = (bf16[2,256,256]{2,1,0:T(8,128)(2,1)S(1)}, bf16[2,256,256]{2,1,0:T(8,128)(2,1)S(1)}, u32[]{:S(2)}, u32[]{:S(2)}) collective-permute-start(bf16[2,256,256]{2,1,0:T(8,128)(2,1)S(1)} %get-tuple-element.19.refs_4_), channel_id=1, source_target_pairs={{0,1},{1,0},{2,3},{3,2},{4,5},{5,4},{6,7},{7,6},{8,9},{9,8},{10,11... | collective-permute-start | bytes 786440 | tf_op jit(solution)/shard_map/ppermute | solution.py:21
  84.5 5.4 %collective-permute-start.12 = (bf16[2,256,256]{2,1,0:T(8,128)(2,1)S(1)}, bf16[2,256,256]{2,1,0:T(8,128)(2,1)S(1)}, u32[]{:S(2)}, u32[]{:S(2)}) collective-permute-start(bf16[2,256,256]{2,1,0:T(8,128)(2,1)S(1)} %get-tuple-element.19.refs_4_), channel_id=1, source_target_pairs={{0,8},{4,12},{8,0},{12,4},{1,9},{5,13},{9,1},{13,5},{2,10},{6,14},... | collective-permute-start | bytes 786440 | tf_op jit(solution)/shard_map/ppermute | solution.py:21
  89.9 1.9 %collective-permute-start.10 = (bf16[2,256,256]{2,1,0:T(8,128)(2,1)S(1)}, bf16[2,256,256]{2,1,0:T(8,128)(2,1)S(1)}, u32[]{:S(2)}, u32[]{:S(2)}) collective-permute-start(bf16[2,256,256]{2,1,0:T(8,128)(2,1)S(1)} %get-tuple-element.19.refs_4_), channel_id=1, source_target_pairs={{0,16},{16,0},{32,48},{48,32},{64,80},{80,64},{96,112},{112,96},{1... | collective-permute-start | bytes 786440 | tf_op jit(solution)/shard_map/ppermute | solution.py:21
  91.8 1.9 %collective-permute-start.15 = (bf16[2,256,256]{2,1,0:T(8,128)(2,1)S(1)}, bf16[2,256,256]{2,1,0:T(8,128)(2,1)S(1)}, u32[]{:S(2)}, u32[]{:S(2)}) collective-permute-start(bf16[2,256,256]{2,1,0:T(8,128)(2,1)S(1)} %get-tuple-element.19.refs_4_), channel_id=1, source_target_pairs={{0,32},{16,48},{32,0},{48,16},{64,96},{80,112},{96,64},{112,80},{1... | collective-permute-start | bytes 786440 | tf_op jit(solution)/shard_map/ppermute | solution.py:21
  93.7 0.8 collective-permute-done.13.refs_4_
  94.5 3.9 %collective-permute-start.14 = (bf16[2,256,256]{2,1,0:T(8,128)(2,1)S(1)}, bf16[2,256,256]{2,1,0:T(8,128)(2,1)S(1)}, u32[]{:S(2)}, u32[]{:S(2)}) collective-permute-start(bf16[2,256,256]{2,1,0:T(8,128)(2,1)S(1)} %broadcast_select_fusion), channel_id=1, source_target_pairs={{0,192},{2,66},{16,208},{18,82},{32,224},{34,98},{48,240},{50,114}... | collective-permute-start | bytes 786440 | tf_op jit(solution)/shard_map/ppermute | solution.py:31
  98.4 1.9 %collective-permute-start.16 = (bf16[2,256,256]{2,1,0:T(8,128)(2,1)S(1)}, bf16[2,256,256]{2,1,0:T(8,128)(2,1)S(1)}, u32[]{:S(2)}, u32[]{:S(2)}) collective-permute-start(bf16[2,256,256]{2,1,0:T(8,128)(2,1)S(1)} %get-tuple-element.19.refs_4_), channel_id=1, source_target_pairs={{0,256},{256,0},{1,257},{257,1},{2,258},{258,2},{3,259},{259,3},{4... | collective-permute-start | bytes 786440 | tf_op jit(solution)/shard_map/ppermute | solution.py:21
  100.4 5.8 %collective-permute-start.17 = (bf16[2,256,256]{2,1,0:T(8,128)(2,1)S(1)}, bf16[2,256,256]{2,1,0:T(8,128)(2,1)S(1)}, u32[]{:S(2)}, u32[]{:S(2)}) collective-permute-start(bf16[2,256,256]{2,1,0:T(8,128)(2,1)S(1)} %get-tuple-element.19.refs_4_), channel_id=1, source_target_pairs={{0,4},{4,0},{8,12},{12,8},{1,5},{5,1},{9,13},{13,9},{2,6},{6,2},{1... | collective-permute-start | bytes 786440 | tf_op jit(solution)/shard_map/ppermute | solution.py:21
  106.2 4.3 %collective-permute-done.10.refs_6_ = bf16[2,256,256]{2,1,0:T(8,128)(2,1)S(1)} collective-permute-done((bf16[2,256,256]{2,1,0:T(8,128)(2,1)S(1)}, bf16[2,256,256]{2,1,0:T(8,128)(2,1)S(1)}, u32[]{:S(2)}, u32[]{:S(2)}) %collective-permute-start.10) | collective-permute-done | bytes 262176 | tf_op jit(solution)/shard_map/ppermute | solution.py:21
  110.5 9.1 %collective-permute-done.15.refs_6_ = bf16[2,256,256]{2,1,0:T(8,128)(2,1)S(1)} collective-permute-done((bf16[2,256,256]{2,1,0:T(8,128)(2,1)S(1)}, bf16[2,256,256]{2,1,0:T(8,128)(2,1)S(1)}, u32[]{:S(2)}, u32[]{:S(2)}) %collective-permute-start.15) | collective-permute-done | bytes 262176 | tf_op jit(solution)/shard_map/ppermute | solution.py:21
  119.6 2.1 %collective-permute-start.18 = (bf16[2,256,256]{2,1,0:T(8,128)(2,1)S(1)}, bf16[2,256,256]{2,1,0:T(8,128)(2,1)S(1)}, u32[]{:S(2)}, u32[]{:S(2)}) collective-permute-start(bf16[2,256,256]{2,1,0:T(8,128)(2,1)S(1)} %get-tuple-element.19.refs_4_), channel_id=1, source_target_pairs={{0,2},{2,0},{1,3},{3,1},{4,6},{6,4},{5,7},{7,5},{8,10},{10,8},{9,1... | collective-permute-start | bytes 786440 | tf_op jit(solution)/shard_map/ppermute | solution.py:21
  121.7 1.6 %shard_map.115.refs_3_ = f32[2,256,256]{2,1,0:T(8,128)S(1)} custom-call(s32[11]{0:T(128)S(1)} %pad_add_fusion.refs_0_, f32[3,9]{1,0:T(4,128)S(1)} %pad_maximum_fusion.1.refs_1_, bf16[12,256,256]{2,1,0:T(8,128)(2,1)S(1)} %copy-done, bf16[2,256,256]{2,1,0:T(8,128)(2,1)S(1)} %copy-done.1, bf16[2,256,256]{2,1,0:T(8,128)(2,1)S(1)} %get-tuple-element.19.refs_4_, ...), custom_call_target="tpu_custom_call" | custom-call | flops 402653184 | bytes 3932312 | tf_op jit(solution)/shard_map/pallas_call | solution.py:172
  123.4 1.9 %shard_map.116 = (f32[2,128,256]{2,1,0:T(8,128)S(1)}, bf16[2,128,256]{2,1,0:T(8,128)(2,1)S(1)}) custom-call(s32[11]{0:T(128)S(1)} %pad_add_fusion.refs_0_, f32[3,9]{1,0:T(4,128)S(1)} %pad_maximum_fusion.1.refs_1_, bf16[12,256,256]{2,1,0:T(8,128)(2,1)S(1)} %copy-done, f32[2,256,256]{2,1,0:T(8,128)S(1)} %shard_map.115.refs_3_, ...), custom_call_target="tpu_custom_call" | custom-call | flops 805306368 | bytes 4063384 | tf_op jit(solution)/shard_map/pallas_call | solution.py:172
  125.3 2.1 %collective-permute-start.19 = (bf16[2,128,256]{2,1,0:T(8,128)(2,1)S(1)}, bf16[2,128,256]{2,1,0:T(8,128)(2,1)S(1)}, u32[]{:S(2)}, u32[]{:S(2)}) collective-permute-start(bf16[2,128,256]{2,1,0:T(8,128)(2,1)S(1)} %get-tuple-element.21), channel_id=1, source_target_pairs={{0,1},{1,0},{2,3},{3,2},{4,5},{5,4},{6,7},{7,6},{8,9},{9,8},{10,11... | collective-permute-start | bytes 393224 | tf_op jit(solution)/shard_map/ppermute | solution.py:21
  127.4 6.2 %collective-permute-done.19 = bf16[2,128,256]{2,1,0:T(8,128)(2,1)S(1)} collective-permute-done((bf16[2,128,256]{2,1,0:T(8,128)(2,1)S(1)}, bf16[2,128,256]{2,1,0:T(8,128)(2,1)S(1)}, u32[]{:S(2)}, u32[]{:S(2)}) %collective-permute-start.19) | collective-permute-done | bytes 131104 | tf_op jit(solution)/shard_map/ppermute | solution.py:21
  133.7 0.9 select_add_fusion
  (42 shorter events, 3.4 us)
Async XLA Ops:
  0.6 63.4 %copy-start = (bf16[12,256,256]{2,1,0:T(8,128)(2,1)S(1)}, bf16[12,256,256]{2,1,0:T(8,128)(2,1)}, u32[]{:S(2)}) copy-start(bf16[12,256,256]{2,1,0:T(8,128)(2,1)} %refs_2_.7) | copy-start | bytes 4718596
  0.6 63.4 %copy-start.1 = (bf16[2,256,256]{2,1,0:T(8,128)(2,1)S(1)}, bf16[2,256,256]{2,1,0:T(8,128)(2,1)}, u32[]{:S(2)}) copy-start(bf16[2,256,256]{2,1,0:T(8,128)(2,1)} %refs_3_.3) | copy-start | bytes 786436
  1.9 8.6 %collective-permute-start = (bf16[2,128,256]{2,1,0:T(8,128)(2,1)S(1)}, bf16[2,128,256]{2,1,0:T(8,128)(2,1)S(1)}, u32[]{:S(2)}, u32[]{:S(2)}) collective-permute-start(bf16[2,128,256]{2,1,0:T(8,128)(2,1)S(1)} %get-tuple-element.29), channel_id=1, source_target_pairs={{0,1},{1,0},{2,3},{3,2},{4,5},{5,4},{6,7},{7,6},{8,9},{9,8},{10,11... | collective-permute-start | bytes 393224 | tf_op jit(solution)/shard_map/ppermute | solution.py:21
  10.6 32.8 %collective-permute-start.4 = (bf16[2,256,256]{2,1,0:T(8,128)(2,1)S(1)}, bf16[2,256,256]{2,1,0:T(8,128)(2,1)S(1)}, u32[]{:S(2)}, u32[]{:S(2)}) collective-permute-start(bf16[2,256,256]{2,1,0:T(8,128)(2,1)S(1)} %maximum_select_fusion.refs_4_.refs_3_), channel_id=1, source_target_pairs={{0,64},{2,130},{16,80},{18,146},{32,96},{34,162},{48,112},{50,178}... | collective-permute-start | bytes 786440 | tf_op jit(solution)/shard_map/ppermute | solution.py:31
  28.2 33.3 %collective-permute-start.1 = (bf16[2,256,256]{2,1,0:T(8,128)(2,1)S(1)}, bf16[2,256,256]{2,1,0:T(8,128)(2,1)S(1)}, u32[]{:S(2)}, u32[]{:S(2)}) collective-permute-start(bf16[2,256,256]{2,1,0:T(8,128)(2,1)S(1)} %maximum_select_fusion.refs_4_.refs_3_), channel_id=1, source_target_pairs={{0,16},{16,0},{32,48},{48,32},{64,80},{80,64},{96,112},{112,96},{1... | collective-permute-start | bytes 786440 | tf_op jit(solution)/shard_map/ppermute | solution.py:21
  30.8 21.3 %collective-permute-start.2 = (bf16[2,256,256]{2,1,0:T(8,128)(2,1)S(1)}, bf16[2,256,256]{2,1,0:T(8,128)(2,1)S(1)}, u32[]{:S(2)}, u32[]{:S(2)}) collective-permute-start(bf16[2,256,256]{2,1,0:T(8,128)(2,1)S(1)} %maximum_select_fusion.refs_4_.refs_3_), channel_id=1, source_target_pairs={{0,1},{1,0},{2,3},{3,2},{4,5},{5,4},{6,7},{7,6},{8,9},{9,8},{10,11... | collective-permute-start | bytes 786440 | tf_op jit(solution)/shard_map/ppermute | solution.py:21
  35.4 20.2 %collective-permute-start.3 = (bf16[2,256,256]{2,1,0:T(8,128)(2,1)S(1)}, bf16[2,256,256]{2,1,0:T(8,128)(2,1)S(1)}, u32[]{:S(2)}, u32[]{:S(2)}) collective-permute-start(bf16[2,256,256]{2,1,0:T(8,128)(2,1)S(1)} %maximum_select_fusion.refs_4_.refs_3_), channel_id=1, source_target_pairs={{0,8},{4,12},{8,0},{12,4},{1,9},{5,13},{9,1},{13,5},{2,10},{6,14},... | collective-permute-start | bytes 786440 | tf_op jit(solution)/shard_map/ppermute | solution.py:21
  40.3 21.8 %collective-permute-start.6 = (bf16[2,256,256]{2,1,0:T(8,128)(2,1)S(1)}, bf16[2,256,256]{2,1,0:T(8,128)(2,1)S(1)}, u32[]{:S(2)}, u32[]{:S(2)}) collective-permute-start(bf16[2,256,256]{2,1,0:T(8,128)(2,1)S(1)} %maximum_select_fusion.refs_4_.refs_3_), channel_id=1, source_target_pairs={{0,32},{16,48},{32,0},{48,16},{64,96},{80,112},{96,64},{112,80},{1... | collective-permute-start | bytes 786440 | tf_op jit(solution)/shard_map/ppermute | solution.py:21
  43.4 22.2 %collective-permute-start.5 = (bf16[2,256,256]{2,1,0:T(8,128)(2,1)S(1)}, bf16[2,256,256]{2,1,0:T(8,128)(2,1)S(1)}, u32[]{:S(2)}, u32[]{:S(2)}) collective-permute-start(bf16[2,256,256]{2,1,0:T(8,128)(2,1)S(1)} %broadcast_select_fusion.1), channel_id=1, source_target_pairs={{0,192},{2,66},{16,208},{18,82},{32,224},{34,98},{48,240},{50,114}... | collective-permute-start | bytes 786440 | tf_op jit(solution)/shard_map/ppermute | solution.py:31
  52.1 13.6 %collective-permute-start.7 = (bf16[2,256,256]{2,1,0:T(8,128)(2,1)S(1)}, bf16[2,256,256]{2,1,0:T(8,128)(2,1)S(1)}, u32[]{:S(2)}, u32[]{:S(2)}) collective-permute-start(bf16[2,256,256]{2,1,0:T(8,128)(2,1)S(1)} %maximum_select_fusion.refs_4_.refs_3_), channel_id=1, source_target_pairs={{0,256},{256,0},{1,257},{257,1},{2,258},{258,2},{3,259},{259,3},{4... | collective-permute-start | bytes 786440 | tf_op jit(solution)/shard_map/ppermute | solution.py:21
  55.6 10.1 %collective-permute-start.8 = (bf16[2,256,256]{2,1,0:T(8,128)(2,1)S(1)}, bf16[2,256,256]{2,1,0:T(8,128)(2,1)S(1)}, u32[]{:S(2)}, u32[]{:S(2)}) collective-permute-start(bf16[2,256,256]{2,1,0:T(8,128)(2,1)S(1)} %maximum_select_fusion.refs_4_.refs_3_), channel_id=1, source_target_pairs={{0,4},{4,0},{8,12},{12,8},{1,5},{5,1},{9,13},{13,9},{2,6},{6,2},{1... | collective-permute-start | bytes 786440 | tf_op jit(solution)/shard_map/ppermute | solution.py:21
  62.1 3.6 %collective-permute-start.9 = (bf16[2,256,256]{2,1,0:T(8,128)(2,1)S(1)}, bf16[2,256,256]{2,1,0:T(8,128)(2,1)S(1)}, u32[]{:S(2)}, u32[]{:S(2)}) collective-permute-start(bf16[2,256,256]{2,1,0:T(8,128)(2,1)S(1)} %maximum_select_fusion.refs_4_.refs_3_), channel_id=1, source_target_pairs={{0,2},{2,0},{1,3},{3,1},{4,6},{6,4},{5,7},{7,5},{8,10},{10,8},{9,1... | collective-permute-start | bytes 786440 | tf_op jit(solution)/shard_map/ppermute | solution.py:21
  67.7 26.8 %collective-permute-start.13 = (bf16[2,256,256]{2,1,0:T(8,128)(2,1)S(1)}, bf16[2,256,256]{2,1,0:T(8,128)(2,1)S(1)}, u32[]{:S(2)}, u32[]{:S(2)}) collective-permute-start(bf16[2,256,256]{2,1,0:T(8,128)(2,1)S(1)} %get-tuple-element.19.refs_4_), channel_id=1, source_target_pairs={{0,64},{2,130},{16,80},{18,146},{32,96},{34,162},{48,112},{50,178}... | collective-permute-start | bytes 786440 | tf_op jit(solution)/shard_map/ppermute | solution.py:31
  80.3 18.2 %collective-permute-start.11 = (bf16[2,256,256]{2,1,0:T(8,128)(2,1)S(1)}, bf16[2,256,256]{2,1,0:T(8,128)(2,1)S(1)}, u32[]{:S(2)}, u32[]{:S(2)}) collective-permute-start(bf16[2,256,256]{2,1,0:T(8,128)(2,1)S(1)} %get-tuple-element.19.refs_4_), channel_id=1, source_target_pairs={{0,1},{1,0},{2,3},{3,2},{4,5},{5,4},{6,7},{7,6},{8,9},{9,8},{10,11... | collective-permute-start | bytes 786440 | tf_op jit(solution)/shard_map/ppermute | solution.py:21
  84.5 15.9 %collective-permute-start.12 = (bf16[2,256,256]{2,1,0:T(8,128)(2,1)S(1)}, bf16[2,256,256]{2,1,0:T(8,128)(2,1)S(1)}, u32[]{:S(2)}, u32[]{:S(2)}) collective-permute-start(bf16[2,256,256]{2,1,0:T(8,128)(2,1)S(1)} %get-tuple-element.19.refs_4_), channel_id=1, source_target_pairs={{0,8},{4,12},{8,0},{12,4},{1,9},{5,13},{9,1},{13,5},{2,10},{6,14},... | collective-permute-start | bytes 786440 | tf_op jit(solution)/shard_map/ppermute | solution.py:21
  89.9 20.6 %collective-permute-start.10 = (bf16[2,256,256]{2,1,0:T(8,128)(2,1)S(1)}, bf16[2,256,256]{2,1,0:T(8,128)(2,1)S(1)}, u32[]{:S(2)}, u32[]{:S(2)}) collective-permute-start(bf16[2,256,256]{2,1,0:T(8,128)(2,1)S(1)} %get-tuple-element.19.refs_4_), channel_id=1, source_target_pairs={{0,16},{16,0},{32,48},{48,32},{64,80},{80,64},{96,112},{112,96},{1... | collective-permute-start | bytes 786440 | tf_op jit(solution)/shard_map/ppermute | solution.py:21
  91.8 27.8 %collective-permute-start.15 = (bf16[2,256,256]{2,1,0:T(8,128)(2,1)S(1)}, bf16[2,256,256]{2,1,0:T(8,128)(2,1)S(1)}, u32[]{:S(2)}, u32[]{:S(2)}) collective-permute-start(bf16[2,256,256]{2,1,0:T(8,128)(2,1)S(1)} %get-tuple-element.19.refs_4_), channel_id=1, source_target_pairs={{0,32},{16,48},{32,0},{48,16},{64,96},{80,112},{96,64},{112,80},{1... | collective-permute-start | bytes 786440 | tf_op jit(solution)/shard_map/ppermute | solution.py:21
  94.5 28.8 %collective-permute-start.14 = (bf16[2,256,256]{2,1,0:T(8,128)(2,1)S(1)}, bf16[2,256,256]{2,1,0:T(8,128)(2,1)S(1)}, u32[]{:S(2)}, u32[]{:S(2)}) collective-permute-start(bf16[2,256,256]{2,1,0:T(8,128)(2,1)S(1)} %broadcast_select_fusion), channel_id=1, source_target_pairs={{0,192},{2,66},{16,208},{18,82},{32,224},{34,98},{48,240},{50,114}... | collective-permute-start | bytes 786440 | tf_op jit(solution)/shard_map/ppermute | solution.py:31
  98.4 24.9 %collective-permute-start.16 = (bf16[2,256,256]{2,1,0:T(8,128)(2,1)S(1)}, bf16[2,256,256]{2,1,0:T(8,128)(2,1)S(1)}, u32[]{:S(2)}, u32[]{:S(2)}) collective-permute-start(bf16[2,256,256]{2,1,0:T(8,128)(2,1)S(1)} %get-tuple-element.19.refs_4_), channel_id=1, source_target_pairs={{0,256},{256,0},{1,257},{257,1},{2,258},{258,2},{3,259},{259,3},{4... | collective-permute-start | bytes 786440 | tf_op jit(solution)/shard_map/ppermute | solution.py:21
  100.4 23.0 %collective-permute-start.17 = (bf16[2,256,256]{2,1,0:T(8,128)(2,1)S(1)}, bf16[2,256,256]{2,1,0:T(8,128)(2,1)S(1)}, u32[]{:S(2)}, u32[]{:S(2)}) collective-permute-start(bf16[2,256,256]{2,1,0:T(8,128)(2,1)S(1)} %get-tuple-element.19.refs_4_), channel_id=1, source_target_pairs={{0,4},{4,0},{8,12},{12,8},{1,5},{5,1},{9,13},{13,9},{2,6},{6,2},{1... | collective-permute-start | bytes 786440 | tf_op jit(solution)/shard_map/ppermute | solution.py:21
  119.6 3.8 %collective-permute-start.18 = (bf16[2,256,256]{2,1,0:T(8,128)(2,1)S(1)}, bf16[2,256,256]{2,1,0:T(8,128)(2,1)S(1)}, u32[]{:S(2)}, u32[]{:S(2)}) collective-permute-start(bf16[2,256,256]{2,1,0:T(8,128)(2,1)S(1)} %get-tuple-element.19.refs_4_), channel_id=1, source_target_pairs={{0,2},{2,0},{1,3},{3,1},{4,6},{6,4},{5,7},{7,5},{8,10},{10,8},{9,1... | collective-permute-start | bytes 786440 | tf_op jit(solution)/shard_map/ppermute | solution.py:21
  125.3 8.4 %copy-start.2 = (f32[2,128,256]{2,1,0:T(8,128)S(1)}, f32[2,128,256]{2,1,0:T(8,128)}, u32[]{:S(2)}) copy-start(f32[2,128,256]{2,1,0:T(8,128)} %param.11) | copy-start | bytes 786436
  125.3 8.4 %copy-start.3 = (f32[2,128,256]{2,1,0:T(8,128)S(1)}, f32[2,128,256]{2,1,0:T(8,128)}, u32[]{:S(2)}) copy-start(f32[2,128,256]{2,1,0:T(8,128)} %param.10) | copy-start | bytes 786436
  125.3 8.3 %collective-permute-start.19 = (bf16[2,128,256]{2,1,0:T(8,128)(2,1)S(1)}, bf16[2,128,256]{2,1,0:T(8,128)(2,1)S(1)}, u32[]{:S(2)}, u32[]{:S(2)}) collective-permute-start(bf16[2,128,256]{2,1,0:T(8,128)(2,1)S(1)} %get-tuple-element.21), channel_id=1, source_target_pairs={{0,1},{1,0},{2,3},{3,2},{4,5},{5,4},{6,7},{7,6},{8,9},{9,8},{10,11... | collective-permute-start | bytes 393224 | tf_op jit(solution)/shard_map/ppermute | solution.py:21
